TPU v7x, 512 devices: a whole 4x4x16 slice. The times are simulated.
512 devices in a mesh: dp: 32 (over x, y, core), seq: 16 (over z).
Axes of the slice: x: 4, y: 4, z: 16, core: 2. Of those that a mesh axis runs over, the one named last changes fastest.
Arguments:
- inputs: bfloat16 [32, 2, 1024, 1024], P('dp', None, 'seq'), may hold values from -6 to 6
- cotangent: bfloat16 [32, 2, 1024, 1024], P('dp', None, 'seq'), may hold values from -6 to 6
- lengths: int32 [32, 2, 3], P('dp'), may hold values from 1 to 512, 1024 in all within a row
- item_ids: int32 [32, 2, 1024], P('dp', None, 'seq'), may hold values from 0 to 8191, as said below
- owner_row: int32 [8192], replicated, may hold values from 0 to 8191, as said below
- w_project: bfloat16 [1024, 4096], P('dp', 'seq'), may hold values from -0.1875 to 0.1875
- w_output: bfloat16 [1024, 1024], P('seq', 'dp'), may hold values from -0.1875 to 0.1875
Outputs:
- grad_w_project: float32 [1024, 4096], P('dp', 'seq')
- grad_w_output: float32 [1024, 1024], P('seq', 'dp')
- grad_table: float32 [8192, 1024], P('dp', 'seq')
Inputs may be any that keep to these rules, and one draw needn't show every extreme that they name: `item_ids`: row owner_row[i] of the item table is held by dp index owner_row[i] // 256. The 128 positions of one device (both packs) hold items of at most 8 positions for any one owner. `owner_row`: A permutation of the rows of the item table.
All inputs are finite; a program needn't handle non-finite values.
Results may differ from a plain program's by a relative error of at most 0.02.
Values may be sent and summed in bfloat16 or wider, within the bound.
No kernel may reach another device: no remote copies, remote signals or barrier semaphores. Data moves between devices by JAX's collectives and lax.ppermute only.
A program may use at most 64 MiB of HBM per device.

v0:
```python
import jax
import jax.numpy as jnp
from jax import lax
from jax.sharding import PartitionSpec as P

HEADS = 8
HEAD_DIM = 128


norm_floor = 1.0


def partner(value, axis, bit):
    mask = 2**bit
    pairs = [(source, source ^ mask) for source in range(lax.axis_size(axis))]
    return lax.ppermute(value, axis, pairs)


def silu_grad(values):
    sigma = jax.nn.sigmoid(values)
    return sigma * (1.0 + values * (1.0 - sigma))


def pick_half(block, parity, half_width):
    shaped = block.reshape(block.shape[0], 2, half_width)
    kept = lax.dynamic_index_in_dim(shaped, parity, 1, keepdims=False)
    other = lax.dynamic_index_in_dim(shaped, 1 - parity, 1, keepdims=False)
    return (kept, other)


def per_device(inputs, cotangent, lengths, item_ids, owner_row, w_project, w_output):
    f32 = jnp.float32
    bf16 = jnp.bfloat16
    n_seq = lax.axis_size("seq")
    n_dp = lax.axis_size("dp")
    half = inputs.shape[2]
    width = inputs.shape[3]
    head_dim = HEAD_DIM
    heads_dev = 2 * HEADS // n_seq
    length = n_seq * half
    parity = lax.axis_index("seq") % 2
    local_x = inputs[0]
    local_dy = cotangent[0]
    whole_x, whole_dy = (
        lax.all_gather(local_x, "seq", axis=1, tiled=True),
        lax.all_gather(local_dy, "seq", axis=1, tiled=True),
    )
    pack_x = lax.dynamic_index_in_dim(whole_x, parity, 0, keepdims=False)
    pack_dy = lax.dynamic_index_in_dim(whole_dy, parity, 0, keepdims=False)
    proj_rows, out_cols = (
        lax.all_gather(w_project, "dp", axis=0, tiled=True),
        lax.all_gather(w_output, "dp", axis=1, tiled=True),
    )
    proj_mate, out_mate = partner((proj_rows, out_cols), "seq", 0)
    is_first = parity == 0
    proj_head = jnp.concatenate(
        [jnp.where(is_first, proj_rows, proj_mate), jnp.where(is_first, proj_mate, proj_rows)],
        axis=1,
    )
    out_head = jnp.concatenate(
        [jnp.where(is_first, out_cols, out_mate), jnp.where(is_first, out_mate, out_cols)], axis=0
    )
    pack_lens = lax.dynamic_index_in_dim(lengths[0], parity, 0, keepdims=False)
    ends = jnp.cumsum(pack_lens)
    positions = jnp.arange(length, dtype=jnp.int32)
    segment = jnp.sum((positions[:, None] >= ends[None, :]).astype(jnp.int32), axis=1)
    z_pre = jnp.dot(pack_x, proj_head, preferred_element_type=f32).reshape(
        length, heads_dev, 4, head_dim
    )
    acted = jax.nn.silu(z_pre).astype(bf16)
    gating = acted[:, :, 0]
    value_part = acted[:, :, 1]
    queries = acted[:, :, 2]
    key_part = acted[:, :, 3]
    scale = head_dim ** (-0.5)
    middle = length // 2
    tiles = [(0, middle, 0, middle), (middle, length - middle, 0, length)]
    saved_scores = []
    saved_masks = []
    saved_attn = []
    mixed_parts = []
    for tile in tiles:
        row_start, row_count, col_start, col_count = tile
        row_pos = positions[row_start : row_start + row_count]
        col_pos = positions[col_start : col_start + col_count]
        masked = (
            segment[row_start : row_start + row_count][:, None]
            == segment[col_start : col_start + col_count][None, :]
        ) & (col_pos[None, :] <= row_pos[:, None])
        scores = (
            jnp.einsum(
                "qhe,khe->hqk",
                queries[row_start : row_start + row_count],
                key_part[col_start : col_start + col_count],
                preferred_element_type=f32,
            )
            * scale
        )
        attn = jnp.where(masked[None], jax.nn.silu(scores), 0.0).astype(bf16)
        saved_scores.append(scores)
        saved_masks.append(masked)
        saved_attn.append(attn)
        mixed_parts.append(
            jnp.einsum(
                "hqk,khe->qhe",
                attn,
                value_part[col_start : col_start + col_count],
                preferred_element_type=f32,
            )
        )
    mixed = jnp.concatenate(mixed_parts, axis=0)
    centred = mixed - jnp.mean(mixed, axis=-1, keepdims=True)
    inv_std = lax.rsqrt(jnp.mean(centred * centred, axis=-1, keepdims=True) + norm_floor)
    normed = centred * inv_std
    gated = (normed * gating).astype(bf16)
    d_gated = jnp.einsum(
        "qd,hed->qhe",
        pack_dy,
        out_head.reshape(heads_dev, head_dim, width),
        preferred_element_type=f32,
    )
    d_gate = d_gated * normed
    d_normed = d_gated * gating
    d_mixed = (
        inv_std
        * (
            d_normed
            - jnp.mean(d_normed, axis=-1, keepdims=True)
            - normed * jnp.mean(d_normed * normed, axis=-1, keepdims=True)
        )
    ).astype(bf16)
    d_value = jnp.zeros((length, heads_dev, head_dim), f32)
    d_query = jnp.zeros((length, heads_dev, head_dim), f32)
    d_key = jnp.zeros((length, heads_dev, head_dim), f32)
    for place in range(len(tiles)):
        row_start, row_count, col_start, col_count = tiles[place]
        grads_here = d_mixed[row_start : row_start + row_count]
        d_attn = jnp.einsum(
            "qhe,khe->hqk",
            grads_here,
            value_part[col_start : col_start + col_count],
            preferred_element_type=f32,
        )
        d_scores = (
            jnp.where(saved_masks[place][None], d_attn * silu_grad(saved_scores[place]), 0.0)
            * scale
        ).astype(bf16)
        d_value = d_value.at[col_start : col_start + col_count].add(
            jnp.einsum("hqk,qhe->khe", saved_attn[place], grads_here, preferred_element_type=f32)
        )
        d_query = d_query.at[row_start : row_start + row_count].add(
            jnp.einsum(
                "hqk,khe->qhe",
                d_scores,
                key_part[col_start : col_start + col_count],
                preferred_element_type=f32,
            )
        )
        d_key = d_key.at[col_start : col_start + col_count].add(
            jnp.einsum(
                "hqk,qhe->khe",
                d_scores,
                queries[row_start : row_start + row_count],
                preferred_element_type=f32,
            )
        )
    d_act = jnp.stack([d_gate, d_value, d_query, d_key], axis=2)
    d_z = (d_act * silu_grad(z_pre)).astype(bf16).reshape(length, heads_dev * 4 * head_dim)
    head_parts = jnp.einsum(
        "lhc,dhc->lhd",
        d_z.reshape(length, heads_dev, 4 * head_dim),
        proj_head.reshape(width, heads_dev, 4 * head_dim),
        preferred_element_type=f32,
    ).astype(bf16)
    returned = lax.all_to_all(
        head_parts.reshape(n_seq, half, heads_dev, width),
        "seq",
        split_axis=0,
        concat_axis=0,
        tiled=True,
    )
    summed = jnp.sum(
        returned.astype(f32).reshape(n_seq // 2, 2, half, heads_dev, width), axis=(0, 3)
    )
    token_grad = (local_dy.astype(f32) + summed).astype(bf16)
    proj_cols = heads_dev * 4 * head_dim
    out_rows = heads_dev * head_dim
    gated_flat = gated.reshape(length, out_rows)
    contract = (((0,), (0,)), ((), ()))
    reduced = lax.psum_scatter(
        jnp.concatenate(
            [
                lax.dot_general(pack_x, d_z, contract, preferred_element_type=f32),
                lax.dot_general(pack_dy, gated_flat, contract, preferred_element_type=f32),
            ],
            axis=1,
        ).astype(jnp.bfloat16),
        "dp",
        scatter_dimension=0,
        tiled=True,
    ).astype(jnp.float32)
    proj_keep, proj_send = pick_half(reduced[:, :proj_cols], parity, proj_cols // 2)
    out_keep, out_send = pick_half(reduced[:, proj_cols:], parity, out_rows // 2)
    proj_got, out_got = (
        partner(proj_send.astype(jnp.bfloat16), "seq", 0).astype(proj_send.dtype),
        partner(out_send.astype(jnp.bfloat16), "seq", 0).astype(out_send.dtype),
    )
    grad_proj = proj_keep + proj_got
    grad_out = (out_keep + out_got).T
    tokens_dev = 2 * half
    cap = max(2, 4 * half // n_dp)
    rows_dev = owner_row.shape[0] // n_dp
    flat_grad = token_grad.reshape(tokens_dev, width)
    table_rows = jnp.take(owner_row, item_ids[0].reshape(tokens_dev))
    owners = table_rows // rows_dev
    local_row = table_rows % rows_dev
    hits = owners[:, None] == jnp.arange(n_dp, dtype=jnp.int32)[None, :]
    ranks = jnp.cumsum(hits.astype(jnp.int32), axis=0) - 1
    slot_index = jnp.sum(jnp.where(hits, ranks, 0), axis=1)
    target = owners * cap + slot_index
    placed = target[None, :] == jnp.arange(n_dp * cap, dtype=jnp.int32)[:, None]
    send_rows = jnp.dot(placed.astype(bf16), flat_grad, preferred_element_type=f32).astype(bf16)
    send_tags = jnp.where(
        jnp.any(placed, axis=1), jnp.sum(jnp.where(placed, local_row[None, :], 0), axis=1), -1
    )
    got_rows, got_tags = (
        lax.all_to_all(
            send_rows.reshape(n_dp, cap, width), "dp", split_axis=0, concat_axis=0, tiled=True
        ),
        lax.all_to_all(send_tags.reshape(n_dp, cap), "dp", split_axis=0, concat_axis=0, tiled=True),
    )
    selector = (
        got_tags.reshape(n_dp * cap)[None, :] == jnp.arange(rows_dev, dtype=jnp.int32)[:, None]
    ).astype(bf16)
    owner_part = jnp.dot(selector, got_rows.reshape(n_dp * cap, width), preferred_element_type=f32)
    grad_table = lax.psum_scatter(
        owner_part.astype(jnp.bfloat16), "seq", scatter_dimension=1, tiled=True
    ).astype(jnp.float32)
    return (grad_proj, grad_out, grad_table)


def solution(mesh):
    return jax.shard_map(
        per_device,
        mesh=mesh,
        in_specs=(
            P("dp", None, "seq", None),
            P("dp", None, "seq", None),
            P("dp", None, None),
            P("dp", None, "seq"),
            P(),
            P("dp", "seq"),
            P("seq", "dp"),
        ),
        out_specs=(P("dp", "seq"), P("seq", "dp"), P("dp", "seq")),
        check_vma=False,
    )
```

profile of v0, /device:TPU:4, one launch (start us, length us, event | category | flops | bytes accessed | tf_op | source)
XLA Modules:
  0.0 394.5 jit_solution(4380948757346964119)
XLA Ops:
  8.7 26.2 %all_gather.14 = bf16[64,1024]{0,1:T(8,128)(2,1)S(1)} all-gather(bf16[64,32]{0,1:T(8,128)(2,1)} %param.29), channel_id=1, replica_groups=mesh['dp'=32,'seq'=16] {'dp'}, dimensions={1}, use_global_device_ids=true | all-gather | bytes 135168 | tf_op jit(solution)/shard_map/all_gather | solution.py:52
  34.9 2.2 collective-permute-start
  37.2 23.9 %all_gather.15 = bf16[1024,256]{1,0:T(8,128)(2,1)S(1)} all-gather(bf16[32,256]{1,0:T(8,128)(2,1)} %param.28), channel_id=1, replica_groups=mesh['dp'=32,'seq'=16] {'dp'}, dimensions={0}, use_global_device_ids=true | all-gather | bytes 540672 | tf_op jit(solution)/shard_map/all_gather | solution.py:51
  61.1 4.1 %collective-permute-start.1 = (bf16[1024,256]{1,0:T(8,128)(2,1)S(1)}, bf16[1024,256]{1,0:T(8,128)(2,1)S(1)}, u32[]{:S(2)}, u32[]{:S(2)}) collective-permute-start(bf16[1024,256]{1,0:T(8,128)(2,1)S(1)} %all_gather.15), channel_id=1, source_target_pairs={{0,1},{1,0},{2,3},{3,2},{4,5},{5,4},{6,7},{7,6},{8,9},{9,8},{10,11... | collective-permute-start | bytes 1572872 | tf_op jit(solution)/shard_map/ppermute | solution.py:16
  67.0 21.7 %collective-permute-done.1 = bf16[1024,256]{1,0:T(8,128)(2,1)S(1)} collective-permute-done((bf16[1024,256]{1,0:T(8,128)(2,1)S(1)}, bf16[1024,256]{1,0:T(8,128)(2,1)S(1)}, u32[]{:S(2)}, u32[]{:S(2)}) %collective-permute-start.1) | collective-permute-done | bytes 524320 | tf_op jit(solution)/shard_map/ppermute | solution.py:16
  89.5 14.9 %all-gather.5.cloned.1.call-done = bf16[1,2,1024,1024]{3,2,1,0:T(8,128)(2,1)} async-done(((bf16[1,2,64,1024]{3,2,1,0:T(8,128)(2,1)}), bf16[1,2,1024,1024]{3,2,1,0:T(8,128)(2,1)}) %all-gather.5.cloned.1.call-update) | async-done | bytes 4194320 | tf_op jit(solution)/shard_map/all_gather | solution.py:45
  104.4 3.0 fusion.7
  109.9 2.3 select_convert_fusion
  113.4 67.3 %all-gather.7.cloned.1.call-done = bf16[1,2,1024,1024]{3,2,1,0:T(8,128)(2,1)} async-done(((bf16[1,2,64,1024]{3,2,1,0:T(8,128)(2,1)}), bf16[1,2,1024,1024]{3,2,1,0:T(8,128)(2,1)}) %all-gather.7.cloned.1.call-update) | async-done | bytes 4194320 | tf_op jit(solution)/shard_map/all_gather | solution.py:46
  180.7 2.7 fusion.46
  190.5 2.7 convolution_convert_fusion
  193.2 7.6 %all-to-all-start.1 = ((bf16[16,64,1,1024]{3,1,2,0:T(8,128)(2,1)}), bf16[16,64,1,1024]{3,1,2,0:T(8,128)(2,1)S(1)}, u32[]{:S(2)}, u32[]{:S(2)}) async-start(bf16[16,64,1,1024]{3,1,2,0:T(8,128)(2,1)} %bitcast.189), calls=%async_computation.1 | async-start | bytes 4194304 | tf_op jit(solution)/shard_map/all_to_all | solution.py:175
  202.9 2.2 fusion.25
  205.1 2.9 fusion.14
  209.1 2.4 copy.30
  212.5 71.5 %all-to-all-done.1 = bf16[16,64,1,1024]{3,1,2,0:T(8,128)(2,1)S(1)} async-done(((bf16[16,64,1,1024]{3,1,2,0:T(8,128)(2,1)}), bf16[16,64,1,1024]{3,1,2,0:T(8,128)(2,1)S(1)}, u32[]{:S(2)}, u32[]{:S(2)}) %all-to-all-start.1) | async-done | bytes 2097184 | tf_op jit(solution)/shard_map/all_to_all | solution.py:175
  284.0 7.5 %all-to-all-start = ((s32[32,1,8]{2,1,0:T(1,128)}), s32[32,1,8]{2,1,0:T(1,128)S(1)}, u32[]{:S(2)}, u32[]{:S(2)}) async-start(s32[32,1,8]{2,1,0:T(1,128)} %bitcast.49), calls=%async_computation | async-start | bytes 32768 | tf_op jit(solution)/shard_map/all_to_all | solution.py:230
  293.1 3.7 all-to-all-done
  296.7 5.9 %all-to-all-start.2 = ((bf16[32,8,1024]{2,1,0:T(8,128)(2,1)}), bf16[32,8,1024]{2,1,0:T(8,128)(2,1)S(1)}, u32[]{:S(2)}, u32[]{:S(2)}) async-start(bf16[32,8,1024]{2,1,0:T(8,128)(2,1)} %fusion.20), calls=%async_computation.2 | async-start | bytes 1048576 | tf_op jit(solution)/shard_map/all_to_all | solution.py:227
  304.0 8.5 %all-to-all-done.2 = bf16[32,8,1024]{2,1,0:T(8,128)(2,1)S(1)} async-done(((bf16[32,8,1024]{2,1,0:T(8,128)(2,1)}), bf16[32,8,1024]{2,1,0:T(8,128)(2,1)S(1)}, u32[]{:S(2)}, u32[]{:S(2)}) %all-to-all-start.2) | async-done | bytes 524320 | tf_op jit(solution)/shard_map/all_to_all | solution.py:227
  315.9 3.6 collective-permute-start.3
  320.7 2.3 collective-permute-start.2
  323.6 2.8 collective-permute-done.2
  327.0 59.6 %reduce-scatter.5.cloned.1.call-done = bf16[256,64]{0,1:T(8,128)(2,1)} async-done(((bf16[256,1024]{0,1:T(8,128)(2,1)}), bf16[256,64]{0,1:T(8,128)(2,1)}) %reduce-scatter.5.cloned.1.call-update) | async-done | bytes 32784 | tf_op jit(solution)/shard_map/reduce_scatter | solution.py:236
  (108 shorter events, 28.8 us)
Async XLA Ops:
  7.2 194.1 %copy-start = (s32[8192]{0:T(1024)S(1)}, s32[8192]{0:T(1024)}, u32[]{:S(2)}) copy-start(s32[8192]{0:T(1024)} %param.27) | copy-start | bytes 98308
  7.2 97.2 %all-gather.5.cloned.1.call-start = ((), (), s32[]{:S(2)}) async-start(), calls=%async_computation.6 | async-start | bytes 4456448 | tf_op jit(solution)/shard_map/all_gather | solution.py:45
  7.9 172.8 %all-gather.7.cloned.1.call-start = ((), (), s32[]{:S(2)}) async-start(), calls=%async_computation.7 | async-start | bytes 4456448 | tf_op jit(solution)/shard_map/all_gather | solution.py:46
  34.9 31.3 %collective-permute-start = (bf16[64,1024]{0,1:T(8,128)(2,1)S(1)}, bf16[64,1024]{0,1:T(8,128)(2,1)S(1)}, u32[]{:S(2)}, u32[]{:S(2)}) collective-permute-start(bf16[64,1024]{0,1:T(8,128)(2,1)S(1)} %all_gather.14), channel_id=1, source_target_pairs={{0,1},{1,0},{2,3},{3,2},{4,5},{5,4},{6,7},{7,6},{8,9},{9,8},{10,11... | collective-permute-start | bytes 393224 | tf_op jit(solution)/shard_map/ppermute | solution.py:16
  61.1 27.6 %collective-permute-start.1 = (bf16[1024,256]{1,0:T(8,128)(2,1)S(1)}, bf16[1024,256]{1,0:T(8,128)(2,1)S(1)}, u32[]{:S(2)}, u32[]{:S(2)}) collective-permute-start(bf16[1024,256]{1,0:T(8,128)(2,1)S(1)} %all_gather.15), channel_id=1, source_target_pairs={{0,1},{1,0},{2,3},{3,2},{4,5},{5,4},{6,7},{7,6},{8,9},{9,8},{10,11... | collective-permute-start | bytes 1572872 | tf_op jit(solution)/shard_map/ppermute | solution.py:16
  89.5 17.9 %copy-start.8 = (bf16[1024,256]{1,0:T(8,128)(2,1)}, bf16[1024,256]{1,0:T(8,128)(2,1)S(1)}, u32[]{:S(2)}) copy-start(bf16[1024,256]{1,0:T(8,128)(2,1)S(1)} %get-tuple-element.97) | copy-start | bytes 1572868
  108.0 4.2 %copy-start.1 = (bf16[1024,1,4,128]{0,3,2,1:T(8,128)(2,1)}, bf16[1024,1,4,128]{0,3,2,1:T(8,128)(2,1)S(1)}, u32[]{:S(2)}) copy-start(bf16[1024,1,4,128]{0,3,2,1:T(8,128)(2,1)S(1)} %multiply_convert_fusion.1) | copy-start | bytes 3145732
  180.7 2.7 copy-start.2
  183.4 1.2 copy-start.12
  184.6 1.6 copy-start.13
  186.2 1.6 copy-start.4
  189.3 1.0 copy-start.9
  189.3 1.2 copy-start.10
  190.5 2.7 copy-start.5
  193.1 7.9 %copy-start.11 = (s32[1,2,64]{2,1,0:T(2,128)S(1)}, s32[1,2,64]{2,1,0:T(2,128)}, u32[]{:S(2)}) copy-start(s32[1,2,64]{2,1,0:T(2,128)} %param.26) | copy-start | bytes 1540
  193.2 90.9 %all-to-all-start.1 = ((bf16[16,64,1,1024]{3,1,2,0:T(8,128)(2,1)}), bf16[16,64,1,1024]{3,1,2,0:T(8,128)(2,1)S(1)}, u32[]{:S(2)}, u32[]{:S(2)}) async-start(bf16[16,64,1,1024]{3,1,2,0:T(8,128)(2,1)} %bitcast.189), calls=%async_computation.1 | async-start | bytes 4194304 | tf_op jit(solution)/shard_map/all_to_all | solution.py:175
  200.8 114.2 %reduce-scatter.7.cloned.1.call-start = ((), (), s32[]{:S(2)}) async-start(), calls=%async_computation.8 | async-start | bytes 1351680
  202.7 2.4 copy-start.6
  211.6 80.3 %copy-start.7 = (bf16[1,2,64,1024]{3,2,1,0:T(8,128)(2,1)S(1)}, bf16[1,2,64,1024]{3,2,1,0:T(8,128)(2,1)}, u32[]{:S(2)}) copy-start(bf16[1,2,64,1024]{3,2,1,0:T(8,128)(2,1)} %param.24) | copy-start | bytes 786436
  284.0 12.7 %all-to-all-start = ((s32[32,1,8]{2,1,0:T(1,128)}), s32[32,1,8]{2,1,0:T(1,128)S(1)}, u32[]{:S(2)}, u32[]{:S(2)}) async-start(s32[32,1,8]{2,1,0:T(1,128)} %bitcast.49), calls=%async_computation | async-start | bytes 32768 | tf_op jit(solution)/shard_map/all_to_all | solution.py:230
  296.7 15.8 %all-to-all-start.2 = ((bf16[32,8,1024]{2,1,0:T(8,128)(2,1)}), bf16[32,8,1024]{2,1,0:T(8,128)(2,1)S(1)}, u32[]{:S(2)}, u32[]{:S(2)}) async-start(bf16[32,8,1024]{2,1,0:T(8,128)(2,1)} %fusion.20), calls=%async_computation.2 | async-start | bytes 1048576 | tf_op jit(solution)/shard_map/all_to_all | solution.py:227
  302.7 83.9 %reduce-scatter.5.cloned.1.call-start = ((), (), s32[]{:S(2)}) async-start(), calls=%async_computation.5 | async-start | bytes 557056 | tf_op jit(solution)/shard_map/reduce_scatter | solution.py:236
  315.9 7.1 %collective-permute-start.3 = (bf16[32,64]{1,0:T(8,128)(2,1)S(1)}, bf16[32,64]{1,0:T(8,128)(2,1)S(1)}, u32[]{:S(2)}, u32[]{:S(2)}) collective-permute-start(bf16[32,64]{1,0:T(8,128)(2,1)S(1)} %bitcast.195), channel_id=1, source_target_pairs={{0,1},{1,0},{2,3},{3,2},{4,5},{5,4},{6,7},{7,6},{8,9},{9,8},{10,11... | collective-permute-start | bytes 12296 | tf_op jit(solution)/shard_map/ppermute | solution.py:16
  320.7 5.6 %collective-permute-start.2 = (bf16[32,256]{1,0:T(8,128)(2,1)S(1)}, bf16[32,256]{1,0:T(8,128)(2,1)S(1)}, u32[]{:S(2)}, u32[]{:S(2)}) collective-permute-start(bf16[32,256]{1,0:T(8,128)(2,1)S(1)} %bitcast.194), channel_id=1, source_target_pairs={{0,1},{1,0},{2,3},{3,2},{4,5},{5,4},{6,7},{7,6},{8,9},{9,8},{10,11... | collective-permute-start | bytes 49160 | tf_op jit(solution)/shard_map/ppermute | solution.py:16
  (1 other events, 1.0 us)
Sparse Core Ops, SparseCore 0:
  10.1 94.2 all-gather.4
  106.5 74.1 all-gather.6
  211.7 103.2 reduce-scatter.6
  317.9 68.6 reduce-scatter.4
where the time goes:
time: 395 us
  waiting for transfers between devices  253 us (64%)
  blocking collectives  50.2 us (13%)
  starting transfers between devices  33.6 us (9%)
  matrix products  24.5 us (6%)
  between operations  14.3 us (4%)
  local copies, waits for them, and re-layouts  10 us (3%)
  other arithmetic  9.33 us (2%)
    all_to_all x1, waiting for transfers between devices, per_device(): lax.all_to_all(head_parts.reshape(n_seq, half, heads_dev, width), 'seq',...  71.5 us
    all_gather x1, waiting for transfers between devices, per_device(): lax.all_gather(local_dy, 'seq', axis=1, tiled=True)  67.3 us
    reduce_scatter x1, waiting for transfers between devices, per_device(): lax.psum_scatter(owner_part.astype(jnp.bfloat16), 'seq', scatter_dimensio...  59.6 us
    all_gather x1, blocking collectives, per_device(): lax.all_gather(w_output, 'dp', axis=1, tiled=True)  26.2 us
    ppermute x4, waiting for transfers between devices, partner(): return lax.ppermute(value, axis, pairs)  24.5 us
    all_gather x1, blocking collectives, per_device(): lax.all_gather(w_project, 'dp', axis=0, tiled=True)  23.9 us
    all_gather x1, waiting for transfers between devices, per_device(): lax.all_gather(local_x, 'seq', axis=1, tiled=True)  14.9 us
    ppermute x4, starting transfers between devices, partner(): return lax.ppermute(value, axis, pairs)  12.2 us
  transfers between devices with their start and end apart: 11, of which 9 were waited for; matrix products, arithmetic and copies ran while one was open for 7% of the time, Pallas kernels for 0%

commit v1 on v0

v1 whole, which is shorter than its diff:
```python
import jax
import jax.numpy as jnp
from jax import lax
from jax.sharding import Mesh, PartitionSpec as P

HEAD_DIM = 128
NORM_FLOOR = 1.0
F32 = jnp.float32
BF16 = jnp.bfloat16

X, Y, C, ZQ, ZR = 4, 4, 2, 4, 4
YC = Y * C
Z = ZQ * ZR
PAIR = ("y", "c")
DP = ("x", "y", "c")
SEQ = ("zq", "zr")
SHARE = ("x", "zr")
ALL = ("x", "y", "c", "zq", "zr")
OWNERS = X * YC
CAP = 8
ROWS = 256
SLOTS = OWNERS * CAP
LANES = 128


def exchange(value, axes):
    return lax.all_to_all(value, axes, split_axis=0, concat_axis=0, tiled=True)


def silu_grad(values):
    sigma = jax.nn.sigmoid(values)
    return sigma * (1.0 + values * (1.0 - sigma))


def routing(item_ids, owner_row):
    rows = jnp.take(owner_row, item_ids.reshape(-1))
    owner = rows // ROWS
    count = owner.shape[0]
    order = jnp.arange(count, dtype=jnp.int32)
    before = (owner[None, :] == owner[:, None]) & (order[None, :] < order[:, None])
    rank = jnp.sum(before.astype(jnp.int32), axis=1)
    return owner * CAP + rank, rows % ROWS


def heads_backward(px, pdy, weights, ends):
    length = px.shape[0]
    hd = HEAD_DIM
    wp = weights[:, : 4 * hd]
    wo = weights[:, 4 * hd :]
    row = jnp.arange(length, dtype=jnp.int32)
    pos = (row // 8) % Z * 64 + row // LANES * 8 + row % 8
    segment = jnp.sum((pos[:, None] >= ends[None, :]).astype(jnp.int32), axis=1)
    masked = (segment[:, None] == segment[None, :]) & (pos[None, :] <= pos[:, None])
    z_pre = jnp.dot(px, wp, preferred_element_type=F32)
    acted = jax.nn.silu(z_pre).astype(BF16)
    gating, value, query, key = (acted[:, m * hd : (m + 1) * hd] for m in range(4))
    scale = hd**-0.5
    scores = lax.dot_general(query, key, (((1,), (1,)), ((), ())), preferred_element_type=F32) * scale
    attn = jnp.where(masked, jax.nn.silu(scores), 0.0).astype(BF16)
    mixed = jnp.dot(attn, value, preferred_element_type=F32)
    centred = mixed - jnp.mean(mixed, axis=-1, keepdims=True)
    inv_std = lax.rsqrt(jnp.mean(centred * centred, axis=-1, keepdims=True) + NORM_FLOOR)
    normed = centred * inv_std
    gated = (normed * gating).astype(BF16)
    d_gated = jnp.dot(pdy, wo, preferred_element_type=F32)
    d_gate = d_gated * normed
    d_normed = d_gated * gating
    d_mixed = (
        inv_std
        * (
            d_normed
            - jnp.mean(d_normed, axis=-1, keepdims=True)
            - normed * jnp.mean(d_normed * normed, axis=-1, keepdims=True)
        )
    ).astype(BF16)
    d_attn = lax.dot_general(d_mixed, value, (((1,), (1,)), ((), ())), preferred_element_type=F32)
    d_scores = (jnp.where(masked, d_attn * silu_grad(scores), 0.0) * scale).astype(BF16)
    first = (((0,), (0,)), ((), ()))
    d_value = lax.dot_general(attn, d_mixed, first, preferred_element_type=F32)
    d_query = jnp.dot(d_scores, key, preferred_element_type=F32)
    d_key = lax.dot_general(d_scores, query, first, preferred_element_type=F32)
    d_act = jnp.concatenate([d_gate, d_value, d_query, d_key], axis=1)
    d_z = (d_act * silu_grad(z_pre)).astype(BF16)
    part = lax.dot_general(d_z, wp, (((1,), (1,)), ((), ())), preferred_element_type=F32).astype(BF16)
    grads = jnp.concatenate(
        [
            lax.dot_general(px, d_z, first, preferred_element_type=F32),
            lax.dot_general(pdy, gated, first, preferred_element_type=F32),
        ],
        axis=1,
    ).astype(BF16)
    return part, grads


def per_device(inputs, cotangent, lengths, item_ids, owner_row, w_project, w_output):
    width = inputs.shape[3]
    blocks = width // LANES
    core = lax.axis_index("c")
    y_here = lax.axis_index("y")
    z_here = lax.axis_index(SEQ)
    lane = jnp.arange(LANES, dtype=jnp.int32)

    slot, local_row = routing(item_ids, owner_row)
    lens = lengths.reshape(-1)
    lens_row = jnp.concatenate([lens // 256, lens % 256])
    lens_row = jnp.pad(lens_row, (0, LANES - lens_row.shape[0]))
    small = jnp.pad(jnp.stack([slot, local_row, lens_row]), ((0, 5), (0, 0))).astype(BF16)
    wp_tiles = w_project.reshape(ZR, 8, 2, LANES).transpose(0, 2, 1, 3)
    wo_t = w_output.T
    wo_tiles = jnp.concatenate([wo_t, wo_t], axis=1).reshape(ZR, 1, 8, LANES)
    small = jnp.broadcast_to(small[None, None], (ZR, 1, 8, LANES))
    w_tiles = jnp.concatenate([wp_tiles, wo_tiles, small], axis=1)

    both = jnp.stack([inputs[0], cotangent[0]]).reshape(2, 2, 8, 8, blocks, LANES)
    spread = exchange(both.transpose(2, 1, 0, 4, 3, 5), PAIR)
    spread = spread.reshape(Z, 2 * blocks, 8, LANES)
    w_tiles = jnp.broadcast_to(w_tiles[None], (ZQ, ZR, 4, 8, LANES)).reshape(Z, 4, 8, LANES)
    arrived = exchange(jnp.concatenate([spread, w_tiles], axis=1), SEQ)
    mine = arrived[:, : 2 * blocks].reshape(Z, 2, blocks, 8, LANES)
    mine = mine.transpose(1, 0, 3, 2, 4).reshape(2, Z * 8, width)
    packs = lax.all_gather(mine, PAIR, axis=1, tiled=True)

    by_head = exchange(arrived[:, 2 * blocks :].reshape(YC, 2, 4, 8, LANES), PAIR)
    wp_part = by_head[:, :, :2].transpose(0, 3, 1, 2, 4).reshape(YC, 8, 4 * HEAD_DIM)
    wo_part = jnp.where(lane < 64, by_head[:, 0, 2], by_head[:, 1, 2])
    w_part = jnp.concatenate([wp_part, wo_part], axis=2)
    w_all = jnp.broadcast_to(w_part[None], (X * ZR,) + w_part.shape)
    weights = exchange(w_all, SHARE).reshape(X, ZR, YC, 8, 5 * HEAD_DIM)
    weights = weights.transpose(0, 2, 1, 3, 4).reshape(width, 5 * HEAD_DIM)

    facts = by_head[:, :, 3].astype(F32)
    slots = facts[:, :, 0].astype(jnp.int32)
    tag_of = facts[:, :, 1]
    lens_all = facts[:, 0, 2, :12].reshape(YC, 2, 2, 3)
    lens_all = (lens_all[:, 0] * 256.0 + lens_all[:, 1]).astype(jnp.int32).reshape(Z, 3)
    pack_lens = lax.dynamic_index_in_dim(lens_all, z_here, 0, keepdims=False)
    ends = jnp.cumsum(pack_lens)

    part, grads = heads_backward(packs[0], packs[1], weights, ends)

    part = part.reshape(8, Y, C, 16, width)
    kept = lax.dynamic_index_in_dim(part, core, 2, keepdims=False)
    sent = lax.dynamic_index_in_dim(part, 1 - core, 2, keepdims=False)
    got = lax.ppermute(sent, "c", [(0, 1), (1, 0)])
    pair_sum = (kept.astype(F32) + got.astype(F32)).astype(BF16).transpose(1, 0, 2, 3)
    quad = lax.dynamic_index_in_dim(pair_sum, y_here, 0, keepdims=False).astype(F32)
    for step in range(1, Y):
        there = lax.dynamic_index_in_dim(pair_sum, (y_here + step) % Y, 0, keepdims=False)
        came = lax.ppermute(there, "y", [(i, (i + step) % Y) for i in range(Y)])
        quad = quad + came.astype(F32)
    own = y_here * C + core
    dy_own = lax.dynamic_index_in_dim(
        packs[1].reshape(8, YC, 16, width), own, 1, keepdims=False
    )
    token = (dy_own.astype(F32) + quad).astype(BF16)
    token = token.reshape(8, 2, 8, Z, 64).transpose(3, 0, 2, 1, 4).reshape(Z, 8, 8, LANES)

    grads = grads.reshape(X, YC, ZR, 8, 5 * HEAD_DIM).transpose(0, 2, 1, 3, 4)
    shared = exchange(grads.reshape(X * ZR, YC, 8, 5 * HEAD_DIM), SHARE)
    w_sum = jnp.sum(shared.astype(F32), axis=0).astype(BF16)
    wp_sum = w_sum[:, :, : 4 * HEAD_DIM].reshape(YC, 8, 2, 2, LANES)
    wp_sum = wp_sum.transpose(0, 2, 3, 1, 4).reshape(Z, 2, 8, LANES)
    wo_sum = w_sum[:, None, None, :, 4 * HEAD_DIM :]
    wo_sum = jnp.broadcast_to(wo_sum, (YC, 2, 1, 8, LANES)).reshape(Z, 1, 8, LANES)

    merged = exchange(jnp.concatenate([token, wp_sum, wo_sum], axis=1), SEQ)
    w_grad = jnp.sum(merged[:, 8:].astype(F32).reshape(ZQ, ZR, 3, 8, LANES), axis=0)
    turn = [
        ((x * YC + a) * Z + b * 2 + s, (x * YC + b) * Z + a * 2 + s)
        for x in range(X)
        for a in range(YC)
        for b in range(YC)
        for s in range(2)
    ]
    w_grad = lax.ppermute(w_grad, ALL, turn)
    grad_proj = w_grad[:, :2].transpose(0, 2, 1, 3).reshape(32, 2 * LANES)
    both_out = w_grad[:, 2].reshape(32, 2, 64)
    grad_out = lax.dynamic_index_in_dim(both_out, z_here % 2, 1, keepdims=False).T

    tokens = merged[:, :8].reshape(YC, LANES, LANES)
    slot_ids = jnp.arange(SLOTS, dtype=jnp.int32)
    placed = slots[:, :, None, :] == slot_ids[None, None, :, None]
    tags = jnp.sum(jnp.where(placed, tag_of[:, :, None, :], 0.0), axis=3)
    moved = jnp.einsum(
        "asut,atl->saul", placed.astype(BF16), tokens, preferred_element_type=F32
    )
    rows_out = jnp.where(lane < 64, moved[0], moved[1]).astype(BF16)
    rows_out = rows_out.reshape(YC, OWNERS, CAP, LANES).transpose(1, 0, 2, 3)
    tags = tags.reshape(YC, 2, OWNERS, CAP).transpose(2, 0, 1, 3).reshape(OWNERS, 1, 1, LANES)
    tags = jnp.pad(tags.astype(BF16), ((0, 0), (0, 0), (0, 7), (0, 0)))
    owned = exchange(jnp.concatenate([rows_out, tags], axis=1), DP)
    got_rows = owned[:, :YC].reshape(OWNERS * YC * CAP, LANES)
    got_tags = owned[:, YC, 0].astype(F32).astype(jnp.int32).reshape(OWNERS, YC, 2, CAP)
    got_tags = got_tags.transpose(2, 0, 1, 3).reshape(2, 1, OWNERS * YC * CAP)
    row_ids = jnp.arange(ROWS, dtype=jnp.int32)
    select = (got_tags == row_ids[None, :, None]).astype(BF16)
    sums = jnp.einsum("srk,kl->srl", select, got_rows, preferred_element_type=F32)
    grad_table = sums[0, :, :64] + sums[1, :, 64:]
    return (grad_proj, grad_out, grad_table)


def solution(mesh):
    fine = Mesh(mesh.devices.reshape(X, Y, C, ZQ, ZR), ALL)
    return jax.shard_map(
        per_device,
        mesh=fine,
        in_specs=(
            P(DP, None, SEQ, None),
            P(DP, None, SEQ, None),
            P(DP, None, None),
            P(DP, None, SEQ),
            P(),
            P(DP, SEQ),
            P(SEQ, DP),
        ),
        out_specs=(P(DP, SEQ), P(SEQ, DP), P(DP, SEQ)),
        check_vma=False,
    )
```

time: 395 us -> 264 us (0.67)
  the two profiles are of different devices: /device:TPU:4 before, /device:TPU:16 now
where the time goes in v1:
time: 264 us; the launch traced here: 263 us
  waiting for transfers between devices  84 us (32%)
  starting transfers between devices  60.3 us (23%)
  blocking collectives  47.2 us (18%)
  local copies, waits for them, and re-layouts  24.1 us (9%)
  matrix products  23.3 us (9%)
  between operations  14.8 us (6%)
  other arithmetic  9.75 us (4%)
    all_to_all x6, waiting for transfers between devices, exchange(): return lax.all_to_all(value, axes, split_axis=0, concat_axis=0, tiled=True)  61.3 us
    all_to_all x1, blocking collectives, exchange(): return lax.all_to_all(value, axes, split_axis=0, concat_axis=0, tiled=True)  47.2 us
    all_to_all x6, starting transfers between devices, exchange(): return lax.all_to_all(value, axes, split_axis=0, concat_axis=0, tiled=True)  41.5 us
    ppermute x1, waiting for transfers between devices, per_device(): w_grad = lax.ppermute(w_grad, ALL, turn)  11.1 us
    ppermute x3, starting transfers between devices, per_device(): came = lax.ppermute(there, 'y', [(i, (i + step) % Y) for i in range(Y)])  10.8 us
    ppermute x3, waiting for transfers between devices, per_device(): came = lax.ppermute(there, 'y', [(i, (i + step) % Y) for i in range(Y)])  8.79 us
    ppermute x1, starting transfers between devices, per_device(): w_grad = lax.ppermute(w_grad, ALL, turn)  6 us
  transfers between devices with their start and end apart: 12, of which 9 were waited for; matrix products, arithmetic and copies ran while one was open for 6% of the time, Pallas kernels for 0%

profile of v1, /device:TPU:16, one launch (start us, length us, event | category | flops | bytes accessed | tf_op | source)
XLA Modules:
  0.0 263.4 jit_solution(18279103674082241674)
XLA Ops:
  9.2 9.1 %all-to-all-start = ((bf16[8,2,2,8,8,128]{5,3,4,1,2,0:T(8,128)(2,1)}), bf16[8,2,2,8,8,128]{5,3,4,1,2,0:T(8,128)(2,1)S(1)}, u32[]{:S(2)}, u32[]{:S(2)}) async-start(bf16[8,2,2,8,8,128]{5,3,4,1,2,0:T(8,128)(2,1)} %copy.95), calls=%async_computation | async-start | bytes 1048576 | tf_op jit(solution)/shard_map/all_to_all | solution.py:27
  20.3 5.2 %all-to-all-done = bf16[8,2,2,8,8,128]{5,3,4,1,2,0:T(8,128)(2,1)S(1)} async-done(((bf16[8,2,2,8,8,128]{5,3,4,1,2,0:T(8,128)(2,1)}), bf16[8,2,2,8,8,128]{5,3,4,1,2,0:T(8,128)(2,1)S(1)}, u32[]{:S(2)}, u32[]{:S(2)}) %all-to-all-start) | async-done | bytes 524320 | tf_op jit(solution)/shard_map/all_to_all | solution.py:27
  25.7 47.2 %all_to_all.35 = bf16[16,20,8,128]{3,2,1,0:T(8,128)(2,1)S(1)} all-to-all(bf16[16,20,8,128]{3,2,1,0:T(8,128)(2,1)S(1)} %pad_maximum_fusion), channel_id=1, replica_groups=mesh['x'=4,'y'=4,'c'=2,'zq'=4,'zr'=4] {'zq','zr'}, dimensions={0} | all-to-all | bytes 1310720 | tf_op jit(solution)/shard_map/all_to_all | solution.py:27
  74.8 6.1 %all-to-all-start.2 = ((bf16[8,2,4,8,128]{4,3,2,1,0:T(8,128)(2,1)}), bf16[8,2,4,8,128]{4,3,2,1,0:T(8,128)(2,1)S(1)}, u32[]{:S(2)}, u32[]{:S(2)}) async-start(bf16[8,2,4,8,128]{4,3,2,1,0:T(8,128)(2,1)} %bitcast.17), calls=%async_computation.2 | async-start | bytes 262144 | tf_op jit(solution)/shard_map/all_to_all | solution.py:27
  81.0 3.4 %all-to-all-done.2 = bf16[8,2,4,8,128]{4,3,2,1,0:T(8,128)(2,1)S(1)} async-done(((bf16[8,2,4,8,128]{4,3,2,1,0:T(8,128)(2,1)}), bf16[8,2,4,8,128]{4,3,2,1,0:T(8,128)(2,1)S(1)}, u32[]{:S(2)}, u32[]{:S(2)}) %all-to-all-start.2) | async-done | bytes 131104 | tf_op jit(solution)/shard_map/all_to_all | solution.py:27
  85.7 6.8 %all-to-all-start.3 = ((bf16[16,8,8,640]{3,2,1,0:T(8,128)(2,1)}), bf16[16,8,8,640]{3,2,1,0:T(8,128)(2,1)S(1)}, u32[]{:S(2)}, u32[]{:S(2)}) async-start(bf16[16,8,8,640]{3,2,1,0:T(8,128)(2,1)} %broadcast_in_dim.50), calls=%async_computation.3 | async-start | bytes 2621440 | tf_op jit(solution)/shard_map/all_to_all | solution.py:27
  93.3 32.6 %all-to-all-done.3 = bf16[16,8,8,640]{3,2,1,0:T(8,128)(2,1)S(1)} async-done(((bf16[16,8,8,640]{3,2,1,0:T(8,128)(2,1)}), bf16[16,8,8,640]{3,2,1,0:T(8,128)(2,1)S(1)}, u32[]{:S(2)}, u32[]{:S(2)}) %all-to-all-start.3) | async-done | bytes 1310752 | tf_op jit(solution)/shard_map/all_to_all | solution.py:27
  126.1 4.9 %multiply_convert_fusion.1 = (bf16[1024,512]{0,1:T(8,128)(2,1)S(1)}, f32[1024,512]{0,1:T(8,128)}) fusion(bf16[1024,640]{1,0:T(8,128)(2,1)S(1)} %bitcast.192, bf16[2,1024,1024]{2,1,0:T(8,128)(2,1)} %all-gather.2.cloned.1.call-done), kind=kOutput, calls=%fused_computation.19 | convolution fusion | flops 1076363264 | bytes 6291456 | tf_op jit(solution)/shard_map/dot_general | solution.py:54
  136.1 2.8 %multiply_convert_fusion = bf16[1024,1024]{1,0:T(8,128)(2,1)S(1)} fusion(f32[1024,1024]{1,0:T(8,128)S(1)} %get-tuple-element.26, bf16[1024,128]{0,1:T(8,128)(2,1)S(1)} %get-tuple-element.13, s32[1024]{0:T(1024)S(1)} %fusion.55, s32[1024]{0:T(1024)S(1)} %convert_reduce_fusion.2, bf16[1024,512]{0,1:T(8,128)(2,1)S(1)} %get-tuple-element.23), kind=kOutput, calls=%fused_computation.2 | convolution fusion | flops 284164096 | bytes 6832128 | tf_op jit(solution)/shard_map/dot_general | solution.py:76
  141.8 2.8 %fusion.75 = (bf16[1,1024,1024]{2,1,0:T(8,128)(2,1)}, bf16[1024,1024]{0,1:T(8,128)(2,1)S(1)}, bf16[1024,1024]{0,1:T(8,128)(2,1)}) fusion(bf16[2,1024,1024]{2,1,0:T(8,128)(2,1)S(1)} %copy-done.1), kind=kLoop, calls=%fused_computation.170 | loop fusion | bytes 10485760 | tf_op jit(solution)/shard_map/slice | solution.py:153
  144.6 3.9 %copy.106 = bf16[1024,1024]{1,0:T(8,128)(2,1)} copy(bf16[1024,1024]{0,1:T(8,128)(2,1)} %get-tuple-element.9) | data formatting | bytes 4194304 | tf_op jit(solution)/shard_map/dot_general | solution.py:87
  148.6 2.6 copy.108
  158.4 3.7 %all-to-all-start.4 = ((bf16[16,8,8,640]{3,2,1,0:T(8,128)(2,1)}), bf16[16,8,8,640]{3,2,1,0:T(8,128)(2,1)S(1)}, u32[]{:S(2)}, u32[]{:S(2)}) async-start(bf16[16,8,8,640]{3,2,1,0:T(8,128)(2,1)} %bitcast.43), calls=%async_computation.4 | async-start | bytes 2621440 | tf_op jit(solution)/shard_map/all_to_all | solution.py:27
  167.8 2.8 %collective-permute-done = bf16[8,4,16,1024]{3,2,0,1:T(8,128)(2,1)S(1)} collective-permute-done((bf16[8,4,16,1024]{3,2,0,1:T(8,128)(2,1)}, bf16[8,4,16,1024]{3,2,0,1:T(8,128)(2,1)S(1)}, u32[]{:S(2)}, u32[]{:S(2)}) %collective-permute-start) | collective-permute-done | bytes 1048608 | tf_op jit(solution)/shard_map/ppermute | solution.py:144
  173.3 3.5 %collective-permute-start.1 = (bf16[8,16,1024]{2,1,0:T(8,128)(2,1)S(1)}, bf16[8,16,1024]{2,1,0:T(8,128)(2,1)S(1)}, u32[]{:S(2)}, u32[]{:S(2)}) collective-permute-start(bf16[8,16,1024]{2,1,0:T(8,128)(2,1)S(1)} %get-tuple-element.16), channel_id=1, source_target_pairs={{0,32},{32,64},{64,96},{96,0},{1,33},{33,65},{65,97},{97,1},{2,34}... | collective-permute-start | bytes 786440 | tf_op jit(solution)/shard_map/ppermute | solution.py:149
  176.8 3.4 %collective-permute-start.2 = (bf16[8,16,1024]{2,1,0:T(8,128)(2,1)S(1)}, bf16[8,16,1024]{2,1,0:T(8,128)(2,1)}, u32[]{:S(2)}, u32[]{:S(2)}) collective-permute-start(bf16[8,16,1024]{2,1,0:T(8,128)(2,1)S(1)} %get-tuple-element.18), channel_id=1, source_target_pairs={{0,64},{32,96},{64,0},{96,32},{1,65},{33,97},{65,1},{97,33},{2,66}... | collective-permute-start | bytes 786440 | tf_op jit(solution)/shard_map/ppermute | solution.py:149
  180.2 4.0 %collective-permute-start.3 = (bf16[8,16,1024]{2,1,0:T(8,128)(2,1)S(1)}, bf16[8,16,1024]{2,1,0:T(8,128)(2,1)}, u32[]{:S(2)}, u32[]{:S(2)}) collective-permute-start(bf16[8,16,1024]{2,1,0:T(8,128)(2,1)S(1)} %get-tuple-element.17), channel_id=1, source_target_pairs={{0,96},{32,0},{64,32},{96,64},{1,97},{33,1},{65,33},{97,65},{2,98}... | collective-permute-start | bytes 786440 | tf_op jit(solution)/shard_map/ppermute | solution.py:149
  184.2 6.1 %collective-permute-done.2 = bf16[8,16,1024]{2,1,0:T(8,128)(2,1)} collective-permute-done((bf16[8,16,1024]{2,1,0:T(8,128)(2,1)S(1)}, bf16[8,16,1024]{2,1,0:T(8,128)(2,1)}, u32[]{:S(2)}, u32[]{:S(2)}) %collective-permute-start.2) | collective-permute-done | bytes 262176 | tf_op jit(solution)/shard_map/ppermute | solution.py:149
  190.3 2.7 %collective-permute-done.3 = bf16[8,16,1024]{2,1,0:T(8,128)(2,1)} collective-permute-done((bf16[8,16,1024]{2,1,0:T(8,128)(2,1)S(1)}, bf16[8,16,1024]{2,1,0:T(8,128)(2,1)}, u32[]{:S(2)}, u32[]{:S(2)}) %collective-permute-start.3) | collective-permute-done | bytes 262176 | tf_op jit(solution)/shard_map/ppermute | solution.py:149
  196.6 5.2 %all-to-all-start.5 = ((bf16[16,11,8,128]{3,2,1,0:T(8,128)(2,1)}), bf16[16,11,8,128]{3,2,1,0:T(8,128)(2,1)S(1)}, u32[]{:S(2)}, u32[]{:S(2)}) async-start(bf16[16,11,8,128]{3,2,1,0:T(8,128)(2,1)} %pad_maximum_fusion.2), calls=%async_computation.5 | async-start | bytes 720896 | tf_op jit(solution)/shard_map/all_to_all | solution.py:27
  203.1 19.9 %all-to-all-done.5 = bf16[16,11,8,128]{3,2,1,0:T(8,128)(2,1)S(1)} async-done(((bf16[16,11,8,128]{3,2,1,0:T(8,128)(2,1)}), bf16[16,11,8,128]{3,2,1,0:T(8,128)(2,1)S(1)}, u32[]{:S(2)}, u32[]{:S(2)}) %all-to-all-start.5) | async-done | bytes 360480 | tf_op jit(solution)/shard_map/all_to_all | solution.py:27
  225.3 10.6 %all-to-all-start.6 = ((bf16[32,9,8,128]{3,2,1,0:T(8,128)(2,1)}), bf16[32,9,8,128]{3,2,1,0:T(8,128)(2,1)S(1)}, u32[]{:S(2)}, u32[]{:S(2)}) async-start(bf16[32,9,8,128]{3,2,1,0:T(8,128)(2,1)} %copy.117), calls=%async_computation.6 | async-start | bytes 1179648 | tf_op jit(solution)/shard_map/all_to_all | solution.py:27
  236.0 6.0 %collective-permute-start.4 = (f32[4,3,8,128]{3,2,1,0:T(8,128)S(1)}, f32[4,3,8,128]{3,2,1,0:T(8,128)S(1)}, u32[]{:S(2)}, u32[]{:S(2)}) collective-permute-start(f32[4,3,8,128]{3,2,1,0:T(8,128)S(1)} %convert_reduce_fusion), channel_id=1, source_target_pairs={{0,0},{1,1},{2,16},{3,17},{4,32},{5,33},{6,48},{7,49},{8,64},{9,65... | collective-permute-start | bytes 147464 | tf_op jit(solution)/shard_map/ppermute | solution.py:175
  242.0 11.1 %collective-permute-done.4 = f32[4,3,8,128]{3,2,1,0:T(8,128)S(1)} collective-permute-done((f32[4,3,8,128]{3,2,1,0:T(8,128)S(1)}, f32[4,3,8,128]{3,2,1,0:T(8,128)S(1)}, u32[]{:S(2)}, u32[]{:S(2)}) %collective-permute-start.4) | collective-permute-done | bytes 49184 | tf_op jit(solution)/shard_map/ppermute | solution.py:175
  (138 shorter events, 42.2 us)
Async XLA Ops:
  7.2 11.5 %copy-start = (s32[8192]{0:T(1024)S(1)}, s32[8192]{0:T(1024)}, u32[]{:S(2)}) copy-start(s32[8192]{0:T(1024)} %param.11) | copy-start | bytes 98308
  7.2 11.2 %copy-start.13 = (s32[1,2,64]{2,1,0:T(2,128)S(1)}, s32[1,2,64]{2,1,0:T(2,128)}, u32[]{:S(2)}) copy-start(s32[1,2,64]{2,1,0:T(2,128)} %param.10) | copy-start | bytes 1540
  7.2 12.8 %copy-start.14 = (s32[1,2,3]{2,1,0:T(2,128)S(1)}, s32[1,2,3]{2,1,0:T(2,128)}, u32[]{:S(2)}) copy-start(s32[1,2,3]{2,1,0:T(2,128)} %param.9) | copy-start | bytes 76
  7.2 13.0 %copy-start.12 = (bf16[64,32]{0,1:T(8,128)(2,1)S(1)}, bf16[64,32]{0,1:T(8,128)(2,1)}, u32[]{:S(2)}) copy-start(bf16[64,32]{0,1:T(8,128)(2,1)} %param.13) | copy-start | bytes 12292
  7.2 13.1 %copy-start.11 = (bf16[32,256]{1,0:T(8,128)(2,1)S(1)}, bf16[32,256]{1,0:T(8,128)(2,1)}, u32[]{:S(2)}) copy-start(bf16[32,256]{1,0:T(8,128)(2,1)} %param.12) | copy-start | bytes 49156
  9.2 16.3 %all-to-all-start = ((bf16[8,2,2,8,8,128]{5,3,4,1,2,0:T(8,128)(2,1)}), bf16[8,2,2,8,8,128]{5,3,4,1,2,0:T(8,128)(2,1)S(1)}, u32[]{:S(2)}, u32[]{:S(2)}) async-start(bf16[8,2,2,8,8,128]{5,3,4,1,2,0:T(8,128)(2,1)} %copy.95), calls=%async_computation | async-start | bytes 1048576 | tf_op jit(solution)/shard_map/all_to_all | solution.py:27
  18.4 107.7 %all-gather.2.cloned.1.call-start = ((), (), s32[]{:S(2)}) async-start(), calls=%async_computation.7 | async-start | bytes 4718592 | tf_op jit(solution)/shard_map/all_gather | solution.py:121
  74.8 9.6 %all-to-all-start.2 = ((bf16[8,2,4,8,128]{4,3,2,1,0:T(8,128)(2,1)}), bf16[8,2,4,8,128]{4,3,2,1,0:T(8,128)(2,1)S(1)}, u32[]{:S(2)}, u32[]{:S(2)}) async-start(bf16[8,2,4,8,128]{4,3,2,1,0:T(8,128)(2,1)} %bitcast.17), calls=%async_computation.2 | async-start | bytes 262144 | tf_op jit(solution)/shard_map/all_to_all | solution.py:27
  85.7 40.2 %all-to-all-start.3 = ((bf16[16,8,8,640]{3,2,1,0:T(8,128)(2,1)}), bf16[16,8,8,640]{3,2,1,0:T(8,128)(2,1)S(1)}, u32[]{:S(2)}, u32[]{:S(2)}) async-start(bf16[16,8,8,640]{3,2,1,0:T(8,128)(2,1)} %broadcast_in_dim.50), calls=%async_computation.3 | async-start | bytes 2621440 | tf_op jit(solution)/shard_map/all_to_all | solution.py:27
  126.0 7.7 %copy-start.7 = (bf16[4,8,4,8,640]{4,3,2,1,0:T(8,128)(2,1)}, bf16[4,8,4,8,640]{4,3,2,1,0:T(8,128)(2,1)S(1)}, u32[]{:S(2)}) copy-start(bf16[4,8,4,8,640]{4,3,2,1,0:T(8,128)(2,1)S(1)} %copy.100) | copy-start | bytes 3932164
  131.0 9.6 %copy-start.6 = (bf16[1024,512]{0,1:T(8,128)(2,1)}, bf16[1024,512]{0,1:T(8,128)(2,1)S(1)}, u32[]{:S(2)}) copy-start(bf16[1024,512]{0,1:T(8,128)(2,1)S(1)} %get-tuple-element.23) | copy-start | bytes 3145732
  131.0 2.8 %copy-start.1 = (bf16[2,1024,1024]{2,1,0:T(8,128)(2,1)S(1)}, bf16[2,1024,1024]{2,1,0:T(8,128)(2,1)}, u32[]{:S(2)}) copy-start(bf16[2,1024,1024]{2,1,0:T(8,128)(2,1)} %all-gather.2.cloned.1.call-done) | copy-start | bytes 12582916
  151.2 2.5 copy-start.2
  151.2 2.5 copy-start.4
  151.2 2.5 copy-start.5
  157.1 5.0 %copy-start.8 = (bf16[4,8,4,8,640]{4,3,2,1,0:T(8,128)(2,1)S(1)}, bf16[4,8,4,8,640]{4,3,2,1,0:T(8,128)(2,1)}, u32[]{:S(2)}) copy-start(bf16[4,8,4,8,640]{4,3,2,1,0:T(8,128)(2,1)} %copy-done.7) | copy-start | bytes 3932164
  158.4 37.3 %all-to-all-start.4 = ((bf16[16,8,8,640]{3,2,1,0:T(8,128)(2,1)}), bf16[16,8,8,640]{3,2,1,0:T(8,128)(2,1)S(1)}, u32[]{:S(2)}, u32[]{:S(2)}) async-start(bf16[16,8,8,640]{3,2,1,0:T(8,128)(2,1)} %bitcast.43), calls=%async_computation.4 | async-start | bytes 2621440 | tf_op jit(solution)/shard_map/all_to_all | solution.py:27
  165.9 4.8 %collective-permute-start = (bf16[8,4,16,1024]{3,2,0,1:T(8,128)(2,1)}, bf16[8,4,16,1024]{3,2,0,1:T(8,128)(2,1)S(1)}, u32[]{:S(2)}, u32[]{:S(2)}) collective-permute-start(bf16[8,4,16,1024]{3,2,0,1:T(8,128)(2,1)} %bitcast.180), channel_id=1, source_target_pairs={{0,16},{16,0},{1,17},{17,1},{2,18},{18,2},{3,19},{19,3},{4,20},{20... | collective-permute-start | bytes 3145736 | tf_op jit(solution)/shard_map/ppermute | solution.py:144
  173.3 10.9 %collective-permute-start.1 = (bf16[8,16,1024]{2,1,0:T(8,128)(2,1)S(1)}, bf16[8,16,1024]{2,1,0:T(8,128)(2,1)S(1)}, u32[]{:S(2)}, u32[]{:S(2)}) collective-permute-start(bf16[8,16,1024]{2,1,0:T(8,128)(2,1)S(1)} %get-tuple-element.16), channel_id=1, source_target_pairs={{0,32},{32,64},{64,96},{96,0},{1,33},{33,65},{65,97},{97,1},{2,34}... | collective-permute-start | bytes 786440 | tf_op jit(solution)/shard_map/ppermute | solution.py:149
  176.8 13.5 %collective-permute-start.2 = (bf16[8,16,1024]{2,1,0:T(8,128)(2,1)S(1)}, bf16[8,16,1024]{2,1,0:T(8,128)(2,1)}, u32[]{:S(2)}, u32[]{:S(2)}) collective-permute-start(bf16[8,16,1024]{2,1,0:T(8,128)(2,1)S(1)} %get-tuple-element.18), channel_id=1, source_target_pairs={{0,64},{32,96},{64,0},{96,32},{1,65},{33,97},{65,1},{97,33},{2,66}... | collective-permute-start | bytes 786440 | tf_op jit(solution)/shard_map/ppermute | solution.py:149
  180.2 12.8 %collective-permute-start.3 = (bf16[8,16,1024]{2,1,0:T(8,128)(2,1)S(1)}, bf16[8,16,1024]{2,1,0:T(8,128)(2,1)}, u32[]{:S(2)}, u32[]{:S(2)}) collective-permute-start(bf16[8,16,1024]{2,1,0:T(8,128)(2,1)S(1)} %get-tuple-element.17), channel_id=1, source_target_pairs={{0,96},{32,0},{64,32},{96,64},{1,97},{33,1},{65,33},{97,65},{2,98}... | collective-permute-start | bytes 786440 | tf_op jit(solution)/shard_map/ppermute | solution.py:149
  196.6 26.4 %all-to-all-start.5 = ((bf16[16,11,8,128]{3,2,1,0:T(8,128)(2,1)}), bf16[16,11,8,128]{3,2,1,0:T(8,128)(2,1)S(1)}, u32[]{:S(2)}, u32[]{:S(2)}) async-start(bf16[16,11,8,128]{3,2,1,0:T(8,128)(2,1)} %pad_maximum_fusion.2), calls=%async_computation.5 | async-start | bytes 720896 | tf_op jit(solution)/shard_map/all_to_all | solution.py:27
  225.3 29.1 %all-to-all-start.6 = ((bf16[32,9,8,128]{3,2,1,0:T(8,128)(2,1)}), bf16[32,9,8,128]{3,2,1,0:T(8,128)(2,1)S(1)}, u32[]{:S(2)}, u32[]{:S(2)}) async-start(bf16[32,9,8,128]{3,2,1,0:T(8,128)(2,1)} %copy.117), calls=%async_computation.6 | async-start | bytes 1179648 | tf_op jit(solution)/shard_map/all_to_all | solution.py:27
  236.0 17.1 %collective-permute-start.4 = (f32[4,3,8,128]{3,2,1,0:T(8,128)S(1)}, f32[4,3,8,128]{3,2,1,0:T(8,128)S(1)}, u32[]{:S(2)}, u32[]{:S(2)}) collective-permute-start(f32[4,3,8,128]{3,2,1,0:T(8,128)S(1)} %convert_reduce_fusion), channel_id=1, source_target_pairs={{0,0},{1,1},{2,16},{3,17},{4,32},{5,33},{6,48},{7,49},{8,64},{9,65... | collective-permute-start | bytes 147464 | tf_op jit(solution)/shard_map/ppermute | solution.py:175
  (3 other events, 4.2 us)
Sparse Core Ops, SparseCore 0:
  74.3 32.6 all-gather.1

commit v2 on v1

v2 whole, which is shorter than its diff:
```python
import jax
import jax.numpy as jnp
from jax import lax
from jax.experimental import pallas as pl
from jax.experimental.pallas import tpu as pltpu
from jax.sharding import Mesh, PartitionSpec as P

HEAD_DIM = 128
NORM_FLOOR = 1.0
F32 = jnp.float32
BF16 = jnp.bfloat16

X, Y, C, ZQ, ZR = 4, 4, 2, 8, 2
YC = Y * C
Z = ZQ * ZR
PAIR = ("y", "c")
DP = ("x", "y", "c")
SEQ = ("zq", "zr")
SHARE = ("x", "zr")
ALL = ("x", "y", "c", "zq", "zr")
OWNERS = X * YC
CAP = 8
ROWS = 256
SLOTS = OWNERS * CAP
LANES = 128
LENGTH = 1024
WIDTH = 1024
HIDDEN = 5 * HEAD_DIM
PART_ROWS = 32 // ZR
STEP = 256


def exchange(value, axes):
    return lax.all_to_all(value, axes, split_axis=0, concat_axis=0, tiled=True)


def routing(item_ids, owner_row):
    rows = jnp.take(owner_row, item_ids.reshape(-1))
    owner = rows // ROWS
    count = owner.shape[0]
    order = jnp.arange(count, dtype=jnp.int32)
    before = (owner[None, :] == owner[:, None]) & (order[None, :] < order[:, None])
    rank = jnp.sum(before.astype(jnp.int32), axis=1)
    return owner * CAP + rank, rows % ROWS


def position(row):
    return ((row >> 3) & 15) * 64 + (row >> 7) * 8 + (row & 7)


def dot_nt(a, b):
    return lax.dot_general(a, b, (((1,), (1,)), ((), ())), preferred_element_type=F32)


def dot_tn(a, b):
    return lax.dot_general(a, b, (((0,), (0,)), ((), ())), preferred_element_type=F32)


def heads_kernel(info, packs, w_in, kept, sent, d_z, gated, w, acts, slope, d_value, d_key):
    hd = HEAD_DIM
    scale = hd**-0.5
    u_cols, v_cols, q_cols, k_cols = (slice(m * hd, (m + 1) * hd) for m in range(4))
    for x in range(X):
        for yc in range(YC):
            start = (x * YC + yc) * 32
            w[start : start + 32, :] = w_in[x, :, yc].reshape(32, HIDDEN)
    d_value[...] = jnp.zeros_like(d_value)
    d_key[...] = jnp.zeros_like(d_key)

    def project(step, carry):
        rows = pl.ds(pl.multiple_of(step * STEP, STEP), STEP)
        z_pre = jnp.dot(packs[0, rows, :], w[:, : 4 * hd], preferred_element_type=F32)
        sigma = jax.nn.sigmoid(z_pre)
        silu = z_pre * sigma
        acts[rows, :] = silu.astype(BF16)
        slope[rows, :] = sigma + silu * (1.0 - sigma)
        return carry

    lax.fori_loop(0, LENGTH // STEP, project, 0)

    pos_k = position(lax.broadcasted_iota(jnp.int32, (1, LENGTH), 1))
    ends = [info[n] for n in range(3)]

    def attend(step, carry):
        base = pl.multiple_of(step * STEP, STEP)
        rows = pl.ds(base, STEP)
        pos_q = position(lax.broadcasted_iota(jnp.int32, (STEP, 1), 0) + base)
        start = jnp.zeros_like(pos_q)
        for end in ends:
            start = jnp.where(pos_q >= end, end, start)
        masked = (pos_k <= pos_q) & (pos_k >= start)
        query = acts[rows, q_cols]
        key = acts[:, k_cols]
        value = acts[:, v_cols]
        scores = dot_nt(query, key) * scale
        sigma = jax.nn.sigmoid(scores)
        silu = scores * sigma
        attn = jnp.where(masked, silu, 0.0).astype(BF16)
        factor = jnp.where(masked, (sigma + silu * (1.0 - sigma)) * scale, 0.0)
        mixed = jnp.dot(attn, value, preferred_element_type=F32)
        centred = mixed - jnp.mean(mixed, axis=-1, keepdims=True)
        inv_std = lax.rsqrt(jnp.mean(centred * centred, axis=-1, keepdims=True) + NORM_FLOOR)
        normed = centred * inv_std
        gating = acts[rows, u_cols].astype(F32)
        gated[rows, :] = (normed * gating).astype(BF16)
        d_gated = jnp.dot(packs[1, rows, :], w[:, 4 * hd :], preferred_element_type=F32)
        d_normed = d_gated * gating
        d_mixed = (
            inv_std
            * (
                d_normed
                - jnp.mean(d_normed, axis=-1, keepdims=True)
                - normed * jnp.mean(d_normed * normed, axis=-1, keepdims=True)
            )
        ).astype(BF16)
        d_scores = (dot_nt(d_mixed, value) * factor).astype(BF16)
        d_query = jnp.dot(d_scores, key, preferred_element_type=F32)
        d_value[...] += dot_tn(attn, d_mixed)
        d_key[...] += dot_tn(d_scores, query)
        d_z[rows, u_cols] = (d_gated * normed * slope[rows, u_cols]).astype(BF16)
        d_z[rows, q_cols] = (d_query * slope[rows, q_cols]).astype(BF16)
        return carry

    lax.fori_loop(0, LENGTH // STEP, attend, 0)
    d_z[:, v_cols] = (d_value[...] * slope[:, v_cols]).astype(BF16)
    d_z[:, k_cols] = (d_key[...] * slope[:, k_cols]).astype(BF16)

    core = info[3]
    groups = STEP // LANES

    def parts(step, carry):
        rows = pl.ds(pl.multiple_of(step * STEP, STEP), STEP)
        part = dot_nt(d_z[rows, :], w[:, : 4 * hd]).astype(BF16)
        for g in range(groups):
            for y in range(Y):
                first = g * LANES + y * 32
                low, high = part[first : first + 16], part[first + 16 : first + 32]

                @pl.when(core == 0)
                def _():
                    kept[y, step * groups + g] = low
                    sent[y, step * groups + g] = high

                @pl.when(core != 0)
                def _():
                    kept[y, step * groups + g] = high
                    sent[y, step * groups + g] = low

        return carry

    lax.fori_loop(0, LENGTH // STEP, parts, 0)


def heads_backward(info, packs, weights):
    vmem = pl.BlockSpec(memory_space=pltpu.VMEM)
    half = jax.ShapeDtypeStruct((Y, 8, 16, WIDTH), BF16)
    return pl.pallas_call(
        heads_kernel,
        out_shape=(
            half,
            half,
            jax.ShapeDtypeStruct((LENGTH, 4 * HEAD_DIM), BF16),
            jax.ShapeDtypeStruct((LENGTH, HEAD_DIM), BF16),
        ),
        in_specs=[pl.BlockSpec(memory_space=pltpu.SMEM), vmem, vmem],
        out_specs=(vmem, vmem, vmem, vmem),
        scratch_shapes=[
            pltpu.VMEM((WIDTH, HIDDEN), BF16),
            pltpu.VMEM((LENGTH, 4 * HEAD_DIM), BF16),
            pltpu.VMEM((LENGTH, 4 * HEAD_DIM), F32),
            pltpu.VMEM((LENGTH, HEAD_DIM), F32),
            pltpu.VMEM((LENGTH, HEAD_DIM), F32),
        ],
        compiler_params=pltpu.CompilerParams(vmem_limit_bytes=44 * 2**20),
        cost_estimate=pl.CostEstimate(
            flops=4_600_000_000, bytes_accessed=9_000_000, transcendentals=3_000_000
        ),
        name="heads",
    )(info, packs, weights)


def grads_kernel(packs, d_z, gated, out):
    for x in range(X):
        cols = slice(x * YC * 32, (x + 1) * YC * 32)
        for dest, source, pack in ((slice(0, 512), d_z, 0), (slice(512, 640), gated, 1)):
            block = dot_tn(packs[pack, :, cols], source[...]).astype(BF16)
            for yc in range(YC):
                for r in range(ZR):
                    first = yc * 32 + r * PART_ROWS
                    out[x, r, yc, :, dest] = block[first : first + PART_ROWS]


def weight_grads(packs, d_z, gated):
    vmem = pl.BlockSpec(memory_space=pltpu.VMEM)
    return pl.pallas_call(
        grads_kernel,
        out_shape=jax.ShapeDtypeStruct((X, ZR, YC, PART_ROWS, HIDDEN), BF16),
        in_specs=[vmem, vmem, vmem],
        out_specs=vmem,
        compiler_params=pltpu.CompilerParams(vmem_limit_bytes=32 * 2**20),
        cost_estimate=pl.CostEstimate(
            flops=1_350_000_000, bytes_accessed=6_800_000, transcendentals=0
        ),
        name="weight_grads",
    )(packs, d_z, gated)


def per_device(inputs, cotangent, lengths, item_ids, owner_row, w_project, w_output):
    width = inputs.shape[3]
    blocks = width // LANES
    core = lax.axis_index("c")
    y_here = lax.axis_index("y")
    z_here = lax.axis_index(SEQ)
    lane = jnp.arange(LANES, dtype=jnp.int32)

    slot, local_row = routing(item_ids, owner_row)
    lens = lengths.reshape(-1)
    lens_row = jnp.concatenate([lens // 256, lens % 256])
    lens_row = jnp.pad(lens_row, (0, LANES - lens_row.shape[0]))
    small = jnp.pad(jnp.stack([slot, local_row, lens_row]), ((0, 5), (0, 0))).astype(BF16)
    high = PART_ROWS // 8
    n_w = 3 * high + 1
    wp_tiles = w_project.reshape(ZR, high, 8, 2, LANES).transpose(0, 1, 3, 2, 4)
    wo_t = w_output.T
    wo_tiles = jnp.concatenate([wo_t, wo_t], axis=1).reshape(ZR, high, 8, LANES)
    small = jnp.broadcast_to(small[None, None], (ZR, 1, 8, LANES))
    w_tiles = jnp.concatenate([wp_tiles.reshape(ZR, 2 * high, 8, LANES), wo_tiles, small], axis=1)

    both = jnp.stack([inputs[0], cotangent[0]]).reshape(2, 2, 8, 8, blocks, LANES)
    spread = exchange(both.transpose(2, 1, 0, 4, 3, 5), PAIR)
    spread = spread.reshape(Z, 2 * blocks, 8, LANES)
    w_tiles = jnp.broadcast_to(w_tiles[None], (ZQ, ZR, n_w, 8, LANES)).reshape(Z, n_w, 8, LANES)
    arrived = exchange(jnp.concatenate([spread, w_tiles], axis=1), SEQ)
    mine = arrived[:, : 2 * blocks].reshape(Z, 2, blocks, 8, LANES)
    mine = mine.transpose(1, 0, 3, 2, 4).reshape(2, Z * 8, width)
    packs = lax.all_gather(mine, PAIR, axis=1, tiled=True)

    by_head = exchange(arrived[:, 2 * blocks :].reshape(YC, 2, n_w, 8, LANES), PAIR)
    wp_part = by_head[:, :, : 2 * high].reshape(YC, 2, high, 2, 8, LANES)
    wp_part = wp_part.transpose(0, 2, 4, 1, 3, 5).reshape(YC, PART_ROWS, 4 * HEAD_DIM)
    wo_part = by_head[:, :, 2 * high : 3 * high]
    wo_part = jnp.where(lane < 64, wo_part[:, 0], wo_part[:, 1])
    w_part = jnp.concatenate([wp_part, wo_part.reshape(YC, PART_ROWS, HEAD_DIM)], axis=2)
    w_all = jnp.broadcast_to(w_part[None], (X * ZR,) + w_part.shape)
    weights = exchange(w_all, SHARE).reshape(X, ZR, YC, PART_ROWS, HIDDEN)

    facts = by_head[:, :, n_w - 1].astype(F32)
    slots = facts[:, :, 0].astype(jnp.int32)
    tag_of = facts[:, :, 1]
    lens_all = facts[:, 0, 2, :12].reshape(YC, 2, 2, 3)
    lens_all = (lens_all[:, 0] * 256.0 + lens_all[:, 1]).astype(jnp.int32).reshape(Z, 3)
    pack_lens = lax.dynamic_index_in_dim(lens_all, z_here, 0, keepdims=False)
    ends = jnp.cumsum(pack_lens)

    info = jnp.concatenate([ends, core[None]]).astype(jnp.int32)
    kept, sent, d_z, gated = heads_backward(info, packs, weights)

    got = lax.ppermute(sent, "c", [(0, 1), (1, 0)])
    pair_sum = (kept.astype(F32) + got.astype(F32)).astype(BF16)
    quad = lax.dynamic_index_in_dim(pair_sum, y_here, 0, keepdims=False).astype(F32)
    for step in range(1, Y):
        there = lax.dynamic_index_in_dim(pair_sum, (y_here + step) % Y, 0, keepdims=False)
        came = lax.ppermute(there, "y", [(i, (i + step) % Y) for i in range(Y)])
        quad = quad + came.astype(F32)
    own = y_here * C + core
    dy_own = lax.dynamic_index_in_dim(
        packs[1].reshape(8, YC, 16, width), own, 1, keepdims=False
    )
    token = (dy_own.astype(F32) + quad).astype(BF16)
    token = token.reshape(8, 2, 8, Z, 64).transpose(3, 0, 2, 1, 4).reshape(Z, 8, 8, LANES)

    grads = weight_grads(packs, d_z, gated)
    shared = exchange(grads.reshape(X * ZR, YC, PART_ROWS, HIDDEN), SHARE)
    w_sum = jnp.sum(shared.astype(F32), axis=0).astype(BF16)
    wp_sum = w_sum[:, :, : 4 * HEAD_DIM].reshape(YC, high, 8, 2, 2, LANES)
    wp_sum = wp_sum.transpose(0, 3, 1, 4, 2, 5).reshape(Z, 2 * high, 8, LANES)
    wo_sum = w_sum[:, None, :, 4 * HEAD_DIM :]
    wo_sum = jnp.broadcast_to(wo_sum, (YC, 2, PART_ROWS, LANES)).reshape(Z, high, 8, LANES)

    merged = exchange(jnp.concatenate([token, wp_sum, wo_sum], axis=1), SEQ)
    w_grad = jnp.sum(merged[:, 8:].astype(F32).reshape(ZQ, ZR, 3 * high, 8, LANES), axis=0)
    turn = [
        ((x * YC + a) * Z + b * 2 + s, (x * YC + b) * Z + a * 2 + s)
        for x in range(X)
        for a in range(YC)
        for b in range(YC)
        for s in range(2)
    ]
    w_grad = lax.ppermute(w_grad, ALL, turn)
    grad_proj = w_grad[:, : 2 * high].reshape(ZR, high, 2, 8, LANES)
    grad_proj = grad_proj.transpose(0, 1, 3, 2, 4).reshape(32, 2 * LANES)
    both_out = w_grad[:, 2 * high :].reshape(32, 2, 64)
    grad_out = lax.dynamic_index_in_dim(both_out, z_here % 2, 1, keepdims=False).T

    tokens = merged[:, :8].reshape(YC, LANES, LANES)
    slot_ids = jnp.arange(SLOTS, dtype=jnp.int32)
    placed = slots[:, :, None, :] == slot_ids[None, None, :, None]
    tags = jnp.sum(jnp.where(placed, tag_of[:, :, None, :], 0.0), axis=3)
    moved = jnp.einsum(
        "asut,atl->saul", placed.astype(BF16), tokens, preferred_element_type=F32
    )
    rows_out = jnp.where(lane < 64, moved[0], moved[1]).astype(BF16)
    rows_out = rows_out.reshape(YC, OWNERS, CAP, LANES).transpose(1, 0, 2, 3)
    tags = tags.reshape(YC, 2, OWNERS, CAP).transpose(2, 0, 1, 3).reshape(OWNERS, 1, 1, LANES)
    tags = jnp.pad(tags.astype(BF16), ((0, 0), (0, 0), (0, 7), (0, 0)))
    owned = exchange(jnp.concatenate([rows_out, tags], axis=1), DP)
    got_rows = owned[:, :YC].reshape(OWNERS * YC * CAP, LANES)
    got_tags = owned[:, YC, 0].astype(F32).astype(jnp.int32).reshape(OWNERS, YC, 2, CAP)
    got_tags = got_tags.transpose(2, 0, 1, 3).reshape(2, 1, OWNERS * YC * CAP)
    row_ids = jnp.arange(ROWS, dtype=jnp.int32)
    select = (got_tags == row_ids[None, :, None]).astype(BF16)
    sums = jnp.einsum("srk,kl->srl", select, got_rows, preferred_element_type=F32)
    grad_table = sums[0, :, :64] + sums[1, :, 64:]
    return (grad_proj, grad_out, grad_table)


def solution(mesh):
    fine = Mesh(mesh.devices.reshape(X, Y, C, ZQ, ZR), ALL)
    return jax.shard_map(
        per_device,
        mesh=fine,
        in_specs=(
            P(DP, None, SEQ, None),
            P(DP, None, SEQ, None),
            P(DP, None, None),
            P(DP, None, SEQ),
            P(),
            P(DP, SEQ),
            P(SEQ, DP),
        ),
        out_specs=(P(DP, SEQ), P(SEQ, DP), P(DP, SEQ)),
        check_vma=False,
    )
```

time: 264 us -> 240 us (0.909)
  matrix products: 23.3 us -> 1.57 us
  Pallas kernels: 0 us -> 15.3 us
  local copies, waits for them, and re-layouts: 24.1 us -> 13.1 us
  waiting for transfers between devices: 84 us -> 76.1 us
  blocking collectives: 47.2 us -> 50.8 us
    dot_general x11 -> x0, matrix products: 21.7 us -> none  [the longest x1 4.88 us: heads_backward(): z_pre = jnp.dot(px, wp, preferred_element_type=F32)]
    pallas_call x0 -> x2, Pallas kernels: none -> 15.3 us  [the longest x1 12.4 us: heads_backward(): pl.pallas_call(heads_kernel, out_shape=(half, half, jax.ShapeDtypeStruct(...]
    all_to_all x6, waiting for transfers between devices: 61.3 us -> 52.6 us  [exchange(): return lax.all_to_all(value, axes, split_axis=0, concat_axis=0, tiled=True)]
    dot_general x2 -> x0, local copies, waits for them, and re-layouts: 6.54 us -> none  [the longest x1 3.93 us: heads_backward(): lax.dot_general(px, d_z, first, preferred_element_type=F32)]
    all_to_all x1, blocking collectives: 47.2 us -> 50.8 us  [exchange(): return lax.all_to_all(value, axes, split_axis=0, concat_axis=0, tiled=True)]
    slice x1 -> x2, local copies, waits for them, and re-layouts: 2.78 us -> 0.01 us  [per_device(): packs[1].reshape(8, YC, 16, width)]
  transfers between devices with their start and end apart: 12 -> 12, of which waited for: 9 -> 9; matrix products, arithmetic and copies ran while one was open for 6% -> 5% of each run, Pallas kernels for 0% -> 0%
where the time goes in v2:
time: 240 us
  waiting for transfers between devices  76.1 us (32%)
  starting transfers between devices  60.7 us (25%)
  blocking collectives  50.8 us (21%)
  Pallas kernels  15.3 us (6%)
  between operations  14.6 us (6%)
  local copies, waits for them, and re-layouts  13.1 us (5%)
  other arithmetic  7.44 us (3%)
    all_to_all x6, waiting for transfers between devices, exchange(): return lax.all_to_all(value, axes, split_axis=0, concat_axis=0, tiled=True)  52.6 us
    all_to_all x1, blocking collectives, exchange(): return lax.all_to_all(value, axes, split_axis=0, concat_axis=0, tiled=True)  50.8 us
    all_to_all x6, starting transfers between devices, exchange(): return lax.all_to_all(value, axes, split_axis=0, concat_axis=0, tiled=True)  41.6 us
    pallas_call x1, Pallas kernels, heads_backward(): pl.pallas_call(heads_kernel, out_shape=(half, half, jax.ShapeDtypeStruct(...  12.4 us
    ppermute x3, starting transfers between devices, per_device(): came = lax.ppermute(there, 'y', [(i, (i + step) % Y) for i in range(Y)])  11.2 us
    ppermute x1, waiting for transfers between devices, per_device(): w_grad = lax.ppermute(w_grad, ALL, turn)  11 us
    ppermute x3, waiting for transfers between devices, per_device(): came = lax.ppermute(there, 'y', [(i, (i + step) % Y) for i in range(Y)])  9.82 us
    ppermute x1, starting transfers between devices, per_device(): w_grad = lax.ppermute(w_grad, ALL, turn)  6.11 us
  transfers between devices with their start and end apart: 12, of which 9 were waited for; matrix products, arithmetic and copies ran while one was open for 5% of the time, Pallas kernels for 0%

profile of v2, /device:TPU:16, one launch (start us, length us, event | category | flops | bytes accessed | tf_op | source)
XLA Modules:
  0.0 239.6 jit_solution(2631546011544293620)
XLA Ops:
  9.2 9.1 %all-to-all-start = ((bf16[8,2,2,8,8,128]{5,3,4,1,2,0:T(8,128)(2,1)}), bf16[8,2,2,8,8,128]{5,3,4,1,2,0:T(8,128)(2,1)S(1)}, u32[]{:S(2)}, u32[]{:S(2)}) async-start(bf16[8,2,2,8,8,128]{5,3,4,1,2,0:T(8,128)(2,1)} %copy.69), calls=%async_computation | async-start | bytes 1048576 | tf_op jit(solution)/shard_map/all_to_all | solution.py:34
  20.3 5.2 %all-to-all-done = bf16[8,2,2,8,8,128]{5,3,4,1,2,0:T(8,128)(2,1)S(1)} async-done(((bf16[8,2,2,8,8,128]{5,3,4,1,2,0:T(8,128)(2,1)}), bf16[8,2,2,8,8,128]{5,3,4,1,2,0:T(8,128)(2,1)S(1)}, u32[]{:S(2)}, u32[]{:S(2)}) %all-to-all-start) | async-done | bytes 524320 | tf_op jit(solution)/shard_map/all_to_all | solution.py:34
  25.8 50.8 %all_to_all.35 = bf16[16,23,8,128]{3,2,1,0:T(8,128)(2,1)S(1)} all-to-all(bf16[16,23,8,128]{3,2,1,0:T(8,128)(2,1)S(1)} %pad_maximum_fusion), channel_id=1, replica_groups=mesh['x'=4,'y'=4,'c'=2,'zq'=8,'zr'=2] {'zq','zr'}, dimensions={0} | all-to-all | bytes 1507328 | tf_op jit(solution)/shard_map/all_to_all | solution.py:34
  78.2 6.2 %all-to-all-start.2 = ((bf16[8,2,7,8,128]{4,3,2,1,0:T(8,128)(2,1)}), bf16[8,2,7,8,128]{4,3,2,1,0:T(8,128)(2,1)S(1)}, u32[]{:S(2)}, u32[]{:S(2)}) async-start(bf16[8,2,7,8,128]{4,3,2,1,0:T(8,128)(2,1)} %bitcast.17), calls=%async_computation.2 | async-start | bytes 458752 | tf_op jit(solution)/shard_map/all_to_all | solution.py:34
  84.4 4.1 %all-to-all-done.2 = bf16[8,2,7,8,128]{4,3,2,1,0:T(8,128)(2,1)S(1)} async-done(((bf16[8,2,7,8,128]{4,3,2,1,0:T(8,128)(2,1)}), bf16[8,2,7,8,128]{4,3,2,1,0:T(8,128)(2,1)S(1)}, u32[]{:S(2)}, u32[]{:S(2)}) %all-to-all-start.2) | async-done | bytes 229408 | tf_op jit(solution)/shard_map/all_to_all | solution.py:34
  89.8 5.7 %all-to-all-start.3 = ((bf16[8,8,16,640]{3,2,1,0:T(8,128)(2,1)}), bf16[8,8,16,640]{3,2,1,0:T(8,128)(2,1)S(1)}, u32[]{:S(2)}, u32[]{:S(2)}) async-start(bf16[8,8,16,640]{3,2,1,0:T(8,128)(2,1)} %broadcast_in_dim.70), calls=%async_computation.3 | async-start | bytes 2621440 | tf_op jit(solution)/shard_map/all_to_all | solution.py:34
  96.2 17.7 %all-to-all-done.3 = bf16[8,8,16,640]{3,2,1,0:T(8,128)(2,1)S(1)} async-done(((bf16[8,8,16,640]{3,2,1,0:T(8,128)(2,1)}), bf16[8,8,16,640]{3,2,1,0:T(8,128)(2,1)S(1)}, u32[]{:S(2)}, u32[]{:S(2)}) %all-to-all-start.3) | async-done | bytes 1310752 | tf_op jit(solution)/shard_map/all_to_all | solution.py:34
  114.0 2.2 copy-done.1
  116.2 12.4 %heads.1 = (bf16[4,8,16,1024]{3,2,1,0:T(8,128)(2,1)S(1)}, bf16[4,8,16,1024]{3,2,1,0:T(8,128)(2,1)S(1)}, bf16[1024,512]{1,0:T(8,128)(2,1)S(1)}, bf16[1024,128]{1,0:T(8,128)(2,1)S(1)}) custom-call(s32[4]{0:T(128)S(1)} %pad_add_fusion.info, bf16[2,1024,1024]{2,1,0:T(8,128)(2,1)S(1)} %copy-done.1, bf16[4,2,8,16,640]{4,3,2,1,0:T(8,128)(2,1)S(1)} %bitcast.138), custom_call_target="tpu_custom_call" | custom-call | flops 4600000000 | bytes 9000000 | tf_op jit(solution)/shard_map/heads/pallas_call | solution.py:157
  128.6 2.9 %weight_grads.1 = bf16[4,2,8,16,640]{4,3,2,1,0:T(8,128)(2,1)} custom-call(bf16[2,1024,1024]{2,1,0:T(8,128)(2,1)S(1)} %copy-done.1, bf16[1024,512]{1,0:T(8,128)(2,1)S(1)} %get-tuple-element.9.d_z, bf16[1024,128]{1,0:T(8,128)(2,1)S(1)} %get-tuple-element.10.gated), custom_call_target="tpu_custom_call" | custom-call | flops 1350000000 | bytes 6800000 | tf_op jit(solution)/shard_map/weight_grads/pallas_call | solution.py:195
  131.5 3.6 %all-to-all-start.4 = ((bf16[8,8,16,640]{3,2,1,0:T(8,128)(2,1)}), bf16[8,8,16,640]{3,2,1,0:T(8,128)(2,1)S(1)}, u32[]{:S(2)}, u32[]{:S(2)}) async-start(bf16[8,8,16,640]{3,2,1,0:T(8,128)(2,1)} %bitcast.32), calls=%async_computation.4 | async-start | bytes 2621440 | tf_op jit(solution)/shard_map/all_to_all | solution.py:34
  135.1 1.9 collective-permute-start
  137.1 2.7 %collective-permute-done = bf16[4,8,16,1024]{3,2,1,0:T(8,128)(2,1)} collective-permute-done((bf16[4,8,16,1024]{3,2,1,0:T(8,128)(2,1)S(1)}, bf16[4,8,16,1024]{3,2,1,0:T(8,128)(2,1)}, u32[]{:S(2)}, u32[]{:S(2)}) %collective-permute-start) | collective-permute-done | bytes 1048608 | tf_op jit(solution)/shard_map/ppermute | solution.py:258
  139.8 1.6 add_convert_fusion
  141.5 3.8 %collective-permute-start.3 = (bf16[8,16,1024]{2,1,0:T(8,128)(2,1)S(1)}, bf16[8,16,1024]{2,1,0:T(8,128)(2,1)S(1)}, u32[]{:S(2)}, u32[]{:S(2)}) collective-permute-start(bf16[8,16,1024]{2,1,0:T(8,128)(2,1)S(1)} %get-tuple-element.16), channel_id=1, source_target_pairs={{0,96},{32,0},{64,32},{96,64},{1,97},{33,1},{65,33},{97,65},{2,98}... | collective-permute-start | bytes 786440 | tf_op jit(solution)/shard_map/ppermute | solution.py:263
  145.3 4.0 %collective-permute-start.2 = (bf16[8,16,1024]{2,1,0:T(8,128)(2,1)S(1)}, bf16[8,16,1024]{2,1,0:T(8,128)(2,1)}, u32[]{:S(2)}, u32[]{:S(2)}) collective-permute-start(bf16[8,16,1024]{2,1,0:T(8,128)(2,1)S(1)} %get-tuple-element.17), channel_id=1, source_target_pairs={{0,64},{32,96},{64,0},{96,32},{1,65},{33,97},{65,1},{97,33},{2,66}... | collective-permute-start | bytes 786440 | tf_op jit(solution)/shard_map/ppermute | solution.py:263
  149.3 3.4 %collective-permute-start.1 = (bf16[8,16,1024]{2,1,0:T(8,128)(2,1)S(1)}, bf16[8,16,1024]{2,1,0:T(8,128)(2,1)}, u32[]{:S(2)}, u32[]{:S(2)}) collective-permute-start(bf16[8,16,1024]{2,1,0:T(8,128)(2,1)S(1)} %get-tuple-element.15), channel_id=1, source_target_pairs={{0,32},{32,64},{64,96},{96,0},{1,33},{33,65},{65,97},{97,1},{2,34}... | collective-permute-start | bytes 786440 | tf_op jit(solution)/shard_map/ppermute | solution.py:263
  152.7 4.1 %collective-permute-done.3 = bf16[8,16,1024]{2,1,0:T(8,128)(2,1)S(1)} collective-permute-done((bf16[8,16,1024]{2,1,0:T(8,128)(2,1)S(1)}, bf16[8,16,1024]{2,1,0:T(8,128)(2,1)S(1)}, u32[]{:S(2)}, u32[]{:S(2)}) %collective-permute-start.3) | collective-permute-done | bytes 262176 | tf_op jit(solution)/shard_map/ppermute | solution.py:263
  158.0 4.4 %collective-permute-done.1 = bf16[8,16,1024]{2,1,0:T(8,128)(2,1)} collective-permute-done((bf16[8,16,1024]{2,1,0:T(8,128)(2,1)S(1)}, bf16[8,16,1024]{2,1,0:T(8,128)(2,1)}, u32[]{:S(2)}, u32[]{:S(2)}) %collective-permute-start.1) | collective-permute-done | bytes 262176 | tf_op jit(solution)/shard_map/ppermute | solution.py:263
  166.0 9.5 %all-to-all-start.5 = ((bf16[16,14,8,128]{3,2,1,0:T(8,128)(2,1)}), bf16[16,14,8,128]{3,2,1,0:T(8,128)(2,1)S(1)}, u32[]{:S(2)}, u32[]{:S(2)}) async-start(bf16[16,14,8,128]{3,2,1,0:T(8,128)(2,1)} %pad_maximum_fusion.2), calls=%async_computation.5 | async-start | bytes 917504 | tf_op jit(solution)/shard_map/all_to_all | solution.py:34
  176.8 25.6 %all-to-all-done.5 = bf16[16,14,8,128]{3,2,1,0:T(8,128)(2,1)S(1)} async-done(((bf16[16,14,8,128]{3,2,1,0:T(8,128)(2,1)}), bf16[16,14,8,128]{3,2,1,0:T(8,128)(2,1)S(1)}, u32[]{:S(2)}, u32[]{:S(2)}) %all-to-all-start.5) | async-done | bytes 458784 | tf_op jit(solution)/shard_map/all_to_all | solution.py:34
  204.7 7.4 %all-to-all-start.6 = ((bf16[32,9,8,128]{3,2,1,0:T(8,128)(2,1)}), bf16[32,9,8,128]{3,2,1,0:T(8,128)(2,1)S(1)}, u32[]{:S(2)}, u32[]{:S(2)}) async-start(bf16[32,9,8,128]{3,2,1,0:T(8,128)(2,1)} %copy.84), calls=%async_computation.6 | async-start | bytes 1179648 | tf_op jit(solution)/shard_map/all_to_all | solution.py:34
  212.2 6.1 %collective-permute-start.4 = (f32[2,6,8,128]{3,2,1,0:T(8,128)S(1)}, f32[2,6,8,128]{3,2,1,0:T(8,128)S(1)}, u32[]{:S(2)}, u32[]{:S(2)}) collective-permute-start(f32[2,6,8,128]{3,2,1,0:T(8,128)S(1)} %convert_reduce_fusion), channel_id=1, source_target_pairs={{0,0},{1,1},{2,16},{3,17},{4,32},{5,33},{6,48},{7,49},{8,64},{9,65... | collective-permute-start | bytes 147464 | tf_op jit(solution)/shard_map/ppermute | solution.py:289
  218.3 11.0 %collective-permute-done.4 = f32[2,6,8,128]{3,2,1,0:T(8,128)S(1)} collective-permute-done((f32[2,6,8,128]{3,2,1,0:T(8,128)S(1)}, f32[2,6,8,128]{3,2,1,0:T(8,128)S(1)}, u32[]{:S(2)}, u32[]{:S(2)}) %collective-permute-start.4) | collective-permute-done | bytes 49184 | tf_op jit(solution)/shard_map/ppermute | solution.py:289
  (99 shorter events, 19.5 us)
Async XLA Ops:
  7.2 11.6 %copy-start = (s32[8192]{0:T(1024)S(1)}, s32[8192]{0:T(1024)}, u32[]{:S(2)}) copy-start(s32[8192]{0:T(1024)} %param.11) | copy-start | bytes 98308
  7.2 11.2 %copy-start.4 = (s32[1,2,64]{2,1,0:T(2,128)S(1)}, s32[1,2,64]{2,1,0:T(2,128)}, u32[]{:S(2)}) copy-start(s32[1,2,64]{2,1,0:T(2,128)} %param.10) | copy-start | bytes 1540
  7.2 11.4 %copy-start.5 = (s32[1,2,3]{2,1,0:T(2,128)S(1)}, s32[1,2,3]{2,1,0:T(2,128)}, u32[]{:S(2)}) copy-start(s32[1,2,3]{2,1,0:T(2,128)} %param.9) | copy-start | bytes 76
  7.2 13.0 %copy-start.3 = (bf16[64,32]{0,1:T(8,128)(2,1)S(1)}, bf16[64,32]{0,1:T(8,128)(2,1)}, u32[]{:S(2)}) copy-start(bf16[64,32]{0,1:T(8,128)(2,1)} %param.13) | copy-start | bytes 12292
  7.2 13.1 %copy-start.2 = (bf16[32,256]{1,0:T(8,128)(2,1)S(1)}, bf16[32,256]{1,0:T(8,128)(2,1)}, u32[]{:S(2)}) copy-start(bf16[32,256]{1,0:T(8,128)(2,1)} %param.12) | copy-start | bytes 49156
  9.2 16.3 %all-to-all-start = ((bf16[8,2,2,8,8,128]{5,3,4,1,2,0:T(8,128)(2,1)}), bf16[8,2,2,8,8,128]{5,3,4,1,2,0:T(8,128)(2,1)S(1)}, u32[]{:S(2)}, u32[]{:S(2)}) async-start(bf16[8,2,2,8,8,128]{5,3,4,1,2,0:T(8,128)(2,1)} %copy.69), calls=%async_computation | async-start | bytes 1048576 | tf_op jit(solution)/shard_map/all_to_all | solution.py:34
  18.4 95.6 %all-gather.2.cloned.1.call-start = ((), (), s32[]{:S(2)}) async-start(), calls=%async_computation.7 | async-start | bytes 4718592 | tf_op jit(solution)/shard_map/all_gather | solution.py:236
  78.2 10.3 %all-to-all-start.2 = ((bf16[8,2,7,8,128]{4,3,2,1,0:T(8,128)(2,1)}), bf16[8,2,7,8,128]{4,3,2,1,0:T(8,128)(2,1)S(1)}, u32[]{:S(2)}, u32[]{:S(2)}) async-start(bf16[8,2,7,8,128]{4,3,2,1,0:T(8,128)(2,1)} %bitcast.17), calls=%async_computation.2 | async-start | bytes 458752 | tf_op jit(solution)/shard_map/all_to_all | solution.py:34
  89.8 24.2 %all-to-all-start.3 = ((bf16[8,8,16,640]{3,2,1,0:T(8,128)(2,1)}), bf16[8,8,16,640]{3,2,1,0:T(8,128)(2,1)S(1)}, u32[]{:S(2)}, u32[]{:S(2)}) async-start(bf16[8,8,16,640]{3,2,1,0:T(8,128)(2,1)} %broadcast_in_dim.70), calls=%async_computation.3 | async-start | bytes 2621440 | tf_op jit(solution)/shard_map/all_to_all | solution.py:34
  114.0 2.2 copy-start.1
  131.5 33.4 %all-to-all-start.4 = ((bf16[8,8,16,640]{3,2,1,0:T(8,128)(2,1)}), bf16[8,8,16,640]{3,2,1,0:T(8,128)(2,1)S(1)}, u32[]{:S(2)}, u32[]{:S(2)}) async-start(bf16[8,8,16,640]{3,2,1,0:T(8,128)(2,1)} %bitcast.32), calls=%async_computation.4 | async-start | bytes 2621440 | tf_op jit(solution)/shard_map/all_to_all | solution.py:34
  135.1 4.7 %collective-permute-start = (bf16[4,8,16,1024]{3,2,1,0:T(8,128)(2,1)S(1)}, bf16[4,8,16,1024]{3,2,1,0:T(8,128)(2,1)}, u32[]{:S(2)}, u32[]{:S(2)}) collective-permute-start(bf16[4,8,16,1024]{3,2,1,0:T(8,128)(2,1)S(1)} %get-tuple-element.8), channel_id=1, source_target_pairs={{0,16},{16,0},{1,17},{17,1},{2,18},{18,2},{3,19},{19,3},{4,20},{20... | collective-permute-start | bytes 3145736 | tf_op jit(solution)/shard_map/ppermute | solution.py:258
  141.5 15.3 %collective-permute-start.3 = (bf16[8,16,1024]{2,1,0:T(8,128)(2,1)S(1)}, bf16[8,16,1024]{2,1,0:T(8,128)(2,1)S(1)}, u32[]{:S(2)}, u32[]{:S(2)}) collective-permute-start(bf16[8,16,1024]{2,1,0:T(8,128)(2,1)S(1)} %get-tuple-element.16), channel_id=1, source_target_pairs={{0,96},{32,0},{64,32},{96,64},{1,97},{33,1},{65,33},{97,65},{2,98}... | collective-permute-start | bytes 786440 | tf_op jit(solution)/shard_map/ppermute | solution.py:263
  145.3 12.7 %collective-permute-start.2 = (bf16[8,16,1024]{2,1,0:T(8,128)(2,1)S(1)}, bf16[8,16,1024]{2,1,0:T(8,128)(2,1)}, u32[]{:S(2)}, u32[]{:S(2)}) collective-permute-start(bf16[8,16,1024]{2,1,0:T(8,128)(2,1)S(1)} %get-tuple-element.17), channel_id=1, source_target_pairs={{0,64},{32,96},{64,0},{96,32},{1,65},{33,97},{65,1},{97,33},{2,66}... | collective-permute-start | bytes 786440 | tf_op jit(solution)/shard_map/ppermute | solution.py:263
  149.3 13.2 %collective-permute-start.1 = (bf16[8,16,1024]{2,1,0:T(8,128)(2,1)S(1)}, bf16[8,16,1024]{2,1,0:T(8,128)(2,1)}, u32[]{:S(2)}, u32[]{:S(2)}) collective-permute-start(bf16[8,16,1024]{2,1,0:T(8,128)(2,1)S(1)} %get-tuple-element.15), channel_id=1, source_target_pairs={{0,32},{32,64},{64,96},{96,0},{1,33},{33,65},{65,97},{97,1},{2,34}... | collective-permute-start | bytes 786440 | tf_op jit(solution)/shard_map/ppermute | solution.py:263
  152.7 9.8 %slice-start = ((bf16[2,1024,1024]{2,1,0:T(8,128)(2,1)}), bf16[1,1024,1024]{2,1,0:T(8,128)(2,1)S(1)}, s32[]{:S(2)}) async-start(bf16[2,1024,1024]{2,1,0:T(8,128)(2,1)} %all-gather.2.cloned.1.call-done.packs), calls=%async_computation.8 | async-start | bytes 4194304 | tf_op jit(solution)/shard_map/slice | solution.py:267
  166.0 36.4 %all-to-all-start.5 = ((bf16[16,14,8,128]{3,2,1,0:T(8,128)(2,1)}), bf16[16,14,8,128]{3,2,1,0:T(8,128)(2,1)S(1)}, u32[]{:S(2)}, u32[]{:S(2)}) async-start(bf16[16,14,8,128]{3,2,1,0:T(8,128)(2,1)} %pad_maximum_fusion.2), calls=%async_computation.5 | async-start | bytes 917504 | tf_op jit(solution)/shard_map/all_to_all | solution.py:34
  204.7 25.9 %all-to-all-start.6 = ((bf16[32,9,8,128]{3,2,1,0:T(8,128)(2,1)}), bf16[32,9,8,128]{3,2,1,0:T(8,128)(2,1)S(1)}, u32[]{:S(2)}, u32[]{:S(2)}) async-start(bf16[32,9,8,128]{3,2,1,0:T(8,128)(2,1)} %copy.84), calls=%async_computation.6 | async-start | bytes 1179648 | tf_op jit(solution)/shard_map/all_to_all | solution.py:34
  212.2 17.1 %collective-permute-start.4 = (f32[2,6,8,128]{3,2,1,0:T(8,128)S(1)}, f32[2,6,8,128]{3,2,1,0:T(8,128)S(1)}, u32[]{:S(2)}, u32[]{:S(2)}) collective-permute-start(f32[2,6,8,128]{3,2,1,0:T(8,128)S(1)} %convert_reduce_fusion), channel_id=1, source_target_pairs={{0,0},{1,1},{2,16},{3,17},{4,32},{5,33},{6,48},{7,49},{8,64},{9,65... | collective-permute-start | bytes 147464 | tf_op jit(solution)/shard_map/ppermute | solution.py:289
Sparse Core Ops, SparseCore 0:
  77.6 33.3 all-gather.1

commit v3 on v2

v3 whole, which is shorter than its diff:
```python
import jax
import jax.numpy as jnp
from jax import lax
from jax.experimental import pallas as pl
from jax.experimental.pallas import tpu as pltpu
from jax.sharding import Mesh, PartitionSpec as P

HEAD_DIM = 128
NORM_FLOOR = 1.0
F32 = jnp.float32
BF16 = jnp.bfloat16

X, Y, C, ZQ, ZR = 4, 4, 2, 8, 2
YC = Y * C
Z = ZQ * ZR
PAIR = ("y", "c")
DP = ("x", "y", "c")
SEQ = ("zq", "zr")
SHARE = ("x", "zr")
SPREAD = ("x", "y", "c", "zr")
ALL = ("x", "y", "c", "zq", "zr")
OWNERS = X * YC
CAP = 8
ROWS = 256
SLOTS = OWNERS * CAP
LANES = 128
LENGTH = 1024
WIDTH = 1024
HIDDEN = 5 * HEAD_DIM
PART_ROWS = 32 // ZR
STEP = 256
REACH = 512


def exchange(value, axes):
    return lax.all_to_all(value, axes, split_axis=0, concat_axis=0, tiled=True)


def routing(item_ids, owner_row):
    rows = jnp.take(owner_row, item_ids.reshape(-1))
    owner = rows // ROWS
    count = owner.shape[0]
    order = jnp.arange(count, dtype=jnp.int32)
    before = (owner[None, :] == owner[:, None]) & (order[None, :] < order[:, None])
    rank = jnp.sum(before.astype(jnp.int32), axis=1)
    return owner * CAP + rank, rows % ROWS


def dot_nt(a, b):
    return lax.dot_general(a, b, (((1,), (1,)), ((), ())), preferred_element_type=F32)


def dot_tn(a, b):
    return lax.dot_general(a, b, (((0,), (0,)), ((), ())), preferred_element_type=F32)


def heads_kernel(
    info, packs, w_in, kept, sent, grads, x_v, dy_v, w, acts, slope, d_value, d_key, d_z, gated, sems
):
    hd = HEAD_DIM
    scale = hd**-0.5
    u_cols, v_cols, q_cols, k_cols = (slice(m * hd, (m + 1) * hd) for m in range(4))
    x_copy = pltpu.make_async_copy(packs.at[:, 0], x_v, sems.at[0])
    dy_copy = pltpu.make_async_copy(packs.at[:, 1], dy_v, sems.at[1])
    x_copy.start()
    dy_copy.start()
    for x in range(X):
        for yc in range(YC):
            start = (x * YC + yc) * 32
            w[start : start + 32, :] = w_in[x, :, yc].reshape(32, HIDDEN)
    d_value[...] = jnp.zeros_like(d_value)
    d_key[...] = jnp.zeros_like(d_key)
    x_copy.wait()

    def project(step, carry):
        rows = pl.ds(pl.multiple_of(step * STEP, STEP), STEP)
        px = jnp.concatenate([x_v[g, rows, :] for g in range(8)], axis=1)
        z_pre = jnp.dot(px, w[:, : 4 * hd], preferred_element_type=F32)
        sigma = jax.nn.sigmoid(z_pre)
        silu = z_pre * sigma
        acts[rows, :] = silu.astype(BF16)
        slope[rows, :] = sigma + silu * (1.0 - sigma)
        return carry

    lax.fori_loop(0, LENGTH // STEP, project, 0)
    dy_copy.wait()

    for step in range(LENGTH // STEP):
        base = step * STEP
        first = max(0, base - REACH)
        rows = slice(base, base + STEP)
        span = slice(first, base + STEP)
        pos_k = lax.broadcasted_iota(jnp.int32, (1, base + STEP - first), 1) + first
        pos_q = lax.broadcasted_iota(jnp.int32, (STEP, 1), 0) + base
        start = jnp.zeros_like(pos_q)
        for n in range(3):
            start = jnp.where(pos_q >= info[n], info[n], start)
        masked = (pos_k <= pos_q) & (pos_k >= start)
        query = acts[rows, q_cols]
        key = acts[span, k_cols]
        value = acts[span, v_cols]
        scores = dot_nt(query, key) * scale
        sigma = jax.nn.sigmoid(scores)
        silu = scores * sigma
        attn = jnp.where(masked, silu, 0.0).astype(BF16)
        factor = jnp.where(masked, (sigma + silu * (1.0 - sigma)) * scale, 0.0)
        mixed = jnp.dot(attn, value, preferred_element_type=F32)
        centred = mixed - jnp.mean(mixed, axis=-1, keepdims=True)
        inv_std = lax.rsqrt(jnp.mean(centred * centred, axis=-1, keepdims=True) + NORM_FLOOR)
        normed = centred * inv_std
        gating = acts[rows, u_cols].astype(F32)
        gated[rows, :] = (normed * gating).astype(BF16)
        pdy = jnp.concatenate([dy_v[g, rows, :] for g in range(8)], axis=1)
        d_gated = jnp.dot(pdy, w[:, 4 * hd :], preferred_element_type=F32)
        d_normed = d_gated * gating
        d_mixed = (
            inv_std
            * (
                d_normed
                - jnp.mean(d_normed, axis=-1, keepdims=True)
                - normed * jnp.mean(d_normed * normed, axis=-1, keepdims=True)
            )
        ).astype(BF16)
        d_scores = (dot_nt(d_mixed, value) * factor).astype(BF16)
        d_query = jnp.dot(d_scores, key, preferred_element_type=F32)
        d_value[span, :] += dot_tn(attn, d_mixed)
        d_key[span, :] += dot_tn(d_scores, query)
        d_z[rows, u_cols] = (d_gated * normed * slope[rows, u_cols]).astype(BF16)
        d_z[rows, q_cols] = (d_query * slope[rows, q_cols]).astype(BF16)

    d_z[:, v_cols] = (d_value[...] * slope[:, v_cols]).astype(BF16)
    d_z[:, k_cols] = (d_key[...] * slope[:, k_cols]).astype(BF16)

    core = info[3]

    def parts(step, carry):
        rows = pl.ds(pl.multiple_of(step * STEP, STEP), STEP)
        part = dot_nt(d_z[rows, :], w[:, : 4 * hd]).astype(BF16)

        @pl.when(core == 0)
        def _():
            kept[step] = part[:LANES]
            sent[step] = part[LANES:]

        @pl.when(core != 0)
        def _():
            kept[step] = part[LANES:]
            sent[step] = part[:LANES]

        return carry

    lax.fori_loop(0, Y, parts, 0)

    for x in range(X):
        for dest, source, pack in ((slice(0, 512), d_z, x_v), (slice(512, 640), gated, dy_v)):
            columns = jnp.concatenate([pack[2 * x], pack[2 * x + 1]], axis=1)
            block = dot_tn(columns, source[...]).astype(BF16)
            for yc in range(YC):
                for r in range(ZR):
                    at = yc * 32 + r * PART_ROWS
                    grads[x, yc, r, :, dest] = block[at : at + PART_ROWS]


def heads_backward(info, packs, weights):
    vmem = pl.BlockSpec(memory_space=pltpu.VMEM)
    half = jax.ShapeDtypeStruct((Y, LANES, WIDTH), BF16)
    return pl.pallas_call(
        heads_kernel,
        out_shape=(
            half,
            half,
            jax.ShapeDtypeStruct((X, YC, ZR, PART_ROWS, HIDDEN), BF16),
        ),
        in_specs=[
            pl.BlockSpec(memory_space=pltpu.SMEM),
            pl.BlockSpec(memory_space=pltpu.HBM),
            vmem,
        ],
        out_specs=(vmem, vmem, vmem),
        scratch_shapes=[
            pltpu.VMEM((8, LENGTH, LANES), BF16),
            pltpu.VMEM((8, LENGTH, LANES), BF16),
            pltpu.VMEM((WIDTH, HIDDEN), BF16),
            pltpu.VMEM((LENGTH, 4 * HEAD_DIM), BF16),
            pltpu.VMEM((LENGTH, 4 * HEAD_DIM), F32),
            pltpu.VMEM((LENGTH, HEAD_DIM), F32),
            pltpu.VMEM((LENGTH, HEAD_DIM), F32),
            pltpu.VMEM((LENGTH, 4 * HEAD_DIM), BF16),
            pltpu.VMEM((LENGTH, HEAD_DIM), BF16),
            pltpu.SemaphoreType.DMA((2,)),
        ],
        compiler_params=pltpu.CompilerParams(vmem_limit_bytes=44 * 2**20),
        cost_estimate=pl.CostEstimate(
            flops=5_000_000_000, bytes_accessed=9_000_000, transcendentals=2_000_000
        ),
        name="heads",
    )(info, packs, weights)


def per_device(inputs, cotangent, lengths, item_ids, owner_row, w_project, w_output):
    core = lax.axis_index("c")
    y_here = lax.axis_index("y")
    z_here = lax.axis_index(SEQ)
    lane = jnp.arange(LANES, dtype=jnp.int32)

    slot, local_row = routing(item_ids, owner_row)
    lens = lengths.reshape(-1)
    lens_row = jnp.concatenate([lens // 256, lens % 256])
    lens_row = jnp.pad(lens_row, (0, LANES - lens_row.shape[0]))
    small = jnp.pad(jnp.stack([slot, local_row, lens_row]), ((0, 5), (0, 0))).astype(BF16)
    high = PART_ROWS // 8
    n_w = 3 * high + 1
    wp_tiles = w_project.reshape(ZR, high, 8, 2, LANES).transpose(0, 1, 3, 2, 4)
    wo_t = w_output.T
    wo_tiles = jnp.concatenate([wo_t, wo_t], axis=1).reshape(ZR, high, 8, LANES)
    small = jnp.broadcast_to(small[None, None], (ZR, 1, 8, LANES))
    w_tiles = jnp.concatenate([wp_tiles.reshape(ZR, 2 * high, 8, LANES), wo_tiles, small], axis=1)

    both = jnp.stack([inputs[0], cotangent[0]]).reshape(2, 2, 64, 8, LANES)
    spread = exchange(both.transpose(3, 1, 0, 2, 4), PAIR)
    spread = spread.reshape(Z, 16, 8, LANES)
    w_tiles = jnp.broadcast_to(w_tiles[None], (ZQ, ZR, n_w, 8, LANES)).reshape(Z, n_w, 8, LANES)
    arrived = exchange(jnp.concatenate([spread, w_tiles], axis=1), SEQ)
    mine = arrived[:, :16].reshape(Z, 2, 64, LANES).transpose(1, 0, 2, 3)
    packs = lax.all_gather(mine.reshape(1, 2, LENGTH, LANES), PAIR, axis=0, tiled=True)

    by_head = exchange(arrived[:, 16:].reshape(YC, 2, n_w, 8, LANES), PAIR)
    wp_part = by_head[:, :, : 2 * high].reshape(YC, 2, high, 2, 8, LANES)
    wp_part = wp_part.transpose(0, 2, 4, 1, 3, 5).reshape(YC, PART_ROWS, 4 * HEAD_DIM)
    wo_part = by_head[:, :, 2 * high : 3 * high]
    wo_part = jnp.where(lane < 64, wo_part[:, 0], wo_part[:, 1])
    w_part = jnp.concatenate([wp_part, wo_part.reshape(YC, PART_ROWS, HEAD_DIM)], axis=2)
    w_all = jnp.broadcast_to(w_part[None], (X * ZR,) + w_part.shape)
    weights = exchange(w_all, SHARE).reshape(X, ZR, YC, PART_ROWS, HIDDEN)

    facts = by_head[:, :, n_w - 1].astype(F32)
    slots = facts[:, :, 0].astype(jnp.int32)
    tag_of = facts[:, :, 1]
    lens_all = facts[:, 0, 2, :12].reshape(YC, 2, 2, 3)
    lens_all = (lens_all[:, 0] * 256.0 + lens_all[:, 1]).astype(jnp.int32).reshape(Z, 3)
    pack_lens = lax.dynamic_index_in_dim(lens_all, z_here, 0, keepdims=False)
    ends = jnp.cumsum(pack_lens)

    info = jnp.concatenate([ends, core[None]]).astype(jnp.int32)
    kept, sent, grads = heads_backward(info, packs, weights)

    shared = exchange(grads.reshape(X * YC * ZR, PART_ROWS, HIDDEN), SPREAD)
    shared = shared.reshape(X, YC, ZR, PART_ROWS, HIDDEN)
    w_sum = jnp.sum(shared.astype(F32), axis=(0, 2)).astype(BF16)
    wp_sum = w_sum[:, :, : 4 * HEAD_DIM].reshape(YC, high, 8, 2, 2, LANES)
    wp_sum = wp_sum.transpose(0, 3, 1, 4, 2, 5).reshape(Z, 2 * high, 8, LANES)
    wo_sum = w_sum[:, None, :, 4 * HEAD_DIM :]
    wo_sum = jnp.broadcast_to(wo_sum, (YC, 2, PART_ROWS, LANES)).reshape(Z, high, 8, LANES)

    got = lax.ppermute(sent, "c", [(0, 1), (1, 0)])
    pair_sum = (kept.astype(F32) + got.astype(F32)).astype(BF16)
    quad = lax.dynamic_index_in_dim(pair_sum, y_here, 0, keepdims=False).astype(F32)
    for step in range(1, Y):
        there = lax.dynamic_index_in_dim(pair_sum, (y_here + step) & (Y - 1), 0, keepdims=False)
        came = lax.ppermute(there, "y", [(i, (i + step) % Y) for i in range(Y)])
        quad = quad + came.astype(F32)
    own = y_here * C + core
    dy_own = lax.dynamic_slice(packs, (0, 1, own * LANES, 0), (YC, 1, LANES, LANES))
    dy_own = dy_own[:, 0].transpose(1, 0, 2).reshape(LANES, WIDTH)
    token = (dy_own.astype(F32) + quad).astype(BF16)
    token = token.reshape(2, 64, Z, 64).transpose(2, 1, 0, 3).reshape(Z, 8, 8, LANES)

    merged = exchange(jnp.concatenate([token, wp_sum, wo_sum], axis=1), SEQ)
    w_grad = jnp.sum(merged[:, 8:].astype(F32).reshape(ZQ, ZR, 3 * high, 8, LANES), axis=0)
    grad_proj = w_grad[:, : 2 * high].reshape(ZR, high, 2, 8, LANES)
    grad_proj = grad_proj.transpose(0, 1, 3, 2, 4).reshape(32, 2 * LANES)
    both_out = w_grad[:, 2 * high :].reshape(32, 2, 64)
    grad_out = lax.dynamic_index_in_dim(both_out, z_here % 2, 1, keepdims=False).T

    tokens = merged[:, :8].reshape(YC, LANES, LANES)
    slot_ids = jnp.arange(SLOTS, dtype=jnp.int32)
    placed = slots[:, :, None, :] == slot_ids[None, None, :, None]
    tags = jnp.sum(jnp.where(placed, tag_of[:, :, None, :], 0.0), axis=3)
    moved = jnp.einsum(
        "asut,atl->saul", placed.astype(BF16), tokens, preferred_element_type=F32
    )
    rows_out = jnp.where(lane < 64, moved[0], moved[1]).astype(BF16)
    rows_out = rows_out.reshape(YC, OWNERS, CAP, LANES).transpose(1, 0, 2, 3)
    tags = tags.reshape(YC, 2, OWNERS, CAP).transpose(2, 0, 1, 3).reshape(OWNERS, 1, 1, LANES)
    tags = jnp.pad(tags.astype(BF16), ((0, 0), (0, 0), (0, 7), (0, 0)))
    owned = exchange(jnp.concatenate([rows_out, tags], axis=1), DP)
    got_rows = owned[:, :YC].reshape(OWNERS * YC * CAP, LANES)
    got_tags = owned[:, YC, 0].astype(F32).astype(jnp.int32).reshape(OWNERS, YC, 2, CAP)
    got_tags = got_tags.transpose(2, 0, 1, 3).reshape(2, 1, OWNERS * YC * CAP)
    row_ids = jnp.arange(ROWS, dtype=jnp.int32)
    select = (got_tags == row_ids[None, :, None]).astype(BF16)
    sums = jnp.einsum("srk,kl->srl", select, got_rows, preferred_element_type=F32)
    grad_table = sums[0, :, :64] + sums[1, :, 64:]
    return (grad_proj, grad_out, grad_table)


def solution(mesh):
    fine = Mesh(mesh.devices.reshape(X, Y, C, ZQ, ZR), ALL)
    return jax.shard_map(
        per_device,
        mesh=fine,
        in_specs=(
            P(DP, None, SEQ, None),
            P(DP, None, SEQ, None),
            P(DP, None, None),
            P(DP, None, SEQ),
            P(),
            P(DP, SEQ),
            P(SEQ, DP),
        ),
        out_specs=(P(DP, SEQ), P(SEQ, DP), P(DP, SEQ)),
        check_vma=False,
    )
```

time: 240 us -> 237 us (0.988)
  the two profiles are of different devices: /device:TPU:16 before, /device:TPU:1 now
where the time goes in v3:
time: 237 us; the launch traced here: 236 us
  waiting for transfers between devices  73.9 us (31%)
  starting transfers between devices  66.5 us (28%)
  blocking collectives  44.6 us (19%)
  local copies, waits for them, and re-layouts  15.3 us (6%)
  between operations  14.6 us (6%)
  Pallas kernels  12.5 us (5%)
  other arithmetic  7.5 us (3%)
    all_to_all x6, waiting for transfers between devices, exchange(): return lax.all_to_all(value, axes, split_axis=0, concat_axis=0, tiled=True)  60.3 us
    all_to_all x6, starting transfers between devices, exchange(): return lax.all_to_all(value, axes, split_axis=0, concat_axis=0, tiled=True)  53.3 us
    all_to_all x1, blocking collectives, exchange(): return lax.all_to_all(value, axes, split_axis=0, concat_axis=0, tiled=True)  44.6 us
    pallas_call x1, Pallas kernels, heads_backward(): pl.pallas_call(heads_kernel, out_shape=(half, half, jax.ShapeDtypeStruct(...  12.5 us
    ppermute x3, waiting for transfers between devices, per_device(): came = lax.ppermute(there, 'y', [(i, (i + step) % Y) for i in range(Y)])  11.2 us
    ppermute x3, starting transfers between devices, per_device(): came = lax.ppermute(there, 'y', [(i, (i + step) % Y) for i in range(Y)])  10.7 us
  transfers between devices with their start and end apart: 11, of which 8 were waited for; matrix products, arithmetic and copies ran while one was open for 6% of the time, Pallas kernels for 0%

profile of v3, /device:TPU:1, one launch (start us, length us, event | category | flops | bytes accessed | tf_op | source)
XLA Modules:
  0.0 236.5 jit_solution(5666448319364089884)
XLA Ops:
  9.3 10.3 %all-to-all-start = ((bf16[8,2,2,64,128]{4,3,1,2,0:T(8,128)(2,1)}), bf16[8,2,2,64,128]{4,3,1,2,0:T(8,128)(2,1)S(1)}, u32[]{:S(2)}, u32[]{:S(2)}) async-start(bf16[8,2,2,64,128]{4,3,1,2,0:T(8,128)(2,1)} %copy.90), calls=%async_computation | async-start | bytes 1048576 | tf_op jit(solution)/shard_map/all_to_all | solution.py:36
  21.6 7.5 %all-to-all-done = bf16[8,2,2,64,128]{4,3,1,2,0:T(8,128)(2,1)S(1)} async-done(((bf16[8,2,2,64,128]{4,3,1,2,0:T(8,128)(2,1)}), bf16[8,2,2,64,128]{4,3,1,2,0:T(8,128)(2,1)S(1)}, u32[]{:S(2)}, u32[]{:S(2)}) %all-to-all-start) | async-done | bytes 524320 | tf_op jit(solution)/shard_map/all_to_all | solution.py:36
  29.3 44.6 %all_to_all.35 = bf16[16,23,8,128]{3,2,1,0:T(8,128)(2,1)S(1)} all-to-all(bf16[16,23,8,128]{3,2,1,0:T(8,128)(2,1)S(1)} %pad_maximum_fusion), channel_id=1, replica_groups=mesh['x'=4,'y'=4,'c'=2,'zq'=8,'zr'=2] {'zq','zr'}, dimensions={0} | all-to-all | bytes 1507328 | tf_op jit(solution)/shard_map/all_to_all | solution.py:36
  75.5 10.1 %all-to-all-start.2 = ((bf16[8,2,7,8,128]{4,3,2,1,0:T(8,128)(2,1)}), bf16[8,2,7,8,128]{4,3,2,1,0:T(8,128)(2,1)S(1)}, u32[]{:S(2)}, u32[]{:S(2)}) async-start(bf16[8,2,7,8,128]{4,3,2,1,0:T(8,128)(2,1)} %bitcast.18), calls=%async_computation.2 | async-start | bytes 458752 | tf_op jit(solution)/shard_map/all_to_all | solution.py:36
  85.6 6.2 %all-to-all-done.2 = bf16[8,2,7,8,128]{4,3,2,1,0:T(8,128)(2,1)S(1)} async-done(((bf16[8,2,7,8,128]{4,3,2,1,0:T(8,128)(2,1)}), bf16[8,2,7,8,128]{4,3,2,1,0:T(8,128)(2,1)S(1)}, u32[]{:S(2)}, u32[]{:S(2)}) %all-to-all-start.2) | async-done | bytes 229408 | tf_op jit(solution)/shard_map/all_to_all | solution.py:36
  91.9 1.2 broadcast_in_dim.70
  93.1 5.4 %all-to-all-start.3 = ((bf16[8,8,16,640]{3,2,1,0:T(8,128)(2,1)}), bf16[8,8,16,640]{3,2,1,0:T(8,128)(2,1)S(1)}, u32[]{:S(2)}, u32[]{:S(2)}) async-start(bf16[8,8,16,640]{3,2,1,0:T(8,128)(2,1)} %broadcast_in_dim.70), calls=%async_computation.3 | async-start | bytes 2621440 | tf_op jit(solution)/shard_map/all_to_all | solution.py:36
  99.3 16.2 %all-to-all-done.3 = bf16[8,8,16,640]{3,2,1,0:T(8,128)(2,1)S(1)} async-done(((bf16[8,8,16,640]{3,2,1,0:T(8,128)(2,1)}), bf16[8,8,16,640]{3,2,1,0:T(8,128)(2,1)S(1)}, u32[]{:S(2)}, u32[]{:S(2)}) %all-to-all-start.3) | async-done | bytes 1310752 | tf_op jit(solution)/shard_map/all_to_all | solution.py:36
  115.5 2.2 copy-done.1
  117.7 12.5 %heads.1 = (bf16[4,128,1024]{2,1,0:T(8,128)(2,1)S(1)}, bf16[4,128,1024]{2,1,0:T(8,128)(2,1)S(1)}, bf16[4,8,2,16,640]{4,3,2,1,0:T(8,128)(2,1)}) custom-call(s32[4]{0:T(128)S(1)} %pad_add_fusion.info, bf16[8,2,1024,128]{3,2,1,0:T(8,128)(2,1)S(1)} %copy-done.1, bf16[4,2,8,16,640]{4,3,2,1,0:T(8,128)(2,1)S(1)} %bitcast.133), custom_call_target="tpu_custom_call" | custom-call | flops 5000000000 | bytes 9000000 | tf_op jit(solution)/shard_map/heads/pallas_call | solution.py:167
  130.2 6.6 %all-to-all-start.4 = ((bf16[64,16,640]{2,1,0:T(8,128)(2,1)}), bf16[64,16,640]{2,1,0:T(8,128)(2,1)S(1)}, u32[]{:S(2)}, u32[]{:S(2)}) async-start(bf16[64,16,640]{2,1,0:T(8,128)(2,1)} %bitcast.33), calls=%async_computation.4 | async-start | bytes 2621440 | tf_op jit(solution)/shard_map/all_to_all | solution.py:36
  136.9 2.5 %collective-permute-start = (bf16[4,128,1024]{2,1,0:T(8,128)(2,1)S(1)}, bf16[4,128,1024]{2,1,0:T(8,128)(2,1)}, u32[]{:S(2)}, u32[]{:S(2)}) collective-permute-start(bf16[4,128,1024]{2,1,0:T(8,128)(2,1)S(1)} %get-tuple-element.7), channel_id=1, source_target_pairs={{0,16},{16,0},{1,17},{17,1},{2,18},{18,2},{3,19},{19,3},{4,20},{20... | collective-permute-start | bytes 3145736 | tf_op jit(solution)/shard_map/ppermute | solution.py:255
  139.3 2.4 %collective-permute-done = bf16[4,128,1024]{2,1,0:T(8,128)(2,1)} collective-permute-done((bf16[4,128,1024]{2,1,0:T(8,128)(2,1)S(1)}, bf16[4,128,1024]{2,1,0:T(8,128)(2,1)}, u32[]{:S(2)}, u32[]{:S(2)}) %collective-permute-start) | collective-permute-done | bytes 1048608 | tf_op jit(solution)/shard_map/ppermute | solution.py:255
  141.7 1.6 add_convert_fusion
  144.3 3.1 %collective-permute-start.1 = (bf16[128,1024]{1,0:T(8,128)(2,1)}, bf16[128,1024]{1,0:T(8,128)(2,1)}, u32[]{:S(2)}, u32[]{:S(2)}) collective-permute-start(bf16[128,1024]{1,0:T(8,128)(2,1)} %get-tuple-element.13), channel_id=1, source_target_pairs={{0,32},{32,64},{64,96},{96,0},{1,33},{33,65},{65,97},{97,1},{2,34}... | collective-permute-start | bytes 786440 | tf_op jit(solution)/shard_map/ppermute | solution.py:260
  147.4 4.4 %collective-permute-start.2 = (bf16[128,1024]{1,0:T(8,128)(2,1)}, bf16[128,1024]{1,0:T(8,128)(2,1)}, u32[]{:S(2)}, u32[]{:S(2)}) collective-permute-start(bf16[128,1024]{1,0:T(8,128)(2,1)} %get-tuple-element.15), channel_id=1, source_target_pairs={{0,64},{32,96},{64,0},{96,32},{1,65},{33,97},{65,1},{97,33},{2,66}... | collective-permute-start | bytes 786440 | tf_op jit(solution)/shard_map/ppermute | solution.py:260
  151.8 3.2 %collective-permute-start.3 = (bf16[128,1024]{1,0:T(8,128)(2,1)}, bf16[128,1024]{1,0:T(8,128)(2,1)}, u32[]{:S(2)}, u32[]{:S(2)}) collective-permute-start(bf16[128,1024]{1,0:T(8,128)(2,1)} %get-tuple-element.14), channel_id=1, source_target_pairs={{0,96},{32,0},{64,32},{96,64},{1,97},{33,1},{65,33},{97,65},{2,98}... | collective-permute-start | bytes 786440 | tf_op jit(solution)/shard_map/ppermute | solution.py:260
  156.4 5.3 %collective-permute-done.1 = bf16[128,1024]{1,0:T(8,128)(2,1)} collective-permute-done((bf16[128,1024]{1,0:T(8,128)(2,1)}, bf16[128,1024]{1,0:T(8,128)(2,1)}, u32[]{:S(2)}, u32[]{:S(2)}) %collective-permute-start.1) | collective-permute-done | bytes 262176 | tf_op jit(solution)/shard_map/ppermute | solution.py:260
  161.7 5.9 %collective-permute-done.2 = bf16[128,1024]{1,0:T(8,128)(2,1)} collective-permute-done((bf16[128,1024]{1,0:T(8,128)(2,1)}, bf16[128,1024]{1,0:T(8,128)(2,1)}, u32[]{:S(2)}, u32[]{:S(2)}) %collective-permute-start.2) | collective-permute-done | bytes 262176 | tf_op jit(solution)/shard_map/ppermute | solution.py:260
  167.7 1.3 fusion.12
  171.2 9.8 %all-to-all-start.5 = ((bf16[16,14,8,128]{3,2,1,0:T(8,128)(2,1)}), bf16[16,14,8,128]{3,2,1,0:T(8,128)(2,1)S(1)}, u32[]{:S(2)}, u32[]{:S(2)}) async-start(bf16[16,14,8,128]{3,2,1,0:T(8,128)(2,1)} %pad_maximum_fusion.2), calls=%async_computation.5 | async-start | bytes 917504 | tf_op jit(solution)/shard_map/all_to_all | solution.py:36
  182.4 19.4 %all-to-all-done.5 = bf16[16,14,8,128]{3,2,1,0:T(8,128)(2,1)S(1)} async-done(((bf16[16,14,8,128]{3,2,1,0:T(8,128)(2,1)}), bf16[16,14,8,128]{3,2,1,0:T(8,128)(2,1)S(1)}, u32[]{:S(2)}, u32[]{:S(2)}) %all-to-all-start.5) | async-done | bytes 458784 | tf_op jit(solution)/shard_map/all_to_all | solution.py:36
  204.1 11.1 %all-to-all-start.6 = ((bf16[32,9,8,128]{3,2,1,0:T(8,128)(2,1)}), bf16[32,9,8,128]{3,2,1,0:T(8,128)(2,1)S(1)}, u32[]{:S(2)}, u32[]{:S(2)}) async-start(bf16[32,9,8,128]{3,2,1,0:T(8,128)(2,1)} %copy.106), calls=%async_computation.6 | async-start | bytes 1179648 | tf_op jit(solution)/shard_map/all_to_all | solution.py:36
  216.6 10.9 %all-to-all-done.6 = bf16[32,9,8,128]{3,2,1,0:T(8,128)(2,1)S(1)} async-done(((bf16[32,9,8,128]{3,2,1,0:T(8,128)(2,1)}), bf16[32,9,8,128]{3,2,1,0:T(8,128)(2,1)S(1)}, u32[]{:S(2)}, u32[]{:S(2)}) %all-to-all-start.6) | async-done | bytes 589856 | tf_op jit(solution)/shard_map/all_to_all | solution.py:36
  (99 shorter events, 18.1 us)
Async XLA Ops:
  7.2 12.7 %copy-start = (s32[8192]{0:T(1024)S(1)}, s32[8192]{0:T(1024)}, u32[]{:S(2)}) copy-start(s32[8192]{0:T(1024)} %param.11) | copy-start | bytes 98308
  7.2 12.4 %copy-start.4 = (s32[1,2,64]{2,1,0:T(2,128)S(1)}, s32[1,2,64]{2,1,0:T(2,128)}, u32[]{:S(2)}) copy-start(s32[1,2,64]{2,1,0:T(2,128)} %param.10) | copy-start | bytes 1540
  8.3 13.0 %copy-start.5 = (s32[1,2,3]{2,1,0:T(2,128)S(1)}, s32[1,2,3]{2,1,0:T(2,128)}, u32[]{:S(2)}) copy-start(s32[1,2,3]{2,1,0:T(2,128)} %param.9) | copy-start | bytes 76
  8.3 13.2 %copy-start.3 = (bf16[64,32]{0,1:T(8,128)(2,1)S(1)}, bf16[64,32]{0,1:T(8,128)(2,1)}, u32[]{:S(2)}) copy-start(bf16[64,32]{0,1:T(8,128)(2,1)} %param.13) | copy-start | bytes 12292
  8.3 13.3 %copy-start.2 = (bf16[32,256]{1,0:T(8,128)(2,1)S(1)}, bf16[32,256]{1,0:T(8,128)(2,1)}, u32[]{:S(2)}) copy-start(bf16[32,256]{1,0:T(8,128)(2,1)} %param.12) | copy-start | bytes 49156
  9.3 19.8 %all-to-all-start = ((bf16[8,2,2,64,128]{4,3,1,2,0:T(8,128)(2,1)}), bf16[8,2,2,64,128]{4,3,1,2,0:T(8,128)(2,1)S(1)}, u32[]{:S(2)}, u32[]{:S(2)}) async-start(bf16[8,2,2,64,128]{4,3,1,2,0:T(8,128)(2,1)} %copy.90), calls=%async_computation | async-start | bytes 1048576 | tf_op jit(solution)/shard_map/all_to_all | solution.py:36
  19.6 95.9 %all-gather.2.cloned.1.call-start = ((), (), s32[]{:S(2)}) async-start(), calls=%async_computation.7 | async-start | bytes 4718592 | tf_op jit(solution)/shard_map/all_gather | solution.py:225
  75.5 16.3 %all-to-all-start.2 = ((bf16[8,2,7,8,128]{4,3,2,1,0:T(8,128)(2,1)}), bf16[8,2,7,8,128]{4,3,2,1,0:T(8,128)(2,1)S(1)}, u32[]{:S(2)}, u32[]{:S(2)}) async-start(bf16[8,2,7,8,128]{4,3,2,1,0:T(8,128)(2,1)} %bitcast.18), calls=%async_computation.2 | async-start | bytes 458752 | tf_op jit(solution)/shard_map/all_to_all | solution.py:36
  93.1 22.4 %all-to-all-start.3 = ((bf16[8,8,16,640]{3,2,1,0:T(8,128)(2,1)}), bf16[8,8,16,640]{3,2,1,0:T(8,128)(2,1)S(1)}, u32[]{:S(2)}, u32[]{:S(2)}) async-start(bf16[8,8,16,640]{3,2,1,0:T(8,128)(2,1)} %broadcast_in_dim.70), calls=%async_computation.3 | async-start | bytes 2621440 | tf_op jit(solution)/shard_map/all_to_all | solution.py:36
  115.5 2.2 copy-start.1
  130.2 39.9 %all-to-all-start.4 = ((bf16[64,16,640]{2,1,0:T(8,128)(2,1)}), bf16[64,16,640]{2,1,0:T(8,128)(2,1)S(1)}, u32[]{:S(2)}, u32[]{:S(2)}) async-start(bf16[64,16,640]{2,1,0:T(8,128)(2,1)} %bitcast.33), calls=%async_computation.4 | async-start | bytes 2621440 | tf_op jit(solution)/shard_map/all_to_all | solution.py:36
  136.9 4.9 %collective-permute-start = (bf16[4,128,1024]{2,1,0:T(8,128)(2,1)S(1)}, bf16[4,128,1024]{2,1,0:T(8,128)(2,1)}, u32[]{:S(2)}, u32[]{:S(2)}) collective-permute-start(bf16[4,128,1024]{2,1,0:T(8,128)(2,1)S(1)} %get-tuple-element.7), channel_id=1, source_target_pairs={{0,16},{16,0},{1,17},{17,1},{2,18},{18,2},{3,19},{19,3},{4,20},{20... | collective-permute-start | bytes 3145736 | tf_op jit(solution)/shard_map/ppermute | solution.py:255
  144.3 17.4 %collective-permute-start.1 = (bf16[128,1024]{1,0:T(8,128)(2,1)}, bf16[128,1024]{1,0:T(8,128)(2,1)}, u32[]{:S(2)}, u32[]{:S(2)}) collective-permute-start(bf16[128,1024]{1,0:T(8,128)(2,1)} %get-tuple-element.13), channel_id=1, source_target_pairs={{0,32},{32,64},{64,96},{96,0},{1,33},{33,65},{65,97},{97,1},{2,34}... | collective-permute-start | bytes 786440 | tf_op jit(solution)/shard_map/ppermute | solution.py:260
  147.4 20.3 %collective-permute-start.2 = (bf16[128,1024]{1,0:T(8,128)(2,1)}, bf16[128,1024]{1,0:T(8,128)(2,1)}, u32[]{:S(2)}, u32[]{:S(2)}) collective-permute-start(bf16[128,1024]{1,0:T(8,128)(2,1)} %get-tuple-element.15), channel_id=1, source_target_pairs={{0,64},{32,96},{64,0},{96,32},{1,65},{33,97},{65,1},{97,33},{2,66}... | collective-permute-start | bytes 786440 | tf_op jit(solution)/shard_map/ppermute | solution.py:260
  151.8 15.9 %collective-permute-start.3 = (bf16[128,1024]{1,0:T(8,128)(2,1)}, bf16[128,1024]{1,0:T(8,128)(2,1)}, u32[]{:S(2)}, u32[]{:S(2)}) collective-permute-start(bf16[128,1024]{1,0:T(8,128)(2,1)} %get-tuple-element.14), channel_id=1, source_target_pairs={{0,96},{32,0},{64,32},{96,64},{1,97},{33,1},{65,33},{97,65},{2,98}... | collective-permute-start | bytes 786440 | tf_op jit(solution)/shard_map/ppermute | solution.py:260
  171.2 30.6 %all-to-all-start.5 = ((bf16[16,14,8,128]{3,2,1,0:T(8,128)(2,1)}), bf16[16,14,8,128]{3,2,1,0:T(8,128)(2,1)S(1)}, u32[]{:S(2)}, u32[]{:S(2)}) async-start(bf16[16,14,8,128]{3,2,1,0:T(8,128)(2,1)} %pad_maximum_fusion.2), calls=%async_computation.5 | async-start | bytes 917504 | tf_op jit(solution)/shard_map/all_to_all | solution.py:36
  204.1 23.4 %all-to-all-start.6 = ((bf16[32,9,8,128]{3,2,1,0:T(8,128)(2,1)}), bf16[32,9,8,128]{3,2,1,0:T(8,128)(2,1)S(1)}, u32[]{:S(2)}, u32[]{:S(2)}) async-start(bf16[32,9,8,128]{3,2,1,0:T(8,128)(2,1)} %copy.106), calls=%async_computation.6 | async-start | bytes 1179648 | tf_op jit(solution)/shard_map/all_to_all | solution.py:36
Sparse Core Ops, SparseCore 0:
  74.9 38.7 all-gather.1

commit v4 on v3

v4 whole, which is shorter than its diff:
```python
import jax
import jax.numpy as jnp
from jax import lax
from jax.experimental import pallas as pl
from jax.experimental.pallas import tpu as pltpu
from jax.sharding import Mesh, PartitionSpec as P

HEAD_DIM = 128
NORM_FLOOR = 1.0
F32 = jnp.float32
BF16 = jnp.bfloat16

X, Y, C, ZQ, ZR = 4, 4, 2, 8, 2
YC = Y * C
Z = ZQ * ZR
PAIR = ("y", "c")
DP = ("x", "y", "c")
SEQ = ("zq", "zr")
SHARE = ("x", "zr")
SPREAD = ("x", "y", "c", "zr")
ALL = ("x", "y", "c", "zq", "zr")
OWNERS = X * YC
CAP = 8
ROWS = 256
SLOTS = OWNERS * CAP
LANES = 128
LENGTH = 1024
WIDTH = 1024
HIDDEN = 5 * HEAD_DIM
PART_ROWS = 32 // ZR
STEP = 256
REACH = 512
VMEM_SPEC = pl.BlockSpec(memory_space=pltpu.VMEM)
SMEM_SPEC = pl.BlockSpec(memory_space=pltpu.SMEM)


def exchange(value, axes):
    return lax.all_to_all(value, axes, split_axis=0, concat_axis=0, tiled=True)


def routing(item_ids, owner_row):
    rows = jnp.take(owner_row, item_ids.reshape(-1))
    owner = rows // ROWS
    count = owner.shape[0]
    order = jnp.arange(count, dtype=jnp.int32)
    before = (owner[None, :] == owner[:, None]) & (order[None, :] < order[:, None])
    rank = jnp.sum(before.astype(jnp.int32), axis=1)
    return owner * CAP + rank, rows % ROWS


def dot_nt(a, b):
    return lax.dot_general(a, b, (((1,), (1,)), ((), ())), preferred_element_type=F32)


def dot_tn(a, b):
    return lax.dot_general(a, b, (((0,), (0,)), ((), ())), preferred_element_type=F32)


def heads_kernel(info, packs, w_in, kept, sent, d_z, gated, w, acts, slope, d_value, d_key):
    hd = HEAD_DIM
    scale = hd**-0.5
    u_cols, v_cols, q_cols, k_cols = (slice(m * hd, (m + 1) * hd) for m in range(4))
    for x in range(X):
        for yc in range(YC):
            start = (x * YC + yc) * 32
            w[start : start + 32, :] = w_in[x, :, yc].reshape(32, HIDDEN)
    d_value[...] = jnp.zeros_like(d_value)
    d_key[...] = jnp.zeros_like(d_key)

    def project(step, carry):
        rows = pl.ds(pl.multiple_of(step * STEP, STEP), STEP)
        px = jnp.concatenate([packs[g, 0, rows, :] for g in range(8)], axis=1)
        z_pre = jnp.dot(px, w[:, : 4 * hd], preferred_element_type=F32)
        sigma = jax.nn.sigmoid(z_pre)
        silu = z_pre * sigma
        acts[rows, :] = silu.astype(BF16)
        slope[rows, :] = sigma + silu * (1.0 - sigma)
        return carry

    lax.fori_loop(0, LENGTH // STEP, project, 0)

    for step in range(LENGTH // STEP):
        base = step * STEP
        first = max(0, base - REACH)
        rows = slice(base, base + STEP)
        span = slice(first, base + STEP)
        pos_k = lax.broadcasted_iota(jnp.int32, (1, base + STEP - first), 1) + first
        pos_q = lax.broadcasted_iota(jnp.int32, (STEP, 1), 0) + base
        start = jnp.zeros_like(pos_q)
        for n in range(3):
            start = jnp.where(pos_q >= info[n], info[n], start)
        masked = (pos_k <= pos_q) & (pos_k >= start)
        query = acts[rows, q_cols]
        key = acts[span, k_cols]
        value = acts[span, v_cols]
        scores = dot_nt(query, key) * scale
        sigma = jax.nn.sigmoid(scores)
        silu = scores * sigma
        attn = jnp.where(masked, silu, 0.0).astype(BF16)
        factor = jnp.where(masked, (sigma + silu * (1.0 - sigma)) * scale, 0.0)
        mixed = jnp.dot(attn, value, preferred_element_type=F32)
        centred = mixed - jnp.mean(mixed, axis=-1, keepdims=True)
        inv_std = lax.rsqrt(jnp.mean(centred * centred, axis=-1, keepdims=True) + NORM_FLOOR)
        normed = centred * inv_std
        gating = acts[rows, u_cols].astype(F32)
        gated[rows, :] = (normed * gating).astype(BF16)
        pdy = jnp.concatenate([packs[g, 1, rows, :] for g in range(8)], axis=1)
        d_gated = jnp.dot(pdy, w[:, 4 * hd :], preferred_element_type=F32)
        d_normed = d_gated * gating
        d_mixed = (
            inv_std
            * (
                d_normed
                - jnp.mean(d_normed, axis=-1, keepdims=True)
                - normed * jnp.mean(d_normed * normed, axis=-1, keepdims=True)
            )
        ).astype(BF16)
        d_scores = (dot_nt(d_mixed, value) * factor).astype(BF16)
        d_query = jnp.dot(d_scores, key, preferred_element_type=F32)
        d_value[span, :] += dot_tn(attn, d_mixed)
        d_key[span, :] += dot_tn(d_scores, query)
        d_z[rows, u_cols] = (d_gated * normed * slope[rows, u_cols]).astype(BF16)
        d_z[rows, q_cols] = (d_query * slope[rows, q_cols]).astype(BF16)

    d_z[:, v_cols] = (d_value[...] * slope[:, v_cols]).astype(BF16)
    d_z[:, k_cols] = (d_key[...] * slope[:, k_cols]).astype(BF16)

    core = info[3]

    def parts(step, carry):
        rows = pl.ds(pl.multiple_of(step * STEP, STEP), STEP)
        part = dot_nt(d_z[rows, :], w[:, : 4 * hd]).astype(BF16)

        @pl.when(core == 0)
        def _():
            kept[step] = part[:LANES]
            sent[step] = part[LANES:]

        @pl.when(core != 0)
        def _():
            kept[step] = part[LANES:]
            sent[step] = part[:LANES]

        return carry

    lax.fori_loop(0, Y, parts, 0)


def heads_backward(info, packs, weights):
    half = jax.ShapeDtypeStruct((Y, LANES, WIDTH), BF16)
    return pl.pallas_call(
        heads_kernel,
        out_shape=(
            half,
            half,
            jax.ShapeDtypeStruct((LENGTH, 4 * HEAD_DIM), BF16),
            jax.ShapeDtypeStruct((LENGTH, HEAD_DIM), BF16),
        ),
        in_specs=[SMEM_SPEC, VMEM_SPEC, VMEM_SPEC],
        out_specs=(VMEM_SPEC,) * 4,
        scratch_shapes=[
            pltpu.VMEM((WIDTH, HIDDEN), BF16),
            pltpu.VMEM((LENGTH, 4 * HEAD_DIM), BF16),
            pltpu.VMEM((LENGTH, 4 * HEAD_DIM), F32),
            pltpu.VMEM((LENGTH, HEAD_DIM), F32),
            pltpu.VMEM((LENGTH, HEAD_DIM), F32),
        ],
        compiler_params=pltpu.CompilerParams(vmem_limit_bytes=44 * 2**20),
        cost_estimate=pl.CostEstimate(
            flops=4_000_000_000, bytes_accessed=9_000_000, transcendentals=2_000_000
        ),
        name="heads",
    )(info, packs, weights)


def grads_kernel(packs, d_z, gated, tags, out):
    for x in range(X):
        for dest, source, t in ((slice(0, 512), d_z, 0), (slice(512, 640), gated, 1)):
            columns = jnp.concatenate([packs[2 * x, t], packs[2 * x + 1, t]], axis=1)
            block = dot_tn(columns, source[...]).astype(BF16)
            for yc in range(YC):
                for r in range(ZR):
                    at = yc * 32 + r * PART_ROWS
                    out[x, yc, r, :, dest] = block[at : at + PART_ROWS]
    for x in range(X):
        for yc in range(YC):
            for r in range(ZR):
                out[x, yc, r, :, HIDDEN:] = tags[x * YC + yc]


def weight_grads(packs, d_z, gated, tags):
    return pl.pallas_call(
        grads_kernel,
        out_shape=jax.ShapeDtypeStruct((X, YC, ZR, PART_ROWS, HIDDEN + LANES), BF16),
        in_specs=[VMEM_SPEC] * 4,
        out_specs=VMEM_SPEC,
        compiler_params=pltpu.CompilerParams(vmem_limit_bytes=32 * 2**20),
        cost_estimate=pl.CostEstimate(
            flops=1_350_000_000, bytes_accessed=6_800_000, transcendentals=0
        ),
        name="weight_grads",
    )(packs, d_z, gated, tags)


def pair_kernel(place, kept, got, own, *to_y):
    y = place[0]
    own[...] = kept[y].astype(F32) + got[y].astype(F32)
    for step in range(1, Y):
        other = (y + step) & (Y - 1)
        to_y[step - 1][...] = (kept[other].astype(F32) + got[other].astype(F32)).astype(BF16)


def pair_sums(y, kept, got):
    block = jax.ShapeDtypeStruct((LANES, WIDTH), BF16)
    return pl.pallas_call(
        pair_kernel,
        out_shape=(jax.ShapeDtypeStruct((LANES, WIDTH), F32),) + (block,) * (Y - 1),
        in_specs=[SMEM_SPEC, VMEM_SPEC, VMEM_SPEC],
        out_specs=(VMEM_SPEC,) * Y,
        compiler_params=pltpu.CompilerParams(vmem_limit_bytes=32 * 2**20),
        cost_estimate=pl.CostEstimate(flops=500_000, bytes_accessed=3_000_000, transcendentals=0),
        name="pair_sums",
    )(y, kept, got)


def payload_kernel(own, came_1, came_2, came_3, dy, shared, out):
    lane = lax.broadcasted_iota(jnp.int32, (64, LANES), 1)
    for m in range(8):
        cols = slice(m * LANES, (m + 1) * LANES)
        total = own[:, cols] + dy[m].astype(F32)
        for came in (came_1, came_2, came_3):
            total = total + came[:, cols].astype(F32)
        low, high = total[:64], total[64:]
        even = jnp.where(lane < 64, low, pltpu.roll(high, 64, 1))
        odd = jnp.where(lane < 64, pltpu.roll(low, 64, 1), high)
        out[2 * m, :64, :] = even.astype(BF16)
        out[2 * m + 1, :64, :] = odd.astype(BF16)
    for h in range(YC):
        total = jnp.zeros((PART_ROWS, HIDDEN), F32)
        for x in range(X):
            for r in range(ZR):
                total = total + shared[x, h, r, :, :HIDDEN].astype(F32)
        total = total.astype(BF16)
        for s in range(2):
            for n, col in enumerate((2 * s, 2 * s + 1, 4)):
                first = 64 + n * PART_ROWS
                out[2 * h + s, first : first + PART_ROWS, :] = total[
                    :, col * LANES : (col + 1) * LANES
                ]


def payload(own, came, dy, shared):
    return pl.pallas_call(
        payload_kernel,
        out_shape=jax.ShapeDtypeStruct((Z, 64 + 3 * PART_ROWS, LANES), BF16),
        in_specs=[VMEM_SPEC] * 6,
        out_specs=VMEM_SPEC,
        compiler_params=pltpu.CompilerParams(vmem_limit_bytes=32 * 2**20),
        cost_estimate=pl.CostEstimate(flops=1_500_000, bytes_accessed=4_000_000, transcendentals=0),
        name="payload",
    )(own, *came, dy, shared)


def place_kernel(slots, merged, out):
    slot_ids = lax.broadcasted_iota(jnp.int32, (SLOTS, LANES), 0)
    lane = lax.broadcasted_iota(jnp.int32, (SLOTS, LANES), 1)
    for pair in range(YC // 2):
        both = []
        for yc in (2 * pair, 2 * pair + 1):
            tokens = jnp.concatenate([merged[2 * yc, :64, :], merged[2 * yc + 1, :64, :]], axis=0)
            moved = [
                jnp.dot(
                    (slots[2 * yc + s : 2 * yc + s + 1, :] == slot_ids).astype(BF16),
                    tokens,
                    preferred_element_type=F32,
                )
                for s in range(2)
            ]
            rows = jnp.where(lane < 64, moved[0], moved[1])
            both.append(rows.reshape(OWNERS, CAP, LANES))
        out[:, pair * 16 : (pair + 1) * 16, :] = jnp.concatenate(both, axis=1).astype(BF16)


def place(slots, merged):
    return pl.pallas_call(
        place_kernel,
        out_shape=jax.ShapeDtypeStruct((OWNERS, YC * CAP, LANES), BF16),
        in_specs=[VMEM_SPEC] * 2,
        out_specs=VMEM_SPEC,
        compiler_params=pltpu.CompilerParams(vmem_limit_bytes=32 * 2**20),
        cost_estimate=pl.CostEstimate(
            flops=135_000_000, bytes_accessed=1_000_000, transcendentals=0
        ),
        name="place",
    )(slots, merged)


def table_kernel(tags, rows, out):
    row_ids = lax.broadcasted_iota(jnp.int32, (ROWS, rows.shape[0]), 0)
    sums = [
        jnp.dot(
            (tags[s : s + 1, :] == row_ids).astype(BF16), rows[...], preferred_element_type=F32
        )
        for s in range(2)
    ]
    out[...] = (sums[0] + pltpu.roll(sums[1], 64, 1)).T[:64]


def table_sum(tags, rows):
    return pl.pallas_call(
        table_kernel,
        out_shape=jax.ShapeDtypeStruct((64, ROWS), F32),
        in_specs=[VMEM_SPEC] * 2,
        out_specs=VMEM_SPEC,
        compiler_params=pltpu.CompilerParams(vmem_limit_bytes=32 * 2**20),
        cost_estimate=pl.CostEstimate(
            flops=270_000_000, bytes_accessed=1_000_000, transcendentals=0
        ),
        name="table_sum",
    )(tags, rows)


def per_device(inputs, cotangent, lengths, item_ids, owner_row, w_project, w_output):
    core = lax.axis_index("c")
    y_here = lax.axis_index("y")
    z_here = lax.axis_index(SEQ)
    lane = jnp.arange(LANES, dtype=jnp.int32)

    slot, local_row = routing(item_ids, owner_row)
    lens = lengths.reshape(-1)
    lens_row = jnp.concatenate([lens // 256, lens % 256])
    lens_row = jnp.pad(lens_row, (0, LANES - lens_row.shape[0]))
    small = jnp.pad(jnp.stack([slot, local_row, lens_row]), ((0, 5), (0, 0))).astype(BF16)
    high = PART_ROWS // 8
    n_w = 3 * high + 1
    wp_tiles = w_project.reshape(ZR, high, 8, 2, LANES).transpose(0, 1, 3, 2, 4)
    wo_t = w_output.T
    wo_tiles = jnp.concatenate([wo_t, wo_t], axis=1).reshape(ZR * high, 8, LANES)
    turned = jnp.concatenate([wp_tiles.reshape(2 * ZR * high, 8, LANES), wo_tiles, small[None]])
    turn = [
        ((x * YC + a) * Z + b * 2 + s, (x * YC + b) * Z + a * 2 + s)
        for x in range(X)
        for a in range(YC)
        for b in range(YC)
        for s in range(2)
    ]
    turned = lax.ppermute(turned, ALL, turn)
    wp_tiles = turned[: 2 * ZR * high].reshape(ZR, 2 * high, 8, LANES)
    wo_tiles = turned[2 * ZR * high : 3 * ZR * high].reshape(ZR, high, 8, LANES)
    small = jnp.broadcast_to(turned[None, -1:], (ZR, 1, 8, LANES))
    w_tiles = jnp.concatenate([wp_tiles, wo_tiles, small], axis=1)

    both = jnp.stack([inputs[0], cotangent[0]]).reshape(2, 2, 64, 8, LANES)
    spread = exchange(both.transpose(3, 1, 0, 2, 4), PAIR)
    spread = spread.reshape(Z, 16, 8, LANES)
    w_tiles = jnp.broadcast_to(w_tiles[None], (ZQ, ZR, n_w, 8, LANES)).reshape(Z, n_w, 8, LANES)
    arrived = exchange(jnp.concatenate([spread, w_tiles], axis=1), SEQ)
    mine = arrived[:, :16].reshape(Z, 2, 64, LANES).transpose(1, 0, 2, 3)
    packs = lax.all_gather(mine.reshape(1, 2, LENGTH, LANES), PAIR, axis=0, tiled=True)

    by_head = arrived[:, 16:].reshape(YC, 2, n_w, 8, LANES)
    wp_part = by_head[:, :, : 2 * high].reshape(YC, 2, high, 2, 8, LANES)
    wp_part = wp_part.transpose(0, 2, 4, 1, 3, 5).reshape(YC, PART_ROWS, 4 * HEAD_DIM)
    wo_part = by_head[:, :, 2 * high : 3 * high]
    wo_part = jnp.where(lane < 64, wo_part[:, 0], wo_part[:, 1])
    w_part = jnp.concatenate([wp_part, wo_part.reshape(YC, PART_ROWS, HEAD_DIM)], axis=2)
    w_all = jnp.broadcast_to(w_part[None], (X * ZR,) + w_part.shape)
    weights = exchange(w_all, SHARE).reshape(X, ZR, YC, PART_ROWS, HIDDEN)

    facts = by_head[:, :, n_w - 1].astype(F32)
    slots = facts[:, :, 0].astype(jnp.int32)
    tag_of = facts[:, :, 1]
    lens_all = facts[:, 0, 2, :12].reshape(YC, 2, 2, 3)
    lens_all = (lens_all[:, 0] * 256.0 + lens_all[:, 1]).astype(jnp.int32).reshape(Z, 3)
    pack_lens = lax.dynamic_index_in_dim(lens_all, z_here, 0, keepdims=False)
    ends = jnp.cumsum(pack_lens)

    info = jnp.concatenate([ends, core[None]]).astype(jnp.int32)
    slot_ids = jnp.arange(SLOTS, dtype=jnp.int32)
    placed = slots[:, :, None, :] == slot_ids[None, None, :, None]
    tags = jnp.sum(jnp.where(placed, tag_of[:, :, None, :], 0.0), axis=3)
    tags = tags.reshape(YC, 2, OWNERS, CAP).transpose(2, 1, 0, 3).reshape(OWNERS, 1, LANES)
    tags = jnp.broadcast_to(tags.astype(BF16), (OWNERS, PART_ROWS, LANES))

    kept, sent, d_z, gated = heads_backward(info, packs, weights)
    got = lax.ppermute(sent, "c", [(0, 1), (1, 0)])

    grads = weight_grads(packs, d_z, gated, tags)
    shared = exchange(grads.reshape(X * YC * ZR, PART_ROWS, HIDDEN + LANES), SPREAD)
    shared = shared.reshape(X, YC, ZR, PART_ROWS, HIDDEN + LANES)

    own, *to_y = pair_sums(y_here[None].astype(jnp.int32), kept, got)
    came = [
        lax.ppermute(to_y[step - 1], "y", [(i, (i + step) % Y) for i in range(Y)])
        for step in range(1, Y)
    ]
    block = (y_here * C + core) * LANES
    dy_own = lax.dynamic_slice(packs, (0, 1, block, 0), (YC, 1, LANES, LANES))[:, 0]

    merged = exchange(payload(own, came, dy_own, shared), SEQ)
    w_grad = merged[:, 64:].astype(F32).reshape(ZQ, ZR, 3, PART_ROWS, LANES)
    w_grad = jnp.sum(w_grad, axis=0)
    grad_proj = w_grad[:, :2].transpose(0, 2, 1, 3).reshape(32, 2 * LANES)
    both_out = w_grad[:, 2].reshape(32, 2, 64)
    grad_out = lax.dynamic_index_in_dim(both_out, z_here & 1, 1, keepdims=False).T

    owned = exchange(place(slots.reshape(2 * YC, LANES), merged), DP)
    got_tags = shared[:, :, 0, 0, HIDDEN:]
    got_tags = got_tags.astype(F32).astype(jnp.int32).reshape(OWNERS, 2, YC * CAP)
    got_tags = got_tags.transpose(1, 0, 2).reshape(2, OWNERS * YC * CAP)
    grad_table = table_sum(got_tags, owned.reshape(OWNERS * YC * CAP, LANES)).T
    return (grad_proj, grad_out, grad_table)


def solution(mesh):
    fine = Mesh(mesh.devices.reshape(X, Y, C, ZQ, ZR), ALL)
    return jax.shard_map(
        per_device,
        mesh=fine,
        in_specs=(
            P(DP, None, SEQ, None),
            P(DP, None, SEQ, None),
            P(DP, None, None),
            P(DP, None, SEQ),
            P(),
            P(DP, SEQ),
            P(SEQ, DP),
        ),
        out_specs=(P(DP, SEQ), P(SEQ, DP), P(DP, SEQ)),
        check_vma=False,
    )
```

time: 237 us -> 243 us (1.025)
  blocking collectives: 44.6 us -> 52.4 us
  waiting for transfers between devices: 73.9 us -> 81.4 us
  Pallas kernels: 12.5 us -> 18.2 us
  other arithmetic: 7.5 us -> 2.84 us
  starting transfers between devices: 66.5 us -> 62 us
  local copies, waits for them, and re-layouts: 15.3 us -> 11.3 us
    all_to_all x6 -> x5, waiting for transfers between devices: 60.3 us -> 43.7 us  [exchange(): return lax.all_to_all(value, axes, split_axis=0, concat_axis=0, tiled=True)]
    all_gather x1, waiting for transfers between devices: 0.01 us -> 16.5 us  [per_device(): lax.all_gather(mine.reshape(1, 2, LENGTH, LANES), PAIR, axis=0, tiled=True)]
    pallas_call x0 -> x5, Pallas kernels: none -> 8.9 us  [the longest x1 3 us: weight_grads(): pl.pallas_call(grads_kernel, out_shape=jax.ShapeDtypeStruct((X, YC, ZR, P...]
    all_to_all x1, blocking collectives: 44.6 us -> 52.4 us  [exchange(): return lax.all_to_all(value, axes, split_axis=0, concat_axis=0, tiled=True)]
    ppermute x3 -> x4, waiting for transfers between devices: 11.2 us -> 18.6 us  [the longest x3 14.5 us: per_device(): lax.ppermute(to_y[step - 1], 'y', [(i, (i + step) % Y) for i in range(Y)])]
    all_to_all x6 -> x5, starting transfers between devices: 53.3 us -> 46.9 us  [exchange(): return lax.all_to_all(value, axes, split_axis=0, concat_axis=0, tiled=True)]
    pallas_call x1, Pallas kernels: 12.5 us -> 9.32 us  [heads_backward(): pl.pallas_call(heads_kernel, out_shape=(half, half, jax.ShapeDtypeStruct(...]
    convert_element_type x4 -> x1, other arithmetic: 2.96 us -> 0.05 us  [per_device(): got_tags.astype(F32).astype(jnp.int32).reshape(OWNERS, 2, YC * CAP)]
  transfers between devices with their start and end apart: 11 -> 11, of which waited for: 8 -> 9; matrix products, arithmetic and copies ran while one was open for 6% -> 3% of each run, Pallas kernels for 0% -> 1%
where the time goes in v4:
time: 243 us
  waiting for transfers between devices  81.4 us (33%)
  starting transfers between devices  62 us (26%)
  blocking collectives  52.4 us (22%)
  Pallas kernels  18.2 us (7%)
  between operations  14.5 us (6%)
  local copies, waits for them, and re-layouts  11.3 us (5%)
  other arithmetic  2.84 us (1%)
    all_to_all x1, blocking collectives, exchange(): return lax.all_to_all(value, axes, split_axis=0, concat_axis=0, tiled=True)  52.4 us
    all_to_all x5, starting transfers between devices, exchange(): return lax.all_to_all(value, axes, split_axis=0, concat_axis=0, tiled=True)  46.9 us
    all_to_all x5, waiting for transfers between devices, exchange(): return lax.all_to_all(value, axes, split_axis=0, concat_axis=0, tiled=True)  43.7 us
    all_gather x1, waiting for transfers between devices, per_device(): lax.all_gather(mine.reshape(1, 2, LENGTH, LANES), PAIR, axis=0, tiled=True)  16.5 us
    ppermute x3, waiting for transfers between devices, per_device(): lax.ppermute(to_y[step - 1], 'y', [(i, (i + step) % Y) for i in range(Y)])  14.5 us
    ppermute x3, starting transfers between devices, per_device(): lax.ppermute(to_y[step - 1], 'y', [(i, (i + step) % Y) for i in range(Y)])  10.8 us
    pallas_call x1, Pallas kernels, heads_backward(): pl.pallas_call(heads_kernel, out_shape=(half, half, jax.ShapeDtypeStruct(...  9.32 us
  transfers between devices with their start and end apart: 11, of which 9 were waited for; matrix products, arithmetic and copies ran while one was open for 3% of the time, Pallas kernels for 1%

profile of v4, /device:TPU:1, one launch (start us, length us, event | category | flops | bytes accessed | tf_op | source)
XLA Modules:
  0.0 242.6 jit_solution(5403376173892104972)
XLA Ops:
  9.4 10.3 %all-to-all-start = ((bf16[8,2,2,64,128]{4,3,1,2,0:T(8,128)(2,1)}), bf16[8,2,2,64,128]{4,3,1,2,0:T(8,128)(2,1)S(1)}, u32[]{:S(2)}, u32[]{:S(2)}) async-start(bf16[8,2,2,64,128]{4,3,1,2,0:T(8,128)(2,1)} %copy.51), calls=%async_computation | async-start | bytes 1048576 | tf_op jit(solution)/shard_map/all_to_all | solution.py:38
  21.6 1.9 collective-permute-start
  23.5 4.1 %collective-permute-done = bf16[13,8,128]{2,1,0:T(8,128)(2,1)S(1)} collective-permute-done((bf16[13,8,128]{2,1,0:T(8,128)(2,1)S(1)}, bf16[13,8,128]{2,1,0:T(8,128)(2,1)S(1)}, u32[]{:S(2)}, u32[]{:S(2)}) %collective-permute-start) | collective-permute-done | bytes 26656 | tf_op jit(solution)/shard_map/ppermute | solution.py:347
  27.7 1.4 all-to-all-done
  29.3 52.4 %all_to_all.30 = bf16[16,23,8,128]{3,2,1,0:T(8,128)(2,1)S(1)} all-to-all(bf16[16,23,8,128]{3,2,1,0:T(8,128)(2,1)S(1)} %pad_maximum_fusion), channel_id=1, replica_groups=mesh['x'=4,'y'=4,'c'=2,'zq'=8,'zr'=2] {'zq','zr'}, dimensions={0} | all-to-all | bytes 1507328 | tf_op jit(solution)/shard_map/all_to_all | solution.py:38
  83.9 7.1 %all-to-all-start.2 = ((bf16[8,8,16,640]{3,2,1,0:T(8,128)(2,1)}), bf16[8,8,16,640]{3,2,1,0:T(8,128)(2,1)S(1)}, u32[]{:S(2)}, u32[]{:S(2)}) async-start(bf16[8,8,16,640]{3,2,1,0:T(8,128)(2,1)} %broadcast_in_dim.75), calls=%async_computation.2 | async-start | bytes 2621440 | tf_op jit(solution)/shard_map/all_to_all | solution.py:38
  93.1 11.6 %all-to-all-done.2 = bf16[8,8,16,640]{3,2,1,0:T(8,128)(2,1)S(1)} async-done(((bf16[8,8,16,640]{3,2,1,0:T(8,128)(2,1)}), bf16[8,8,16,640]{3,2,1,0:T(8,128)(2,1)S(1)}, u32[]{:S(2)}, u32[]{:S(2)}) %all-to-all-start.2) | async-done | bytes 1310752 | tf_op jit(solution)/shard_map/all_to_all | solution.py:38
  104.7 16.5 %all-gather.2.cloned.1.call-done.packs = bf16[8,2,1024,128]{3,2,1,0:T(8,128)(2,1)} async-done(((bf16[1,2,1024,128]{3,2,1,0:T(8,128)(2,1)}), bf16[8,2,1024,128]{3,2,1,0:T(8,128)(2,1)}) %all-gather.2.cloned.1.call-update) | async-done | bytes 4194320 | tf_op jit(solution)/shard_map/all_gather | solution.py:359
  121.2 2.2 copy-done.1
  123.4 9.3 %heads.1 = (bf16[4,128,1024]{2,1,0:T(8,128)(2,1)S(1)}, bf16[4,128,1024]{2,1,0:T(8,128)(2,1)S(1)}, bf16[1024,512]{1,0:T(8,128)(2,1)S(1)}, bf16[1024,128]{1,0:T(8,128)(2,1)S(1)}) custom-call(s32[4]{0:T(128)S(1)} %pad_add_fusion.info, bf16[8,2,1024,128]{3,2,1,0:T(8,128)(2,1)S(1)} %copy-done.1, bf16[4,2,8,16,640]{4,3,2,1,0:T(8,128)(2,1)S(1)} %bitcast.99), custom_call_target="tpu_custom_call" | custom-call | flops 4000000000 | bytes 9000000 | tf_op jit(solution)/shard_map/heads/pallas_call | solution.py:151
  133.7 3.0 %weight_grads.1 = bf16[4,8,2,16,768]{4,3,2,1,0:T(8,128)(2,1)} custom-call(bf16[8,2,1024,128]{3,2,1,0:T(8,128)(2,1)S(1)} %copy-done.1, bf16[1024,512]{1,0:T(8,128)(2,1)S(1)} %get-tuple-element.17.d_z, bf16[1024,128]{1,0:T(8,128)(2,1)S(1)} %get-tuple-element.18.gated, bf16[32,16,128]{2,1,0:T(8,128)(2,1)S(1)} %broadcast_in_dim.79.tags), custom_call_target="tpu_custom_call" | custom-call | flops 1350000000 | bytes 6800000 | tf_op jit(solution)/shard_map/weight_grads/pallas_call | solution.py:192
  136.7 7.2 %all-to-all-start.3 = ((bf16[64,16,768]{2,1,0:T(8,128)(2,1)}), bf16[64,16,768]{2,1,0:T(8,128)(2,1)S(1)}, u32[]{:S(2)}, u32[]{:S(2)}) async-start(bf16[64,16,768]{2,1,0:T(8,128)(2,1)} %bitcast.36), calls=%async_computation.3 | async-start | bytes 3145728 | tf_op jit(solution)/shard_map/all_to_all | solution.py:38
  143.9 2.4 collective-permute-start.1
  146.3 2.6 %collective-permute-done.1.got = bf16[4,128,1024]{2,1,0:T(8,128)(2,1)} collective-permute-done((bf16[4,128,1024]{2,1,0:T(8,128)(2,1)}, bf16[4,128,1024]{2,1,0:T(8,128)(2,1)}, u32[]{:S(2)}, u32[]{:S(2)}) %collective-permute-start.1) | collective-permute-done | bytes 1048608 | tf_op jit(solution)/shard_map/ppermute | solution.py:386
  148.9 2.1 pair_sums.1
  151.0 3.2 %collective-permute-start.2 = (bf16[128,1024]{1,0:T(8,128)(2,1)}, bf16[128,1024]{1,0:T(8,128)(2,1)S(1)}, u32[]{:S(2)}, u32[]{:S(2)}) collective-permute-start(bf16[128,1024]{1,0:T(8,128)(2,1)} %get-tuple-element.14), channel_id=1, source_target_pairs={{0,32},{32,64},{64,96},{96,0},{1,33},{33,65},{65,97},{97,1},{2,34}... | collective-permute-start | bytes 786440 | tf_op jit(solution)/shard_map/ppermute | solution.py:394
  154.2 4.3 %collective-permute-start.3 = (bf16[128,1024]{1,0:T(8,128)(2,1)}, bf16[128,1024]{1,0:T(8,128)(2,1)S(1)}, u32[]{:S(2)}, u32[]{:S(2)}) collective-permute-start(bf16[128,1024]{1,0:T(8,128)(2,1)} %get-tuple-element.15), channel_id=1, source_target_pairs={{0,64},{32,96},{64,0},{96,32},{1,65},{33,97},{65,1},{97,33},{2,66}... | collective-permute-start | bytes 786440 | tf_op jit(solution)/shard_map/ppermute | solution.py:394
  158.5 3.3 %collective-permute-start.4 = (bf16[128,1024]{1,0:T(8,128)(2,1)S(1)}, bf16[128,1024]{1,0:T(8,128)(2,1)S(1)}, u32[]{:S(2)}, u32[]{:S(2)}) collective-permute-start(bf16[128,1024]{1,0:T(8,128)(2,1)S(1)} %get-tuple-element.16), channel_id=1, source_target_pairs={{0,96},{32,0},{64,32},{96,64},{1,97},{33,1},{65,33},{97,65},{2,98}... | collective-permute-start | bytes 786440 | tf_op jit(solution)/shard_map/ppermute | solution.py:394
  162.8 8.6 %collective-permute-done.2.came_1 = bf16[128,1024]{1,0:T(8,128)(2,1)S(1)} collective-permute-done((bf16[128,1024]{1,0:T(8,128)(2,1)}, bf16[128,1024]{1,0:T(8,128)(2,1)S(1)}, u32[]{:S(2)}, u32[]{:S(2)}) %collective-permute-start.2) | collective-permute-done | bytes 262176 | tf_op jit(solution)/shard_map/ppermute | solution.py:394
  171.4 5.9 %collective-permute-done.3.came_2 = bf16[128,1024]{1,0:T(8,128)(2,1)S(1)} collective-permute-done((bf16[128,1024]{1,0:T(8,128)(2,1)}, bf16[128,1024]{1,0:T(8,128)(2,1)S(1)}, u32[]{:S(2)}, u32[]{:S(2)}) %collective-permute-start.3) | collective-permute-done | bytes 262176 | tf_op jit(solution)/shard_map/ppermute | solution.py:394
  178.4 11.1 %all-to-all-start.4 = ((bf16[16,112,128]{2,1,0:T(8,128)(2,1)}), bf16[16,112,128]{2,1,0:T(8,128)(2,1)S(1)}, u32[]{:S(2)}, u32[]{:S(2)}) async-start(bf16[16,112,128]{2,1,0:T(8,128)(2,1)} %payload.1), calls=%async_computation.4 | async-start | bytes 917504 | tf_op jit(solution)/shard_map/all_to_all | solution.py:38
  189.5 20.7 %all-to-all-done.4.merged = bf16[16,112,128]{2,1,0:T(8,128)(2,1)S(1)} async-done(((bf16[16,112,128]{2,1,0:T(8,128)(2,1)}), bf16[16,112,128]{2,1,0:T(8,128)(2,1)S(1)}, u32[]{:S(2)}, u32[]{:S(2)}) %all-to-all-start.4) | async-done | bytes 458784 | tf_op jit(solution)/shard_map/all_to_all | solution.py:38
  211.5 11.2 %all-to-all-start.5 = ((bf16[32,64,128]{2,1,0:T(8,128)(2,1)}), bf16[32,64,128]{2,1,0:T(8,128)(2,1)S(1)}, u32[]{:S(2)}, u32[]{:S(2)}) async-start(bf16[32,64,128]{2,1,0:T(8,128)(2,1)} %place.1), calls=%async_computation.5 | async-start | bytes 1048576 | tf_op jit(solution)/shard_map/all_to_all | solution.py:38
  224.4 9.9 %all-to-all-done.5 = bf16[32,64,128]{2,1,0:T(8,128)(2,1)S(1)} async-done(((bf16[32,64,128]{2,1,0:T(8,128)(2,1)}), bf16[32,64,128]{2,1,0:T(8,128)(2,1)S(1)}, u32[]{:S(2)}, u32[]{:S(2)}) %all-to-all-start.5) | async-done | bytes 524320 | tf_op jit(solution)/shard_map/all_to_all | solution.py:38
  (86 shorter events, 15.8 us)
Async XLA Ops:
  7.2 12.8 %copy-start = (s32[8192]{0:T(1024)S(1)}, s32[8192]{0:T(1024)}, u32[]{:S(2)}) copy-start(s32[8192]{0:T(1024)} %param.11) | copy-start | bytes 98308
  7.2 12.5 %copy-start.5 = (s32[1,2,64]{2,1,0:T(2,128)S(1)}, s32[1,2,64]{2,1,0:T(2,128)}, u32[]{:S(2)}) copy-start(s32[1,2,64]{2,1,0:T(2,128)} %param.10) | copy-start | bytes 1540
  7.2 12.7 %copy-start.6 = (s32[1,2,3]{2,1,0:T(2,128)S(1)}, s32[1,2,3]{2,1,0:T(2,128)}, u32[]{:S(2)}) copy-start(s32[1,2,3]{2,1,0:T(2,128)} %param.9) | copy-start | bytes 76
  8.3 13.1 %copy-start.4 = (bf16[64,32]{0,1:T(8,128)(2,1)S(1)}, bf16[64,32]{0,1:T(8,128)(2,1)}, u32[]{:S(2)}) copy-start(bf16[64,32]{0,1:T(8,128)(2,1)} %param.13) | copy-start | bytes 12292
  8.3 13.3 %copy-start.3 = (bf16[32,256]{1,0:T(8,128)(2,1)S(1)}, bf16[32,256]{1,0:T(8,128)(2,1)}, u32[]{:S(2)}) copy-start(bf16[32,256]{1,0:T(8,128)(2,1)} %param.12) | copy-start | bytes 49156
  9.4 19.8 %all-to-all-start = ((bf16[8,2,2,64,128]{4,3,1,2,0:T(8,128)(2,1)}), bf16[8,2,2,64,128]{4,3,1,2,0:T(8,128)(2,1)S(1)}, u32[]{:S(2)}, u32[]{:S(2)}) async-start(bf16[8,2,2,64,128]{4,3,1,2,0:T(8,128)(2,1)} %copy.51), calls=%async_computation | async-start | bytes 1048576 | tf_op jit(solution)/shard_map/all_to_all | solution.py:38
  19.6 101.6 %all-gather.2.cloned.1.call-start = ((), (), s32[]{:S(2)}) async-start(), calls=%async_computation.6 | async-start | bytes 4718592 | tf_op jit(solution)/shard_map/all_gather | solution.py:359
  21.6 6.1 %collective-permute-start = (bf16[13,8,128]{2,1,0:T(8,128)(2,1)S(1)}, bf16[13,8,128]{2,1,0:T(8,128)(2,1)S(1)}, u32[]{:S(2)}, u32[]{:S(2)}) collective-permute-start(bf16[13,8,128]{2,1,0:T(8,128)(2,1)S(1)} %pad_maximum_fusion.4), channel_id=1, source_target_pairs={{0,0},{1,1},{2,16},{3,17},{4,32},{5,33},{6,48},{7,49},{8,64},{9,65... | collective-permute-start | bytes 79880 | tf_op jit(solution)/shard_map/ppermute | solution.py:347
  83.9 20.8 %all-to-all-start.2 = ((bf16[8,8,16,640]{3,2,1,0:T(8,128)(2,1)}), bf16[8,8,16,640]{3,2,1,0:T(8,128)(2,1)S(1)}, u32[]{:S(2)}, u32[]{:S(2)}) async-start(bf16[8,8,16,640]{3,2,1,0:T(8,128)(2,1)} %broadcast_in_dim.75), calls=%async_computation.2 | async-start | bytes 2621440 | tf_op jit(solution)/shard_map/all_to_all | solution.py:38
  121.2 2.2 copy-start.1
  132.7 1.0 copy-start.2
  136.7 40.6 %all-to-all-start.3 = ((bf16[64,16,768]{2,1,0:T(8,128)(2,1)}), bf16[64,16,768]{2,1,0:T(8,128)(2,1)S(1)}, u32[]{:S(2)}, u32[]{:S(2)}) async-start(bf16[64,16,768]{2,1,0:T(8,128)(2,1)} %bitcast.36), calls=%async_computation.3 | async-start | bytes 3145728 | tf_op jit(solution)/shard_map/all_to_all | solution.py:38
  143.9 5.0 %collective-permute-start.1 = (bf16[4,128,1024]{2,1,0:T(8,128)(2,1)}, bf16[4,128,1024]{2,1,0:T(8,128)(2,1)}, u32[]{:S(2)}, u32[]{:S(2)}) collective-permute-start(bf16[4,128,1024]{2,1,0:T(8,128)(2,1)} %copy-done.2), channel_id=1, source_target_pairs={{0,16},{16,0},{1,17},{17,1},{2,18},{18,2},{3,19},{19,3},{4,20},{20... | collective-permute-start | bytes 3145736 | tf_op jit(solution)/shard_map/ppermute | solution.py:386
  151.0 20.4 %collective-permute-start.2 = (bf16[128,1024]{1,0:T(8,128)(2,1)}, bf16[128,1024]{1,0:T(8,128)(2,1)S(1)}, u32[]{:S(2)}, u32[]{:S(2)}) collective-permute-start(bf16[128,1024]{1,0:T(8,128)(2,1)} %get-tuple-element.14), channel_id=1, source_target_pairs={{0,32},{32,64},{64,96},{96,0},{1,33},{33,65},{65,97},{97,1},{2,34}... | collective-permute-start | bytes 786440 | tf_op jit(solution)/shard_map/ppermute | solution.py:394
  154.2 23.0 %collective-permute-start.3 = (bf16[128,1024]{1,0:T(8,128)(2,1)}, bf16[128,1024]{1,0:T(8,128)(2,1)S(1)}, u32[]{:S(2)}, u32[]{:S(2)}) collective-permute-start(bf16[128,1024]{1,0:T(8,128)(2,1)} %get-tuple-element.15), channel_id=1, source_target_pairs={{0,64},{32,96},{64,0},{96,32},{1,65},{33,97},{65,1},{97,33},{2,66}... | collective-permute-start | bytes 786440 | tf_op jit(solution)/shard_map/ppermute | solution.py:394
  158.5 18.7 %collective-permute-start.4 = (bf16[128,1024]{1,0:T(8,128)(2,1)S(1)}, bf16[128,1024]{1,0:T(8,128)(2,1)S(1)}, u32[]{:S(2)}, u32[]{:S(2)}) collective-permute-start(bf16[128,1024]{1,0:T(8,128)(2,1)S(1)} %get-tuple-element.16), channel_id=1, source_target_pairs={{0,96},{32,0},{64,32},{96,64},{1,97},{33,1},{65,33},{97,65},{2,98}... | collective-permute-start | bytes 786440 | tf_op jit(solution)/shard_map/ppermute | solution.py:394
  178.4 31.8 %all-to-all-start.4 = ((bf16[16,112,128]{2,1,0:T(8,128)(2,1)}), bf16[16,112,128]{2,1,0:T(8,128)(2,1)S(1)}, u32[]{:S(2)}, u32[]{:S(2)}) async-start(bf16[16,112,128]{2,1,0:T(8,128)(2,1)} %payload.1), calls=%async_computation.4 | async-start | bytes 917504 | tf_op jit(solution)/shard_map/all_to_all | solution.py:38
  211.5 22.9 %all-to-all-start.5 = ((bf16[32,64,128]{2,1,0:T(8,128)(2,1)}), bf16[32,64,128]{2,1,0:T(8,128)(2,1)S(1)}, u32[]{:S(2)}, u32[]{:S(2)}) async-start(bf16[32,64,128]{2,1,0:T(8,128)(2,1)} %place.1), calls=%async_computation.5 | async-start | bytes 1048576 | tf_op jit(solution)/shard_map/all_to_all | solution.py:38
Sparse Core Ops, SparseCore 0:
  82.7 38.3 all-gather.1

commit v5 on v4

--- a/solution.py
+++ b/solution.py
@@ -173,7 +173,7 @@
     )(info, packs, weights)
 
 
-def grads_kernel(packs, d_z, gated, tags, out):
+def grads_kernel(packs, d_z, gated, out):
     for x in range(X):
         for dest, source, t in ((slice(0, 512), d_z, 0), (slice(512, 640), gated, 1)):
             columns = jnp.concatenate([packs[2 * x, t], packs[2 * x + 1, t]], axis=1)
@@ -182,24 +182,20 @@
                 for r in range(ZR):
                     at = yc * 32 + r * PART_ROWS
                     out[x, yc, r, :, dest] = block[at : at + PART_ROWS]
-    for x in range(X):
-        for yc in range(YC):
-            for r in range(ZR):
-                out[x, yc, r, :, HIDDEN:] = tags[x * YC + yc]
-
-
-def weight_grads(packs, d_z, gated, tags):
+
+
+def weight_grads(packs, d_z, gated):
     return pl.pallas_call(
         grads_kernel,
-        out_shape=jax.ShapeDtypeStruct((X, YC, ZR, PART_ROWS, HIDDEN + LANES), BF16),
-        in_specs=[VMEM_SPEC] * 4,
+        out_shape=jax.ShapeDtypeStruct((X, YC, ZR, PART_ROWS, HIDDEN), BF16),
+        in_specs=[VMEM_SPEC] * 3,
         out_specs=VMEM_SPEC,
         compiler_params=pltpu.CompilerParams(vmem_limit_bytes=32 * 2**20),
         cost_estimate=pl.CostEstimate(
             flops=1_350_000_000, bytes_accessed=6_800_000, transcendentals=0
         ),
         name="weight_grads",
-    )(packs, d_z, gated, tags)
+    )(packs, d_z, gated)
 
 
 def pair_kernel(place, kept, got, own, *to_y):
@@ -239,7 +235,7 @@
         total = jnp.zeros((PART_ROWS, HIDDEN), F32)
         for x in range(X):
             for r in range(ZR):
-                total = total + shared[x, h, r, :, :HIDDEN].astype(F32)
+                total = total + shared[x, h, r].astype(F32)
         total = total.astype(BF16)
         for s in range(2):
             for n, col in enumerate((2 * s, 2 * s + 1, 4)):
@@ -261,7 +257,7 @@
     )(own, *came, dy, shared)
 
 
-def place_kernel(slots, merged, out):
+def place_kernel(slots, tags, merged, out):
     slot_ids = lax.broadcasted_iota(jnp.int32, (SLOTS, LANES), 0)
     lane = lax.broadcasted_iota(jnp.int32, (SLOTS, LANES), 1)
     for pair in range(YC // 2):
@@ -279,45 +275,75 @@
             rows = jnp.where(lane < 64, moved[0], moved[1])
             both.append(rows.reshape(OWNERS, CAP, LANES))
         out[:, pair * 16 : (pair + 1) * 16, :] = jnp.concatenate(both, axis=1).astype(BF16)
-
-
-def place(slots, merged):
+    out[:, YC * CAP :, :] = tags[...]
+
+
+def place(slots, tags, merged):
     return pl.pallas_call(
         place_kernel,
-        out_shape=jax.ShapeDtypeStruct((OWNERS, YC * CAP, LANES), BF16),
+        out_shape=jax.ShapeDtypeStruct((OWNERS, YC * CAP + 16, LANES), BF16),
+        in_specs=[VMEM_SPEC] * 3,
+        out_specs=VMEM_SPEC,
+        compiler_params=pltpu.CompilerParams(vmem_limit_bytes=32 * 2**20),
+        cost_estimate=pl.CostEstimate(
+            flops=135_000_000, bytes_accessed=1_000_000, transcendentals=0
+        ),
+        name="place",
+    )(slots, tags, merged)
+
+
+def table_kernel(owned, out):
+    count = YC * CAP
+    row_ids = lax.broadcasted_iota(jnp.int32, (ROWS, LANES), 0).astype(F32)
+    left = lax.broadcasted_iota(jnp.int32, (count, LANES), 1) < 64
+    total = jnp.zeros((ROWS, LANES), F32)
+    for pair in range(OWNERS // 2):
+        select, rows = [], []
+        for source in (2 * pair, 2 * pair + 1):
+            tag = owned[source, count:, :].astype(F32)[:1]
+            select.append((tag == row_ids).astype(BF16))
+            here = owned[source, :count, :].astype(F32)
+            rows.append(jnp.where(left, here, 0.0).astype(BF16))
+            rows.append(jnp.where(left, 0.0, here).astype(BF16))
+        total = total + jnp.dot(
+            jnp.concatenate(select, axis=1),
+            jnp.concatenate(rows, axis=0),
+            preferred_element_type=F32,
+        )
+    out[...] = (total + pltpu.roll(total, 64, 1)).T[:64]
+
+
+def table_sum(owned):
+    return pl.pallas_call(
+        table_kernel,
+        out_shape=jax.ShapeDtypeStruct((64, ROWS), F32),
+        in_specs=[VMEM_SPEC],
+        out_specs=VMEM_SPEC,
+        compiler_params=pltpu.CompilerParams(vmem_limit_bytes=32 * 2**20),
+        cost_estimate=pl.CostEstimate(
+            flops=270_000_000, bytes_accessed=1_000_000, transcendentals=0
+        ),
+        name="table_sum",
+    )(owned)
+
+
+def split_kernel(inputs, cotangent, out):
+    for g in range(8):
+        for p in range(2):
+            for t, source in enumerate((inputs, cotangent)):
+                out[g, p, t] = source[p, :, g * LANES : (g + 1) * LANES]
+
+
+def split_columns(inputs, cotangent):
+    return pl.pallas_call(
+        split_kernel,
+        out_shape=jax.ShapeDtypeStruct((8, 2, 2, 64, LANES), BF16),
         in_specs=[VMEM_SPEC] * 2,
         out_specs=VMEM_SPEC,
         compiler_params=pltpu.CompilerParams(vmem_limit_bytes=32 * 2**20),
-        cost_estimate=pl.CostEstimate(
-            flops=135_000_000, bytes_accessed=1_000_000, transcendentals=0
-        ),
-        name="place",
-    )(slots, merged)
-
-
-def table_kernel(tags, rows, out):
-    row_ids = lax.broadcasted_iota(jnp.int32, (ROWS, rows.shape[0]), 0)
-    sums = [
-        jnp.dot(
-            (tags[s : s + 1, :] == row_ids).astype(BF16), rows[...], preferred_element_type=F32
-        )
-        for s in range(2)
-    ]
-    out[...] = (sums[0] + pltpu.roll(sums[1], 64, 1)).T[:64]
-
-
-def table_sum(tags, rows):
-    return pl.pallas_call(
-        table_kernel,
-        out_shape=jax.ShapeDtypeStruct((64, ROWS), F32),
-        in_specs=[VMEM_SPEC] * 2,
-        out_specs=VMEM_SPEC,
-        compiler_params=pltpu.CompilerParams(vmem_limit_bytes=32 * 2**20),
-        cost_estimate=pl.CostEstimate(
-            flops=270_000_000, bytes_accessed=1_000_000, transcendentals=0
-        ),
-        name="table_sum",
-    )(tags, rows)
+        cost_estimate=pl.CostEstimate(flops=0, bytes_accessed=1_000_000, transcendentals=0),
+        name="split_columns",
+    )(inputs, cotangent)
 
 
 def per_device(inputs, cotangent, lengths, item_ids, owner_row, w_project, w_output):
@@ -332,37 +358,25 @@
     lens_row = jnp.pad(lens_row, (0, LANES - lens_row.shape[0]))
     small = jnp.pad(jnp.stack([slot, local_row, lens_row]), ((0, 5), (0, 0))).astype(BF16)
     high = PART_ROWS // 8
-    n_w = 3 * high + 1
+    wp_high = 2 * high
+    n_w = wp_high + 2
     wp_tiles = w_project.reshape(ZR, high, 8, 2, LANES).transpose(0, 1, 3, 2, 4)
-    wo_t = w_output.T
-    wo_tiles = jnp.concatenate([wo_t, wo_t], axis=1).reshape(ZR * high, 8, LANES)
-    turned = jnp.concatenate([wp_tiles.reshape(2 * ZR * high, 8, LANES), wo_tiles, small[None]])
-    turn = [
-        ((x * YC + a) * Z + b * 2 + s, (x * YC + b) * Z + a * 2 + s)
-        for x in range(X)
-        for a in range(YC)
-        for b in range(YC)
-        for s in range(2)
-    ]
-    turned = lax.ppermute(turned, ALL, turn)
-    wp_tiles = turned[: 2 * ZR * high].reshape(ZR, 2 * high, 8, LANES)
-    wo_tiles = turned[2 * ZR * high : 3 * ZR * high].reshape(ZR, high, 8, LANES)
-    small = jnp.broadcast_to(turned[None, -1:], (ZR, 1, 8, LANES))
+    wp_tiles = wp_tiles.reshape(ZR, wp_high, 8, LANES)
+    wo_tiles = w_output.T.reshape(ZR, high, 8, 64).transpose(0, 2, 1, 3).reshape(ZR, 1, 8, LANES)
+    small = jnp.broadcast_to(small[None, None], (ZR, 1, 8, LANES))
     w_tiles = jnp.concatenate([wp_tiles, wo_tiles, small], axis=1)
 
-    both = jnp.stack([inputs[0], cotangent[0]]).reshape(2, 2, 64, 8, LANES)
-    spread = exchange(both.transpose(3, 1, 0, 2, 4), PAIR)
+    spread = exchange(split_columns(inputs[0], cotangent[0]), PAIR)
     spread = spread.reshape(Z, 16, 8, LANES)
     w_tiles = jnp.broadcast_to(w_tiles[None], (ZQ, ZR, n_w, 8, LANES)).reshape(Z, n_w, 8, LANES)
     arrived = exchange(jnp.concatenate([spread, w_tiles], axis=1), SEQ)
     mine = arrived[:, :16].reshape(Z, 2, 64, LANES).transpose(1, 0, 2, 3)
     packs = lax.all_gather(mine.reshape(1, 2, LENGTH, LANES), PAIR, axis=0, tiled=True)
 
-    by_head = arrived[:, 16:].reshape(YC, 2, n_w, 8, LANES)
-    wp_part = by_head[:, :, : 2 * high].reshape(YC, 2, high, 2, 8, LANES)
+    by_head = exchange(arrived[:, 16:].reshape(YC, 2, n_w, 8, LANES), PAIR)
+    wp_part = by_head[:, :, :wp_high].reshape(YC, 2, high, 2, 8, LANES)
     wp_part = wp_part.transpose(0, 2, 4, 1, 3, 5).reshape(YC, PART_ROWS, 4 * HEAD_DIM)
-    wo_part = by_head[:, :, 2 * high : 3 * high]
-    wo_part = jnp.where(lane < 64, wo_part[:, 0], wo_part[:, 1])
+    wo_part = by_head[:, :, wp_high].reshape(YC, 2, 8, high, 64).transpose(0, 3, 2, 1, 4)
     w_part = jnp.concatenate([wp_part, wo_part.reshape(YC, PART_ROWS, HEAD_DIM)], axis=2)
     w_all = jnp.broadcast_to(w_part[None], (X * ZR,) + w_part.shape)
     weights = exchange(w_all, SHARE).reshape(X, ZR, YC, PART_ROWS, HIDDEN)
@@ -380,16 +394,17 @@
     placed = slots[:, :, None, :] == slot_ids[None, None, :, None]
     tags = jnp.sum(jnp.where(placed, tag_of[:, :, None, :], 0.0), axis=3)
     tags = tags.reshape(YC, 2, OWNERS, CAP).transpose(2, 1, 0, 3).reshape(OWNERS, 1, LANES)
-    tags = jnp.broadcast_to(tags.astype(BF16), (OWNERS, PART_ROWS, LANES))
+    tags = jnp.broadcast_to(tags.astype(BF16), (OWNERS, 16, LANES))
 
     kept, sent, d_z, gated = heads_backward(info, packs, weights)
     got = lax.ppermute(sent, "c", [(0, 1), (1, 0)])
 
-    grads = weight_grads(packs, d_z, gated, tags)
-    shared = exchange(grads.reshape(X * YC * ZR, PART_ROWS, HIDDEN + LANES), SPREAD)
-    shared = shared.reshape(X, YC, ZR, PART_ROWS, HIDDEN + LANES)
-
+    grads = weight_grads(packs, d_z, gated)
     own, *to_y = pair_sums(y_here[None].astype(jnp.int32), kept, got)
+    grads, own = lax.optimization_barrier((grads, own))
+
+    shared = exchange(grads.reshape(X * YC * ZR, PART_ROWS, HIDDEN), SPREAD)
+    shared = shared.reshape(X, YC, ZR, PART_ROWS, HIDDEN)
     came = [
         lax.ppermute(to_y[step - 1], "y", [(i, (i + step) % Y) for i in range(Y)])
         for step in range(1, Y)
@@ -404,12 +419,8 @@
     both_out = w_grad[:, 2].reshape(32, 2, 64)
     grad_out = lax.dynamic_index_in_dim(both_out, z_here & 1, 1, keepdims=False).T
 
-    owned = exchange(place(slots.reshape(2 * YC, LANES), merged), DP)
-    got_tags = shared[:, :, 0, 0, HIDDEN:]
-    got_tags = got_tags.astype(F32).astype(jnp.int32).reshape(OWNERS, 2, YC * CAP)
-    got_tags = got_tags.transpose(1, 0, 2).reshape(2, OWNERS * YC * CAP)
-    grad_table = table_sum(got_tags, owned.reshape(OWNERS * YC * CAP, LANES)).T
-    return (grad_proj, grad_out, grad_table)
+    owned = exchange(place(slots.reshape(2 * YC, LANES), tags, merged), DP)
+    return (grad_proj, grad_out, table_sum(owned).T)
 
 
 def solution(mesh):

time: 243 us -> 241 us (level)
  waiting for transfers between devices: 81.4 us -> 73 us
  blocking collectives: 52.4 us -> 58.4 us
  local copies, waits for them, and re-layouts: 11.3 us -> 15.8 us
  starting transfers between devices: 62 us -> 58.2 us
    all_gather x1, waiting for transfers between devices: 16.5 us -> 0.01 us  [per_device(): lax.all_gather(mine.reshape(1, 2, LENGTH, LANES), PAIR, axis=0, tiled=True)]
    all_to_all x5, waiting for transfers between devices: 43.7 us -> 54.8 us  [exchange(): return lax.all_to_all(value, axes, split_axis=0, concat_axis=0, tiled=True)]
    all_to_all x1 -> x2, blocking collectives: 52.4 us -> 58.4 us  [exchange(): return lax.all_to_all(value, axes, split_axis=0, concat_axis=0, tiled=True)]
    unnamed x16 -> x25, local copies, waits for them, and re-layouts: 3.9 us -> 9.28 us
    ppermute x1 -> x0, waiting for transfers between devices: 4.14 us -> none  [per_device(): turned = lax.ppermute(turned, ALL, turn)]
    all_to_all x5, starting transfers between devices: 46.9 us -> 43.1 us  [exchange(): return lax.all_to_all(value, axes, split_axis=0, concat_axis=0, tiled=True)]
    ppermute x3, waiting for transfers between devices: 14.5 us -> 18.2 us  [per_device(): lax.ppermute(to_y[step - 1], 'y', [(i, (i + step) % Y) for i in range(Y)])]
    ppermute x1, waiting for transfers between devices: 2.6 us -> 0.01 us  [per_device(): got = lax.ppermute(sent, 'c', [(0, 1), (1, 0)])]
  transfers between devices with their start and end apart: 11 -> 10, of which waited for: 9 -> 6; matrix products, arithmetic and copies ran while one was open for 3% -> 3% of each run, Pallas kernels for 1% -> 1%
where the time goes in v5:
time: 241 us; the launch traced here: 240 us
  waiting for transfers between devices  73 us (30%)
  blocking collectives  58.4 us (24%)
  starting transfers between devices  58.2 us (24%)
  Pallas kernels  18.3 us (8%)
  local copies, waits for them, and re-layouts  15.8 us (7%)
  between operations  14.4 us (6%)
    all_to_all x2, blocking collectives, exchange(): return lax.all_to_all(value, axes, split_axis=0, concat_axis=0, tiled=True)  58.4 us
    all_to_all x5, waiting for transfers between devices, exchange(): return lax.all_to_all(value, axes, split_axis=0, concat_axis=0, tiled=True)  54.8 us
    all_to_all x5, starting transfers between devices, exchange(): return lax.all_to_all(value, axes, split_axis=0, concat_axis=0, tiled=True)  43.1 us
    ppermute x3, waiting for transfers between devices, per_device(): lax.ppermute(to_y[step - 1], 'y', [(i, (i + step) % Y) for i in range(Y)])  18.2 us
    ppermute x3, starting transfers between devices, per_device(): lax.ppermute(to_y[step - 1], 'y', [(i, (i + step) % Y) for i in range(Y)])  10.7 us
    pallas_call x1, Pallas kernels, heads_backward(): pl.pallas_call(heads_kernel, out_shape=(half, half, jax.ShapeDtypeStruct(...  10.3 us
    unnamed x25, local copies, waits for them, and re-layouts  9.28 us
  transfers between devices with their start and end apart: 10, of which 6 were waited for; matrix products, arithmetic and copies ran while one was open for 3% of the time, Pallas kernels for 1%

profile of v5, /device:TPU:1, one launch (start us, length us, event | category | flops | bytes accessed | tf_op | source)
XLA Modules:
  0.0 239.7 jit_solution(6108704281038619307)
XLA Ops:
  10.0 10.3 %all-to-all-start = ((bf16[8,2,2,64,128]{4,3,2,1,0:T(8,128)(2,1)}), bf16[8,2,2,64,128]{4,3,2,1,0:T(8,128)(2,1)S(1)}, u32[]{:S(2)}, u32[]{:S(2)}) async-start(bf16[8,2,2,64,128]{4,3,2,1,0:T(8,128)(2,1)} %split_columns.1), calls=%async_computation | async-start | bytes 1048576 | tf_op jit(solution)/shard_map/all_to_all | solution.py:38
  22.3 7.5 %all-to-all-done = bf16[8,2,2,64,128]{4,3,2,1,0:T(8,128)(2,1)S(1)} async-done(((bf16[8,2,2,64,128]{4,3,2,1,0:T(8,128)(2,1)}), bf16[8,2,2,64,128]{4,3,2,1,0:T(8,128)(2,1)S(1)}, u32[]{:S(2)}, u32[]{:S(2)}) %all-to-all-start) | async-done | bytes 524320 | tf_op jit(solution)/shard_map/all_to_all | solution.py:38
  29.9 44.5 %all_to_all.35 = bf16[16,22,8,128]{3,2,1,0:T(8,128)(2,1)S(1)} all-to-all(bf16[16,22,8,128]{3,2,1,0:T(8,128)(2,1)S(1)} %pad_maximum_fusion), channel_id=1, replica_groups=mesh['x'=4,'y'=4,'c'=2,'zq'=8,'zr'=2] {'zq','zr'}, dimensions={0} | all-to-all | bytes 1441792 | tf_op jit(solution)/shard_map/all_to_all | solution.py:38
  75.3 13.9 %all_to_all.36 = bf16[8,2,6,8,128]{4,3,2,1,0:T(8,128)(2,1)S(1)} all-to-all(bf16[8,2,6,8,128]{4,3,2,1,0:T(8,128)(2,1)S(1)} %bitcast.92), channel_id=1, replica_groups=mesh['x'=4,'y'=4,'c'=2,'zq'=8,'zr'=2] {'y','c'}, dimensions={0} | all-to-all | bytes 393216 | tf_op jit(solution)/shard_map/all_to_all | solution.py:38
  89.6 1.2 broadcast_in_dim.62
  90.8 5.6 %all-to-all-start.3 = ((bf16[8,8,16,640]{3,2,1,0:T(8,128)(2,1)}), bf16[8,8,16,640]{3,2,1,0:T(8,128)(2,1)S(1)}, u32[]{:S(2)}, u32[]{:S(2)}) async-start(bf16[8,8,16,640]{3,2,1,0:T(8,128)(2,1)} %broadcast_in_dim.62), calls=%async_computation.3 | async-start | bytes 2621440 | tf_op jit(solution)/shard_map/all_to_all | solution.py:38
  97.2 16.3 %all-to-all-done.3 = bf16[8,8,16,640]{3,2,1,0:T(8,128)(2,1)S(1)} async-done(((bf16[8,8,16,640]{3,2,1,0:T(8,128)(2,1)}), bf16[8,8,16,640]{3,2,1,0:T(8,128)(2,1)S(1)}, u32[]{:S(2)}, u32[]{:S(2)}) %all-to-all-start.3) | async-done | bytes 1310752 | tf_op jit(solution)/shard_map/all_to_all | solution.py:38
  113.5 2.2 copy-done.1
  115.7 10.3 %heads.1 = (bf16[4,128,1024]{2,1,0:T(8,128)(2,1)S(1)}, bf16[4,128,1024]{2,1,0:T(8,128)(2,1)}, bf16[1024,512]{1,0:T(8,128)(2,1)S(1)}, bf16[1024,128]{1,0:T(8,128)(2,1)S(1)}) custom-call(s32[4]{0:T(128)S(1)} %pad_add_fusion.info, bf16[8,2,1024,128]{3,2,1,0:T(8,128)(2,1)S(1)} %copy-done.1, bf16[4,2,8,16,640]{4,3,2,1,0:T(8,128)(2,1)S(1)} %bitcast.84), custom_call_target="tpu_custom_call" | custom-call | flops 4000000000 | bytes 9000000 | tf_op jit(solution)/shard_map/heads/pallas_call | solution.py:151
  126.7 4.4 %collective-permute-start = (bf16[4,128,1024]{2,1,0:T(8,128)(2,1)}, bf16[4,128,1024]{2,1,0:T(8,128)(2,1)S(1)}, u32[]{:S(2)}, u32[]{:S(2)}) collective-permute-start(bf16[4,128,1024]{2,1,0:T(8,128)(2,1)} %get-tuple-element.16), channel_id=1, source_target_pairs={{0,16},{16,0},{1,17},{17,1},{2,18},{18,2},{3,19},{19,3},{4,20},{20... | collective-permute-start | bytes 3145736 | tf_op jit(solution)/shard_map/ppermute | solution.py:400
  131.1 2.2 copy-done.2
  134.2 2.9 %weight_grads.1 = bf16[4,8,2,16,640]{4,3,2,1,0:T(8,128)(2,1)} custom-call(bf16[8,2,1024,128]{3,2,1,0:T(8,128)(2,1)S(1)} %copy-done.2, bf16[1024,512]{1,0:T(8,128)(2,1)S(1)} %get-tuple-element.13.d_z, bf16[1024,128]{1,0:T(8,128)(2,1)S(1)} %copy-done.6), custom_call_target="tpu_custom_call" | custom-call | flops 1350000000 | bytes 6800000 | tf_op jit(solution)/shard_map/weight_grads/pallas_call | solution.py:188
  138.1 4.4 %all-to-all-start.4 = ((bf16[64,16,640]{2,1,0:T(8,128)(2,1)}), bf16[64,16,640]{2,1,0:T(8,128)(2,1)S(1)}, u32[]{:S(2)}, u32[]{:S(2)}) async-start(bf16[64,16,640]{2,1,0:T(8,128)(2,1)} %bitcast.29), calls=%async_computation.4 | async-start | bytes 2621440 | tf_op jit(solution)/shard_map/all_to_all | solution.py:38
  142.6 3.3 %collective-permute-start.1 = (bf16[128,1024]{1,0:T(8,128)(2,1)}, bf16[128,1024]{1,0:T(8,128)(2,1)S(1)}, u32[]{:S(2)}, u32[]{:S(2)}) collective-permute-start(bf16[128,1024]{1,0:T(8,128)(2,1)} %copy-done.7), channel_id=1, source_target_pairs={{0,32},{32,64},{64,96},{96,0},{1,33},{33,65},{65,97},{97,1},{2,34}... | collective-permute-start | bytes 786440 | tf_op jit(solution)/shard_map/ppermute | solution.py:409
  145.9 4.3 %collective-permute-start.2 = (bf16[128,1024]{1,0:T(8,128)(2,1)S(1)}, bf16[128,1024]{1,0:T(8,128)(2,1)S(1)}, u32[]{:S(2)}, u32[]{:S(2)}) collective-permute-start(bf16[128,1024]{1,0:T(8,128)(2,1)S(1)} %get-tuple-element.20), channel_id=1, source_target_pairs={{0,64},{32,96},{64,0},{96,32},{1,65},{33,97},{65,1},{97,33},{2,66}... | collective-permute-start | bytes 786440 | tf_op jit(solution)/shard_map/ppermute | solution.py:409
  150.2 3.1 %collective-permute-start.3 = (bf16[128,1024]{1,0:T(8,128)(2,1)S(1)}, bf16[128,1024]{1,0:T(8,128)(2,1)S(1)}, u32[]{:S(2)}, u32[]{:S(2)}) collective-permute-start(bf16[128,1024]{1,0:T(8,128)(2,1)S(1)} %get-tuple-element.21), channel_id=1, source_target_pairs={{0,96},{32,0},{64,32},{96,64},{1,97},{33,1},{65,33},{97,65},{2,98}... | collective-permute-start | bytes 786440 | tf_op jit(solution)/shard_map/ppermute | solution.py:409
  154.3 11.8 %collective-permute-done.1.came_1 = bf16[128,1024]{1,0:T(8,128)(2,1)S(1)} collective-permute-done((bf16[128,1024]{1,0:T(8,128)(2,1)}, bf16[128,1024]{1,0:T(8,128)(2,1)S(1)}, u32[]{:S(2)}, u32[]{:S(2)}) %collective-permute-start.1) | collective-permute-done | bytes 262176 | tf_op jit(solution)/shard_map/ppermute | solution.py:409
  166.1 6.4 %collective-permute-done.2.came_2 = bf16[128,1024]{1,0:T(8,128)(2,1)S(1)} collective-permute-done((bf16[128,1024]{1,0:T(8,128)(2,1)S(1)}, bf16[128,1024]{1,0:T(8,128)(2,1)S(1)}, u32[]{:S(2)}, u32[]{:S(2)}) %collective-permute-start.2) | collective-permute-done | bytes 262176 | tf_op jit(solution)/shard_map/ppermute | solution.py:409
  173.6 11.1 %all-to-all-start.5 = ((bf16[16,112,128]{2,1,0:T(8,128)(2,1)}), bf16[16,112,128]{2,1,0:T(8,128)(2,1)S(1)}, u32[]{:S(2)}, u32[]{:S(2)}) async-start(bf16[16,112,128]{2,1,0:T(8,128)(2,1)} %payload.1), calls=%async_computation.5 | async-start | bytes 917504 | tf_op jit(solution)/shard_map/all_to_all | solution.py:38
  186.0 19.5 %all-to-all-done.5.merged = bf16[16,112,128]{2,1,0:T(8,128)(2,1)S(1)} async-done(((bf16[16,112,128]{2,1,0:T(8,128)(2,1)}), bf16[16,112,128]{2,1,0:T(8,128)(2,1)S(1)}, u32[]{:S(2)}, u32[]{:S(2)}) %all-to-all-start.5) | async-done | bytes 458784 | tf_op jit(solution)/shard_map/all_to_all | solution.py:38
  205.5 1.3 place.1
  206.7 11.7 %all-to-all-start.6 = ((bf16[32,80,128]{2,1,0:T(8,128)(2,1)}), bf16[32,80,128]{2,1,0:T(8,128)(2,1)S(1)}, u32[]{:S(2)}, u32[]{:S(2)}) async-start(bf16[32,80,128]{2,1,0:T(8,128)(2,1)} %place.1), calls=%async_computation.6 | async-start | bytes 1310720 | tf_op jit(solution)/shard_map/all_to_all | solution.py:38
  219.9 11.5 %all-to-all-done.6.owned = bf16[32,80,128]{2,1,0:T(8,128)(2,1)S(1)} async-done(((bf16[32,80,128]{2,1,0:T(8,128)(2,1)}), bf16[32,80,128]{2,1,0:T(8,128)(2,1)S(1)}, u32[]{:S(2)}, u32[]{:S(2)}) %all-to-all-start.6) | async-done | bytes 655392 | tf_op jit(solution)/shard_map/all_to_all | solution.py:38
  231.4 1.5 table_sum.1
  (86 shorter events, 14.1 us)
Async XLA Ops:
  7.2 13.4 %copy-start = (s32[8192]{0:T(1024)S(1)}, s32[8192]{0:T(1024)}, u32[]{:S(2)}) copy-start(s32[8192]{0:T(1024)} %param.11) | copy-start | bytes 98308
  7.2 13.1 %copy-start.10 = (s32[1,2,64]{2,1,0:T(2,128)S(1)}, s32[1,2,64]{2,1,0:T(2,128)}, u32[]{:S(2)}) copy-start(s32[1,2,64]{2,1,0:T(2,128)} %param.10) | copy-start | bytes 1540
  7.2 14.7 %copy-start.11 = (s32[1,2,3]{2,1,0:T(2,128)S(1)}, s32[1,2,3]{2,1,0:T(2,128)}, u32[]{:S(2)}) copy-start(s32[1,2,3]{2,1,0:T(2,128)} %param.9) | copy-start | bytes 76
  7.2 1.0 copy-start.3
  8.2 0.9 copy-start.4
  9.1 13.0 %copy-start.9 = (bf16[64,32]{0,1:T(8,128)(2,1)S(1)}, bf16[64,32]{0,1:T(8,128)(2,1)}, u32[]{:S(2)}) copy-start(bf16[64,32]{0,1:T(8,128)(2,1)} %param.13) | copy-start | bytes 12292
  9.1 13.1 %copy-start.8 = (bf16[32,256]{1,0:T(8,128)(2,1)S(1)}, bf16[32,256]{1,0:T(8,128)(2,1)}, u32[]{:S(2)}) copy-start(bf16[32,256]{1,0:T(8,128)(2,1)} %param.12) | copy-start | bytes 49156
  10.0 19.8 %all-to-all-start = ((bf16[8,2,2,64,128]{4,3,2,1,0:T(8,128)(2,1)}), bf16[8,2,2,64,128]{4,3,2,1,0:T(8,128)(2,1)S(1)}, u32[]{:S(2)}, u32[]{:S(2)}) async-start(bf16[8,2,2,64,128]{4,3,2,1,0:T(8,128)(2,1)} %split_columns.1), calls=%async_computation | async-start | bytes 1048576 | tf_op jit(solution)/shard_map/all_to_all | solution.py:38
  20.3 93.2 %all-gather.2.cloned.1.call-start = ((), (), s32[]{:S(2)}) async-start(), calls=%async_computation.7 | async-start | bytes 4718592 | tf_op jit(solution)/shard_map/all_gather | solution.py:374
  90.8 22.7 %all-to-all-start.3 = ((bf16[8,8,16,640]{3,2,1,0:T(8,128)(2,1)}), bf16[8,8,16,640]{3,2,1,0:T(8,128)(2,1)S(1)}, u32[]{:S(2)}, u32[]{:S(2)}) async-start(bf16[8,8,16,640]{3,2,1,0:T(8,128)(2,1)} %broadcast_in_dim.62), calls=%async_computation.3 | async-start | bytes 2621440 | tf_op jit(solution)/shard_map/all_to_all | solution.py:38
  113.5 2.2 copy-start.1
  126.0 0.7 copy-start.5
  126.7 10.5 %collective-permute-start = (bf16[4,128,1024]{2,1,0:T(8,128)(2,1)}, bf16[4,128,1024]{2,1,0:T(8,128)(2,1)S(1)}, u32[]{:S(2)}, u32[]{:S(2)}) collective-permute-start(bf16[4,128,1024]{2,1,0:T(8,128)(2,1)} %get-tuple-element.16), channel_id=1, source_target_pairs={{0,16},{16,0},{1,17},{17,1},{2,18},{18,2},{3,19},{19,3},{4,20},{20... | collective-permute-start | bytes 3145736 | tf_op jit(solution)/shard_map/ppermute | solution.py:400
  131.1 2.2 copy-start.2
  133.3 0.9 copy-start.6
  137.4 0.7 copy-start.7
  138.1 34.3 %all-to-all-start.4 = ((bf16[64,16,640]{2,1,0:T(8,128)(2,1)}), bf16[64,16,640]{2,1,0:T(8,128)(2,1)S(1)}, u32[]{:S(2)}, u32[]{:S(2)}) async-start(bf16[64,16,640]{2,1,0:T(8,128)(2,1)} %bitcast.29), calls=%async_computation.4 | async-start | bytes 2621440 | tf_op jit(solution)/shard_map/all_to_all | solution.py:38
  142.6 23.5 %collective-permute-start.1 = (bf16[128,1024]{1,0:T(8,128)(2,1)}, bf16[128,1024]{1,0:T(8,128)(2,1)S(1)}, u32[]{:S(2)}, u32[]{:S(2)}) collective-permute-start(bf16[128,1024]{1,0:T(8,128)(2,1)} %copy-done.7), channel_id=1, source_target_pairs={{0,32},{32,64},{64,96},{96,0},{1,33},{33,65},{65,97},{97,1},{2,34}... | collective-permute-start | bytes 786440 | tf_op jit(solution)/shard_map/ppermute | solution.py:409
  145.9 26.6 %collective-permute-start.2 = (bf16[128,1024]{1,0:T(8,128)(2,1)S(1)}, bf16[128,1024]{1,0:T(8,128)(2,1)S(1)}, u32[]{:S(2)}, u32[]{:S(2)}) collective-permute-start(bf16[128,1024]{1,0:T(8,128)(2,1)S(1)} %get-tuple-element.20), channel_id=1, source_target_pairs={{0,64},{32,96},{64,0},{96,32},{1,65},{33,97},{65,1},{97,33},{2,66}... | collective-permute-start | bytes 786440 | tf_op jit(solution)/shard_map/ppermute | solution.py:409
  150.2 22.3 %collective-permute-start.3 = (bf16[128,1024]{1,0:T(8,128)(2,1)S(1)}, bf16[128,1024]{1,0:T(8,128)(2,1)S(1)}, u32[]{:S(2)}, u32[]{:S(2)}) collective-permute-start(bf16[128,1024]{1,0:T(8,128)(2,1)S(1)} %get-tuple-element.21), channel_id=1, source_target_pairs={{0,96},{32,0},{64,32},{96,64},{1,97},{33,1},{65,33},{97,65},{2,98}... | collective-permute-start | bytes 786440 | tf_op jit(solution)/shard_map/ppermute | solution.py:409
  173.6 31.8 %all-to-all-start.5 = ((bf16[16,112,128]{2,1,0:T(8,128)(2,1)}), bf16[16,112,128]{2,1,0:T(8,128)(2,1)S(1)}, u32[]{:S(2)}, u32[]{:S(2)}) async-start(bf16[16,112,128]{2,1,0:T(8,128)(2,1)} %payload.1), calls=%async_computation.5 | async-start | bytes 917504 | tf_op jit(solution)/shard_map/all_to_all | solution.py:38
  206.7 24.7 %all-to-all-start.6 = ((bf16[32,80,128]{2,1,0:T(8,128)(2,1)}), bf16[32,80,128]{2,1,0:T(8,128)(2,1)S(1)}, u32[]{:S(2)}, u32[]{:S(2)}) async-start(bf16[32,80,128]{2,1,0:T(8,128)(2,1)} %place.1), calls=%async_computation.6 | async-start | bytes 1310720 | tf_op jit(solution)/shard_map/all_to_all | solution.py:38
Sparse Core Ops, SparseCore 0:
  75.4 37.4 all-gather.1

commit v6 on v5

--- a/solution.py
+++ b/solution.py
@@ -31,6 +31,8 @@
 STEP = 256
 REACH = 512
 VMEM_SPEC = pl.BlockSpec(memory_space=pltpu.VMEM)
+GRANT = 58
+HBM_SPEC = pl.BlockSpec(memory_space=pltpu.HBM)
 SMEM_SPEC = pl.BlockSpec(memory_space=pltpu.SMEM)
 
 
@@ -56,30 +58,69 @@
     return lax.dot_general(a, b, (((0,), (0,)), ((), ())), preferred_element_type=F32)
 
 
-def heads_kernel(info, packs, w_in, kept, sent, d_z, gated, w, acts, slope, d_value, d_key):
+def heads_kernel(
+    info,
+    packs,
+    weights,
+    kept,
+    sent,
+    grads,
+    x_v,
+    dy_v,
+    w_v,
+    acts,
+    slope,
+    d_value,
+    d_key,
+    d_z,
+    gated,
+    kept_v,
+    sent_v,
+    grads_v,
+    sems,
+    w_sems,
+    out_sems,
+):
     hd = HEAD_DIM
     scale = hd**-0.5
     u_cols, v_cols, q_cols, k_cols = (slice(m * hd, (m + 1) * hd) for m in range(4))
-    for x in range(X):
-        for yc in range(YC):
-            start = (x * YC + yc) * 32
-            w[start : start + 32, :] = w_in[x, :, yc].reshape(32, HIDDEN)
+    steps = LENGTH // STEP
+    copies = [
+        pltpu.make_async_copy(
+            packs.at[:, t, pl.ds(n * STEP, STEP)],
+            held.at[:, pl.ds(n * STEP, STEP)],
+            sems.at[t * steps + n],
+        )
+        for t, held in enumerate((x_v, dy_v))
+        for n in range(steps)
+    ]
+    w_copies = [
+        pltpu.make_async_copy(weights.at[x, r], w_v.at[x, :, r], w_sems.at[x * ZR + r])
+        for x in range(X)
+        for r in range(ZR)
+    ]
+    for copy in copies[:1] + w_copies + copies[1:]:
+        copy.start()
     d_value[...] = jnp.zeros_like(d_value)
     d_key[...] = jnp.zeros_like(d_key)
 
-    def project(step, carry):
-        rows = pl.ds(pl.multiple_of(step * STEP, STEP), STEP)
-        px = jnp.concatenate([packs[g, 0, rows, :] for g in range(8)], axis=1)
-        z_pre = jnp.dot(px, w[:, : 4 * hd], preferred_element_type=F32)
+    for copy in w_copies:
+        copy.wait()
+    wp = w_v[..., : 4 * hd].reshape(WIDTH, 4 * hd)
+    wo = w_v[..., 4 * hd :].reshape(WIDTH, hd)
+
+    for step in range(steps):
+        copies[step].wait()
+        rows = slice(step * STEP, (step + 1) * STEP)
+        px = jnp.concatenate([x_v[g, rows, :] for g in range(8)], axis=1)
+        z_pre = jnp.dot(px, wp, preferred_element_type=F32)
         sigma = jax.nn.sigmoid(z_pre)
         silu = z_pre * sigma
         acts[rows, :] = silu.astype(BF16)
         slope[rows, :] = sigma + silu * (1.0 - sigma)
-        return carry
-
-    lax.fori_loop(0, LENGTH // STEP, project, 0)
-
-    for step in range(LENGTH // STEP):
+
+    for step in range(steps):
+        copies[steps + step].wait()
         base = step * STEP
         first = max(0, base - REACH)
         rows = slice(base, base + STEP)
@@ -104,8 +145,8 @@
         normed = centred * inv_std
         gating = acts[rows, u_cols].astype(F32)
         gated[rows, :] = (normed * gating).astype(BF16)
-        pdy = jnp.concatenate([packs[g, 1, rows, :] for g in range(8)], axis=1)
-        d_gated = jnp.dot(pdy, w[:, 4 * hd :], preferred_element_type=F32)
+        pdy = jnp.concatenate([dy_v[g, rows, :] for g in range(8)], axis=1)
+        d_gated = jnp.dot(pdy, wo, preferred_element_type=F32)
         d_normed = d_gated * gating
         d_mixed = (
             inv_std
@@ -126,24 +167,33 @@
     d_z[:, k_cols] = (d_key[...] * slope[:, k_cols]).astype(BF16)
 
     core = info[3]
-
-    def parts(step, carry):
-        rows = pl.ds(pl.multiple_of(step * STEP, STEP), STEP)
-        part = dot_nt(d_z[rows, :], w[:, : 4 * hd]).astype(BF16)
+    outs = []
+    for y in range(Y):
+        part = dot_nt(d_z[y * STEP : (y + 1) * STEP, :], wp).astype(BF16)
 
         @pl.when(core == 0)
         def _():
-            kept[step] = part[:LANES]
-            sent[step] = part[LANES:]
+            kept_v[y] = part[:LANES]
+            sent_v[y] = part[LANES:]
 
         @pl.when(core != 0)
         def _():
-            kept[step] = part[LANES:]
-            sent[step] = part[:LANES]
-
-        return carry
-
-    lax.fori_loop(0, Y, parts, 0)
+            kept_v[y] = part[LANES:]
+            sent_v[y] = part[:LANES]
+
+        for held, out in ((sent_v, sent), (kept_v, kept)):
+            outs.append(pltpu.make_async_copy(held.at[y], out.at[y], out_sems.at[len(outs)]))
+            outs[-1].start()
+
+    for x in range(X):
+        for dest, source, pack in ((slice(0, 512), d_z, x_v), (slice(512, 640), gated, dy_v)):
+            columns = jnp.concatenate([pack[2 * x], pack[2 * x + 1]], axis=1)
+            block = dot_tn(columns, source[...]).astype(BF16)
+            grads_v[x, :, :, :, dest] = block.reshape(YC, ZR, PART_ROWS, block.shape[1])
+        outs.append(pltpu.make_async_copy(grads_v.at[x], grads.at[x], out_sems.at[len(outs)]))
+        outs[-1].start()
+    for copy in outs:
+        copy.wait()
 
 
 def heads_backward(info, packs, weights):
@@ -153,49 +203,33 @@
         out_shape=(
             half,
             half,
-            jax.ShapeDtypeStruct((LENGTH, 4 * HEAD_DIM), BF16),
-            jax.ShapeDtypeStruct((LENGTH, HEAD_DIM), BF16),
+            jax.ShapeDtypeStruct((X, YC, ZR, PART_ROWS, HIDDEN), BF16),
         ),
-        in_specs=[SMEM_SPEC, VMEM_SPEC, VMEM_SPEC],
-        out_specs=(VMEM_SPEC,) * 4,
+        in_specs=[SMEM_SPEC, HBM_SPEC, HBM_SPEC],
+        out_specs=(HBM_SPEC,) * 3,
         scratch_shapes=[
-            pltpu.VMEM((WIDTH, HIDDEN), BF16),
+            pltpu.VMEM((8, LENGTH, LANES), BF16),
+            pltpu.VMEM((8, LENGTH, LANES), BF16),
+            pltpu.VMEM((X, YC, ZR, PART_ROWS, HIDDEN), BF16),
             pltpu.VMEM((LENGTH, 4 * HEAD_DIM), BF16),
             pltpu.VMEM((LENGTH, 4 * HEAD_DIM), F32),
             pltpu.VMEM((LENGTH, HEAD_DIM), F32),
             pltpu.VMEM((LENGTH, HEAD_DIM), F32),
+            pltpu.VMEM((LENGTH, 4 * HEAD_DIM), BF16),
+            pltpu.VMEM((LENGTH, HEAD_DIM), BF16),
+            pltpu.VMEM((Y, LANES, WIDTH), BF16),
+            pltpu.VMEM((Y, LANES, WIDTH), BF16),
+            pltpu.VMEM((X, YC, ZR, PART_ROWS, HIDDEN), BF16),
+            pltpu.SemaphoreType.DMA((2 * LENGTH // STEP,)),
+            pltpu.SemaphoreType.DMA((X * ZR,)),
+            pltpu.SemaphoreType.DMA((2 * Y + X,)),
         ],
-        compiler_params=pltpu.CompilerParams(vmem_limit_bytes=44 * 2**20),
+        compiler_params=pltpu.CompilerParams(vmem_limit_bytes=GRANT * 2**20),
         cost_estimate=pl.CostEstimate(
-            flops=4_000_000_000, bytes_accessed=9_000_000, transcendentals=2_000_000
+            flops=5_000_000_000, bytes_accessed=9_000_000, transcendentals=2_000_000
         ),
         name="heads",
     )(info, packs, weights)
-
-
-def grads_kernel(packs, d_z, gated, out):
-    for x in range(X):
-        for dest, source, t in ((slice(0, 512), d_z, 0), (slice(512, 640), gated, 1)):
-            columns = jnp.concatenate([packs[2 * x, t], packs[2 * x + 1, t]], axis=1)
-            block = dot_tn(columns, source[...]).astype(BF16)
-            for yc in range(YC):
-                for r in range(ZR):
-                    at = yc * 32 + r * PART_ROWS
-                    out[x, yc, r, :, dest] = block[at : at + PART_ROWS]
-
-
-def weight_grads(packs, d_z, gated):
-    return pl.pallas_call(
-        grads_kernel,
-        out_shape=jax.ShapeDtypeStruct((X, YC, ZR, PART_ROWS, HIDDEN), BF16),
-        in_specs=[VMEM_SPEC] * 3,
-        out_specs=VMEM_SPEC,
-        compiler_params=pltpu.CompilerParams(vmem_limit_bytes=32 * 2**20),
-        cost_estimate=pl.CostEstimate(
-            flops=1_350_000_000, bytes_accessed=6_800_000, transcendentals=0
-        ),
-        name="weight_grads",
-    )(packs, d_z, gated)
 
 
 def pair_kernel(place, kept, got, own, *to_y):
@@ -327,19 +361,27 @@
     )(owned)
 
 
-def split_kernel(inputs, cotangent, out):
-    for g in range(8):
-        for p in range(2):
-            for t, source in enumerate((inputs, cotangent)):
-                out[g, p, t] = source[p, :, g * LANES : (g + 1) * LANES]
+def split_kernel(inputs, cotangent, out, sems):
+    copies = [
+        pltpu.make_async_copy(
+            source.at[:, :, pl.ds(g * LANES, LANES)], out.at[g, :, t], sems.at[2 * g + t]
+        )
+        for g in range(8)
+        for t, source in enumerate((inputs, cotangent))
+    ]
+    for copy in copies:
+        copy.start()
+    for copy in copies:
+        copy.wait()
 
 
 def split_columns(inputs, cotangent):
     return pl.pallas_call(
         split_kernel,
         out_shape=jax.ShapeDtypeStruct((8, 2, 2, 64, LANES), BF16),
-        in_specs=[VMEM_SPEC] * 2,
-        out_specs=VMEM_SPEC,
+        in_specs=[HBM_SPEC] * 2,
+        out_specs=HBM_SPEC,
+        scratch_shapes=[pltpu.SemaphoreType.DMA((16,))],
         compiler_params=pltpu.CompilerParams(vmem_limit_bytes=32 * 2**20),
         cost_estimate=pl.CostEstimate(flops=0, bytes_accessed=1_000_000, transcendentals=0),
         name="split_columns",
@@ -396,15 +438,13 @@
     tags = tags.reshape(YC, 2, OWNERS, CAP).transpose(2, 1, 0, 3).reshape(OWNERS, 1, LANES)
     tags = jnp.broadcast_to(tags.astype(BF16), (OWNERS, 16, LANES))
 
-    kept, sent, d_z, gated = heads_backward(info, packs, weights)
-    got = lax.ppermute(sent, "c", [(0, 1), (1, 0)])
-
-    grads = weight_grads(packs, d_z, gated)
-    own, *to_y = pair_sums(y_here[None].astype(jnp.int32), kept, got)
-    grads, own = lax.optimization_barrier((grads, own))
+    kept, sent, grads = heads_backward(info, packs, weights)
 
     shared = exchange(grads.reshape(X * YC * ZR, PART_ROWS, HIDDEN), SPREAD)
     shared = shared.reshape(X, YC, ZR, PART_ROWS, HIDDEN)
+
+    got = lax.ppermute(sent, "c", [(0, 1), (1, 0)])
+    own, *to_y = pair_sums(y_here[None].astype(jnp.int32), kept, got)
     came = [
         lax.ppermute(to_y[step - 1], "y", [(i, (i + step) % Y) for i in range(Y)])
         for step in range(1, Y)

time: 241 us -> 234 us (0.971)
  local copies, waits for them, and re-layouts: 15.8 us -> 12 us
  waiting for transfers between devices: 73 us -> 69.2 us
    ppermute x3, waiting for transfers between devices: 18.2 us -> 12.4 us  [per_device(): lax.ppermute(to_y[step - 1], 'y', [(i, (i + step) % Y) for i in range(Y)])]
    pallas_call x1, Pallas kernels: 10.3 us -> 14.7 us  [heads_backward(): pl.pallas_call(heads_kernel, out_shape=(half, half, jax.ShapeDtypeStruct(...]
    unnamed x25 -> x23, local copies, waits for them, and re-layouts: 9.28 us -> 5.43 us
    pallas_call x1 -> x0, Pallas kernels: 2.95 us -> none  [weight_grads(): pl.pallas_call(grads_kernel, out_shape=jax.ShapeDtypeStruct((X, YC, ZR, P...]
    ppermute x1, waiting for transfers between devices: 0.01 us -> 2.47 us  [per_device(): got = lax.ppermute(sent, 'c', [(0, 1), (1, 0)])]
  transfers between devices with their start and end apart: 10 -> 10, of which waited for: 6 -> 7; matrix products, arithmetic and copies ran while one was open for 3% -> 4% of each run, Pallas kernels for 1% -> 0%
where the time goes in v6:
time: 234 us; the launch traced here: 233 us
  waiting for transfers between devices  69.2 us (30%)
  blocking collectives  58.4 us (25%)
  starting transfers between devices  56.6 us (24%)
  Pallas kernels  20.6 us (9%)
  between operations  14.4 us (6%)
  local copies, waits for them, and re-layouts  12 us (5%)
    all_to_all x2, blocking collectives, exchange(): return lax.all_to_all(value, axes, split_axis=0, concat_axis=0, tiled=True)  58.4 us
    all_to_all x5, waiting for transfers between devices, exchange(): return lax.all_to_all(value, axes, split_axis=0, concat_axis=0, tiled=True)  54.3 us
    all_to_all x5, starting transfers between devices, exchange(): return lax.all_to_all(value, axes, split_axis=0, concat_axis=0, tiled=True)  43.6 us
    pallas_call x1, Pallas kernels, heads_backward(): pl.pallas_call(heads_kernel, out_shape=(half, half, jax.ShapeDtypeStruct(...  14.7 us
    ppermute x3, waiting for transfers between devices, per_device(): lax.ppermute(to_y[step - 1], 'y', [(i, (i + step) % Y) for i in range(Y)])  12.4 us
    ppermute x3, starting transfers between devices, per_device(): lax.ppermute(to_y[step - 1], 'y', [(i, (i + step) % Y) for i in range(Y)])  10.5 us
    unnamed x23, local copies, waits for them, and re-layouts  5.43 us
  transfers between devices with their start and end apart: 10, of which 7 were waited for; matrix products, arithmetic and copies ran while one was open for 4% of the time, Pallas kernels for 0%

profile of v6, /device:TPU:1, one launch (start us, length us, event | category | flops | bytes accessed | tf_op | source)
XLA Modules:
  0.0 233.2 jit_solution(7874907890182164450)
XLA Ops:
  10.1 10.3 %all-to-all-start = ((bf16[8,2,2,64,128]{4,3,2,1,0:T(8,128)(2,1)}), bf16[8,2,2,64,128]{4,3,2,1,0:T(8,128)(2,1)S(1)}, u32[]{:S(2)}, u32[]{:S(2)}) async-start(bf16[8,2,2,64,128]{4,3,2,1,0:T(8,128)(2,1)} %split_columns.1), calls=%async_computation | async-start | bytes 1048576 | tf_op jit(solution)/shard_map/all_to_all | solution.py:40
  20.6 1.1 gather_fusion
  22.3 7.5 %all-to-all-done = bf16[8,2,2,64,128]{4,3,2,1,0:T(8,128)(2,1)S(1)} async-done(((bf16[8,2,2,64,128]{4,3,2,1,0:T(8,128)(2,1)}), bf16[8,2,2,64,128]{4,3,2,1,0:T(8,128)(2,1)S(1)}, u32[]{:S(2)}, u32[]{:S(2)}) %all-to-all-start) | async-done | bytes 524320 | tf_op jit(solution)/shard_map/all_to_all | solution.py:40
  30.0 44.5 %all_to_all.35 = bf16[16,22,8,128]{3,2,1,0:T(8,128)(2,1)S(1)} all-to-all(bf16[16,22,8,128]{3,2,1,0:T(8,128)(2,1)S(1)} %pad_maximum_fusion), channel_id=1, replica_groups=mesh['x'=4,'y'=4,'c'=2,'zq'=8,'zr'=2] {'zq','zr'}, dimensions={0} | all-to-all | bytes 1441792 | tf_op jit(solution)/shard_map/all_to_all | solution.py:40
  75.4 13.9 %all_to_all.36 = bf16[8,2,6,8,128]{4,3,2,1,0:T(8,128)(2,1)S(1)} all-to-all(bf16[8,2,6,8,128]{4,3,2,1,0:T(8,128)(2,1)S(1)} %bitcast.93), channel_id=1, replica_groups=mesh['x'=4,'y'=4,'c'=2,'zq'=8,'zr'=2] {'y','c'}, dimensions={0} | all-to-all | bytes 393216 | tf_op jit(solution)/shard_map/all_to_all | solution.py:40
  89.7 1.2 broadcast_in_dim.63
  90.9 5.6 %all-to-all-start.3 = ((bf16[8,8,16,640]{3,2,1,0:T(8,128)(2,1)}), bf16[8,8,16,640]{3,2,1,0:T(8,128)(2,1)S(1)}, u32[]{:S(2)}, u32[]{:S(2)}) async-start(bf16[8,8,16,640]{3,2,1,0:T(8,128)(2,1)} %broadcast_in_dim.63), calls=%async_computation.3 | async-start | bytes 2621440 | tf_op jit(solution)/shard_map/all_to_all | solution.py:40
  97.8 15.8 %all-to-all-done.3 = bf16[8,8,16,640]{3,2,1,0:T(8,128)(2,1)S(1)} async-done(((bf16[8,8,16,640]{3,2,1,0:T(8,128)(2,1)}), bf16[8,8,16,640]{3,2,1,0:T(8,128)(2,1)S(1)}, u32[]{:S(2)}, u32[]{:S(2)}) %all-to-all-start.3) | async-done | bytes 1310752 | tf_op jit(solution)/shard_map/all_to_all | solution.py:40
  114.6 14.7 %heads.1 = (bf16[4,128,1024]{2,1,0:T(8,128)(2,1)}, bf16[4,128,1024]{2,1,0:T(8,128)(2,1)}, bf16[4,8,2,16,640]{4,3,2,1,0:T(8,128)(2,1)}) custom-call(s32[4]{0:T(128)} %pad_add_fusion.info, bf16[8,2,1024,128]{3,2,1,0:T(8,128)(2,1)} %all-gather.2.cloned.1.call-done.packs, bf16[4,2,8,16,640]{4,3,2,1,0:T(8,128)(2,1)} %bitcast.92), custom_call_target="tpu_custom_call" | custom-call | flops 5000000000 | bytes 9000000 | tf_op jit(solution)/shard_map/heads/pallas_call | solution.py:201
  129.4 6.9 %all-to-all-start.4 = ((bf16[64,16,640]{2,1,0:T(8,128)(2,1)}), bf16[64,16,640]{2,1,0:T(8,128)(2,1)S(1)}, u32[]{:S(2)}, u32[]{:S(2)}) async-start(bf16[64,16,640]{2,1,0:T(8,128)(2,1)} %bitcast.91), calls=%async_computation.4 | async-start | bytes 2621440 | tf_op jit(solution)/shard_map/all_to_all | solution.py:40
  136.3 2.5 %collective-permute-start = (bf16[4,128,1024]{2,1,0:T(8,128)(2,1)}, bf16[4,128,1024]{2,1,0:T(8,128)(2,1)S(1)}, u32[]{:S(2)}, u32[]{:S(2)}) collective-permute-start(bf16[4,128,1024]{2,1,0:T(8,128)(2,1)} %get-tuple-element.11), channel_id=1, source_target_pairs={{0,16},{16,0},{1,17},{17,1},{2,18},{18,2},{3,19},{19,3},{4,20},{20... | collective-permute-start | bytes 3145736 | tf_op jit(solution)/shard_map/ppermute | solution.py:446
  138.8 2.5 %collective-permute-done.got = bf16[4,128,1024]{2,1,0:T(8,128)(2,1)S(1)} collective-permute-done((bf16[4,128,1024]{2,1,0:T(8,128)(2,1)}, bf16[4,128,1024]{2,1,0:T(8,128)(2,1)S(1)}, u32[]{:S(2)}, u32[]{:S(2)}) %collective-permute-start) | collective-permute-done | bytes 1048608 | tf_op jit(solution)/shard_map/ppermute | solution.py:446
  143.0 3.1 %collective-permute-start.1 = (bf16[128,1024]{1,0:T(8,128)(2,1)}, bf16[128,1024]{1,0:T(8,128)(2,1)S(1)}, u32[]{:S(2)}, u32[]{:S(2)}) collective-permute-start(bf16[128,1024]{1,0:T(8,128)(2,1)} %get-tuple-element.13), channel_id=1, source_target_pairs={{0,32},{32,64},{64,96},{96,0},{1,33},{33,65},{65,97},{97,1},{2,34}... | collective-permute-start | bytes 786440 | tf_op jit(solution)/shard_map/ppermute | solution.py:449
  146.1 4.4 %collective-permute-start.2 = (bf16[128,1024]{1,0:T(8,128)(2,1)}, bf16[128,1024]{1,0:T(8,128)(2,1)S(1)}, u32[]{:S(2)}, u32[]{:S(2)}) collective-permute-start(bf16[128,1024]{1,0:T(8,128)(2,1)} %get-tuple-element.14), channel_id=1, source_target_pairs={{0,64},{32,96},{64,0},{96,32},{1,65},{33,97},{65,1},{97,33},{2,66}... | collective-permute-start | bytes 786440 | tf_op jit(solution)/shard_map/ppermute | solution.py:449
  150.5 3.1 %collective-permute-start.3 = (bf16[128,1024]{1,0:T(8,128)(2,1)}, bf16[128,1024]{1,0:T(8,128)(2,1)S(1)}, u32[]{:S(2)}, u32[]{:S(2)}) collective-permute-start(bf16[128,1024]{1,0:T(8,128)(2,1)} %get-tuple-element.15), channel_id=1, source_target_pairs={{0,96},{32,0},{64,32},{96,64},{1,97},{33,1},{65,33},{97,65},{2,98}... | collective-permute-start | bytes 786440 | tf_op jit(solution)/shard_map/ppermute | solution.py:449
  154.6 6.1 %collective-permute-done.1.came_1 = bf16[128,1024]{1,0:T(8,128)(2,1)S(1)} collective-permute-done((bf16[128,1024]{1,0:T(8,128)(2,1)}, bf16[128,1024]{1,0:T(8,128)(2,1)S(1)}, u32[]{:S(2)}, u32[]{:S(2)}) %collective-permute-start.1) | collective-permute-done | bytes 262176 | tf_op jit(solution)/shard_map/ppermute | solution.py:449
  160.7 6.3 %collective-permute-done.2.came_2 = bf16[128,1024]{1,0:T(8,128)(2,1)S(1)} collective-permute-done((bf16[128,1024]{1,0:T(8,128)(2,1)}, bf16[128,1024]{1,0:T(8,128)(2,1)S(1)}, u32[]{:S(2)}, u32[]{:S(2)}) %collective-permute-start.2) | collective-permute-done | bytes 262176 | tf_op jit(solution)/shard_map/ppermute | solution.py:449
  168.0 1.1 payload.1
  169.2 9.8 %all-to-all-start.5 = ((bf16[16,112,128]{2,1,0:T(8,128)(2,1)}), bf16[16,112,128]{2,1,0:T(8,128)(2,1)S(1)}, u32[]{:S(2)}, u32[]{:S(2)}) async-start(bf16[16,112,128]{2,1,0:T(8,128)(2,1)} %payload.1), calls=%async_computation.5 | async-start | bytes 917504 | tf_op jit(solution)/shard_map/all_to_all | solution.py:40
  180.3 19.5 %all-to-all-done.5.merged = bf16[16,112,128]{2,1,0:T(8,128)(2,1)S(1)} async-done(((bf16[16,112,128]{2,1,0:T(8,128)(2,1)}), bf16[16,112,128]{2,1,0:T(8,128)(2,1)S(1)}, u32[]{:S(2)}, u32[]{:S(2)}) %all-to-all-start.5) | async-done | bytes 458784 | tf_op jit(solution)/shard_map/all_to_all | solution.py:40
  199.8 1.3 place.1
  201.0 10.9 %all-to-all-start.6 = ((bf16[32,80,128]{2,1,0:T(8,128)(2,1)}), bf16[32,80,128]{2,1,0:T(8,128)(2,1)S(1)}, u32[]{:S(2)}, u32[]{:S(2)}) async-start(bf16[32,80,128]{2,1,0:T(8,128)(2,1)} %place.1), calls=%async_computation.6 | async-start | bytes 1310720 | tf_op jit(solution)/shard_map/all_to_all | solution.py:40
  213.4 11.5 %all-to-all-done.6.owned = bf16[32,80,128]{2,1,0:T(8,128)(2,1)S(1)} async-done(((bf16[32,80,128]{2,1,0:T(8,128)(2,1)}), bf16[32,80,128]{2,1,0:T(8,128)(2,1)S(1)}, u32[]{:S(2)}, u32[]{:S(2)}) %all-to-all-start.6) | async-done | bytes 655392 | tf_op jit(solution)/shard_map/all_to_all | solution.py:40
  224.9 1.5 table_sum.1
  (83 shorter events, 13.7 us)
Async XLA Ops:
  7.2 13.5 %copy-start = (s32[8192]{0:T(1024)S(1)}, s32[8192]{0:T(1024)}, u32[]{:S(2)}) copy-start(s32[8192]{0:T(1024)} %param.11) | copy-start | bytes 98308
  7.2 13.2 %copy-start.9 = (s32[1,2,64]{2,1,0:T(2,128)S(1)}, s32[1,2,64]{2,1,0:T(2,128)}, u32[]{:S(2)}) copy-start(s32[1,2,64]{2,1,0:T(2,128)} %param.10) | copy-start | bytes 1540
  7.2 14.8 %copy-start.10 = (s32[1,2,3]{2,1,0:T(2,128)S(1)}, s32[1,2,3]{2,1,0:T(2,128)}, u32[]{:S(2)}) copy-start(s32[1,2,3]{2,1,0:T(2,128)} %param.9) | copy-start | bytes 76
  7.2 1.0 copy-start.4
  8.2 0.9 copy-start.5
  9.1 13.1 %copy-start.8 = (bf16[64,32]{0,1:T(8,128)(2,1)S(1)}, bf16[64,32]{0,1:T(8,128)(2,1)}, u32[]{:S(2)}) copy-start(bf16[64,32]{0,1:T(8,128)(2,1)} %param.13) | copy-start | bytes 12292
  9.1 13.2 %copy-start.7 = (bf16[32,256]{1,0:T(8,128)(2,1)S(1)}, bf16[32,256]{1,0:T(8,128)(2,1)}, u32[]{:S(2)}) copy-start(bf16[32,256]{1,0:T(8,128)(2,1)} %param.12) | copy-start | bytes 49156
  10.1 19.8 %all-to-all-start = ((bf16[8,2,2,64,128]{4,3,2,1,0:T(8,128)(2,1)}), bf16[8,2,2,64,128]{4,3,2,1,0:T(8,128)(2,1)S(1)}, u32[]{:S(2)}, u32[]{:S(2)}) async-start(bf16[8,2,2,64,128]{4,3,2,1,0:T(8,128)(2,1)} %split_columns.1), calls=%async_computation | async-start | bytes 1048576 | tf_op jit(solution)/shard_map/all_to_all | solution.py:40
  20.4 93.2 %all-gather.2.cloned.1.call-start = ((), (), s32[]{:S(2)}) async-start(), calls=%async_computation.7 | async-start | bytes 4718592 | tf_op jit(solution)/shard_map/all_gather | solution.py:416
  90.9 22.7 %all-to-all-start.3 = ((bf16[8,8,16,640]{3,2,1,0:T(8,128)(2,1)}), bf16[8,8,16,640]{3,2,1,0:T(8,128)(2,1)S(1)}, u32[]{:S(2)}, u32[]{:S(2)}) async-start(bf16[8,8,16,640]{3,2,1,0:T(8,128)(2,1)} %broadcast_in_dim.63), calls=%async_computation.3 | async-start | bytes 2621440 | tf_op jit(solution)/shard_map/all_to_all | solution.py:40
  113.6 1.1 copy-start.6
  129.4 11.8 %copy-start.1 = (bf16[4,128,1024]{2,1,0:T(8,128)(2,1)S(1)}, bf16[4,128,1024]{2,1,0:T(8,128)(2,1)}, u32[]{:S(2)}) copy-start(bf16[4,128,1024]{2,1,0:T(8,128)(2,1)} %get-tuple-element.10.kept) | copy-start | bytes 3145732
  129.4 37.6 %all-to-all-start.4 = ((bf16[64,16,640]{2,1,0:T(8,128)(2,1)}), bf16[64,16,640]{2,1,0:T(8,128)(2,1)S(1)}, u32[]{:S(2)}, u32[]{:S(2)}) async-start(bf16[64,16,640]{2,1,0:T(8,128)(2,1)} %bitcast.91), calls=%async_computation.4 | async-start | bytes 2621440 | tf_op jit(solution)/shard_map/all_to_all | solution.py:40
  136.3 5.0 %collective-permute-start = (bf16[4,128,1024]{2,1,0:T(8,128)(2,1)}, bf16[4,128,1024]{2,1,0:T(8,128)(2,1)S(1)}, u32[]{:S(2)}, u32[]{:S(2)}) collective-permute-start(bf16[4,128,1024]{2,1,0:T(8,128)(2,1)} %get-tuple-element.11), channel_id=1, source_target_pairs={{0,16},{16,0},{1,17},{17,1},{2,18},{18,2},{3,19},{19,3},{4,20},{20... | collective-permute-start | bytes 3145736 | tf_op jit(solution)/shard_map/ppermute | solution.py:446
  142.2 0.8 copy-start.2
  143.0 17.7 %collective-permute-start.1 = (bf16[128,1024]{1,0:T(8,128)(2,1)}, bf16[128,1024]{1,0:T(8,128)(2,1)S(1)}, u32[]{:S(2)}, u32[]{:S(2)}) collective-permute-start(bf16[128,1024]{1,0:T(8,128)(2,1)} %get-tuple-element.13), channel_id=1, source_target_pairs={{0,32},{32,64},{64,96},{96,0},{1,33},{33,65},{65,97},{97,1},{2,34}... | collective-permute-start | bytes 786440 | tf_op jit(solution)/shard_map/ppermute | solution.py:449
  146.1 20.9 %collective-permute-start.2 = (bf16[128,1024]{1,0:T(8,128)(2,1)}, bf16[128,1024]{1,0:T(8,128)(2,1)S(1)}, u32[]{:S(2)}, u32[]{:S(2)}) collective-permute-start(bf16[128,1024]{1,0:T(8,128)(2,1)} %get-tuple-element.14), channel_id=1, source_target_pairs={{0,64},{32,96},{64,0},{96,32},{1,65},{33,97},{65,1},{97,33},{2,66}... | collective-permute-start | bytes 786440 | tf_op jit(solution)/shard_map/ppermute | solution.py:449
  150.5 16.5 %collective-permute-start.3 = (bf16[128,1024]{1,0:T(8,128)(2,1)}, bf16[128,1024]{1,0:T(8,128)(2,1)S(1)}, u32[]{:S(2)}, u32[]{:S(2)}) collective-permute-start(bf16[128,1024]{1,0:T(8,128)(2,1)} %get-tuple-element.15), channel_id=1, source_target_pairs={{0,96},{32,0},{64,32},{96,64},{1,97},{33,1},{65,33},{97,65},{2,98}... | collective-permute-start | bytes 786440 | tf_op jit(solution)/shard_map/ppermute | solution.py:449
  167.0 1.0 copy-start.3
  169.2 30.6 %all-to-all-start.5 = ((bf16[16,112,128]{2,1,0:T(8,128)(2,1)}), bf16[16,112,128]{2,1,0:T(8,128)(2,1)S(1)}, u32[]{:S(2)}, u32[]{:S(2)}) async-start(bf16[16,112,128]{2,1,0:T(8,128)(2,1)} %payload.1), calls=%async_computation.5 | async-start | bytes 917504 | tf_op jit(solution)/shard_map/all_to_all | solution.py:40
  201.0 23.9 %all-to-all-start.6 = ((bf16[32,80,128]{2,1,0:T(8,128)(2,1)}), bf16[32,80,128]{2,1,0:T(8,128)(2,1)S(1)}, u32[]{:S(2)}, u32[]{:S(2)}) async-start(bf16[32,80,128]{2,1,0:T(8,128)(2,1)} %place.1), calls=%async_computation.6 | async-start | bytes 1310720 | tf_op jit(solution)/shard_map/all_to_all | solution.py:40
Sparse Core Ops, SparseCore 0:
  75.5 37.4 all-gather.1

commit v7 on v6

--- a/solution.py
+++ b/solution.py
@@ -109,9 +109,10 @@
     wp = w_v[..., : 4 * hd].reshape(WIDTH, 4 * hd)
     wo = w_v[..., 4 * hd :].reshape(WIDTH, hd)
 
-    for step in range(steps):
+    for step in range(0, steps, 2):
         copies[step].wait()
-        rows = slice(step * STEP, (step + 1) * STEP)
+        copies[step + 1].wait()
+        rows = slice(step * STEP, (step + 2) * STEP)
         px = jnp.concatenate([x_v[g, rows, :] for g in range(8)], axis=1)
         z_pre = jnp.dot(px, wp, preferred_element_type=F32)
         sigma = jax.nn.sigmoid(z_pre)
@@ -121,6 +122,7 @@
 
     for step in range(steps):
         copies[steps + step].wait()
+    for step in range(steps):
         base = step * STEP
         first = max(0, base - REACH)
         rows = slice(base, base + STEP)
@@ -135,10 +137,10 @@
         key = acts[span, k_cols]
         value = acts[span, v_cols]
         scores = dot_nt(query, key) * scale
-        sigma = jax.nn.sigmoid(scores)
+        sigma = jnp.where(masked, jax.nn.sigmoid(scores), 0.0)
         silu = scores * sigma
-        attn = jnp.where(masked, silu, 0.0).astype(BF16)
-        factor = jnp.where(masked, (sigma + silu * (1.0 - sigma)) * scale, 0.0)
+        attn = silu.astype(BF16)
+        factor = sigma + silu * (1.0 - sigma)
         mixed = jnp.dot(attn, value, preferred_element_type=F32)
         centred = mixed - jnp.mean(mixed, axis=-1, keepdims=True)
         inv_std = lax.rsqrt(jnp.mean(centred * centred, axis=-1, keepdims=True) + NORM_FLOOR)
@@ -158,18 +160,19 @@
         ).astype(BF16)
         d_scores = (dot_nt(d_mixed, value) * factor).astype(BF16)
         d_query = jnp.dot(d_scores, key, preferred_element_type=F32)
-        d_value[span, :] += dot_tn(attn, d_mixed)
-        d_key[span, :] += dot_tn(d_scores, query)
+        d_value[:, span] += jnp.dot(d_mixed.T, attn, preferred_element_type=F32)
+        d_key[:, span] += jnp.dot(query.T, d_scores, preferred_element_type=F32)
         d_z[rows, u_cols] = (d_gated * normed * slope[rows, u_cols]).astype(BF16)
-        d_z[rows, q_cols] = (d_query * slope[rows, q_cols]).astype(BF16)
-
-    d_z[:, v_cols] = (d_value[...] * slope[:, v_cols]).astype(BF16)
-    d_z[:, k_cols] = (d_key[...] * slope[:, k_cols]).astype(BF16)
+        d_z[rows, q_cols] = (d_query * (slope[rows, q_cols] * scale)).astype(BF16)
+
+    d_z[:, v_cols] = (d_value[...].T * slope[:, v_cols]).astype(BF16)
+    d_z[:, k_cols] = (d_key[...].T * (slope[:, k_cols] * scale)).astype(BF16)
 
     core = info[3]
     outs = []
+    whole = dot_nt(d_z[...], wp).astype(BF16)
     for y in range(Y):
-        part = dot_nt(d_z[y * STEP : (y + 1) * STEP, :], wp).astype(BF16)
+        part = whole[y * STEP : (y + 1) * STEP]
 
         @pl.when(core == 0)
         def _():
@@ -205,7 +208,7 @@
             half,
             jax.ShapeDtypeStruct((X, YC, ZR, PART_ROWS, HIDDEN), BF16),
         ),
-        in_specs=[SMEM_SPEC, HBM_SPEC, HBM_SPEC],
+        in_specs=[SMEM_SPEC, HBM_SPEC, pl.BlockSpec(memory_space=pl.ANY)],
         out_specs=(HBM_SPEC,) * 3,
         scratch_shapes=[
             pltpu.VMEM((8, LENGTH, LANES), BF16),
@@ -213,8 +216,8 @@
             pltpu.VMEM((X, YC, ZR, PART_ROWS, HIDDEN), BF16),
             pltpu.VMEM((LENGTH, 4 * HEAD_DIM), BF16),
             pltpu.VMEM((LENGTH, 4 * HEAD_DIM), F32),
-            pltpu.VMEM((LENGTH, HEAD_DIM), F32),
-            pltpu.VMEM((LENGTH, HEAD_DIM), F32),
+            pltpu.VMEM((HEAD_DIM, LENGTH), F32),
+            pltpu.VMEM((HEAD_DIM, LENGTH), F32),
             pltpu.VMEM((LENGTH, 4 * HEAD_DIM), BF16),
             pltpu.VMEM((LENGTH, HEAD_DIM), BF16),
             pltpu.VMEM((Y, LANES, WIDTH), BF16),
@@ -232,12 +235,15 @@
     )(info, packs, weights)
 
 
-def pair_kernel(place, kept, got, own, *to_y):
+def pair_kernel(place, kept, got, own, to_1, to_2, to_3, own_v, sem):
     y = place[0]
-    own[...] = kept[y].astype(F32) + got[y].astype(F32)
-    for step in range(1, Y):
+    own_v[...] = kept[y].astype(F32) + got[y].astype(F32)
+    copy = pltpu.make_async_copy(own_v, own, sem)
+    copy.start()
+    for step, block in ((1, to_1), (2, to_2), (3, to_3)):
         other = (y + step) & (Y - 1)
-        to_y[step - 1][...] = (kept[other].astype(F32) + got[other].astype(F32)).astype(BF16)
+        block[...] = (kept[other].astype(F32) + got[other].astype(F32)).astype(BF16)
+    copy.wait()
 
 
 def pair_sums(y, kept, got):
@@ -246,25 +252,17 @@
         pair_kernel,
         out_shape=(jax.ShapeDtypeStruct((LANES, WIDTH), F32),) + (block,) * (Y - 1),
         in_specs=[SMEM_SPEC, VMEM_SPEC, VMEM_SPEC],
-        out_specs=(VMEM_SPEC,) * Y,
+        out_specs=(HBM_SPEC,) + (VMEM_SPEC,) * (Y - 1),
+        scratch_shapes=[pltpu.VMEM((LANES, WIDTH), F32), pltpu.SemaphoreType.DMA],
         compiler_params=pltpu.CompilerParams(vmem_limit_bytes=32 * 2**20),
         cost_estimate=pl.CostEstimate(flops=500_000, bytes_accessed=3_000_000, transcendentals=0),
         name="pair_sums",
     )(y, kept, got)
 
 
-def payload_kernel(own, came_1, came_2, came_3, dy, shared, out):
-    lane = lax.broadcasted_iota(jnp.int32, (64, LANES), 1)
-    for m in range(8):
-        cols = slice(m * LANES, (m + 1) * LANES)
-        total = own[:, cols] + dy[m].astype(F32)
-        for came in (came_1, came_2, came_3):
-            total = total + came[:, cols].astype(F32)
-        low, high = total[:64], total[64:]
-        even = jnp.where(lane < 64, low, pltpu.roll(high, 64, 1))
-        odd = jnp.where(lane < 64, pltpu.roll(low, 64, 1), high)
-        out[2 * m, :64, :] = even.astype(BF16)
-        out[2 * m + 1, :64, :] = odd.astype(BF16)
+def payload_kernel(own, came_1, came_2, came_3, dy, shared, out, own_v, sem):
+    copy = pltpu.make_async_copy(own, own_v, sem)
+    copy.start()
     for h in range(YC):
         total = jnp.zeros((PART_ROWS, HIDDEN), F32)
         for x in range(X):
@@ -277,14 +275,27 @@
                 out[2 * h + s, first : first + PART_ROWS, :] = total[
                     :, col * LANES : (col + 1) * LANES
                 ]
+    copy.wait()
+    lane = lax.broadcasted_iota(jnp.int32, (64, LANES), 1)
+    for m in range(8):
+        cols = slice(m * LANES, (m + 1) * LANES)
+        total = own_v[:, cols] + dy[m].astype(F32)
+        for came in (came_1, came_2, came_3):
+            total = total + came[:, cols].astype(F32)
+        low, high = total[:64], total[64:]
+        even = jnp.where(lane < 64, low, pltpu.roll(high, 64, 1))
+        odd = jnp.where(lane < 64, pltpu.roll(low, 64, 1), high)
+        out[2 * m, :64, :] = even.astype(BF16)
+        out[2 * m + 1, :64, :] = odd.astype(BF16)
 
 
 def payload(own, came, dy, shared):
     return pl.pallas_call(
         payload_kernel,
         out_shape=jax.ShapeDtypeStruct((Z, 64 + 3 * PART_ROWS, LANES), BF16),
-        in_specs=[VMEM_SPEC] * 6,
+        in_specs=[HBM_SPEC] + [VMEM_SPEC] * 5,
         out_specs=VMEM_SPEC,
+        scratch_shapes=[pltpu.VMEM((LANES, WIDTH), F32), pltpu.SemaphoreType.DMA],
         compiler_params=pltpu.CompilerParams(vmem_limit_bytes=32 * 2**20),
         cost_estimate=pl.CostEstimate(flops=1_500_000, bytes_accessed=4_000_000, transcendentals=0),
         name="payload",
@@ -382,7 +393,7 @@
         in_specs=[HBM_SPEC] * 2,
         out_specs=HBM_SPEC,
         scratch_shapes=[pltpu.SemaphoreType.DMA((16,))],
-        compiler_params=pltpu.CompilerParams(vmem_limit_bytes=32 * 2**20),
+        compiler_params=pltpu.CompilerParams(vmem_limit_bytes=GRANT * 2**20),
         cost_estimate=pl.CostEstimate(flops=0, bytes_accessed=1_000_000, transcendentals=0),
         name="split_columns",
     )(inputs, cotangent)

time: 234 us -> 247 us (1.056)
  Pallas kernels: 20.6 us -> 35.3 us
    pallas_call x1, Pallas kernels: 0.95 us -> 17.1 us  [split_columns(): pl.pallas_call(split_kernel, out_shape=jax.ShapeDtypeStruct((8, 2, 2, 64,...]
    unnamed x23 -> x19, local copies, waits for them, and re-layouts: 5.43 us -> 3.54 us
  transfers between devices with their start and end apart: 10 -> 10, of which waited for: 7 -> 7; matrix products, arithmetic and copies ran while one was open for 4% -> 3% of each run, Pallas kernels for 0% -> 0%
where the time goes in v7:
time: 247 us; the launch traced here: 246 us
  waiting for transfers between devices  68.8 us (28%)
  blocking collectives  58.4 us (24%)
  starting transfers between devices  56.6 us (23%)
  Pallas kernels  35.3 us (14%)
  between operations  14.4 us (6%)
  local copies, waits for them, and re-layouts  10.1 us (4%)
    all_to_all x2, blocking collectives, exchange(): return lax.all_to_all(value, axes, split_axis=0, concat_axis=0, tiled=True)  58.4 us
    all_to_all x5, waiting for transfers between devices, exchange(): return lax.all_to_all(value, axes, split_axis=0, concat_axis=0, tiled=True)  54.3 us
    all_to_all x5, starting transfers between devices, exchange(): return lax.all_to_all(value, axes, split_axis=0, concat_axis=0, tiled=True)  43.5 us
    pallas_call x1, Pallas kernels, split_columns(): pl.pallas_call(split_kernel, out_shape=jax.ShapeDtypeStruct((8, 2, 2, 64,...  17.1 us
    pallas_call x1, Pallas kernels, heads_backward(): pl.pallas_call(heads_kernel, out_shape=(half, half, jax.ShapeDtypeStruct(...  13 us
    ppermute x3, waiting for transfers between devices, per_device(): lax.ppermute(to_y[step - 1], 'y', [(i, (i + step) % Y) for i in range(Y)])  12 us
    ppermute x3, starting transfers between devices, per_device(): lax.ppermute(to_y[step - 1], 'y', [(i, (i + step) % Y) for i in range(Y)])  10.7 us
  transfers between devices with their start and end apart: 10, of which 7 were waited for; matrix products, arithmetic and copies ran while one was open for 3% of the time, Pallas kernels for 0%

profile of v7, /device:TPU:1, one launch (start us, length us, event | category | flops | bytes accessed | tf_op | source)
XLA Modules:
  0.0 245.7 jit_solution(3804343079237445763)
XLA Ops:
  7.2 17.1 %split_columns.1 = bf16[8,2,2,64,128]{4,3,2,1,0:T(8,128)(2,1)} custom-call(bf16[2,64,1024]{2,1,0:T(8,128)(2,1)} %bitcast.98, bf16[2,64,1024]{2,1,0:T(8,128)(2,1)} %bitcast.99), custom_call_target="tpu_custom_call" | custom-call | bytes 1000000 | tf_op jit(solution)/shard_map/split_columns/pallas_call | solution.py:390
  24.4 10.3 %all-to-all-start = ((bf16[8,2,2,64,128]{4,3,2,1,0:T(8,128)(2,1)}), bf16[8,2,2,64,128]{4,3,2,1,0:T(8,128)(2,1)S(1)}, u32[]{:S(2)}, u32[]{:S(2)}) async-start(bf16[8,2,2,64,128]{4,3,2,1,0:T(8,128)(2,1)} %split_columns.1), calls=%async_computation | async-start | bytes 1048576 | tf_op jit(solution)/shard_map/all_to_all | solution.py:40
  36.6 7.5 %all-to-all-done = bf16[8,2,2,64,128]{4,3,2,1,0:T(8,128)(2,1)S(1)} async-done(((bf16[8,2,2,64,128]{4,3,2,1,0:T(8,128)(2,1)}), bf16[8,2,2,64,128]{4,3,2,1,0:T(8,128)(2,1)S(1)}, u32[]{:S(2)}, u32[]{:S(2)}) %all-to-all-start) | async-done | bytes 524320 | tf_op jit(solution)/shard_map/all_to_all | solution.py:40
  44.2 44.5 %all_to_all.35 = bf16[16,22,8,128]{3,2,1,0:T(8,128)(2,1)S(1)} all-to-all(bf16[16,22,8,128]{3,2,1,0:T(8,128)(2,1)S(1)} %pad_maximum_fusion), channel_id=1, replica_groups=mesh['x'=4,'y'=4,'c'=2,'zq'=8,'zr'=2] {'zq','zr'}, dimensions={0} | all-to-all | bytes 1441792 | tf_op jit(solution)/shard_map/all_to_all | solution.py:40
  89.7 13.9 %all_to_all.36 = bf16[8,2,6,8,128]{4,3,2,1,0:T(8,128)(2,1)S(1)} all-to-all(bf16[8,2,6,8,128]{4,3,2,1,0:T(8,128)(2,1)S(1)} %bitcast.91), channel_id=1, replica_groups=mesh['x'=4,'y'=4,'c'=2,'zq'=8,'zr'=2] {'y','c'}, dimensions={0} | all-to-all | bytes 393216 | tf_op jit(solution)/shard_map/all_to_all | solution.py:40
  103.9 1.2 broadcast_in_dim.63
  105.2 5.6 %all-to-all-start.3 = ((bf16[8,8,16,640]{3,2,1,0:T(8,128)(2,1)}), bf16[8,8,16,640]{3,2,1,0:T(8,128)(2,1)S(1)}, u32[]{:S(2)}, u32[]{:S(2)}) async-start(bf16[8,8,16,640]{3,2,1,0:T(8,128)(2,1)} %broadcast_in_dim.63), calls=%async_computation.3 | async-start | bytes 2621440 | tf_op jit(solution)/shard_map/all_to_all | solution.py:40
  112.0 15.8 %all-to-all-done.3 = bf16[8,8,16,640]{3,2,1,0:T(8,128)(2,1)S(1)} async-done(((bf16[8,8,16,640]{3,2,1,0:T(8,128)(2,1)}), bf16[8,8,16,640]{3,2,1,0:T(8,128)(2,1)S(1)}, u32[]{:S(2)}, u32[]{:S(2)}) %all-to-all-start.3) | async-done | bytes 1310752 | tf_op jit(solution)/shard_map/all_to_all | solution.py:40
  128.9 13.0 %heads.1 = (bf16[4,128,1024]{2,1,0:T(8,128)(2,1)}, bf16[4,128,1024]{2,1,0:T(8,128)(2,1)}, bf16[4,8,2,16,640]{4,3,2,1,0:T(8,128)(2,1)}) custom-call(s32[4]{0:T(128)} %pad_add_fusion.info, bf16[8,2,1024,128]{3,2,1,0:T(8,128)(2,1)} %all-gather.2.cloned.1.call-done.packs, bf16[4,2,8,16,640]{4,3,2,1,0:T(8,128)(2,1)} %bitcast.90), custom_call_target="tpu_custom_call" | custom-call | flops 5000000000 | bytes 9000000 | tf_op jit(solution)/shard_map/heads/pallas_call | solution.py:204
  141.9 6.7 %all-to-all-start.4 = ((bf16[64,16,640]{2,1,0:T(8,128)(2,1)}), bf16[64,16,640]{2,1,0:T(8,128)(2,1)S(1)}, u32[]{:S(2)}, u32[]{:S(2)}) async-start(bf16[64,16,640]{2,1,0:T(8,128)(2,1)} %bitcast.89), calls=%async_computation.4 | async-start | bytes 2621440 | tf_op jit(solution)/shard_map/all_to_all | solution.py:40
  148.6 2.5 %collective-permute-start = (bf16[4,128,1024]{2,1,0:T(8,128)(2,1)}, bf16[4,128,1024]{2,1,0:T(8,128)(2,1)S(1)}, u32[]{:S(2)}, u32[]{:S(2)}) collective-permute-start(bf16[4,128,1024]{2,1,0:T(8,128)(2,1)} %get-tuple-element.11), channel_id=1, source_target_pairs={{0,16},{16,0},{1,17},{17,1},{2,18},{18,2},{3,19},{19,3},{4,20},{20... | collective-permute-start | bytes 3145736 | tf_op jit(solution)/shard_map/ppermute | solution.py:457
  151.1 2.5 %collective-permute-done.got = bf16[4,128,1024]{2,1,0:T(8,128)(2,1)S(1)} collective-permute-done((bf16[4,128,1024]{2,1,0:T(8,128)(2,1)}, bf16[4,128,1024]{2,1,0:T(8,128)(2,1)S(1)}, u32[]{:S(2)}, u32[]{:S(2)}) %collective-permute-start) | collective-permute-done | bytes 1048608 | tf_op jit(solution)/shard_map/ppermute | solution.py:457
  155.6 3.1 %collective-permute-start.1 = (bf16[128,1024]{1,0:T(8,128)(2,1)}, bf16[128,1024]{1,0:T(8,128)(2,1)S(1)}, u32[]{:S(2)}, u32[]{:S(2)}) collective-permute-start(bf16[128,1024]{1,0:T(8,128)(2,1)} %get-tuple-element.13), channel_id=1, source_target_pairs={{0,32},{32,64},{64,96},{96,0},{1,33},{33,65},{65,97},{97,1},{2,34}... | collective-permute-start | bytes 786440 | tf_op jit(solution)/shard_map/ppermute | solution.py:460
  158.7 4.4 %collective-permute-start.2 = (bf16[128,1024]{1,0:T(8,128)(2,1)}, bf16[128,1024]{1,0:T(8,128)(2,1)S(1)}, u32[]{:S(2)}, u32[]{:S(2)}) collective-permute-start(bf16[128,1024]{1,0:T(8,128)(2,1)} %get-tuple-element.14), channel_id=1, source_target_pairs={{0,64},{32,96},{64,0},{96,32},{1,65},{33,97},{65,1},{97,33},{2,66}... | collective-permute-start | bytes 786440 | tf_op jit(solution)/shard_map/ppermute | solution.py:460
  163.1 3.2 %collective-permute-start.3 = (bf16[128,1024]{1,0:T(8,128)(2,1)}, bf16[128,1024]{1,0:T(8,128)(2,1)S(1)}, u32[]{:S(2)}, u32[]{:S(2)}) collective-permute-start(bf16[128,1024]{1,0:T(8,128)(2,1)} %get-tuple-element.15), channel_id=1, source_target_pairs={{0,96},{32,0},{64,32},{96,64},{1,97},{33,1},{65,33},{97,65},{2,98}... | collective-permute-start | bytes 786440 | tf_op jit(solution)/shard_map/ppermute | solution.py:460
  167.3 5.7 %collective-permute-done.1.came_1 = bf16[128,1024]{1,0:T(8,128)(2,1)S(1)} collective-permute-done((bf16[128,1024]{1,0:T(8,128)(2,1)}, bf16[128,1024]{1,0:T(8,128)(2,1)S(1)}, u32[]{:S(2)}, u32[]{:S(2)}) %collective-permute-start.1) | collective-permute-done | bytes 262176 | tf_op jit(solution)/shard_map/ppermute | solution.py:460
  173.0 6.3 %collective-permute-done.2.came_2 = bf16[128,1024]{1,0:T(8,128)(2,1)S(1)} collective-permute-done((bf16[128,1024]{1,0:T(8,128)(2,1)}, bf16[128,1024]{1,0:T(8,128)(2,1)S(1)}, u32[]{:S(2)}, u32[]{:S(2)}) %collective-permute-start.2) | collective-permute-done | bytes 262176 | tf_op jit(solution)/shard_map/ppermute | solution.py:460
  180.4 1.2 payload.1
  181.6 10.0 %all-to-all-start.5 = ((bf16[16,112,128]{2,1,0:T(8,128)(2,1)}), bf16[16,112,128]{2,1,0:T(8,128)(2,1)S(1)}, u32[]{:S(2)}, u32[]{:S(2)}) async-start(bf16[16,112,128]{2,1,0:T(8,128)(2,1)} %payload.1), calls=%async_computation.5 | async-start | bytes 917504 | tf_op jit(solution)/shard_map/all_to_all | solution.py:40
  192.9 19.5 %all-to-all-done.5.merged = bf16[16,112,128]{2,1,0:T(8,128)(2,1)S(1)} async-done(((bf16[16,112,128]{2,1,0:T(8,128)(2,1)}), bf16[16,112,128]{2,1,0:T(8,128)(2,1)S(1)}, u32[]{:S(2)}, u32[]{:S(2)}) %all-to-all-start.5) | async-done | bytes 458784 | tf_op jit(solution)/shard_map/all_to_all | solution.py:40
  212.4 1.3 place.1
  213.7 10.8 %all-to-all-start.6 = ((bf16[32,80,128]{2,1,0:T(8,128)(2,1)}), bf16[32,80,128]{2,1,0:T(8,128)(2,1)S(1)}, u32[]{:S(2)}, u32[]{:S(2)}) async-start(bf16[32,80,128]{2,1,0:T(8,128)(2,1)} %place.1), calls=%async_computation.6 | async-start | bytes 1310720 | tf_op jit(solution)/shard_map/all_to_all | solution.py:40
  225.9 11.5 %all-to-all-done.6.owned = bf16[32,80,128]{2,1,0:T(8,128)(2,1)S(1)} async-done(((bf16[32,80,128]{2,1,0:T(8,128)(2,1)}), bf16[32,80,128]{2,1,0:T(8,128)(2,1)S(1)}, u32[]{:S(2)}, u32[]{:S(2)}) %all-to-all-start.6) | async-done | bytes 655392 | tf_op jit(solution)/shard_map/all_to_all | solution.py:40
  237.4 1.5 table_sum.1
  (79 shorter events, 12.2 us)
Async XLA Ops:
  7.2 27.7 %copy-start = (s32[8192]{0:T(1024)S(1)}, s32[8192]{0:T(1024)}, u32[]{:S(2)}) copy-start(s32[8192]{0:T(1024)} %param.11) | copy-start | bytes 98308
  7.2 27.5 %copy-start.7 = (s32[1,2,64]{2,1,0:T(2,128)S(1)}, s32[1,2,64]{2,1,0:T(2,128)}, u32[]{:S(2)}) copy-start(s32[1,2,64]{2,1,0:T(2,128)} %param.10) | copy-start | bytes 1540
  7.2 29.1 %copy-start.8 = (s32[1,2,3]{2,1,0:T(2,128)S(1)}, s32[1,2,3]{2,1,0:T(2,128)}, u32[]{:S(2)}) copy-start(s32[1,2,3]{2,1,0:T(2,128)} %param.9) | copy-start | bytes 76
  7.2 29.3 %copy-start.6 = (bf16[64,32]{0,1:T(8,128)(2,1)S(1)}, bf16[64,32]{0,1:T(8,128)(2,1)}, u32[]{:S(2)}) copy-start(bf16[64,32]{0,1:T(8,128)(2,1)} %param.13) | copy-start | bytes 12292
  7.2 29.4 %copy-start.5 = (bf16[32,256]{1,0:T(8,128)(2,1)S(1)}, bf16[32,256]{1,0:T(8,128)(2,1)}, u32[]{:S(2)}) copy-start(bf16[32,256]{1,0:T(8,128)(2,1)} %param.12) | copy-start | bytes 49156
  24.4 19.8 %all-to-all-start = ((bf16[8,2,2,64,128]{4,3,2,1,0:T(8,128)(2,1)}), bf16[8,2,2,64,128]{4,3,2,1,0:T(8,128)(2,1)S(1)}, u32[]{:S(2)}, u32[]{:S(2)}) async-start(bf16[8,2,2,64,128]{4,3,2,1,0:T(8,128)(2,1)} %split_columns.1), calls=%async_computation | async-start | bytes 1048576 | tf_op jit(solution)/shard_map/all_to_all | solution.py:40
  34.6 93.2 %all-gather.2.cloned.1.call-start = ((), (), s32[]{:S(2)}) async-start(), calls=%async_computation.7 | async-start | bytes 4718592 | tf_op jit(solution)/shard_map/all_gather | solution.py:427
  105.2 22.7 %all-to-all-start.3 = ((bf16[8,8,16,640]{3,2,1,0:T(8,128)(2,1)}), bf16[8,8,16,640]{3,2,1,0:T(8,128)(2,1)S(1)}, u32[]{:S(2)}, u32[]{:S(2)}) async-start(bf16[8,8,16,640]{3,2,1,0:T(8,128)(2,1)} %broadcast_in_dim.63), calls=%async_computation.3 | async-start | bytes 2621440 | tf_op jit(solution)/shard_map/all_to_all | solution.py:40
  127.8 1.1 copy-start.4
  141.9 11.7 %copy-start.1 = (bf16[4,128,1024]{2,1,0:T(8,128)(2,1)S(1)}, bf16[4,128,1024]{2,1,0:T(8,128)(2,1)}, u32[]{:S(2)}) copy-start(bf16[4,128,1024]{2,1,0:T(8,128)(2,1)} %get-tuple-element.10.kept) | copy-start | bytes 3145732
  141.9 37.4 %all-to-all-start.4 = ((bf16[64,16,640]{2,1,0:T(8,128)(2,1)}), bf16[64,16,640]{2,1,0:T(8,128)(2,1)S(1)}, u32[]{:S(2)}, u32[]{:S(2)}) async-start(bf16[64,16,640]{2,1,0:T(8,128)(2,1)} %bitcast.89), calls=%async_computation.4 | async-start | bytes 2621440 | tf_op jit(solution)/shard_map/all_to_all | solution.py:40
  148.6 5.0 %collective-permute-start = (bf16[4,128,1024]{2,1,0:T(8,128)(2,1)}, bf16[4,128,1024]{2,1,0:T(8,128)(2,1)S(1)}, u32[]{:S(2)}, u32[]{:S(2)}) collective-permute-start(bf16[4,128,1024]{2,1,0:T(8,128)(2,1)} %get-tuple-element.11), channel_id=1, source_target_pairs={{0,16},{16,0},{1,17},{17,1},{2,18},{18,2},{3,19},{19,3},{4,20},{20... | collective-permute-start | bytes 3145736 | tf_op jit(solution)/shard_map/ppermute | solution.py:457
  154.8 0.8 copy-start.2
  155.6 17.4 %collective-permute-start.1 = (bf16[128,1024]{1,0:T(8,128)(2,1)}, bf16[128,1024]{1,0:T(8,128)(2,1)S(1)}, u32[]{:S(2)}, u32[]{:S(2)}) collective-permute-start(bf16[128,1024]{1,0:T(8,128)(2,1)} %get-tuple-element.13), channel_id=1, source_target_pairs={{0,32},{32,64},{64,96},{96,0},{1,33},{33,65},{65,97},{97,1},{2,34}... | collective-permute-start | bytes 786440 | tf_op jit(solution)/shard_map/ppermute | solution.py:460
  158.7 20.6 %collective-permute-start.2 = (bf16[128,1024]{1,0:T(8,128)(2,1)}, bf16[128,1024]{1,0:T(8,128)(2,1)S(1)}, u32[]{:S(2)}, u32[]{:S(2)}) collective-permute-start(bf16[128,1024]{1,0:T(8,128)(2,1)} %get-tuple-element.14), channel_id=1, source_target_pairs={{0,64},{32,96},{64,0},{96,32},{1,65},{33,97},{65,1},{97,33},{2,66}... | collective-permute-start | bytes 786440 | tf_op jit(solution)/shard_map/ppermute | solution.py:460
  163.1 16.3 %collective-permute-start.3 = (bf16[128,1024]{1,0:T(8,128)(2,1)}, bf16[128,1024]{1,0:T(8,128)(2,1)S(1)}, u32[]{:S(2)}, u32[]{:S(2)}) collective-permute-start(bf16[128,1024]{1,0:T(8,128)(2,1)} %get-tuple-element.15), channel_id=1, source_target_pairs={{0,96},{32,0},{64,32},{96,64},{1,97},{33,1},{65,33},{97,65},{2,98}... | collective-permute-start | bytes 786440 | tf_op jit(solution)/shard_map/ppermute | solution.py:460
  179.3 1.0 copy-start.3
  181.6 30.8 %all-to-all-start.5 = ((bf16[16,112,128]{2,1,0:T(8,128)(2,1)}), bf16[16,112,128]{2,1,0:T(8,128)(2,1)S(1)}, u32[]{:S(2)}, u32[]{:S(2)}) async-start(bf16[16,112,128]{2,1,0:T(8,128)(2,1)} %payload.1), calls=%async_computation.5 | async-start | bytes 917504 | tf_op jit(solution)/shard_map/all_to_all | solution.py:40
  213.7 23.8 %all-to-all-start.6 = ((bf16[32,80,128]{2,1,0:T(8,128)(2,1)}), bf16[32,80,128]{2,1,0:T(8,128)(2,1)S(1)}, u32[]{:S(2)}, u32[]{:S(2)}) async-start(bf16[32,80,128]{2,1,0:T(8,128)(2,1)} %place.1), calls=%async_computation.6 | async-start | bytes 1310720 | tf_op jit(solution)/shard_map/all_to_all | solution.py:40
Sparse Core Ops, SparseCore 0:
  89.8 37.4 all-gather.1

commit v8 on v7

--- a/solution.py
+++ b/solution.py
@@ -237,7 +237,7 @@
 
 def pair_kernel(place, kept, got, own, to_1, to_2, to_3, own_v, sem):
     y = place[0]
-    own_v[...] = kept[y].astype(F32) + got[y].astype(F32)
+    own_v[...] = (kept[y].astype(F32) + got[y].astype(F32)).astype(BF16)
     copy = pltpu.make_async_copy(own_v, own, sem)
     copy.start()
     for step, block in ((1, to_1), (2, to_2), (3, to_3)):
@@ -250,10 +250,10 @@
     block = jax.ShapeDtypeStruct((LANES, WIDTH), BF16)
     return pl.pallas_call(
         pair_kernel,
-        out_shape=(jax.ShapeDtypeStruct((LANES, WIDTH), F32),) + (block,) * (Y - 1),
+        out_shape=(block,) * Y,
         in_specs=[SMEM_SPEC, VMEM_SPEC, VMEM_SPEC],
         out_specs=(HBM_SPEC,) + (VMEM_SPEC,) * (Y - 1),
-        scratch_shapes=[pltpu.VMEM((LANES, WIDTH), F32), pltpu.SemaphoreType.DMA],
+        scratch_shapes=[pltpu.VMEM((LANES, WIDTH), BF16), pltpu.SemaphoreType.DMA],
         compiler_params=pltpu.CompilerParams(vmem_limit_bytes=32 * 2**20),
         cost_estimate=pl.CostEstimate(flops=500_000, bytes_accessed=3_000_000, transcendentals=0),
         name="pair_sums",
@@ -279,7 +279,7 @@
     lane = lax.broadcasted_iota(jnp.int32, (64, LANES), 1)
     for m in range(8):
         cols = slice(m * LANES, (m + 1) * LANES)
-        total = own_v[:, cols] + dy[m].astype(F32)
+        total = own_v[:, cols].astype(F32) + dy[m].astype(F32)
         for came in (came_1, came_2, came_3):
             total = total + came[:, cols].astype(F32)
         low, high = total[:64], total[64:]
@@ -295,7 +295,7 @@
         out_shape=jax.ShapeDtypeStruct((Z, 64 + 3 * PART_ROWS, LANES), BF16),
         in_specs=[HBM_SPEC] + [VMEM_SPEC] * 5,
         out_specs=VMEM_SPEC,
-        scratch_shapes=[pltpu.VMEM((LANES, WIDTH), F32), pltpu.SemaphoreType.DMA],
+        scratch_shapes=[pltpu.VMEM((LANES, WIDTH), BF16), pltpu.SemaphoreType.DMA],
         compiler_params=pltpu.CompilerParams(vmem_limit_bytes=32 * 2**20),
         cost_estimate=pl.CostEstimate(flops=1_500_000, bytes_accessed=4_000_000, transcendentals=0),
         name="payload",
@@ -391,9 +391,9 @@
         split_kernel,
         out_shape=jax.ShapeDtypeStruct((8, 2, 2, 64, LANES), BF16),
         in_specs=[HBM_SPEC] * 2,
-        out_specs=HBM_SPEC,
+        out_specs=VMEM_SPEC,
         scratch_shapes=[pltpu.SemaphoreType.DMA((16,))],
-        compiler_params=pltpu.CompilerParams(vmem_limit_bytes=GRANT * 2**20),
+        compiler_params=pltpu.CompilerParams(vmem_limit_bytes=60 * 2**20),
         cost_estimate=pl.CostEstimate(flops=0, bytes_accessed=1_000_000, transcendentals=0),
         name="split_columns",
     )(inputs, cotangent)

time: 247 us -> 231 us (0.935)
  Pallas kernels: 35.3 us -> 20.1 us
    pallas_call x1, Pallas kernels: 17.1 us -> 1.97 us  [split_columns(): pl.pallas_call(split_kernel, out_shape=jax.ShapeDtypeStruct((8, 2, 2, 64,...]
  transfers between devices with their start and end apart: 10 -> 10, of which waited for: 7 -> 7; matrix products, arithmetic and copies ran while one was open for 3% -> 4% of each run, Pallas kernels for 0% -> 1%
where the time goes in v8:
time: 231 us; the launch traced here: 230 us
  waiting for transfers between devices  68.9 us (30%)
  blocking collectives  58.4 us (25%)
  starting transfers between devices  56.6 us (25%)
  Pallas kernels  20.1 us (9%)
  between operations  14.4 us (6%)
  local copies, waits for them, and re-layouts  9.91 us (4%)
    all_to_all x2, blocking collectives, exchange(): return lax.all_to_all(value, axes, split_axis=0, concat_axis=0, tiled=True)  58.4 us
    all_to_all x5, waiting for transfers between devices, exchange(): return lax.all_to_all(value, axes, split_axis=0, concat_axis=0, tiled=True)  54.3 us
    all_to_all x5, starting transfers between devices, exchange(): return lax.all_to_all(value, axes, split_axis=0, concat_axis=0, tiled=True)  43.4 us
    pallas_call x1, Pallas kernels, heads_backward(): pl.pallas_call(heads_kernel, out_shape=(half, half, jax.ShapeDtypeStruct(...  13 us
    ppermute x3, waiting for transfers between devices, per_device(): lax.ppermute(to_y[step - 1], 'y', [(i, (i + step) % Y) for i in range(Y)])  12.1 us
    ppermute x3, starting transfers between devices, per_device(): lax.ppermute(to_y[step - 1], 'y', [(i, (i + step) % Y) for i in range(Y)])  10.7 us
  transfers between devices with their start and end apart: 10, of which 7 were waited for; matrix products, arithmetic and copies ran while one was open for 4% of the time, Pallas kernels for 1%

profile of v8, /device:TPU:1, one launch (start us, length us, event | category | flops | bytes accessed | tf_op | source)
XLA Modules:
  0.0 230.4 jit_solution(15767035102739623383)
XLA Ops:
  7.2 2.0 split_columns.1
  9.2 10.3 %all-to-all-start = ((bf16[8,2,2,64,128]{4,3,2,1,0:T(8,128)(2,1)}), bf16[8,2,2,64,128]{4,3,2,1,0:T(8,128)(2,1)S(1)}, u32[]{:S(2)}, u32[]{:S(2)}) async-start(bf16[8,2,2,64,128]{4,3,2,1,0:T(8,128)(2,1)} %split_columns.1), calls=%async_computation | async-start | bytes 1048576 | tf_op jit(solution)/shard_map/all_to_all | solution.py:40
  21.5 7.5 %all-to-all-done = bf16[8,2,2,64,128]{4,3,2,1,0:T(8,128)(2,1)S(1)} async-done(((bf16[8,2,2,64,128]{4,3,2,1,0:T(8,128)(2,1)}), bf16[8,2,2,64,128]{4,3,2,1,0:T(8,128)(2,1)S(1)}, u32[]{:S(2)}, u32[]{:S(2)}) %all-to-all-start) | async-done | bytes 524320 | tf_op jit(solution)/shard_map/all_to_all | solution.py:40
  29.1 44.5 %all_to_all.35 = bf16[16,22,8,128]{3,2,1,0:T(8,128)(2,1)S(1)} all-to-all(bf16[16,22,8,128]{3,2,1,0:T(8,128)(2,1)S(1)} %pad_maximum_fusion), channel_id=1, replica_groups=mesh['x'=4,'y'=4,'c'=2,'zq'=8,'zr'=2] {'zq','zr'}, dimensions={0} | all-to-all | bytes 1441792 | tf_op jit(solution)/shard_map/all_to_all | solution.py:40
  74.5 13.9 %all_to_all.36 = bf16[8,2,6,8,128]{4,3,2,1,0:T(8,128)(2,1)S(1)} all-to-all(bf16[8,2,6,8,128]{4,3,2,1,0:T(8,128)(2,1)S(1)} %bitcast.91), channel_id=1, replica_groups=mesh['x'=4,'y'=4,'c'=2,'zq'=8,'zr'=2] {'y','c'}, dimensions={0} | all-to-all | bytes 393216 | tf_op jit(solution)/shard_map/all_to_all | solution.py:40
  88.8 1.2 broadcast_in_dim.63
  90.0 5.6 %all-to-all-start.3 = ((bf16[8,8,16,640]{3,2,1,0:T(8,128)(2,1)}), bf16[8,8,16,640]{3,2,1,0:T(8,128)(2,1)S(1)}, u32[]{:S(2)}, u32[]{:S(2)}) async-start(bf16[8,8,16,640]{3,2,1,0:T(8,128)(2,1)} %broadcast_in_dim.63), calls=%async_computation.3 | async-start | bytes 2621440 | tf_op jit(solution)/shard_map/all_to_all | solution.py:40
  96.9 15.8 %all-to-all-done.3 = bf16[8,8,16,640]{3,2,1,0:T(8,128)(2,1)S(1)} async-done(((bf16[8,8,16,640]{3,2,1,0:T(8,128)(2,1)}), bf16[8,8,16,640]{3,2,1,0:T(8,128)(2,1)S(1)}, u32[]{:S(2)}, u32[]{:S(2)}) %all-to-all-start.3) | async-done | bytes 1310752 | tf_op jit(solution)/shard_map/all_to_all | solution.py:40
  113.7 13.0 %heads.1 = (bf16[4,128,1024]{2,1,0:T(8,128)(2,1)}, bf16[4,128,1024]{2,1,0:T(8,128)(2,1)}, bf16[4,8,2,16,640]{4,3,2,1,0:T(8,128)(2,1)}) custom-call(s32[4]{0:T(128)} %pad_add_fusion.info, bf16[8,2,1024,128]{3,2,1,0:T(8,128)(2,1)} %all-gather.2.cloned.1.call-done.packs, bf16[4,2,8,16,640]{4,3,2,1,0:T(8,128)(2,1)} %bitcast.90), custom_call_target="tpu_custom_call" | custom-call | flops 5000000000 | bytes 9000000 | tf_op jit(solution)/shard_map/heads/pallas_call | solution.py:204
  126.8 6.7 %all-to-all-start.4 = ((bf16[64,16,640]{2,1,0:T(8,128)(2,1)}), bf16[64,16,640]{2,1,0:T(8,128)(2,1)S(1)}, u32[]{:S(2)}, u32[]{:S(2)}) async-start(bf16[64,16,640]{2,1,0:T(8,128)(2,1)} %bitcast.89), calls=%async_computation.4 | async-start | bytes 2621440 | tf_op jit(solution)/shard_map/all_to_all | solution.py:40
  133.5 2.5 %collective-permute-start = (bf16[4,128,1024]{2,1,0:T(8,128)(2,1)}, bf16[4,128,1024]{2,1,0:T(8,128)(2,1)S(1)}, u32[]{:S(2)}, u32[]{:S(2)}) collective-permute-start(bf16[4,128,1024]{2,1,0:T(8,128)(2,1)} %get-tuple-element.11), channel_id=1, source_target_pairs={{0,16},{16,0},{1,17},{17,1},{2,18},{18,2},{3,19},{19,3},{4,20},{20... | collective-permute-start | bytes 3145736 | tf_op jit(solution)/shard_map/ppermute | solution.py:457
  135.9 2.5 %collective-permute-done.got = bf16[4,128,1024]{2,1,0:T(8,128)(2,1)S(1)} collective-permute-done((bf16[4,128,1024]{2,1,0:T(8,128)(2,1)}, bf16[4,128,1024]{2,1,0:T(8,128)(2,1)S(1)}, u32[]{:S(2)}, u32[]{:S(2)}) %collective-permute-start) | collective-permute-done | bytes 1048608 | tf_op jit(solution)/shard_map/ppermute | solution.py:457
  140.3 3.1 %collective-permute-start.1 = (bf16[128,1024]{1,0:T(8,128)(2,1)}, bf16[128,1024]{1,0:T(8,128)(2,1)S(1)}, u32[]{:S(2)}, u32[]{:S(2)}) collective-permute-start(bf16[128,1024]{1,0:T(8,128)(2,1)} %get-tuple-element.13), channel_id=1, source_target_pairs={{0,32},{32,64},{64,96},{96,0},{1,33},{33,65},{65,97},{97,1},{2,34}... | collective-permute-start | bytes 786440 | tf_op jit(solution)/shard_map/ppermute | solution.py:460
  143.4 4.4 %collective-permute-start.2 = (bf16[128,1024]{1,0:T(8,128)(2,1)}, bf16[128,1024]{1,0:T(8,128)(2,1)S(1)}, u32[]{:S(2)}, u32[]{:S(2)}) collective-permute-start(bf16[128,1024]{1,0:T(8,128)(2,1)} %get-tuple-element.14), channel_id=1, source_target_pairs={{0,64},{32,96},{64,0},{96,32},{1,65},{33,97},{65,1},{97,33},{2,66}... | collective-permute-start | bytes 786440 | tf_op jit(solution)/shard_map/ppermute | solution.py:460
  147.8 3.2 %collective-permute-start.3 = (bf16[128,1024]{1,0:T(8,128)(2,1)}, bf16[128,1024]{1,0:T(8,128)(2,1)S(1)}, u32[]{:S(2)}, u32[]{:S(2)}) collective-permute-start(bf16[128,1024]{1,0:T(8,128)(2,1)} %get-tuple-element.15), channel_id=1, source_target_pairs={{0,96},{32,0},{64,32},{96,64},{1,97},{33,1},{65,33},{97,65},{2,98}... | collective-permute-start | bytes 786440 | tf_op jit(solution)/shard_map/ppermute | solution.py:460
  152.0 5.8 %collective-permute-done.1.came_1 = bf16[128,1024]{1,0:T(8,128)(2,1)S(1)} collective-permute-done((bf16[128,1024]{1,0:T(8,128)(2,1)}, bf16[128,1024]{1,0:T(8,128)(2,1)S(1)}, u32[]{:S(2)}, u32[]{:S(2)}) %collective-permute-start.1) | collective-permute-done | bytes 262176 | tf_op jit(solution)/shard_map/ppermute | solution.py:460
  157.9 6.3 %collective-permute-done.2.came_2 = bf16[128,1024]{1,0:T(8,128)(2,1)S(1)} collective-permute-done((bf16[128,1024]{1,0:T(8,128)(2,1)}, bf16[128,1024]{1,0:T(8,128)(2,1)S(1)}, u32[]{:S(2)}, u32[]{:S(2)}) %collective-permute-start.2) | collective-permute-done | bytes 262176 | tf_op jit(solution)/shard_map/ppermute | solution.py:460
  165.1 1.2 payload.1
  166.4 10.0 %all-to-all-start.5 = ((bf16[16,112,128]{2,1,0:T(8,128)(2,1)}), bf16[16,112,128]{2,1,0:T(8,128)(2,1)S(1)}, u32[]{:S(2)}, u32[]{:S(2)}) async-start(bf16[16,112,128]{2,1,0:T(8,128)(2,1)} %payload.1), calls=%async_computation.5 | async-start | bytes 917504 | tf_op jit(solution)/shard_map/all_to_all | solution.py:40
  177.7 19.5 %all-to-all-done.5.merged = bf16[16,112,128]{2,1,0:T(8,128)(2,1)S(1)} async-done(((bf16[16,112,128]{2,1,0:T(8,128)(2,1)}), bf16[16,112,128]{2,1,0:T(8,128)(2,1)S(1)}, u32[]{:S(2)}, u32[]{:S(2)}) %all-to-all-start.5) | async-done | bytes 458784 | tf_op jit(solution)/shard_map/all_to_all | solution.py:40
  197.2 1.3 place.1
  198.4 10.8 %all-to-all-start.6 = ((bf16[32,80,128]{2,1,0:T(8,128)(2,1)}), bf16[32,80,128]{2,1,0:T(8,128)(2,1)S(1)}, u32[]{:S(2)}, u32[]{:S(2)}) async-start(bf16[32,80,128]{2,1,0:T(8,128)(2,1)} %place.1), calls=%async_computation.6 | async-start | bytes 1310720 | tf_op jit(solution)/shard_map/all_to_all | solution.py:40
  210.6 11.5 %all-to-all-done.6.owned = bf16[32,80,128]{2,1,0:T(8,128)(2,1)S(1)} async-done(((bf16[32,80,128]{2,1,0:T(8,128)(2,1)}), bf16[32,80,128]{2,1,0:T(8,128)(2,1)S(1)}, u32[]{:S(2)}, u32[]{:S(2)}) %all-to-all-start.6) | async-done | bytes 655392 | tf_op jit(solution)/shard_map/all_to_all | solution.py:40
  222.1 1.4 table_sum.1
  (79 shorter events, 12.0 us)
Async XLA Ops:
  7.2 12.6 %copy-start = (s32[8192]{0:T(1024)S(1)}, s32[8192]{0:T(1024)}, u32[]{:S(2)}) copy-start(s32[8192]{0:T(1024)} %param.11) | copy-start | bytes 98308
  7.2 12.3 %copy-start.7 = (s32[1,2,64]{2,1,0:T(2,128)S(1)}, s32[1,2,64]{2,1,0:T(2,128)}, u32[]{:S(2)}) copy-start(s32[1,2,64]{2,1,0:T(2,128)} %param.10) | copy-start | bytes 1540
  7.2 13.9 %copy-start.8 = (s32[1,2,3]{2,1,0:T(2,128)S(1)}, s32[1,2,3]{2,1,0:T(2,128)}, u32[]{:S(2)}) copy-start(s32[1,2,3]{2,1,0:T(2,128)} %param.9) | copy-start | bytes 76
  7.2 14.1 %copy-start.6 = (bf16[64,32]{0,1:T(8,128)(2,1)S(1)}, bf16[64,32]{0,1:T(8,128)(2,1)}, u32[]{:S(2)}) copy-start(bf16[64,32]{0,1:T(8,128)(2,1)} %param.13) | copy-start | bytes 12292
  7.2 14.2 %copy-start.5 = (bf16[32,256]{1,0:T(8,128)(2,1)S(1)}, bf16[32,256]{1,0:T(8,128)(2,1)}, u32[]{:S(2)}) copy-start(bf16[32,256]{1,0:T(8,128)(2,1)} %param.12) | copy-start | bytes 49156
  9.2 19.8 %all-to-all-start = ((bf16[8,2,2,64,128]{4,3,2,1,0:T(8,128)(2,1)}), bf16[8,2,2,64,128]{4,3,2,1,0:T(8,128)(2,1)S(1)}, u32[]{:S(2)}, u32[]{:S(2)}) async-start(bf16[8,2,2,64,128]{4,3,2,1,0:T(8,128)(2,1)} %split_columns.1), calls=%async_computation | async-start | bytes 1048576 | tf_op jit(solution)/shard_map/all_to_all | solution.py:40
  19.5 93.2 %all-gather.2.cloned.1.call-start = ((), (), s32[]{:S(2)}) async-start(), calls=%async_computation.7 | async-start | bytes 4718592 | tf_op jit(solution)/shard_map/all_gather | solution.py:427
  90.0 22.7 %all-to-all-start.3 = ((bf16[8,8,16,640]{3,2,1,0:T(8,128)(2,1)}), bf16[8,8,16,640]{3,2,1,0:T(8,128)(2,1)S(1)}, u32[]{:S(2)}, u32[]{:S(2)}) async-start(bf16[8,8,16,640]{3,2,1,0:T(8,128)(2,1)} %broadcast_in_dim.63), calls=%async_computation.3 | async-start | bytes 2621440 | tf_op jit(solution)/shard_map/all_to_all | solution.py:40
  112.7 1.1 copy-start.4
  126.8 11.7 %copy-start.1 = (bf16[4,128,1024]{2,1,0:T(8,128)(2,1)S(1)}, bf16[4,128,1024]{2,1,0:T(8,128)(2,1)}, u32[]{:S(2)}) copy-start(bf16[4,128,1024]{2,1,0:T(8,128)(2,1)} %get-tuple-element.10.kept) | copy-start | bytes 3145732
  126.8 37.4 %all-to-all-start.4 = ((bf16[64,16,640]{2,1,0:T(8,128)(2,1)}), bf16[64,16,640]{2,1,0:T(8,128)(2,1)S(1)}, u32[]{:S(2)}, u32[]{:S(2)}) async-start(bf16[64,16,640]{2,1,0:T(8,128)(2,1)} %bitcast.89), calls=%async_computation.4 | async-start | bytes 2621440 | tf_op jit(solution)/shard_map/all_to_all | solution.py:40
  133.5 5.0 %collective-permute-start = (bf16[4,128,1024]{2,1,0:T(8,128)(2,1)}, bf16[4,128,1024]{2,1,0:T(8,128)(2,1)S(1)}, u32[]{:S(2)}, u32[]{:S(2)}) collective-permute-start(bf16[4,128,1024]{2,1,0:T(8,128)(2,1)} %get-tuple-element.11), channel_id=1, source_target_pairs={{0,16},{16,0},{1,17},{17,1},{2,18},{18,2},{3,19},{19,3},{4,20},{20... | collective-permute-start | bytes 3145736 | tf_op jit(solution)/shard_map/ppermute | solution.py:457
  139.6 0.7 copy-start.2
  140.3 17.6 %collective-permute-start.1 = (bf16[128,1024]{1,0:T(8,128)(2,1)}, bf16[128,1024]{1,0:T(8,128)(2,1)S(1)}, u32[]{:S(2)}, u32[]{:S(2)}) collective-permute-start(bf16[128,1024]{1,0:T(8,128)(2,1)} %get-tuple-element.13), channel_id=1, source_target_pairs={{0,32},{32,64},{64,96},{96,0},{1,33},{33,65},{65,97},{97,1},{2,34}... | collective-permute-start | bytes 786440 | tf_op jit(solution)/shard_map/ppermute | solution.py:460
  143.4 20.7 %collective-permute-start.2 = (bf16[128,1024]{1,0:T(8,128)(2,1)}, bf16[128,1024]{1,0:T(8,128)(2,1)S(1)}, u32[]{:S(2)}, u32[]{:S(2)}) collective-permute-start(bf16[128,1024]{1,0:T(8,128)(2,1)} %get-tuple-element.14), channel_id=1, source_target_pairs={{0,64},{32,96},{64,0},{96,32},{1,65},{33,97},{65,1},{97,33},{2,66}... | collective-permute-start | bytes 786440 | tf_op jit(solution)/shard_map/ppermute | solution.py:460
  147.8 16.4 %collective-permute-start.3 = (bf16[128,1024]{1,0:T(8,128)(2,1)}, bf16[128,1024]{1,0:T(8,128)(2,1)S(1)}, u32[]{:S(2)}, u32[]{:S(2)}) collective-permute-start(bf16[128,1024]{1,0:T(8,128)(2,1)} %get-tuple-element.15), channel_id=1, source_target_pairs={{0,96},{32,0},{64,32},{96,64},{1,97},{33,1},{65,33},{97,65},{2,98}... | collective-permute-start | bytes 786440 | tf_op jit(solution)/shard_map/ppermute | solution.py:460
  164.2 1.0 copy-start.3
  166.4 30.8 %all-to-all-start.5 = ((bf16[16,112,128]{2,1,0:T(8,128)(2,1)}), bf16[16,112,128]{2,1,0:T(8,128)(2,1)S(1)}, u32[]{:S(2)}, u32[]{:S(2)}) async-start(bf16[16,112,128]{2,1,0:T(8,128)(2,1)} %payload.1), calls=%async_computation.5 | async-start | bytes 917504 | tf_op jit(solution)/shard_map/all_to_all | solution.py:40
  198.4 23.7 %all-to-all-start.6 = ((bf16[32,80,128]{2,1,0:T(8,128)(2,1)}), bf16[32,80,128]{2,1,0:T(8,128)(2,1)S(1)}, u32[]{:S(2)}, u32[]{:S(2)}) async-start(bf16[32,80,128]{2,1,0:T(8,128)(2,1)} %place.1), calls=%async_computation.6 | async-start | bytes 1310720 | tf_op jit(solution)/shard_map/all_to_all | solution.py:40
Sparse Core Ops, SparseCore 0:
  74.6 37.4 all-gather.1

commit v9 on v8

--- a/solution.py
+++ b/solution.py
@@ -260,21 +260,9 @@
     )(y, kept, got)
 
 
-def payload_kernel(own, came_1, came_2, came_3, dy, shared, out, own_v, sem):
+def payload_kernel(own, came_1, came_2, came_3, dy, out, own_v, sem):
     copy = pltpu.make_async_copy(own, own_v, sem)
     copy.start()
-    for h in range(YC):
-        total = jnp.zeros((PART_ROWS, HIDDEN), F32)
-        for x in range(X):
-            for r in range(ZR):
-                total = total + shared[x, h, r].astype(F32)
-        total = total.astype(BF16)
-        for s in range(2):
-            for n, col in enumerate((2 * s, 2 * s + 1, 4)):
-                first = 64 + n * PART_ROWS
-                out[2 * h + s, first : first + PART_ROWS, :] = total[
-                    :, col * LANES : (col + 1) * LANES
-                ]
     copy.wait()
     lane = lax.broadcasted_iota(jnp.int32, (64, LANES), 1)
     for m in range(8):
@@ -285,21 +273,45 @@
         low, high = total[:64], total[64:]
         even = jnp.where(lane < 64, low, pltpu.roll(high, 64, 1))
         odd = jnp.where(lane < 64, pltpu.roll(low, 64, 1), high)
-        out[2 * m, :64, :] = even.astype(BF16)
-        out[2 * m + 1, :64, :] = odd.astype(BF16)
-
-
-def payload(own, came, dy, shared):
+        out[2 * m] = even.astype(BF16)
+        out[2 * m + 1] = odd.astype(BF16)
+
+
+def payload(own, came, dy):
     return pl.pallas_call(
         payload_kernel,
-        out_shape=jax.ShapeDtypeStruct((Z, 64 + 3 * PART_ROWS, LANES), BF16),
-        in_specs=[HBM_SPEC] + [VMEM_SPEC] * 5,
+        out_shape=jax.ShapeDtypeStruct((Z, 64, LANES), BF16),
+        in_specs=[HBM_SPEC] + [VMEM_SPEC] * 4,
         out_specs=VMEM_SPEC,
         scratch_shapes=[pltpu.VMEM((LANES, WIDTH), BF16), pltpu.SemaphoreType.DMA],
         compiler_params=pltpu.CompilerParams(vmem_limit_bytes=32 * 2**20),
-        cost_estimate=pl.CostEstimate(flops=1_500_000, bytes_accessed=4_000_000, transcendentals=0),
+        cost_estimate=pl.CostEstimate(flops=700_000, bytes_accessed=1_500_000, transcendentals=0),
         name="payload",
-    )(own, *came, dy, shared)
+    )(own, *came, dy)
+
+
+def weight_sum_kernel(shared, out):
+    for h in range(YC):
+        total = jnp.zeros((PART_ROWS, HIDDEN), F32)
+        for x in range(X):
+            for r in range(ZR):
+                total = total + shared[x, h, r].astype(F32)
+        for s in range(2):
+            for n, col in enumerate((2 * s, 2 * s + 1, 4)):
+                first = n * PART_ROWS
+                out[h, s, first : first + PART_ROWS, :] = total[:, col * LANES : (col + 1) * LANES]
+
+
+def weight_sum(shared):
+    return pl.pallas_call(
+        weight_sum_kernel,
+        out_shape=jax.ShapeDtypeStruct((YC, 2, 3 * PART_ROWS, LANES), F32),
+        in_specs=[VMEM_SPEC],
+        out_specs=VMEM_SPEC,
+        compiler_params=pltpu.CompilerParams(vmem_limit_bytes=32 * 2**20),
+        cost_estimate=pl.CostEstimate(flops=700_000, bytes_accessed=1_700_000, transcendentals=0),
+        name="weight_sum",
+    )(shared)
 
 
 def place_kernel(slots, tags, merged, out):
@@ -308,7 +320,7 @@
     for pair in range(YC // 2):
         both = []
         for yc in (2 * pair, 2 * pair + 1):
-            tokens = jnp.concatenate([merged[2 * yc, :64, :], merged[2 * yc + 1, :64, :]], axis=0)
+            tokens = jnp.concatenate([merged[2 * yc], merged[2 * yc + 1]], axis=0)
             moved = [
                 jnp.dot(
                     (slots[2 * yc + s : 2 * yc + s + 1, :] == slot_ids).astype(BF16),
@@ -463,9 +475,15 @@
     block = (y_here * C + core) * LANES
     dy_own = lax.dynamic_slice(packs, (0, 1, block, 0), (YC, 1, LANES, LANES))[:, 0]
 
-    merged = exchange(payload(own, came, dy_own, shared), SEQ)
-    w_grad = merged[:, 64:].astype(F32).reshape(ZQ, ZR, 3, PART_ROWS, LANES)
-    w_grad = jnp.sum(w_grad, axis=0)
+    merged = exchange(payload(own, came, dy_own), SEQ)
+
+    low = lax.axis_index("zr")
+    rest = lax.psum_scatter(weight_sum(shared), "zq", scatter_dimension=0, tiled=True)[0]
+    mine = lax.dynamic_index_in_dim(rest, low, 0, keepdims=False)
+    other = lax.dynamic_index_in_dim(rest, 1 - low, 0, keepdims=False)
+    other = lax.ppermute(other, "zr", [(0, 1), (1, 0)])
+    w_grad = jnp.where(low == 0, jnp.stack([mine, other]), jnp.stack([other, mine]))
+    w_grad = w_grad.reshape(ZR, 3, PART_ROWS, LANES)
     grad_proj = w_grad[:, :2].transpose(0, 2, 1, 3).reshape(32, 2 * LANES)
     both_out = w_grad[:, 2].reshape(32, 2, 64)
     grad_out = lax.dynamic_index_in_dim(both_out, z_here & 1, 1, keepdims=False).T

time: 231 us -> 241 us (1.043)
  the two profiles are of different devices: /device:TPU:1 before, /device:TPU:4 now
where the time goes in v9:
time: 241 us; the launch traced here: 240 us
  waiting for transfers between devices  79 us (33%)
  blocking collectives  62.8 us (26%)
  starting transfers between devices  50.4 us (21%)
  Pallas kernels  20.8 us (9%)
  between operations  14.4 us (6%)
  local copies, waits for them, and re-layouts  10.7 us (4%)
    all_to_all x2, blocking collectives, exchange(): return lax.all_to_all(value, axes, split_axis=0, concat_axis=0, tiled=True)  62.8 us
    all_to_all x5, waiting for transfers between devices, exchange(): return lax.all_to_all(value, axes, split_axis=0, concat_axis=0, tiled=True)  38.9 us
    all_to_all x5, starting transfers between devices, exchange(): return lax.all_to_all(value, axes, split_axis=0, concat_axis=0, tiled=True)  34.3 us
    reduce_scatter x1, waiting for transfers between devices, per_device(): lax.psum_scatter(weight_sum(shared), 'zq', scatter_dimension=0, tiled=True)  25.8 us
    pallas_call x1, Pallas kernels, heads_backward(): pl.pallas_call(heads_kernel, out_shape=(half, half, jax.ShapeDtypeStruct(...  13 us
    ppermute x3, starting transfers between devices, per_device(): lax.ppermute(to_y[step - 1], 'y', [(i, (i + step) % Y) for i in range(Y)])  11.5 us
    ppermute x3, waiting for transfers between devices, per_device(): lax.ppermute(to_y[step - 1], 'y', [(i, (i + step) % Y) for i in range(Y)])  9.82 us
  transfers between devices with their start and end apart: 12, of which 8 were waited for; matrix products, arithmetic and copies ran while one was open for 3% of the time, Pallas kernels for 2%

profile of v9, /device:TPU:4, one launch (start us, length us, event | category | flops | bytes accessed | tf_op | source)
XLA Modules:
  0.0 240.3 jit_solution(2800390927303794834)
XLA Ops:
  7.2 2.0 split_columns.1
  9.2 4.5 %all-to-all-start = ((bf16[8,2,2,64,128]{4,3,2,1,0:T(8,128)(2,1)}), bf16[8,2,2,64,128]{4,3,2,1,0:T(8,128)(2,1)S(1)}, u32[]{:S(2)}, u32[]{:S(2)}) async-start(bf16[8,2,2,64,128]{4,3,2,1,0:T(8,128)(2,1)} %split_columns.1), calls=%async_computation | async-start | bytes 1048576 | tf_op jit(solution)/shard_map/all_to_all | solution.py:40
  15.7 8.3 %all-to-all-done = bf16[8,2,2,64,128]{4,3,2,1,0:T(8,128)(2,1)S(1)} async-done(((bf16[8,2,2,64,128]{4,3,2,1,0:T(8,128)(2,1)}), bf16[8,2,2,64,128]{4,3,2,1,0:T(8,128)(2,1)S(1)}, u32[]{:S(2)}, u32[]{:S(2)}) %all-to-all-start) | async-done | bytes 524320 | tf_op jit(solution)/shard_map/all_to_all | solution.py:40
  24.2 53.6 %all_to_all.35 = bf16[16,22,8,128]{3,2,1,0:T(8,128)(2,1)S(1)} all-to-all(bf16[16,22,8,128]{3,2,1,0:T(8,128)(2,1)S(1)} %pad_maximum_fusion), channel_id=1, replica_groups=mesh['x'=4,'y'=4,'c'=2,'zq'=8,'zr'=2] {'zq','zr'}, dimensions={0} | all-to-all | bytes 1441792 | tf_op jit(solution)/shard_map/all_to_all | solution.py:40
  78.7 9.2 %all_to_all.36 = bf16[8,2,6,8,128]{4,3,2,1,0:T(8,128)(2,1)S(1)} all-to-all(bf16[8,2,6,8,128]{4,3,2,1,0:T(8,128)(2,1)S(1)} %bitcast.93), channel_id=1, replica_groups=mesh['x'=4,'y'=4,'c'=2,'zq'=8,'zr'=2] {'y','c'}, dimensions={0} | all-to-all | bytes 393216 | tf_op jit(solution)/shard_map/all_to_all | solution.py:40
  89.5 6.4 %all-to-all-start.3 = ((bf16[8,8,16,640]{3,2,1,0:T(8,128)(2,1)}), bf16[8,8,16,640]{3,2,1,0:T(8,128)(2,1)S(1)}, u32[]{:S(2)}, u32[]{:S(2)}) async-start(bf16[8,8,16,640]{3,2,1,0:T(8,128)(2,1)} %broadcast_in_dim.62), calls=%async_computation.3 | async-start | bytes 2621440 | tf_op jit(solution)/shard_map/all_to_all | solution.py:40
  97.1 14.3 %all-to-all-done.3 = bf16[8,8,16,640]{3,2,1,0:T(8,128)(2,1)S(1)} async-done(((bf16[8,8,16,640]{3,2,1,0:T(8,128)(2,1)}), bf16[8,8,16,640]{3,2,1,0:T(8,128)(2,1)S(1)}, u32[]{:S(2)}, u32[]{:S(2)}) %all-to-all-start.3) | async-done | bytes 1310752 | tf_op jit(solution)/shard_map/all_to_all | solution.py:40
  112.6 13.0 %heads.1 = (bf16[4,128,1024]{2,1,0:T(8,128)(2,1)}, bf16[4,128,1024]{2,1,0:T(8,128)(2,1)}, bf16[4,8,2,16,640]{4,3,2,1,0:T(8,128)(2,1)}) custom-call(s32[4]{0:T(128)} %pad_add_fusion.info, bf16[8,2,1024,128]{3,2,1,0:T(8,128)(2,1)} %all-gather.2.cloned.1.call-done.packs, bf16[4,2,8,16,640]{4,3,2,1,0:T(8,128)(2,1)} %bitcast.92), custom_call_target="tpu_custom_call" | custom-call | flops 5000000000 | bytes 9000000 | tf_op jit(solution)/shard_map/heads/pallas_call | solution.py:204
  125.6 7.1 %all-to-all-start.4 = ((bf16[64,16,640]{2,1,0:T(8,128)(2,1)}), bf16[64,16,640]{2,1,0:T(8,128)(2,1)S(1)}, u32[]{:S(2)}, u32[]{:S(2)}) async-start(bf16[64,16,640]{2,1,0:T(8,128)(2,1)} %bitcast.91), calls=%async_computation.4 | async-start | bytes 2621440 | tf_op jit(solution)/shard_map/all_to_all | solution.py:40
  132.7 2.1 collective-permute-start.1
  134.8 2.7 %collective-permute-done.1.got = bf16[4,128,1024]{2,1,0:T(8,128)(2,1)S(1)} collective-permute-done((bf16[4,128,1024]{2,1,0:T(8,128)(2,1)}, bf16[4,128,1024]{2,1,0:T(8,128)(2,1)S(1)}, u32[]{:S(2)}, u32[]{:S(2)}) %collective-permute-start.1) | collective-permute-done | bytes 1048608 | tf_op jit(solution)/shard_map/ppermute | solution.py:469
  139.4 3.4 %collective-permute-start.2 = (bf16[128,1024]{1,0:T(8,128)(2,1)}, bf16[128,1024]{1,0:T(8,128)(2,1)S(1)}, u32[]{:S(2)}, u32[]{:S(2)}) collective-permute-start(bf16[128,1024]{1,0:T(8,128)(2,1)} %get-tuple-element.14), channel_id=1, source_target_pairs={{0,32},{32,64},{64,96},{96,0},{1,33},{33,65},{65,97},{97,1},{2,34}... | collective-permute-start | bytes 786440 | tf_op jit(solution)/shard_map/ppermute | solution.py:472
  142.8 4.6 %collective-permute-start.3 = (bf16[128,1024]{1,0:T(8,128)(2,1)}, bf16[128,1024]{1,0:T(8,128)(2,1)S(1)}, u32[]{:S(2)}, u32[]{:S(2)}) collective-permute-start(bf16[128,1024]{1,0:T(8,128)(2,1)} %get-tuple-element.15), channel_id=1, source_target_pairs={{0,64},{32,96},{64,0},{96,32},{1,65},{33,97},{65,1},{97,33},{2,66}... | collective-permute-start | bytes 786440 | tf_op jit(solution)/shard_map/ppermute | solution.py:472
  147.4 3.5 %collective-permute-start.4 = (bf16[128,1024]{1,0:T(8,128)(2,1)}, bf16[128,1024]{1,0:T(8,128)(2,1)S(1)}, u32[]{:S(2)}, u32[]{:S(2)}) collective-permute-start(bf16[128,1024]{1,0:T(8,128)(2,1)} %get-tuple-element.16), channel_id=1, source_target_pairs={{0,96},{32,0},{64,32},{96,64},{1,97},{33,1},{65,33},{97,65},{2,98}... | collective-permute-start | bytes 786440 | tf_op jit(solution)/shard_map/ppermute | solution.py:472
  151.9 4.2 %collective-permute-done.2.came_1 = bf16[128,1024]{1,0:T(8,128)(2,1)S(1)} collective-permute-done((bf16[128,1024]{1,0:T(8,128)(2,1)}, bf16[128,1024]{1,0:T(8,128)(2,1)S(1)}, u32[]{:S(2)}, u32[]{:S(2)}) %collective-permute-start.2) | collective-permute-done | bytes 262176 | tf_op jit(solution)/shard_map/ppermute | solution.py:472
  156.2 5.6 %collective-permute-done.3.came_2 = bf16[128,1024]{1,0:T(8,128)(2,1)S(1)} collective-permute-done((bf16[128,1024]{1,0:T(8,128)(2,1)}, bf16[128,1024]{1,0:T(8,128)(2,1)S(1)}, u32[]{:S(2)}, u32[]{:S(2)}) %collective-permute-start.3) | collective-permute-done | bytes 262176 | tf_op jit(solution)/shard_map/ppermute | solution.py:472
  163.7 10.5 %all-to-all-start.5 = ((bf16[16,64,128]{2,1,0:T(8,128)(2,1)}), bf16[16,64,128]{2,1,0:T(8,128)(2,1)S(1)}, u32[]{:S(2)}, u32[]{:S(2)}) async-start(bf16[16,64,128]{2,1,0:T(8,128)(2,1)} %payload.1), calls=%async_computation.6 | async-start | bytes 524288 | tf_op jit(solution)/shard_map/all_to_all | solution.py:40
  176.5 16.2 %all-to-all-done.5.merged = bf16[16,64,128]{2,1,0:T(8,128)(2,1)S(1)} async-done(((bf16[16,64,128]{2,1,0:T(8,128)(2,1)}), bf16[16,64,128]{2,1,0:T(8,128)(2,1)S(1)}, u32[]{:S(2)}, u32[]{:S(2)}) %all-to-all-start.5) | async-done | bytes 262176 | tf_op jit(solution)/shard_map/all_to_all | solution.py:40
  192.8 1.3 place.1
  194.1 5.7 %all-to-all-start.6 = ((bf16[32,80,128]{2,1,0:T(8,128)(2,1)}), bf16[32,80,128]{2,1,0:T(8,128)(2,1)S(1)}, u32[]{:S(2)}, u32[]{:S(2)}) async-start(bf16[32,80,128]{2,1,0:T(8,128)(2,1)} %place.1), calls=%async_computation.7 | async-start | bytes 1310720 | tf_op jit(solution)/shard_map/all_to_all | solution.py:40
  199.8 25.8 %reduce-scatter.2.cloned.1.call-done = f32[1,2,48,128]{3,2,1,0:T(8,128)} async-done(((f32[8,2,48,128]{3,2,1,0:T(8,128)}), f32[1,2,48,128]{3,2,1,0:T(8,128)}) %reduce-scatter.2.cloned.1.call-update) | async-done | bytes 49168 | tf_op jit(solution)/shard_map/reduce_scatter | solution.py:481
  226.3 2.5 %collective-permute-start = (f32[48,128]{1,0:T(8,128)S(1)}, f32[48,128]{1,0:T(8,128)S(1)}, u32[]{:S(2)}, u32[]{:S(2)}) collective-permute-start(f32[48,128]{1,0:T(8,128)S(1)} %get-tuple-element.24), channel_id=1, source_target_pairs={{0,1},{1,0},{2,3},{3,2},{4,5},{5,4},{6,7},{7,6},{8,9},{9,8},{10,11... | collective-permute-start | bytes 73736 | tf_op jit(solution)/shard_map/ppermute | solution.py:484
  228.9 1.5 table_sum.1
  230.3 1.7 collective-permute-done
  (85 shorter events, 16.0 us)
Async XLA Ops:
  7.2 6.9 %copy-start = (s32[8192]{0:T(1024)S(1)}, s32[8192]{0:T(1024)}, u32[]{:S(2)}) copy-start(s32[8192]{0:T(1024)} %param.11) | copy-start | bytes 98308
  7.2 6.6 %copy-start.7 = (s32[1,2,64]{2,1,0:T(2,128)S(1)}, s32[1,2,64]{2,1,0:T(2,128)}, u32[]{:S(2)}) copy-start(s32[1,2,64]{2,1,0:T(2,128)} %param.10) | copy-start | bytes 1540
  7.2 8.2 %copy-start.8 = (s32[1,2,3]{2,1,0:T(2,128)S(1)}, s32[1,2,3]{2,1,0:T(2,128)}, u32[]{:S(2)}) copy-start(s32[1,2,3]{2,1,0:T(2,128)} %param.9) | copy-start | bytes 76
  7.2 8.4 %copy-start.6 = (bf16[64,32]{0,1:T(8,128)(2,1)S(1)}, bf16[64,32]{0,1:T(8,128)(2,1)}, u32[]{:S(2)}) copy-start(bf16[64,32]{0,1:T(8,128)(2,1)} %param.13) | copy-start | bytes 12292
  7.2 8.5 %copy-start.5 = (bf16[32,256]{1,0:T(8,128)(2,1)S(1)}, bf16[32,256]{1,0:T(8,128)(2,1)}, u32[]{:S(2)}) copy-start(bf16[32,256]{1,0:T(8,128)(2,1)} %param.12) | copy-start | bytes 49156
  9.2 14.8 %all-to-all-start = ((bf16[8,2,2,64,128]{4,3,2,1,0:T(8,128)(2,1)}), bf16[8,2,2,64,128]{4,3,2,1,0:T(8,128)(2,1)S(1)}, u32[]{:S(2)}, u32[]{:S(2)}) async-start(bf16[8,2,2,64,128]{4,3,2,1,0:T(8,128)(2,1)} %split_columns.1), calls=%async_computation | async-start | bytes 1048576 | tf_op jit(solution)/shard_map/all_to_all | solution.py:40
  13.7 97.8 %all-gather.2.cloned.1.call-start = ((), (), s32[]{:S(2)}) async-start(), calls=%async_computation.8 | async-start | bytes 4718592 | tf_op jit(solution)/shard_map/all_gather | solution.py:439
  89.5 22.0 %all-to-all-start.3 = ((bf16[8,8,16,640]{3,2,1,0:T(8,128)(2,1)}), bf16[8,8,16,640]{3,2,1,0:T(8,128)(2,1)S(1)}, u32[]{:S(2)}, u32[]{:S(2)}) async-start(bf16[8,8,16,640]{3,2,1,0:T(8,128)(2,1)} %broadcast_in_dim.62), calls=%async_computation.3 | async-start | bytes 2621440 | tf_op jit(solution)/shard_map/all_to_all | solution.py:40
  111.5 1.1 copy-start.4
  125.6 11.9 %copy-start.1 = (bf16[4,128,1024]{2,1,0:T(8,128)(2,1)S(1)}, bf16[4,128,1024]{2,1,0:T(8,128)(2,1)}, u32[]{:S(2)}) copy-start(bf16[4,128,1024]{2,1,0:T(8,128)(2,1)} %get-tuple-element.11.kept) | copy-start | bytes 3145732
  125.6 38.1 %all-to-all-start.4 = ((bf16[64,16,640]{2,1,0:T(8,128)(2,1)}), bf16[64,16,640]{2,1,0:T(8,128)(2,1)S(1)}, u32[]{:S(2)}, u32[]{:S(2)}) async-start(bf16[64,16,640]{2,1,0:T(8,128)(2,1)} %bitcast.91), calls=%async_computation.4 | async-start | bytes 2621440 | tf_op jit(solution)/shard_map/all_to_all | solution.py:40
  132.7 4.8 %collective-permute-start.1 = (bf16[4,128,1024]{2,1,0:T(8,128)(2,1)}, bf16[4,128,1024]{2,1,0:T(8,128)(2,1)S(1)}, u32[]{:S(2)}, u32[]{:S(2)}) collective-permute-start(bf16[4,128,1024]{2,1,0:T(8,128)(2,1)} %get-tuple-element.12), channel_id=1, source_target_pairs={{0,16},{16,0},{1,17},{17,1},{2,18},{18,2},{3,19},{19,3},{4,20},{20... | collective-permute-start | bytes 3145736 | tf_op jit(solution)/shard_map/ppermute | solution.py:469
  138.7 0.7 copy-start.2
  139.4 16.8 %collective-permute-start.2 = (bf16[128,1024]{1,0:T(8,128)(2,1)}, bf16[128,1024]{1,0:T(8,128)(2,1)S(1)}, u32[]{:S(2)}, u32[]{:S(2)}) collective-permute-start(bf16[128,1024]{1,0:T(8,128)(2,1)} %get-tuple-element.14), channel_id=1, source_target_pairs={{0,32},{32,64},{64,96},{96,0},{1,33},{33,65},{65,97},{97,1},{2,34}... | collective-permute-start | bytes 786440 | tf_op jit(solution)/shard_map/ppermute | solution.py:472
  142.8 19.0 %collective-permute-start.3 = (bf16[128,1024]{1,0:T(8,128)(2,1)}, bf16[128,1024]{1,0:T(8,128)(2,1)S(1)}, u32[]{:S(2)}, u32[]{:S(2)}) collective-permute-start(bf16[128,1024]{1,0:T(8,128)(2,1)} %get-tuple-element.15), channel_id=1, source_target_pairs={{0,64},{32,96},{64,0},{96,32},{1,65},{33,97},{65,1},{97,33},{2,66}... | collective-permute-start | bytes 786440 | tf_op jit(solution)/shard_map/ppermute | solution.py:472
  147.4 14.3 %collective-permute-start.4 = (bf16[128,1024]{1,0:T(8,128)(2,1)}, bf16[128,1024]{1,0:T(8,128)(2,1)S(1)}, u32[]{:S(2)}, u32[]{:S(2)}) collective-permute-start(bf16[128,1024]{1,0:T(8,128)(2,1)} %get-tuple-element.16), channel_id=1, source_target_pairs={{0,96},{32,0},{64,32},{96,64},{1,97},{33,1},{65,33},{97,65},{2,98}... | collective-permute-start | bytes 786440 | tf_op jit(solution)/shard_map/ppermute | solution.py:472
  161.8 1.0 copy-start.3
  163.7 29.0 %all-to-all-start.5 = ((bf16[16,64,128]{2,1,0:T(8,128)(2,1)}), bf16[16,64,128]{2,1,0:T(8,128)(2,1)S(1)}, u32[]{:S(2)}, u32[]{:S(2)}) async-start(bf16[16,64,128]{2,1,0:T(8,128)(2,1)} %payload.1), calls=%async_computation.6 | async-start | bytes 524288 | tf_op jit(solution)/shard_map/all_to_all | solution.py:40
  174.3 51.3 %reduce-scatter.2.cloned.1.call-start = ((), (), s32[]{:S(2)}) async-start(), calls=%async_computation.9 | async-start | bytes 442368 | tf_op jit(solution)/shard_map/reduce_scatter | solution.py:481
  194.1 34.8 %all-to-all-start.6 = ((bf16[32,80,128]{2,1,0:T(8,128)(2,1)}), bf16[32,80,128]{2,1,0:T(8,128)(2,1)S(1)}, u32[]{:S(2)}, u32[]{:S(2)}) async-start(bf16[32,80,128]{2,1,0:T(8,128)(2,1)} %place.1), calls=%async_computation.7 | async-start | bytes 1310720 | tf_op jit(solution)/shard_map/all_to_all | solution.py:40
  226.3 5.7 %collective-permute-start = (f32[48,128]{1,0:T(8,128)S(1)}, f32[48,128]{1,0:T(8,128)S(1)}, u32[]{:S(2)}, u32[]{:S(2)}) collective-permute-start(f32[48,128]{1,0:T(8,128)S(1)} %get-tuple-element.24), channel_id=1, source_target_pairs={{0,1},{1,0},{2,3},{3,2},{4,5},{5,4},{6,7},{7,6},{8,9},{9,8},{10,11... | collective-permute-start | bytes 73736 | tf_op jit(solution)/shard_map/ppermute | solution.py:484
Sparse Core Ops, SparseCore 0:
  78.8 32.0 all-gather.1
  177.9 47.6 reduce-scatter.1

commit v10 on v9

--- a/solution.py
+++ b/solution.py
@@ -291,6 +291,7 @@
 
 
 def weight_sum_kernel(shared, out):
+    out[..., LANES:] = jnp.zeros((YC, 2, 3 * PART_ROWS, LANES), F32)
     for h in range(YC):
         total = jnp.zeros((PART_ROWS, HIDDEN), F32)
         for x in range(X):
@@ -299,13 +300,14 @@
         for s in range(2):
             for n, col in enumerate((2 * s, 2 * s + 1, 4)):
                 first = n * PART_ROWS
-                out[h, s, first : first + PART_ROWS, :] = total[:, col * LANES : (col + 1) * LANES]
+                block = total[:, col * LANES : (col + 1) * LANES]
+                out[h, s, first : first + PART_ROWS, :LANES] = block
 
 
 def weight_sum(shared):
     return pl.pallas_call(
         weight_sum_kernel,
-        out_shape=jax.ShapeDtypeStruct((YC, 2, 3 * PART_ROWS, LANES), F32),
+        out_shape=jax.ShapeDtypeStruct((YC, 2, 3 * PART_ROWS, 2 * LANES), F32),
         in_specs=[VMEM_SPEC],
         out_specs=VMEM_SPEC,
         compiler_params=pltpu.CompilerParams(vmem_limit_bytes=32 * 2**20),
@@ -475,10 +477,12 @@
     block = (y_here * C + core) * LANES
     dy_own = lax.dynamic_slice(packs, (0, 1, block, 0), (YC, 1, LANES, LANES))[:, 0]
 
+    w_sum, came[0] = lax.optimization_barrier((weight_sum(shared), came[0]))
     merged = exchange(payload(own, came, dy_own), SEQ)
 
     low = lax.axis_index("zr")
-    rest = lax.psum_scatter(weight_sum(shared), "zq", scatter_dimension=0, tiled=True)[0]
+    rest = lax.psum_scatter(w_sum, "zq", scatter_dimension=0, tiled=True)
+    rest = rest[0, :, :, :LANES]
     mine = lax.dynamic_index_in_dim(rest, low, 0, keepdims=False)
     other = lax.dynamic_index_in_dim(rest, 1 - low, 0, keepdims=False)
     other = lax.ppermute(other, "zr", [(0, 1), (1, 0)])

time: 241 us -> 237 us (0.983)
  the two profiles are of different devices: /device:TPU:4 before, /device:TPU:1 now
where the time goes in v10:
time: 237 us; the launch traced here: 236 us
  waiting for transfers between devices  74.2 us (31%)
  blocking collectives  58.4 us (25%)
  starting transfers between devices  55.3 us (23%)
  Pallas kernels  20.7 us (9%)
  between operations  14.4 us (6%)
  local copies, waits for them, and re-layouts  11.2 us (5%)
    all_to_all x2, blocking collectives, exchange(): return lax.all_to_all(value, axes, split_axis=0, concat_axis=0, tiled=True)  58.4 us
    all_to_all x5, waiting for transfers between devices, exchange(): return lax.all_to_all(value, axes, split_axis=0, concat_axis=0, tiled=True)  56.8 us
    all_to_all x5, starting transfers between devices, exchange(): return lax.all_to_all(value, axes, split_axis=0, concat_axis=0, tiled=True)  42.1 us
    ppermute x3, waiting for transfers between devices, per_device(): lax.ppermute(to_y[step - 1], 'y', [(i, (i + step) % Y) for i in range(Y)])  13.2 us
    pallas_call x1, Pallas kernels, heads_backward(): pl.pallas_call(heads_kernel, out_shape=(half, half, jax.ShapeDtypeStruct(...  13 us
    ppermute x3, starting transfers between devices, per_device(): lax.ppermute(to_y[step - 1], 'y', [(i, (i + step) % Y) for i in range(Y)])  7.5 us
  transfers between devices with their start and end apart: 12, of which 10 were waited for; matrix products, arithmetic and copies ran while one was open for 4% of the time, Pallas kernels for 2%

profile of v10, /device:TPU:1, one launch (start us, length us, event | category | flops | bytes accessed | tf_op | source)
XLA Modules:
  0.0 236.4 jit_solution(13100048618837956392)
XLA Ops:
  7.2 2.0 split_columns.1
  9.2 10.3 %all-to-all-start = ((bf16[8,2,2,64,128]{4,3,2,1,0:T(8,128)(2,1)}), bf16[8,2,2,64,128]{4,3,2,1,0:T(8,128)(2,1)S(1)}, u32[]{:S(2)}, u32[]{:S(2)}) async-start(bf16[8,2,2,64,128]{4,3,2,1,0:T(8,128)(2,1)} %split_columns.1), calls=%async_computation | async-start | bytes 1048576 | tf_op jit(solution)/shard_map/all_to_all | solution.py:40
  21.5 7.5 %all-to-all-done = bf16[8,2,2,64,128]{4,3,2,1,0:T(8,128)(2,1)S(1)} async-done(((bf16[8,2,2,64,128]{4,3,2,1,0:T(8,128)(2,1)}), bf16[8,2,2,64,128]{4,3,2,1,0:T(8,128)(2,1)S(1)}, u32[]{:S(2)}, u32[]{:S(2)}) %all-to-all-start) | async-done | bytes 524320 | tf_op jit(solution)/shard_map/all_to_all | solution.py:40
  29.1 44.5 %all_to_all.35 = bf16[16,22,8,128]{3,2,1,0:T(8,128)(2,1)S(1)} all-to-all(bf16[16,22,8,128]{3,2,1,0:T(8,128)(2,1)S(1)} %pad_maximum_fusion), channel_id=1, replica_groups=mesh['x'=4,'y'=4,'c'=2,'zq'=8,'zr'=2] {'zq','zr'}, dimensions={0} | all-to-all | bytes 1441792 | tf_op jit(solution)/shard_map/all_to_all | solution.py:40
  74.5 13.9 %all_to_all.36 = bf16[8,2,6,8,128]{4,3,2,1,0:T(8,128)(2,1)S(1)} all-to-all(bf16[8,2,6,8,128]{4,3,2,1,0:T(8,128)(2,1)S(1)} %bitcast.93), channel_id=1, replica_groups=mesh['x'=4,'y'=4,'c'=2,'zq'=8,'zr'=2] {'y','c'}, dimensions={0} | all-to-all | bytes 393216 | tf_op jit(solution)/shard_map/all_to_all | solution.py:40
  90.0 5.6 %all-to-all-start.3 = ((bf16[8,8,16,640]{3,2,1,0:T(8,128)(2,1)}), bf16[8,8,16,640]{3,2,1,0:T(8,128)(2,1)S(1)}, u32[]{:S(2)}, u32[]{:S(2)}) async-start(bf16[8,8,16,640]{3,2,1,0:T(8,128)(2,1)} %broadcast_in_dim.62), calls=%async_computation.3 | async-start | bytes 2621440 | tf_op jit(solution)/shard_map/all_to_all | solution.py:40
  96.9 15.8 %all-to-all-done.3 = bf16[8,8,16,640]{3,2,1,0:T(8,128)(2,1)S(1)} async-done(((bf16[8,8,16,640]{3,2,1,0:T(8,128)(2,1)}), bf16[8,8,16,640]{3,2,1,0:T(8,128)(2,1)S(1)}, u32[]{:S(2)}, u32[]{:S(2)}) %all-to-all-start.3) | async-done | bytes 1310752 | tf_op jit(solution)/shard_map/all_to_all | solution.py:40
  113.8 13.0 %heads.1 = (bf16[4,128,1024]{2,1,0:T(8,128)(2,1)}, bf16[4,128,1024]{2,1,0:T(8,128)(2,1)}, bf16[4,8,2,16,640]{4,3,2,1,0:T(8,128)(2,1)}) custom-call(s32[4]{0:T(128)} %pad_add_fusion.info, bf16[8,2,1024,128]{3,2,1,0:T(8,128)(2,1)} %all-gather.2.cloned.1.call-done.packs, bf16[4,2,8,16,640]{4,3,2,1,0:T(8,128)(2,1)} %bitcast.91), custom_call_target="tpu_custom_call" | custom-call | flops 5000000000 | bytes 9000000 | tf_op jit(solution)/shard_map/heads/pallas_call | solution.py:204
  126.8 6.7 %all-to-all-start.4 = ((bf16[64,16,640]{2,1,0:T(8,128)(2,1)}), bf16[64,16,640]{2,1,0:T(8,128)(2,1)S(1)}, u32[]{:S(2)}, u32[]{:S(2)}) async-start(bf16[64,16,640]{2,1,0:T(8,128)(2,1)} %bitcast.92), calls=%async_computation.4 | async-start | bytes 2621440 | tf_op jit(solution)/shard_map/all_to_all | solution.py:40
  133.5 2.5 %collective-permute-start = (bf16[4,128,1024]{2,1,0:T(8,128)(2,1)}, bf16[4,128,1024]{2,1,0:T(8,128)(2,1)S(1)}, u32[]{:S(2)}, u32[]{:S(2)}) collective-permute-start(bf16[4,128,1024]{2,1,0:T(8,128)(2,1)} %get-tuple-element.14), channel_id=1, source_target_pairs={{0,16},{16,0},{1,17},{17,1},{2,18},{18,2},{3,19},{19,3},{4,20},{20... | collective-permute-start | bytes 3145736 | tf_op jit(solution)/shard_map/ppermute | solution.py:471
  136.0 2.5 %collective-permute-done.got = bf16[4,128,1024]{2,1,0:T(8,128)(2,1)S(1)} collective-permute-done((bf16[4,128,1024]{2,1,0:T(8,128)(2,1)}, bf16[4,128,1024]{2,1,0:T(8,128)(2,1)S(1)}, u32[]{:S(2)}, u32[]{:S(2)}) %collective-permute-start) | collective-permute-done | bytes 1048608 | tf_op jit(solution)/shard_map/ppermute | solution.py:471
  141.6 3.4 %collective-permute-start.1 = (bf16[128,1024]{1,0:T(8,128)(2,1)}, bf16[128,1024]{1,0:T(8,128)(2,1)S(1)}, u32[]{:S(2)}, u32[]{:S(2)}) collective-permute-start(bf16[128,1024]{1,0:T(8,128)(2,1)} %get-tuple-element.15), channel_id=1, source_target_pairs={{0,32},{32,64},{64,96},{96,0},{1,33},{33,65},{65,97},{97,1},{2,34}... | collective-permute-start | bytes 786440 | tf_op jit(solution)/shard_map/ppermute | solution.py:474
  145.0 8.6 %all-to-all-done.4 = bf16[64,16,640]{2,1,0:T(8,128)(2,1)S(1)} async-done(((bf16[64,16,640]{2,1,0:T(8,128)(2,1)}), bf16[64,16,640]{2,1,0:T(8,128)(2,1)S(1)}, u32[]{:S(2)}, u32[]{:S(2)}) %all-to-all-start.4) | async-done | bytes 1310752 | tf_op jit(solution)/shard_map/all_to_all | solution.py:40
  154.7 4.0 %collective-permute-done.1.came_1 = bf16[128,1024]{1,0:T(8,128)(2,1)S(1)} collective-permute-done((bf16[128,1024]{1,0:T(8,128)(2,1)}, bf16[128,1024]{1,0:T(8,128)(2,1)S(1)}, u32[]{:S(2)}, u32[]{:S(2)}) %collective-permute-start.1) | collective-permute-done | bytes 262176 | tf_op jit(solution)/shard_map/ppermute | solution.py:474
  158.7 1.9 collective-permute-start.3
  160.7 2.2 collective-permute-start.4
  163.8 5.8 %collective-permute-done.3.came_2 = bf16[128,1024]{1,0:T(8,128)(2,1)S(1)} collective-permute-done((bf16[128,1024]{1,0:T(8,128)(2,1)S(1)}, bf16[128,1024]{1,0:T(8,128)(2,1)S(1)}, u32[]{:S(2)}, u32[]{:S(2)}) %collective-permute-start.3) | collective-permute-done | bytes 262176 | tf_op jit(solution)/shard_map/ppermute | solution.py:474
  169.6 3.4 %collective-permute-done.4.came_3 = bf16[128,1024]{1,0:T(8,128)(2,1)S(1)} collective-permute-done((bf16[128,1024]{1,0:T(8,128)(2,1)S(1)}, bf16[128,1024]{1,0:T(8,128)(2,1)S(1)}, u32[]{:S(2)}, u32[]{:S(2)}) %collective-permute-start.4) | collective-permute-done | bytes 262176 | tf_op jit(solution)/shard_map/ppermute | solution.py:474
  174.0 10.0 %all-to-all-start.5 = ((bf16[16,64,128]{2,1,0:T(8,128)(2,1)}), bf16[16,64,128]{2,1,0:T(8,128)(2,1)S(1)}, u32[]{:S(2)}, u32[]{:S(2)}) async-start(bf16[16,64,128]{2,1,0:T(8,128)(2,1)} %payload.1), calls=%async_computation.6 | async-start | bytes 524288 | tf_op jit(solution)/shard_map/all_to_all | solution.py:40
  185.3 19.1 %all-to-all-done.5.merged = bf16[16,64,128]{2,1,0:T(8,128)(2,1)S(1)} async-done(((bf16[16,64,128]{2,1,0:T(8,128)(2,1)}), bf16[16,64,128]{2,1,0:T(8,128)(2,1)S(1)}, u32[]{:S(2)}, u32[]{:S(2)}) %all-to-all-start.5) | async-done | bytes 262176 | tf_op jit(solution)/shard_map/all_to_all | solution.py:40
  205.6 9.5 %all-to-all-start.6 = ((bf16[32,80,128]{2,1,0:T(8,128)(2,1)}), bf16[32,80,128]{2,1,0:T(8,128)(2,1)S(1)}, u32[]{:S(2)}, u32[]{:S(2)}) async-start(bf16[32,80,128]{2,1,0:T(8,128)(2,1)} %place.1), calls=%async_computation.7 | async-start | bytes 1310720 | tf_op jit(solution)/shard_map/all_to_all | solution.py:40
  216.0 3.2 %collective-permute-start.2 = (f32[48,128]{1,0:T(8,128)S(1)}, f32[48,128]{1,0:T(8,128)S(1)}, u32[]{:S(2)}, u32[]{:S(2)}) collective-permute-start(f32[48,128]{1,0:T(8,128)S(1)} %get-tuple-element.28), channel_id=1, source_target_pairs={{0,1},{1,0},{2,3},{3,2},{4,5},{5,4},{6,7},{7,6},{8,9},{9,8},{10,11... | collective-permute-start | bytes 73736 | tf_op jit(solution)/shard_map/ppermute | solution.py:488
  219.2 1.7 collective-permute-done.2
  222.2 5.9 %all-to-all-done.6.owned = bf16[32,80,128]{2,1,0:T(8,128)(2,1)S(1)} async-done(((bf16[32,80,128]{2,1,0:T(8,128)(2,1)}), bf16[32,80,128]{2,1,0:T(8,128)(2,1)S(1)}, u32[]{:S(2)}, u32[]{:S(2)}) %all-to-all-start.6) | async-done | bytes 655392 | tf_op jit(solution)/shard_map/all_to_all | solution.py:40
  (94 shorter events, 19.1 us)
Async XLA Ops:
  7.2 12.6 %copy-start = (s32[8192]{0:T(1024)S(1)}, s32[8192]{0:T(1024)}, u32[]{:S(2)}) copy-start(s32[8192]{0:T(1024)} %param.11) | copy-start | bytes 98308
  7.2 12.3 %copy-start.11 = (s32[1,2,64]{2,1,0:T(2,128)S(1)}, s32[1,2,64]{2,1,0:T(2,128)}, u32[]{:S(2)}) copy-start(s32[1,2,64]{2,1,0:T(2,128)} %param.10) | copy-start | bytes 1540
  7.2 13.9 %copy-start.12 = (s32[1,2,3]{2,1,0:T(2,128)S(1)}, s32[1,2,3]{2,1,0:T(2,128)}, u32[]{:S(2)}) copy-start(s32[1,2,3]{2,1,0:T(2,128)} %param.9) | copy-start | bytes 76
  7.2 14.1 %copy-start.10 = (bf16[64,32]{0,1:T(8,128)(2,1)S(1)}, bf16[64,32]{0,1:T(8,128)(2,1)}, u32[]{:S(2)}) copy-start(bf16[64,32]{0,1:T(8,128)(2,1)} %param.13) | copy-start | bytes 12292
  7.2 14.3 %copy-start.9 = (bf16[32,256]{1,0:T(8,128)(2,1)S(1)}, bf16[32,256]{1,0:T(8,128)(2,1)}, u32[]{:S(2)}) copy-start(bf16[32,256]{1,0:T(8,128)(2,1)} %param.12) | copy-start | bytes 49156
  9.2 19.8 %all-to-all-start = ((bf16[8,2,2,64,128]{4,3,2,1,0:T(8,128)(2,1)}), bf16[8,2,2,64,128]{4,3,2,1,0:T(8,128)(2,1)S(1)}, u32[]{:S(2)}, u32[]{:S(2)}) async-start(bf16[8,2,2,64,128]{4,3,2,1,0:T(8,128)(2,1)} %split_columns.1), calls=%async_computation | async-start | bytes 1048576 | tf_op jit(solution)/shard_map/all_to_all | solution.py:40
  19.5 93.2 %all-gather.2.cloned.1.call-start = ((), (), s32[]{:S(2)}) async-start(), calls=%async_computation.8 | async-start | bytes 4718592 | tf_op jit(solution)/shard_map/all_gather | solution.py:441
  90.0 22.7 %all-to-all-start.3 = ((bf16[8,8,16,640]{3,2,1,0:T(8,128)(2,1)}), bf16[8,8,16,640]{3,2,1,0:T(8,128)(2,1)S(1)}, u32[]{:S(2)}, u32[]{:S(2)}) async-start(bf16[8,8,16,640]{3,2,1,0:T(8,128)(2,1)} %broadcast_in_dim.62), calls=%async_computation.3 | async-start | bytes 2621440 | tf_op jit(solution)/shard_map/all_to_all | solution.py:40
  112.7 1.1 copy-start.8
  126.8 11.7 %copy-start.1 = (bf16[4,128,1024]{2,1,0:T(8,128)(2,1)S(1)}, bf16[4,128,1024]{2,1,0:T(8,128)(2,1)}, u32[]{:S(2)}) copy-start(bf16[4,128,1024]{2,1,0:T(8,128)(2,1)} %get-tuple-element.13.kept) | copy-start | bytes 3145732
  126.8 26.8 %all-to-all-start.4 = ((bf16[64,16,640]{2,1,0:T(8,128)(2,1)}), bf16[64,16,640]{2,1,0:T(8,128)(2,1)S(1)}, u32[]{:S(2)}, u32[]{:S(2)}) async-start(bf16[64,16,640]{2,1,0:T(8,128)(2,1)} %bitcast.92), calls=%async_computation.4 | async-start | bytes 2621440 | tf_op jit(solution)/shard_map/all_to_all | solution.py:40
  133.5 81.7 %reduce-scatter.2.cloned.1.call-start = ((), (), s32[]{:S(2)}) async-start(), calls=%async_computation.9 | async-start | bytes 884736 | tf_op jit(solution)/shard_map/reduce_scatter | solution.py:484
  133.5 5.0 %collective-permute-start = (bf16[4,128,1024]{2,1,0:T(8,128)(2,1)}, bf16[4,128,1024]{2,1,0:T(8,128)(2,1)S(1)}, u32[]{:S(2)}, u32[]{:S(2)}) collective-permute-start(bf16[4,128,1024]{2,1,0:T(8,128)(2,1)} %get-tuple-element.14), channel_id=1, source_target_pairs={{0,16},{16,0},{1,17},{17,1},{2,18},{18,2},{3,19},{19,3},{4,20},{20... | collective-permute-start | bytes 3145736 | tf_op jit(solution)/shard_map/ppermute | solution.py:471
  139.5 0.7 copy-start.2
  140.9 0.7 copy-start.6
  141.6 17.1 %copy-start.7 = (bf16[128,1024]{1,0:T(8,128)(2,1)S(1)}, bf16[128,1024]{1,0:T(8,128)(2,1)}, u32[]{:S(2)}) copy-start(bf16[128,1024]{1,0:T(8,128)(2,1)} %copy-done.6) | copy-start | bytes 786436
  141.6 19.0 %copy-start.5 = (bf16[128,1024]{1,0:T(8,128)(2,1)S(1)}, bf16[128,1024]{1,0:T(8,128)(2,1)}, u32[]{:S(2)}) copy-start(bf16[128,1024]{1,0:T(8,128)(2,1)} %copy-done.4) | copy-start | bytes 786436
  141.6 31.4 %copy-start.3 = (bf16[128,1024]{1,0:T(8,128)(2,1)S(1)}, bf16[128,1024]{1,0:T(8,128)(2,1)}, u32[]{:S(2)}) copy-start(bf16[128,1024]{1,0:T(8,128)(2,1)} %copy-done.2) | copy-start | bytes 786436
  141.6 17.1 %collective-permute-start.1 = (bf16[128,1024]{1,0:T(8,128)(2,1)}, bf16[128,1024]{1,0:T(8,128)(2,1)S(1)}, u32[]{:S(2)}, u32[]{:S(2)}) collective-permute-start(bf16[128,1024]{1,0:T(8,128)(2,1)} %get-tuple-element.15), channel_id=1, source_target_pairs={{0,32},{32,64},{64,96},{96,0},{1,33},{33,65},{65,97},{97,1},{2,34}... | collective-permute-start | bytes 786440 | tf_op jit(solution)/shard_map/ppermute | solution.py:474
  158.7 10.9 %collective-permute-start.3 = (bf16[128,1024]{1,0:T(8,128)(2,1)S(1)}, bf16[128,1024]{1,0:T(8,128)(2,1)S(1)}, u32[]{:S(2)}, u32[]{:S(2)}) collective-permute-start(bf16[128,1024]{1,0:T(8,128)(2,1)S(1)} %copy-done.7), channel_id=1, source_target_pairs={{0,64},{32,96},{64,0},{96,32},{1,65},{33,97},{65,1},{97,33},{2,66}... | collective-permute-start | bytes 786440 | tf_op jit(solution)/shard_map/ppermute | solution.py:474
  160.7 12.3 %collective-permute-start.4 = (bf16[128,1024]{1,0:T(8,128)(2,1)S(1)}, bf16[128,1024]{1,0:T(8,128)(2,1)S(1)}, u32[]{:S(2)}, u32[]{:S(2)}) collective-permute-start(bf16[128,1024]{1,0:T(8,128)(2,1)S(1)} %copy-done.5), channel_id=1, source_target_pairs={{0,96},{32,0},{64,32},{96,64},{1,97},{33,1},{65,33},{97,65},{2,98}... | collective-permute-start | bytes 786440 | tf_op jit(solution)/shard_map/ppermute | solution.py:474
  174.0 30.4 %all-to-all-start.5 = ((bf16[16,64,128]{2,1,0:T(8,128)(2,1)}), bf16[16,64,128]{2,1,0:T(8,128)(2,1)S(1)}, u32[]{:S(2)}, u32[]{:S(2)}) async-start(bf16[16,64,128]{2,1,0:T(8,128)(2,1)} %payload.1), calls=%async_computation.6 | async-start | bytes 524288 | tf_op jit(solution)/shard_map/all_to_all | solution.py:40
  205.6 22.4 %all-to-all-start.6 = ((bf16[32,80,128]{2,1,0:T(8,128)(2,1)}), bf16[32,80,128]{2,1,0:T(8,128)(2,1)S(1)}, u32[]{:S(2)}, u32[]{:S(2)}) async-start(bf16[32,80,128]{2,1,0:T(8,128)(2,1)} %place.1), calls=%async_computation.7 | async-start | bytes 1310720 | tf_op jit(solution)/shard_map/all_to_all | solution.py:40
  216.0 4.9 %collective-permute-start.2 = (f32[48,128]{1,0:T(8,128)S(1)}, f32[48,128]{1,0:T(8,128)S(1)}, u32[]{:S(2)}, u32[]{:S(2)}) collective-permute-start(f32[48,128]{1,0:T(8,128)S(1)} %get-tuple-element.28), channel_id=1, source_target_pairs={{0,1},{1,0},{2,3},{3,2},{4,5},{5,4},{6,7},{7,6},{8,9},{9,8},{10,11... | collective-permute-start | bytes 73736 | tf_op jit(solution)/shard_map/ppermute | solution.py:488
  (1 other events, 0.7 us)
Sparse Core Ops, SparseCore 0:
  74.6 37.4 all-gather.1
  158.8 49.3 reduce-scatter.1

commit v11 on v10

--- a/solution.py
+++ b/solution.py
@@ -290,7 +290,8 @@
     )(own, *came, dy)
 
 
-def weight_sum_kernel(shared, out):
+def weight_sum_kernel(shared, out, done):
+    done[...] = jnp.zeros_like(done)
     out[..., LANES:] = jnp.zeros((YC, 2, 3 * PART_ROWS, LANES), F32)
     for h in range(YC):
         total = jnp.zeros((PART_ROWS, HIDDEN), F32)
@@ -307,9 +308,12 @@
 def weight_sum(shared):
     return pl.pallas_call(
         weight_sum_kernel,
-        out_shape=jax.ShapeDtypeStruct((YC, 2, 3 * PART_ROWS, 2 * LANES), F32),
+        out_shape=(
+            jax.ShapeDtypeStruct((YC, 2, 3 * PART_ROWS, 2 * LANES), F32),
+            jax.ShapeDtypeStruct((8, LANES), F32),
+        ),
         in_specs=[VMEM_SPEC],
-        out_specs=VMEM_SPEC,
+        out_specs=(VMEM_SPEC, VMEM_SPEC),
         compiler_params=pltpu.CompilerParams(vmem_limit_bytes=32 * 2**20),
         cost_estimate=pl.CostEstimate(flops=700_000, bytes_accessed=1_700_000, transcendentals=0),
         name="weight_sum",
@@ -477,7 +481,8 @@
     block = (y_here * C + core) * LANES
     dy_own = lax.dynamic_slice(packs, (0, 1, block, 0), (YC, 1, LANES, LANES))[:, 0]
 
-    w_sum, came[0] = lax.optimization_barrier((weight_sum(shared), came[0]))
+    w_sum, done = weight_sum(shared)
+    done, *came = lax.optimization_barrier((done, *came))
     merged = exchange(payload(own, came, dy_own), SEQ)
 
     low = lax.axis_index("zr")

time: 237 us -> 229 us (0.966)
  waiting for transfers between devices: 74.2 us -> 64.1 us
  starting transfers between devices: 55.3 us -> 58.1 us
    all_to_all x5, waiting for transfers between devices: 56.8 us -> 51.3 us  [exchange(): return lax.all_to_all(value, axes, split_axis=0, concat_axis=0, tiled=True)]
    ppermute x3, waiting for transfers between devices: 13.2 us -> 8.55 us  [per_device(): lax.ppermute(to_y[step - 1], 'y', [(i, (i + step) % Y) for i in range(Y)])]
    ppermute x3, starting transfers between devices: 7.5 us -> 10.8 us  [per_device(): lax.ppermute(to_y[step - 1], 'y', [(i, (i + step) % Y) for i in range(Y)])]
  transfers between devices with their start and end apart: 12 -> 12, of which waited for: 10 -> 9; matrix products, arithmetic and copies ran while one was open for 4% -> 3% of each run, Pallas kernels for 2% -> 3%
where the time goes in v11:
time: 229 us; the launch traced here: 228 us
  waiting for transfers between devices  64.1 us (28%)
  blocking collectives  58.4 us (26%)
  starting transfers between devices  58.1 us (25%)
  Pallas kernels  20.9 us (9%)
  between operations  14.4 us (6%)
  local copies, waits for them, and re-layouts  9.77 us (4%)
    all_to_all x2, blocking collectives, exchange(): return lax.all_to_all(value, axes, split_axis=0, concat_axis=0, tiled=True)  58.4 us
    all_to_all x5, waiting for transfers between devices, exchange(): return lax.all_to_all(value, axes, split_axis=0, concat_axis=0, tiled=True)  51.3 us
    all_to_all x5, starting transfers between devices, exchange(): return lax.all_to_all(value, axes, split_axis=0, concat_axis=0, tiled=True)  42.8 us
    pallas_call x1, Pallas kernels, heads_backward(): pl.pallas_call(heads_kernel, out_shape=(half, half, jax.ShapeDtypeStruct(...  13 us
    ppermute x3, starting transfers between devices, per_device(): lax.ppermute(to_y[step - 1], 'y', [(i, (i + step) % Y) for i in range(Y)])  10.8 us
    ppermute x3, waiting for transfers between devices, per_device(): lax.ppermute(to_y[step - 1], 'y', [(i, (i + step) % Y) for i in range(Y)])  8.55 us
  transfers between devices with their start and end apart: 12, of which 9 were waited for; matrix products, arithmetic and copies ran while one was open for 3% of the time, Pallas kernels for 3%

profile of v11, /device:TPU:1, one launch (start us, length us, event | category | flops | bytes accessed | tf_op | source)
XLA Modules:
  0.0 227.9 jit_solution(11011979140856081405)
XLA Ops:
  7.2 2.0 split_columns.1
  9.2 10.3 %all-to-all-start = ((bf16[8,2,2,64,128]{4,3,2,1,0:T(8,128)(2,1)}), bf16[8,2,2,64,128]{4,3,2,1,0:T(8,128)(2,1)S(1)}, u32[]{:S(2)}, u32[]{:S(2)}) async-start(bf16[8,2,2,64,128]{4,3,2,1,0:T(8,128)(2,1)} %split_columns.1), calls=%async_computation | async-start | bytes 1048576 | tf_op jit(solution)/shard_map/all_to_all | solution.py:40
  21.5 7.5 %all-to-all-done = bf16[8,2,2,64,128]{4,3,2,1,0:T(8,128)(2,1)S(1)} async-done(((bf16[8,2,2,64,128]{4,3,2,1,0:T(8,128)(2,1)}), bf16[8,2,2,64,128]{4,3,2,1,0:T(8,128)(2,1)S(1)}, u32[]{:S(2)}, u32[]{:S(2)}) %all-to-all-start) | async-done | bytes 524320 | tf_op jit(solution)/shard_map/all_to_all | solution.py:40
  29.1 44.5 %all_to_all.35 = bf16[16,22,8,128]{3,2,1,0:T(8,128)(2,1)S(1)} all-to-all(bf16[16,22,8,128]{3,2,1,0:T(8,128)(2,1)S(1)} %pad_maximum_fusion), channel_id=1, replica_groups=mesh['x'=4,'y'=4,'c'=2,'zq'=8,'zr'=2] {'zq','zr'}, dimensions={0} | all-to-all | bytes 1441792 | tf_op jit(solution)/shard_map/all_to_all | solution.py:40
  74.5 13.9 %all_to_all.36 = bf16[8,2,6,8,128]{4,3,2,1,0:T(8,128)(2,1)S(1)} all-to-all(bf16[8,2,6,8,128]{4,3,2,1,0:T(8,128)(2,1)S(1)} %bitcast.93), channel_id=1, replica_groups=mesh['x'=4,'y'=4,'c'=2,'zq'=8,'zr'=2] {'y','c'}, dimensions={0} | all-to-all | bytes 393216 | tf_op jit(solution)/shard_map/all_to_all | solution.py:40
  90.0 5.6 %all-to-all-start.3 = ((bf16[8,8,16,640]{3,2,1,0:T(8,128)(2,1)}), bf16[8,8,16,640]{3,2,1,0:T(8,128)(2,1)S(1)}, u32[]{:S(2)}, u32[]{:S(2)}) async-start(bf16[8,8,16,640]{3,2,1,0:T(8,128)(2,1)} %broadcast_in_dim.62), calls=%async_computation.3 | async-start | bytes 2621440 | tf_op jit(solution)/shard_map/all_to_all | solution.py:40
  96.9 15.8 %all-to-all-done.3 = bf16[8,8,16,640]{3,2,1,0:T(8,128)(2,1)S(1)} async-done(((bf16[8,8,16,640]{3,2,1,0:T(8,128)(2,1)}), bf16[8,8,16,640]{3,2,1,0:T(8,128)(2,1)S(1)}, u32[]{:S(2)}, u32[]{:S(2)}) %all-to-all-start.3) | async-done | bytes 1310752 | tf_op jit(solution)/shard_map/all_to_all | solution.py:40
  113.8 13.0 %heads.1 = (bf16[4,128,1024]{2,1,0:T(8,128)(2,1)}, bf16[4,128,1024]{2,1,0:T(8,128)(2,1)}, bf16[4,8,2,16,640]{4,3,2,1,0:T(8,128)(2,1)}) custom-call(s32[4]{0:T(128)} %pad_add_fusion.info, bf16[8,2,1024,128]{3,2,1,0:T(8,128)(2,1)} %all-gather.2.cloned.1.call-done.packs, bf16[4,2,8,16,640]{4,3,2,1,0:T(8,128)(2,1)} %bitcast.91), custom_call_target="tpu_custom_call" | custom-call | flops 5000000000 | bytes 9000000 | tf_op jit(solution)/shard_map/heads/pallas_call | solution.py:204
  126.8 6.7 %all-to-all-start.4 = ((bf16[64,16,640]{2,1,0:T(8,128)(2,1)}), bf16[64,16,640]{2,1,0:T(8,128)(2,1)S(1)}, u32[]{:S(2)}, u32[]{:S(2)}) async-start(bf16[64,16,640]{2,1,0:T(8,128)(2,1)} %bitcast.92), calls=%async_computation.4 | async-start | bytes 2621440 | tf_op jit(solution)/shard_map/all_to_all | solution.py:40
  133.5 2.5 %collective-permute-start.1 = (bf16[4,128,1024]{2,1,0:T(8,128)(2,1)}, bf16[4,128,1024]{2,1,0:T(8,128)(2,1)S(1)}, u32[]{:S(2)}, u32[]{:S(2)}) collective-permute-start(bf16[4,128,1024]{2,1,0:T(8,128)(2,1)} %get-tuple-element.17), channel_id=1, source_target_pairs={{0,16},{16,0},{1,17},{17,1},{2,18},{18,2},{3,19},{19,3},{4,20},{20... | collective-permute-start | bytes 3145736 | tf_op jit(solution)/shard_map/ppermute | solution.py:475
  136.0 2.5 %collective-permute-done.1.got = bf16[4,128,1024]{2,1,0:T(8,128)(2,1)S(1)} collective-permute-done((bf16[4,128,1024]{2,1,0:T(8,128)(2,1)}, bf16[4,128,1024]{2,1,0:T(8,128)(2,1)S(1)}, u32[]{:S(2)}, u32[]{:S(2)}) %collective-permute-start.1) | collective-permute-done | bytes 1048608 | tf_op jit(solution)/shard_map/ppermute | solution.py:475
  140.4 3.2 %collective-permute-start.2 = (bf16[128,1024]{1,0:T(8,128)(2,1)}, bf16[128,1024]{1,0:T(8,128)(2,1)S(1)}, u32[]{:S(2)}, u32[]{:S(2)}) collective-permute-start(bf16[128,1024]{1,0:T(8,128)(2,1)} %get-tuple-element.19), channel_id=1, source_target_pairs={{0,32},{32,64},{64,96},{96,0},{1,33},{33,65},{65,97},{97,1},{2,34}... | collective-permute-start | bytes 786440 | tf_op jit(solution)/shard_map/ppermute | solution.py:478
  143.6 4.4 %collective-permute-start.3 = (bf16[128,1024]{1,0:T(8,128)(2,1)}, bf16[128,1024]{1,0:T(8,128)(2,1)S(1)}, u32[]{:S(2)}, u32[]{:S(2)}) collective-permute-start(bf16[128,1024]{1,0:T(8,128)(2,1)} %get-tuple-element.20), channel_id=1, source_target_pairs={{0,64},{32,96},{64,0},{96,32},{1,65},{33,97},{65,1},{97,33},{2,66}... | collective-permute-start | bytes 786440 | tf_op jit(solution)/shard_map/ppermute | solution.py:478
  148.0 3.2 %collective-permute-start.4 = (bf16[128,1024]{1,0:T(8,128)(2,1)}, bf16[128,1024]{1,0:T(8,128)(2,1)S(1)}, u32[]{:S(2)}, u32[]{:S(2)}) collective-permute-start(bf16[128,1024]{1,0:T(8,128)(2,1)} %get-tuple-element.21), channel_id=1, source_target_pairs={{0,96},{32,0},{64,32},{96,64},{1,97},{33,1},{65,33},{97,65},{2,98}... | collective-permute-start | bytes 786440 | tf_op jit(solution)/shard_map/ppermute | solution.py:478
  151.2 2.3 %all-to-all-done.4 = bf16[64,16,640]{2,1,0:T(8,128)(2,1)S(1)} async-done(((bf16[64,16,640]{2,1,0:T(8,128)(2,1)}), bf16[64,16,640]{2,1,0:T(8,128)(2,1)S(1)}, u32[]{:S(2)}, u32[]{:S(2)}) %all-to-all-start.4) | async-done | bytes 1310752 | tf_op jit(solution)/shard_map/all_to_all | solution.py:40
  155.6 2.3 collective-permute-done.2.came_1
  157.9 6.3 %collective-permute-done.3.came_2 = bf16[128,1024]{1,0:T(8,128)(2,1)S(1)} collective-permute-done((bf16[128,1024]{1,0:T(8,128)(2,1)}, bf16[128,1024]{1,0:T(8,128)(2,1)S(1)}, u32[]{:S(2)}, u32[]{:S(2)}) %collective-permute-start.3) | collective-permute-done | bytes 262176 | tf_op jit(solution)/shard_map/ppermute | solution.py:478
  165.2 10.0 %all-to-all-start.5 = ((bf16[16,64,128]{2,1,0:T(8,128)(2,1)}), bf16[16,64,128]{2,1,0:T(8,128)(2,1)S(1)}, u32[]{:S(2)}, u32[]{:S(2)}) async-start(bf16[16,64,128]{2,1,0:T(8,128)(2,1)} %payload.1), calls=%async_computation.6 | async-start | bytes 524288 | tf_op jit(solution)/shard_map/all_to_all | solution.py:40
  176.5 17.2 %all-to-all-done.5.merged = bf16[16,64,128]{2,1,0:T(8,128)(2,1)S(1)} async-done(((bf16[16,64,128]{2,1,0:T(8,128)(2,1)}), bf16[16,64,128]{2,1,0:T(8,128)(2,1)S(1)}, u32[]{:S(2)}, u32[]{:S(2)}) %all-to-all-start.5) | async-done | bytes 262176 | tf_op jit(solution)/shard_map/all_to_all | solution.py:40
  195.0 10.2 %all-to-all-start.6 = ((bf16[32,80,128]{2,1,0:T(8,128)(2,1)}), bf16[32,80,128]{2,1,0:T(8,128)(2,1)S(1)}, u32[]{:S(2)}, u32[]{:S(2)}) async-start(bf16[32,80,128]{2,1,0:T(8,128)(2,1)} %place.1), calls=%async_computation.7 | async-start | bytes 1310720 | tf_op jit(solution)/shard_map/all_to_all | solution.py:40
  205.3 1.8 reduce-scatter.2.cloned.1.call-done
  207.9 1.9 collective-permute-start
  209.8 8.4 %all-to-all-done.6.owned = bf16[32,80,128]{2,1,0:T(8,128)(2,1)S(1)} async-done(((bf16[32,80,128]{2,1,0:T(8,128)(2,1)}), bf16[32,80,128]{2,1,0:T(8,128)(2,1)S(1)}, u32[]{:S(2)}, u32[]{:S(2)}) %all-to-all-start.6) | async-done | bytes 655392 | tf_op jit(solution)/shard_map/all_to_all | solution.py:40
  218.2 1.4 table_sum.1
  (86 shorter events, 16.4 us)
Async XLA Ops:
  7.2 12.6 %copy-start = (s32[8192]{0:T(1024)S(1)}, s32[8192]{0:T(1024)}, u32[]{:S(2)}) copy-start(s32[8192]{0:T(1024)} %param.11) | copy-start | bytes 98308
  7.2 12.3 %copy-start.7 = (s32[1,2,64]{2,1,0:T(2,128)S(1)}, s32[1,2,64]{2,1,0:T(2,128)}, u32[]{:S(2)}) copy-start(s32[1,2,64]{2,1,0:T(2,128)} %param.10) | copy-start | bytes 1540
  7.2 13.9 %copy-start.8 = (s32[1,2,3]{2,1,0:T(2,128)S(1)}, s32[1,2,3]{2,1,0:T(2,128)}, u32[]{:S(2)}) copy-start(s32[1,2,3]{2,1,0:T(2,128)} %param.9) | copy-start | bytes 76
  7.2 14.1 %copy-start.6 = (bf16[64,32]{0,1:T(8,128)(2,1)S(1)}, bf16[64,32]{0,1:T(8,128)(2,1)}, u32[]{:S(2)}) copy-start(bf16[64,32]{0,1:T(8,128)(2,1)} %param.13) | copy-start | bytes 12292
  7.2 14.3 %copy-start.5 = (bf16[32,256]{1,0:T(8,128)(2,1)S(1)}, bf16[32,256]{1,0:T(8,128)(2,1)}, u32[]{:S(2)}) copy-start(bf16[32,256]{1,0:T(8,128)(2,1)} %param.12) | copy-start | bytes 49156
  9.2 19.8 %all-to-all-start = ((bf16[8,2,2,64,128]{4,3,2,1,0:T(8,128)(2,1)}), bf16[8,2,2,64,128]{4,3,2,1,0:T(8,128)(2,1)S(1)}, u32[]{:S(2)}, u32[]{:S(2)}) async-start(bf16[8,2,2,64,128]{4,3,2,1,0:T(8,128)(2,1)} %split_columns.1), calls=%async_computation | async-start | bytes 1048576 | tf_op jit(solution)/shard_map/all_to_all | solution.py:40
  19.5 93.2 %all-gather.2.cloned.1.call-start = ((), (), s32[]{:S(2)}) async-start(), calls=%async_computation.8 | async-start | bytes 4718592 | tf_op jit(solution)/shard_map/all_gather | solution.py:445
  90.0 22.7 %all-to-all-start.3 = ((bf16[8,8,16,640]{3,2,1,0:T(8,128)(2,1)}), bf16[8,8,16,640]{3,2,1,0:T(8,128)(2,1)S(1)}, u32[]{:S(2)}, u32[]{:S(2)}) async-start(bf16[8,8,16,640]{3,2,1,0:T(8,128)(2,1)} %broadcast_in_dim.62), calls=%async_computation.3 | async-start | bytes 2621440 | tf_op jit(solution)/shard_map/all_to_all | solution.py:40
  112.7 1.1 copy-start.4
  126.8 11.7 %copy-start.1 = (bf16[4,128,1024]{2,1,0:T(8,128)(2,1)S(1)}, bf16[4,128,1024]{2,1,0:T(8,128)(2,1)}, u32[]{:S(2)}) copy-start(bf16[4,128,1024]{2,1,0:T(8,128)(2,1)} %get-tuple-element.16.kept) | copy-start | bytes 3145732
  126.8 26.8 %all-to-all-start.4 = ((bf16[64,16,640]{2,1,0:T(8,128)(2,1)}), bf16[64,16,640]{2,1,0:T(8,128)(2,1)S(1)}, u32[]{:S(2)}, u32[]{:S(2)}) async-start(bf16[64,16,640]{2,1,0:T(8,128)(2,1)} %bitcast.92), calls=%async_computation.4 | async-start | bytes 2621440 | tf_op jit(solution)/shard_map/all_to_all | solution.py:40
  133.5 73.6 %reduce-scatter.2.cloned.1.call-start = ((), (), s32[]{:S(2)}) async-start(), calls=%async_computation.9 | async-start | bytes 884736 | tf_op jit(solution)/shard_map/reduce_scatter | solution.py:489
  133.5 5.0 %collective-permute-start.1 = (bf16[4,128,1024]{2,1,0:T(8,128)(2,1)}, bf16[4,128,1024]{2,1,0:T(8,128)(2,1)S(1)}, u32[]{:S(2)}, u32[]{:S(2)}) collective-permute-start(bf16[4,128,1024]{2,1,0:T(8,128)(2,1)} %get-tuple-element.17), channel_id=1, source_target_pairs={{0,16},{16,0},{1,17},{17,1},{2,18},{18,2},{3,19},{19,3},{4,20},{20... | collective-permute-start | bytes 3145736 | tf_op jit(solution)/shard_map/ppermute | solution.py:475
  139.7 0.7 copy-start.2
  140.4 23.8 %copy-start.3 = (bf16[128,1024]{1,0:T(8,128)(2,1)S(1)}, bf16[128,1024]{1,0:T(8,128)(2,1)}, u32[]{:S(2)}) copy-start(bf16[128,1024]{1,0:T(8,128)(2,1)} %copy-done.2) | copy-start | bytes 786436
  140.4 17.5 %collective-permute-start.2 = (bf16[128,1024]{1,0:T(8,128)(2,1)}, bf16[128,1024]{1,0:T(8,128)(2,1)S(1)}, u32[]{:S(2)}, u32[]{:S(2)}) collective-permute-start(bf16[128,1024]{1,0:T(8,128)(2,1)} %get-tuple-element.19), channel_id=1, source_target_pairs={{0,32},{32,64},{64,96},{96,0},{1,33},{33,65},{65,97},{97,1},{2,34}... | collective-permute-start | bytes 786440 | tf_op jit(solution)/shard_map/ppermute | solution.py:478
  143.6 20.6 %collective-permute-start.3 = (bf16[128,1024]{1,0:T(8,128)(2,1)}, bf16[128,1024]{1,0:T(8,128)(2,1)S(1)}, u32[]{:S(2)}, u32[]{:S(2)}) collective-permute-start(bf16[128,1024]{1,0:T(8,128)(2,1)} %get-tuple-element.20), channel_id=1, source_target_pairs={{0,64},{32,96},{64,0},{96,32},{1,65},{33,97},{65,1},{97,33},{2,66}... | collective-permute-start | bytes 786440 | tf_op jit(solution)/shard_map/ppermute | solution.py:478
  148.0 16.2 %collective-permute-start.4 = (bf16[128,1024]{1,0:T(8,128)(2,1)}, bf16[128,1024]{1,0:T(8,128)(2,1)S(1)}, u32[]{:S(2)}, u32[]{:S(2)}) collective-permute-start(bf16[128,1024]{1,0:T(8,128)(2,1)} %get-tuple-element.21), channel_id=1, source_target_pairs={{0,96},{32,0},{64,32},{96,64},{1,97},{33,1},{65,33},{97,65},{2,98}... | collective-permute-start | bytes 786440 | tf_op jit(solution)/shard_map/ppermute | solution.py:478
  165.2 28.5 %all-to-all-start.5 = ((bf16[16,64,128]{2,1,0:T(8,128)(2,1)}), bf16[16,64,128]{2,1,0:T(8,128)(2,1)S(1)}, u32[]{:S(2)}, u32[]{:S(2)}) async-start(bf16[16,64,128]{2,1,0:T(8,128)(2,1)} %payload.1), calls=%async_computation.6 | async-start | bytes 524288 | tf_op jit(solution)/shard_map/all_to_all | solution.py:40
  195.0 23.2 %all-to-all-start.6 = ((bf16[32,80,128]{2,1,0:T(8,128)(2,1)}), bf16[32,80,128]{2,1,0:T(8,128)(2,1)S(1)}, u32[]{:S(2)}, u32[]{:S(2)}) async-start(bf16[32,80,128]{2,1,0:T(8,128)(2,1)} %place.1), calls=%async_computation.7 | async-start | bytes 1310720 | tf_op jit(solution)/shard_map/all_to_all | solution.py:40
  207.9 11.8 %collective-permute-start = (f32[48,128]{1,0:T(8,128)S(1)}, f32[48,128]{1,0:T(8,128)S(1)}, u32[]{:S(2)}, u32[]{:S(2)}) collective-permute-start(f32[48,128]{1,0:T(8,128)S(1)} %get-tuple-element.32), channel_id=1, source_target_pairs={{0,1},{1,0},{2,3},{3,2},{4,5},{5,4},{6,7},{7,6},{8,9},{9,8},{10,11... | collective-permute-start | bytes 73736 | tf_op jit(solution)/shard_map/ppermute | solution.py:493
Sparse Core Ops, SparseCore 0:
  74.6 37.4 all-gather.1
  154.8 52.2 reduce-scatter.1

commit v12 on v11

--- a/solution.py
+++ b/solution.py
@@ -29,6 +29,7 @@
 HIDDEN = 5 * HEAD_DIM
 PART_ROWS = 32 // ZR
 STEP = 256
+SUM_ROWS = 64
 REACH = 512
 VMEM_SPEC = pl.BlockSpec(memory_space=pltpu.VMEM)
 GRANT = 58
@@ -292,7 +293,7 @@
 
 def weight_sum_kernel(shared, out, done):
     done[...] = jnp.zeros_like(done)
-    out[..., LANES:] = jnp.zeros((YC, 2, 3 * PART_ROWS, LANES), F32)
+    out[:, :, 3 * PART_ROWS :, :] = jnp.zeros((YC, 2, SUM_ROWS - 3 * PART_ROWS, LANES), F32)
     for h in range(YC):
         total = jnp.zeros((PART_ROWS, HIDDEN), F32)
         for x in range(X):
@@ -302,14 +303,14 @@
             for n, col in enumerate((2 * s, 2 * s + 1, 4)):
                 first = n * PART_ROWS
                 block = total[:, col * LANES : (col + 1) * LANES]
-                out[h, s, first : first + PART_ROWS, :LANES] = block
+                out[h, s, first : first + PART_ROWS, :] = block
 
 
 def weight_sum(shared):
     return pl.pallas_call(
         weight_sum_kernel,
         out_shape=(
-            jax.ShapeDtypeStruct((YC, 2, 3 * PART_ROWS, 2 * LANES), F32),
+            jax.ShapeDtypeStruct((YC, 2, SUM_ROWS, LANES), F32),
             jax.ShapeDtypeStruct((8, LANES), F32),
         ),
         in_specs=[VMEM_SPEC],
@@ -487,7 +488,7 @@
 
     low = lax.axis_index("zr")
     rest = lax.psum_scatter(w_sum, "zq", scatter_dimension=0, tiled=True)
-    rest = rest[0, :, :, :LANES]
+    rest = rest[0, :, : 3 * PART_ROWS]
     mine = lax.dynamic_index_in_dim(rest, low, 0, keepdims=False)
     other = lax.dynamic_index_in_dim(rest, 1 - low, 0, keepdims=False)
     other = lax.ppermute(other, "zr", [(0, 1), (1, 0)])
@@ -498,6 +499,7 @@
     grad_out = lax.dynamic_index_in_dim(both_out, z_here & 1, 1, keepdims=False).T
 
     owned = exchange(place(slots.reshape(2 * YC, LANES), tags, merged), DP)
+    owned, grad_proj, grad_out = lax.optimization_barrier((owned, grad_proj, grad_out))
     return (grad_proj, grad_out, table_sum(owned).T)
 
 

time: 229 us -> 226 us (0.987)
  waiting for transfers between devices: 64.1 us -> 60.2 us
    all_to_all x5, waiting for transfers between devices: 51.3 us -> 47.5 us  [exchange(): return lax.all_to_all(value, axes, split_axis=0, concat_axis=0, tiled=True)]
  transfers between devices with their start and end apart: 12 -> 12, of which waited for: 9 -> 9; matrix products, arithmetic and copies ran while one was open for 3% -> 4% of each run, Pallas kernels for 3% -> 2%
where the time goes in v12:
time: 226 us; the launch traced here: 225 us
  waiting for transfers between devices  60.2 us (27%)
  starting transfers between devices  59.4 us (26%)
  blocking collectives  58.4 us (26%)
  Pallas kernels  20.9 us (9%)
  between operations  14.4 us (6%)
  local copies, waits for them, and re-layouts  9.78 us (4%)
    all_to_all x2, blocking collectives, exchange(): return lax.all_to_all(value, axes, split_axis=0, concat_axis=0, tiled=True)  58.4 us
    all_to_all x5, waiting for transfers between devices, exchange(): return lax.all_to_all(value, axes, split_axis=0, concat_axis=0, tiled=True)  47.5 us
    all_to_all x5, starting transfers between devices, exchange(): return lax.all_to_all(value, axes, split_axis=0, concat_axis=0, tiled=True)  42.8 us
    pallas_call x1, Pallas kernels, heads_backward(): pl.pallas_call(heads_kernel, out_shape=(half, half, jax.ShapeDtypeStruct(...  13 us
    ppermute x3, starting transfers between devices, per_device(): lax.ppermute(to_y[step - 1], 'y', [(i, (i + step) % Y) for i in range(Y)])  10.8 us
    ppermute x3, waiting for transfers between devices, per_device(): lax.ppermute(to_y[step - 1], 'y', [(i, (i + step) % Y) for i in range(Y)])  8.63 us
  transfers between devices with their start and end apart: 12, of which 9 were waited for; matrix products, arithmetic and copies ran while one was open for 4% of the time, Pallas kernels for 2%

profile of v12, /device:TPU:1, one launch (start us, length us, event | category | flops | bytes accessed | tf_op | source)
XLA Modules:
  0.0 225.2 jit_solution(7640149159090354543)
XLA Ops:
  7.2 2.0 split_columns.1
  9.2 10.3 %all-to-all-start = ((bf16[8,2,2,64,128]{4,3,2,1,0:T(8,128)(2,1)}), bf16[8,2,2,64,128]{4,3,2,1,0:T(8,128)(2,1)S(1)}, u32[]{:S(2)}, u32[]{:S(2)}) async-start(bf16[8,2,2,64,128]{4,3,2,1,0:T(8,128)(2,1)} %split_columns.1), calls=%async_computation | async-start | bytes 1048576 | tf_op jit(solution)/shard_map/all_to_all | solution.py:41
  21.5 7.5 %all-to-all-done = bf16[8,2,2,64,128]{4,3,2,1,0:T(8,128)(2,1)S(1)} async-done(((bf16[8,2,2,64,128]{4,3,2,1,0:T(8,128)(2,1)}), bf16[8,2,2,64,128]{4,3,2,1,0:T(8,128)(2,1)S(1)}, u32[]{:S(2)}, u32[]{:S(2)}) %all-to-all-start) | async-done | bytes 524320 | tf_op jit(solution)/shard_map/all_to_all | solution.py:41
  29.1 44.5 %all_to_all.35 = bf16[16,22,8,128]{3,2,1,0:T(8,128)(2,1)S(1)} all-to-all(bf16[16,22,8,128]{3,2,1,0:T(8,128)(2,1)S(1)} %pad_maximum_fusion), channel_id=1, replica_groups=mesh['x'=4,'y'=4,'c'=2,'zq'=8,'zr'=2] {'zq','zr'}, dimensions={0} | all-to-all | bytes 1441792 | tf_op jit(solution)/shard_map/all_to_all | solution.py:41
  74.5 13.9 %all_to_all.36 = bf16[8,2,6,8,128]{4,3,2,1,0:T(8,128)(2,1)S(1)} all-to-all(bf16[8,2,6,8,128]{4,3,2,1,0:T(8,128)(2,1)S(1)} %bitcast.93), channel_id=1, replica_groups=mesh['x'=4,'y'=4,'c'=2,'zq'=8,'zr'=2] {'y','c'}, dimensions={0} | all-to-all | bytes 393216 | tf_op jit(solution)/shard_map/all_to_all | solution.py:41
  90.0 5.6 %all-to-all-start.3 = ((bf16[8,8,16,640]{3,2,1,0:T(8,128)(2,1)}), bf16[8,8,16,640]{3,2,1,0:T(8,128)(2,1)S(1)}, u32[]{:S(2)}, u32[]{:S(2)}) async-start(bf16[8,8,16,640]{3,2,1,0:T(8,128)(2,1)} %broadcast_in_dim.67), calls=%async_computation.3 | async-start | bytes 2621440 | tf_op jit(solution)/shard_map/all_to_all | solution.py:41
  96.9 15.8 %all-to-all-done.3 = bf16[8,8,16,640]{3,2,1,0:T(8,128)(2,1)S(1)} async-done(((bf16[8,8,16,640]{3,2,1,0:T(8,128)(2,1)}), bf16[8,8,16,640]{3,2,1,0:T(8,128)(2,1)S(1)}, u32[]{:S(2)}, u32[]{:S(2)}) %all-to-all-start.3) | async-done | bytes 1310752 | tf_op jit(solution)/shard_map/all_to_all | solution.py:41
  113.8 13.0 %heads.1 = (bf16[4,128,1024]{2,1,0:T(8,128)(2,1)}, bf16[4,128,1024]{2,1,0:T(8,128)(2,1)}, bf16[4,8,2,16,640]{4,3,2,1,0:T(8,128)(2,1)}) custom-call(s32[4]{0:T(128)} %pad_add_fusion.info, bf16[8,2,1024,128]{3,2,1,0:T(8,128)(2,1)} %all-gather.2.cloned.1.call-done.packs, bf16[4,2,8,16,640]{4,3,2,1,0:T(8,128)(2,1)} %bitcast.91), custom_call_target="tpu_custom_call" | custom-call | flops 5000000000 | bytes 9000000 | tf_op jit(solution)/shard_map/heads/pallas_call | solution.py:205
  126.8 6.7 %all-to-all-start.6 = ((bf16[64,16,640]{2,1,0:T(8,128)(2,1)}), bf16[64,16,640]{2,1,0:T(8,128)(2,1)S(1)}, u32[]{:S(2)}, u32[]{:S(2)}) async-start(bf16[64,16,640]{2,1,0:T(8,128)(2,1)} %bitcast.92), calls=%async_computation.6 | async-start | bytes 2621440 | tf_op jit(solution)/shard_map/all_to_all | solution.py:41
  133.5 2.5 %collective-permute-start = (bf16[4,128,1024]{2,1,0:T(8,128)(2,1)}, bf16[4,128,1024]{2,1,0:T(8,128)(2,1)S(1)}, u32[]{:S(2)}, u32[]{:S(2)}) collective-permute-start(bf16[4,128,1024]{2,1,0:T(8,128)(2,1)} %get-tuple-element.18), channel_id=1, source_target_pairs={{0,16},{16,0},{1,17},{17,1},{2,18},{18,2},{3,19},{19,3},{4,20},{20... | collective-permute-start | bytes 3145736 | tf_op jit(solution)/shard_map/ppermute | solution.py:476
  136.0 2.5 %collective-permute-done.got = bf16[4,128,1024]{2,1,0:T(8,128)(2,1)S(1)} collective-permute-done((bf16[4,128,1024]{2,1,0:T(8,128)(2,1)}, bf16[4,128,1024]{2,1,0:T(8,128)(2,1)S(1)}, u32[]{:S(2)}, u32[]{:S(2)}) %collective-permute-start) | collective-permute-done | bytes 1048608 | tf_op jit(solution)/shard_map/ppermute | solution.py:476
  140.4 3.2 %collective-permute-start.1 = (bf16[128,1024]{1,0:T(8,128)(2,1)}, bf16[128,1024]{1,0:T(8,128)(2,1)S(1)}, u32[]{:S(2)}, u32[]{:S(2)}) collective-permute-start(bf16[128,1024]{1,0:T(8,128)(2,1)} %get-tuple-element.20), channel_id=1, source_target_pairs={{0,32},{32,64},{64,96},{96,0},{1,33},{33,65},{65,97},{97,1},{2,34}... | collective-permute-start | bytes 786440 | tf_op jit(solution)/shard_map/ppermute | solution.py:479
  143.6 4.4 %collective-permute-start.2 = (bf16[128,1024]{1,0:T(8,128)(2,1)}, bf16[128,1024]{1,0:T(8,128)(2,1)S(1)}, u32[]{:S(2)}, u32[]{:S(2)}) collective-permute-start(bf16[128,1024]{1,0:T(8,128)(2,1)} %get-tuple-element.21), channel_id=1, source_target_pairs={{0,64},{32,96},{64,0},{96,32},{1,65},{33,97},{65,1},{97,33},{2,66}... | collective-permute-start | bytes 786440 | tf_op jit(solution)/shard_map/ppermute | solution.py:479
  148.0 3.2 %collective-permute-start.3 = (bf16[128,1024]{1,0:T(8,128)(2,1)}, bf16[128,1024]{1,0:T(8,128)(2,1)S(1)}, u32[]{:S(2)}, u32[]{:S(2)}) collective-permute-start(bf16[128,1024]{1,0:T(8,128)(2,1)} %get-tuple-element.22), channel_id=1, source_target_pairs={{0,96},{32,0},{64,32},{96,64},{1,97},{33,1},{65,33},{97,65},{2,98}... | collective-permute-start | bytes 786440 | tf_op jit(solution)/shard_map/ppermute | solution.py:479
  151.2 2.3 %all-to-all-done.6 = bf16[64,16,640]{2,1,0:T(8,128)(2,1)S(1)} async-done(((bf16[64,16,640]{2,1,0:T(8,128)(2,1)}), bf16[64,16,640]{2,1,0:T(8,128)(2,1)S(1)}, u32[]{:S(2)}, u32[]{:S(2)}) %all-to-all-start.6) | async-done | bytes 1310752 | tf_op jit(solution)/shard_map/all_to_all | solution.py:41
  155.6 2.3 %collective-permute-done.1.came_1 = bf16[128,1024]{1,0:T(8,128)(2,1)S(1)} collective-permute-done((bf16[128,1024]{1,0:T(8,128)(2,1)}, bf16[128,1024]{1,0:T(8,128)(2,1)S(1)}, u32[]{:S(2)}, u32[]{:S(2)}) %collective-permute-start.1) | collective-permute-done | bytes 262176 | tf_op jit(solution)/shard_map/ppermute | solution.py:479
  157.9 6.3 %collective-permute-done.2.came_2 = bf16[128,1024]{1,0:T(8,128)(2,1)S(1)} collective-permute-done((bf16[128,1024]{1,0:T(8,128)(2,1)}, bf16[128,1024]{1,0:T(8,128)(2,1)S(1)}, u32[]{:S(2)}, u32[]{:S(2)}) %collective-permute-start.2) | collective-permute-done | bytes 262176 | tf_op jit(solution)/shard_map/ppermute | solution.py:479
  165.2 10.0 %all-to-all-start.4 = ((bf16[16,64,128]{2,1,0:T(8,128)(2,1)}), bf16[16,64,128]{2,1,0:T(8,128)(2,1)S(1)}, u32[]{:S(2)}, u32[]{:S(2)}) async-start(bf16[16,64,128]{2,1,0:T(8,128)(2,1)} %payload.1), calls=%async_computation.4 | async-start | bytes 524288 | tf_op jit(solution)/shard_map/all_to_all | solution.py:41
  176.5 16.0 %all-to-all-done.4.merged = bf16[16,64,128]{2,1,0:T(8,128)(2,1)S(1)} async-done(((bf16[16,64,128]{2,1,0:T(8,128)(2,1)}), bf16[16,64,128]{2,1,0:T(8,128)(2,1)S(1)}, u32[]{:S(2)}, u32[]{:S(2)}) %all-to-all-start.4) | async-done | bytes 262176 | tf_op jit(solution)/shard_map/all_to_all | solution.py:41
  193.7 10.2 %all-to-all-start.5 = ((bf16[32,80,128]{2,1,0:T(8,128)(2,1)}), bf16[32,80,128]{2,1,0:T(8,128)(2,1)S(1)}, u32[]{:S(2)}, u32[]{:S(2)}) async-start(bf16[32,80,128]{2,1,0:T(8,128)(2,1)} %place.1), calls=%async_computation.5 | async-start | bytes 1310720 | tf_op jit(solution)/shard_map/all_to_all | solution.py:41
  204.8 3.2 %collective-permute-start.4 = (f32[48,128]{1,0:T(8,128)S(1)}, f32[48,128]{1,0:T(8,128)S(1)}, u32[]{:S(2)}, u32[]{:S(2)}) collective-permute-start(f32[48,128]{1,0:T(8,128)S(1)} %get-tuple-element.38), channel_id=1, source_target_pairs={{0,1},{1,0},{2,3},{3,2},{4,5},{5,4},{6,7},{7,6},{8,9},{9,8},{10,11... | collective-permute-start | bytes 73736 | tf_op jit(solution)/shard_map/ppermute | solution.py:494
  208.0 1.6 collective-permute-done.4
  211.0 5.8 %all-to-all-done.5.owned = bf16[32,80,128]{2,1,0:T(8,128)(2,1)S(1)} async-done(((bf16[32,80,128]{2,1,0:T(8,128)(2,1)}), bf16[32,80,128]{2,1,0:T(8,128)(2,1)S(1)}, u32[]{:S(2)}, u32[]{:S(2)}) %all-to-all-start.5) | async-done | bytes 655392 | tf_op jit(solution)/shard_map/all_to_all | solution.py:41
  216.9 1.5 table_sum.1
  (86 shorter events, 16.4 us)
Async XLA Ops:
  7.2 12.6 %copy-start = (s32[8192]{0:T(1024)S(1)}, s32[8192]{0:T(1024)}, u32[]{:S(2)}) copy-start(s32[8192]{0:T(1024)} %param.11) | copy-start | bytes 98308
  7.2 12.3 %copy-start.7 = (s32[1,2,64]{2,1,0:T(2,128)S(1)}, s32[1,2,64]{2,1,0:T(2,128)}, u32[]{:S(2)}) copy-start(s32[1,2,64]{2,1,0:T(2,128)} %param.10) | copy-start | bytes 1540
  7.2 13.9 %copy-start.8 = (s32[1,2,3]{2,1,0:T(2,128)S(1)}, s32[1,2,3]{2,1,0:T(2,128)}, u32[]{:S(2)}) copy-start(s32[1,2,3]{2,1,0:T(2,128)} %param.9) | copy-start | bytes 76
  7.2 14.1 %copy-start.6 = (bf16[64,32]{0,1:T(8,128)(2,1)S(1)}, bf16[64,32]{0,1:T(8,128)(2,1)}, u32[]{:S(2)}) copy-start(bf16[64,32]{0,1:T(8,128)(2,1)} %param.13) | copy-start | bytes 12292
  7.2 14.3 %copy-start.5 = (bf16[32,256]{1,0:T(8,128)(2,1)S(1)}, bf16[32,256]{1,0:T(8,128)(2,1)}, u32[]{:S(2)}) copy-start(bf16[32,256]{1,0:T(8,128)(2,1)} %param.12) | copy-start | bytes 49156
  9.2 19.8 %all-to-all-start = ((bf16[8,2,2,64,128]{4,3,2,1,0:T(8,128)(2,1)}), bf16[8,2,2,64,128]{4,3,2,1,0:T(8,128)(2,1)S(1)}, u32[]{:S(2)}, u32[]{:S(2)}) async-start(bf16[8,2,2,64,128]{4,3,2,1,0:T(8,128)(2,1)} %split_columns.1), calls=%async_computation | async-start | bytes 1048576 | tf_op jit(solution)/shard_map/all_to_all | solution.py:41
  19.5 93.2 %all-gather.2.cloned.1.call-start = ((), (), s32[]{:S(2)}) async-start(), calls=%async_computation.8 | async-start | bytes 4718592 | tf_op jit(solution)/shard_map/all_gather | solution.py:446
  90.0 22.7 %all-to-all-start.3 = ((bf16[8,8,16,640]{3,2,1,0:T(8,128)(2,1)}), bf16[8,8,16,640]{3,2,1,0:T(8,128)(2,1)S(1)}, u32[]{:S(2)}, u32[]{:S(2)}) async-start(bf16[8,8,16,640]{3,2,1,0:T(8,128)(2,1)} %broadcast_in_dim.67), calls=%async_computation.3 | async-start | bytes 2621440 | tf_op jit(solution)/shard_map/all_to_all | solution.py:41
  112.7 1.1 copy-start.4
  126.8 11.7 %copy-start.1 = (bf16[4,128,1024]{2,1,0:T(8,128)(2,1)S(1)}, bf16[4,128,1024]{2,1,0:T(8,128)(2,1)}, u32[]{:S(2)}) copy-start(bf16[4,128,1024]{2,1,0:T(8,128)(2,1)} %get-tuple-element.17.kept) | copy-start | bytes 3145732
  126.8 26.8 %all-to-all-start.6 = ((bf16[64,16,640]{2,1,0:T(8,128)(2,1)}), bf16[64,16,640]{2,1,0:T(8,128)(2,1)S(1)}, u32[]{:S(2)}, u32[]{:S(2)}) async-start(bf16[64,16,640]{2,1,0:T(8,128)(2,1)} %bitcast.92), calls=%async_computation.6 | async-start | bytes 2621440 | tf_op jit(solution)/shard_map/all_to_all | solution.py:41
  133.5 70.5 %reduce-scatter.2.cloned.1.call-start = ((), (), s32[]{:S(2)}) async-start(), calls=%async_computation.9 | async-start | bytes 589824 | tf_op jit(solution)/shard_map/reduce_scatter | solution.py:490
  133.5 5.0 %collective-permute-start = (bf16[4,128,1024]{2,1,0:T(8,128)(2,1)}, bf16[4,128,1024]{2,1,0:T(8,128)(2,1)S(1)}, u32[]{:S(2)}, u32[]{:S(2)}) collective-permute-start(bf16[4,128,1024]{2,1,0:T(8,128)(2,1)} %get-tuple-element.18), channel_id=1, source_target_pairs={{0,16},{16,0},{1,17},{17,1},{2,18},{18,2},{3,19},{19,3},{4,20},{20... | collective-permute-start | bytes 3145736 | tf_op jit(solution)/shard_map/ppermute | solution.py:476
  139.7 0.7 copy-start.2
  140.4 23.8 %copy-start.3 = (bf16[128,1024]{1,0:T(8,128)(2,1)S(1)}, bf16[128,1024]{1,0:T(8,128)(2,1)}, u32[]{:S(2)}) copy-start(bf16[128,1024]{1,0:T(8,128)(2,1)} %copy-done.2) | copy-start | bytes 786436
  140.4 17.5 %collective-permute-start.1 = (bf16[128,1024]{1,0:T(8,128)(2,1)}, bf16[128,1024]{1,0:T(8,128)(2,1)S(1)}, u32[]{:S(2)}, u32[]{:S(2)}) collective-permute-start(bf16[128,1024]{1,0:T(8,128)(2,1)} %get-tuple-element.20), channel_id=1, source_target_pairs={{0,32},{32,64},{64,96},{96,0},{1,33},{33,65},{65,97},{97,1},{2,34}... | collective-permute-start | bytes 786440 | tf_op jit(solution)/shard_map/ppermute | solution.py:479
  143.6 20.6 %collective-permute-start.2 = (bf16[128,1024]{1,0:T(8,128)(2,1)}, bf16[128,1024]{1,0:T(8,128)(2,1)S(1)}, u32[]{:S(2)}, u32[]{:S(2)}) collective-permute-start(bf16[128,1024]{1,0:T(8,128)(2,1)} %get-tuple-element.21), channel_id=1, source_target_pairs={{0,64},{32,96},{64,0},{96,32},{1,65},{33,97},{65,1},{97,33},{2,66}... | collective-permute-start | bytes 786440 | tf_op jit(solution)/shard_map/ppermute | solution.py:479
  148.0 16.2 %collective-permute-start.3 = (bf16[128,1024]{1,0:T(8,128)(2,1)}, bf16[128,1024]{1,0:T(8,128)(2,1)S(1)}, u32[]{:S(2)}, u32[]{:S(2)}) collective-permute-start(bf16[128,1024]{1,0:T(8,128)(2,1)} %get-tuple-element.22), channel_id=1, source_target_pairs={{0,96},{32,0},{64,32},{96,64},{1,97},{33,1},{65,33},{97,65},{2,98}... | collective-permute-start | bytes 786440 | tf_op jit(solution)/shard_map/ppermute | solution.py:479
  165.2 27.2 %all-to-all-start.4 = ((bf16[16,64,128]{2,1,0:T(8,128)(2,1)}), bf16[16,64,128]{2,1,0:T(8,128)(2,1)S(1)}, u32[]{:S(2)}, u32[]{:S(2)}) async-start(bf16[16,64,128]{2,1,0:T(8,128)(2,1)} %payload.1), calls=%async_computation.4 | async-start | bytes 524288 | tf_op jit(solution)/shard_map/all_to_all | solution.py:41
  193.7 23.1 %all-to-all-start.5 = ((bf16[32,80,128]{2,1,0:T(8,128)(2,1)}), bf16[32,80,128]{2,1,0:T(8,128)(2,1)S(1)}, u32[]{:S(2)}, u32[]{:S(2)}) async-start(bf16[32,80,128]{2,1,0:T(8,128)(2,1)} %place.1), calls=%async_computation.5 | async-start | bytes 1310720 | tf_op jit(solution)/shard_map/all_to_all | solution.py:41
  204.8 4.9 %collective-permute-start.4 = (f32[48,128]{1,0:T(8,128)S(1)}, f32[48,128]{1,0:T(8,128)S(1)}, u32[]{:S(2)}, u32[]{:S(2)}) collective-permute-start(f32[48,128]{1,0:T(8,128)S(1)} %get-tuple-element.38), channel_id=1, source_target_pairs={{0,1},{1,0},{2,3},{3,2},{4,5},{5,4},{6,7},{7,6},{8,9},{9,8},{10,11... | collective-permute-start | bytes 73736 | tf_op jit(solution)/shard_map/ppermute | solution.py:494
Sparse Core Ops, SparseCore 0:
  74.6 37.4 all-gather.1
  154.7 47.8 reduce-scatter.1

commit v13 on v12

--- a/solution.py
+++ b/solution.py
@@ -484,7 +484,9 @@
 
     w_sum, done = weight_sum(shared)
     done, *came = lax.optimization_barrier((done, *came))
-    merged = exchange(payload(own, came, dy_own), SEQ)
+    own = lax.dynamic_index_in_dim(kept, y_here, 0, keepdims=False).astype(F32)
+    own = own + lax.dynamic_index_in_dim(got, y_here, 0, keepdims=False).astype(F32)
+    merged = exchange(payload(own.astype(BF16), came, dy_own), SEQ)
 
     low = lax.axis_index("zr")
     rest = lax.psum_scatter(w_sum, "zq", scatter_dimension=0, tiled=True)

time: 226 us -> 229 us (1.013)
  starting transfers between devices: 59.4 us -> 55.3 us
  waiting for transfers between devices: 60.2 us -> 64.3 us
    all_to_all x5, starting transfers between devices: 42.8 us -> 40.1 us  [exchange(): return lax.all_to_all(value, axes, split_axis=0, concat_axis=0, tiled=True)]
    all_to_all x5, waiting for transfers between devices: 47.5 us -> 49.8 us  [exchange(): return lax.all_to_all(value, axes, split_axis=0, concat_axis=0, tiled=True)]
where the time goes in v13:
time: 229 us; the launch traced here: 228 us
  waiting for transfers between devices  64.3 us (28%)
  blocking collectives  58.4 us (26%)
  starting transfers between devices  55.3 us (24%)
  Pallas kernels  22.1 us (10%)
  between operations  14.4 us (6%)
  local copies, waits for them, and re-layouts  11.5 us (5%)
    all_to_all x2, blocking collectives, exchange(): return lax.all_to_all(value, axes, split_axis=0, concat_axis=0, tiled=True)  58.4 us
    all_to_all x5, waiting for transfers between devices, exchange(): return lax.all_to_all(value, axes, split_axis=0, concat_axis=0, tiled=True)  49.8 us
    all_to_all x5, starting transfers between devices, exchange(): return lax.all_to_all(value, axes, split_axis=0, concat_axis=0, tiled=True)  40.1 us
    pallas_call x1, Pallas kernels, heads_backward(): pl.pallas_call(heads_kernel, out_shape=(half, half, jax.ShapeDtypeStruct(...  13 us
    ppermute x3, starting transfers between devices, per_device(): lax.ppermute(to_y[step - 1], 'y', [(i, (i + step) % Y) for i in range(Y)])  10.7 us
    ppermute x3, waiting for transfers between devices, per_device(): lax.ppermute(to_y[step - 1], 'y', [(i, (i + step) % Y) for i in range(Y)])  9.16 us
  transfers between devices with their start and end apart: 12, of which 9 were waited for; matrix products, arithmetic and copies ran while one was open for 4% of the time, Pallas kernels for 2%

profile of v13, /device:TPU:1, one launch (start us, length us, event | category | flops | bytes accessed | tf_op | source)
XLA Modules:
  0.0 228.3 jit_solution(18168437449976903646)
XLA Ops:
  7.2 2.0 split_columns.1
  9.2 10.3 %all-to-all-start = ((bf16[8,2,2,64,128]{4,3,2,1,0:T(8,128)(2,1)}), bf16[8,2,2,64,128]{4,3,2,1,0:T(8,128)(2,1)S(1)}, u32[]{:S(2)}, u32[]{:S(2)}) async-start(bf16[8,2,2,64,128]{4,3,2,1,0:T(8,128)(2,1)} %split_columns.1), calls=%async_computation | async-start | bytes 1048576 | tf_op jit(solution)/shard_map/all_to_all | solution.py:41
  21.5 7.5 %all-to-all-done = bf16[8,2,2,64,128]{4,3,2,1,0:T(8,128)(2,1)S(1)} async-done(((bf16[8,2,2,64,128]{4,3,2,1,0:T(8,128)(2,1)}), bf16[8,2,2,64,128]{4,3,2,1,0:T(8,128)(2,1)S(1)}, u32[]{:S(2)}, u32[]{:S(2)}) %all-to-all-start) | async-done | bytes 524320 | tf_op jit(solution)/shard_map/all_to_all | solution.py:41
  29.1 44.5 %all_to_all.35 = bf16[16,22,8,128]{3,2,1,0:T(8,128)(2,1)S(1)} all-to-all(bf16[16,22,8,128]{3,2,1,0:T(8,128)(2,1)S(1)} %pad_maximum_fusion), channel_id=1, replica_groups=mesh['x'=4,'y'=4,'c'=2,'zq'=8,'zr'=2] {'zq','zr'}, dimensions={0} | all-to-all | bytes 1441792 | tf_op jit(solution)/shard_map/all_to_all | solution.py:41
  74.5 13.9 %all_to_all.36 = bf16[8,2,6,8,128]{4,3,2,1,0:T(8,128)(2,1)S(1)} all-to-all(bf16[8,2,6,8,128]{4,3,2,1,0:T(8,128)(2,1)S(1)} %bitcast.95), channel_id=1, replica_groups=mesh['x'=4,'y'=4,'c'=2,'zq'=8,'zr'=2] {'y','c'}, dimensions={0} | all-to-all | bytes 393216 | tf_op jit(solution)/shard_map/all_to_all | solution.py:41
  90.0 5.6 %all-to-all-start.3 = ((bf16[8,8,16,640]{3,2,1,0:T(8,128)(2,1)}), bf16[8,8,16,640]{3,2,1,0:T(8,128)(2,1)S(1)}, u32[]{:S(2)}, u32[]{:S(2)}) async-start(bf16[8,8,16,640]{3,2,1,0:T(8,128)(2,1)} %broadcast_in_dim.66), calls=%async_computation.3 | async-start | bytes 2621440 | tf_op jit(solution)/shard_map/all_to_all | solution.py:41
  96.9 15.8 %all-to-all-done.3 = bf16[8,8,16,640]{3,2,1,0:T(8,128)(2,1)S(1)} async-done(((bf16[8,8,16,640]{3,2,1,0:T(8,128)(2,1)}), bf16[8,8,16,640]{3,2,1,0:T(8,128)(2,1)S(1)}, u32[]{:S(2)}, u32[]{:S(2)}) %all-to-all-start.3) | async-done | bytes 1310752 | tf_op jit(solution)/shard_map/all_to_all | solution.py:41
  113.8 13.0 %heads.1 = (bf16[4,128,1024]{2,1,0:T(8,128)(2,1)}, bf16[4,128,1024]{2,1,0:T(8,128)(2,1)}, bf16[4,8,2,16,640]{4,3,2,1,0:T(8,128)(2,1)}) custom-call(s32[4]{0:T(128)} %pad_add_fusion.info, bf16[8,2,1024,128]{3,2,1,0:T(8,128)(2,1)} %all-gather.2.cloned.1.call-done.packs, bf16[4,2,8,16,640]{4,3,2,1,0:T(8,128)(2,1)} %bitcast.94), custom_call_target="tpu_custom_call" | custom-call | flops 5000000000 | bytes 9000000 | tf_op jit(solution)/shard_map/heads/pallas_call | solution.py:205
  126.8 6.7 %all-to-all-start.6 = ((bf16[64,16,640]{2,1,0:T(8,128)(2,1)}), bf16[64,16,640]{2,1,0:T(8,128)(2,1)S(1)}, u32[]{:S(2)}, u32[]{:S(2)}) async-start(bf16[64,16,640]{2,1,0:T(8,128)(2,1)} %bitcast.93), calls=%async_computation.6 | async-start | bytes 2621440 | tf_op jit(solution)/shard_map/all_to_all | solution.py:41
  133.5 2.5 %collective-permute-start = (bf16[4,128,1024]{2,1,0:T(8,128)(2,1)}, bf16[4,128,1024]{2,1,0:T(8,128)(2,1)S(1)}, u32[]{:S(2)}, u32[]{:S(2)}) collective-permute-start(bf16[4,128,1024]{2,1,0:T(8,128)(2,1)} %get-tuple-element.17), channel_id=1, source_target_pairs={{0,16},{16,0},{1,17},{17,1},{2,18},{18,2},{3,19},{19,3},{4,20},{20... | collective-permute-start | bytes 3145736 | tf_op jit(solution)/shard_map/ppermute | solution.py:476
  136.0 2.5 %collective-permute-done.got = bf16[4,128,1024]{2,1,0:T(8,128)(2,1)S(1)} collective-permute-done((bf16[4,128,1024]{2,1,0:T(8,128)(2,1)}, bf16[4,128,1024]{2,1,0:T(8,128)(2,1)S(1)}, u32[]{:S(2)}, u32[]{:S(2)}) %collective-permute-start) | collective-permute-done | bytes 1048608 | tf_op jit(solution)/shard_map/ppermute | solution.py:476
  138.5 1.7 pair_sums.1
  140.2 3.1 %collective-permute-start.1 = (bf16[128,1024]{1,0:T(8,128)(2,1)}, bf16[128,1024]{1,0:T(8,128)(2,1)}, u32[]{:S(2)}, u32[]{:S(2)}) collective-permute-start(bf16[128,1024]{1,0:T(8,128)(2,1)} %get-tuple-element.18), channel_id=1, source_target_pairs={{0,32},{32,64},{64,96},{96,0},{1,33},{33,65},{65,97},{97,1},{2,34}... | collective-permute-start | bytes 786440 | tf_op jit(solution)/shard_map/ppermute | solution.py:479
  143.3 4.4 %collective-permute-start.2 = (bf16[128,1024]{1,0:T(8,128)(2,1)}, bf16[128,1024]{1,0:T(8,128)(2,1)}, u32[]{:S(2)}, u32[]{:S(2)}) collective-permute-start(bf16[128,1024]{1,0:T(8,128)(2,1)} %get-tuple-element.19), channel_id=1, source_target_pairs={{0,64},{32,96},{64,0},{96,32},{1,65},{33,97},{65,1},{97,33},{2,66}... | collective-permute-start | bytes 786440 | tf_op jit(solution)/shard_map/ppermute | solution.py:479
  147.7 3.2 %collective-permute-start.3 = (bf16[128,1024]{1,0:T(8,128)(2,1)}, bf16[128,1024]{1,0:T(8,128)(2,1)}, u32[]{:S(2)}, u32[]{:S(2)}) collective-permute-start(bf16[128,1024]{1,0:T(8,128)(2,1)} %get-tuple-element.20), channel_id=1, source_target_pairs={{0,96},{32,0},{64,32},{96,64},{1,97},{33,1},{65,33},{97,65},{2,98}... | collective-permute-start | bytes 786440 | tf_op jit(solution)/shard_map/ppermute | solution.py:479
  155.1 2.9 %collective-permute-done.1.came_1 = bf16[128,1024]{1,0:T(8,128)(2,1)} collective-permute-done((bf16[128,1024]{1,0:T(8,128)(2,1)}, bf16[128,1024]{1,0:T(8,128)(2,1)}, u32[]{:S(2)}, u32[]{:S(2)}) %collective-permute-start.1) | collective-permute-done | bytes 262176 | tf_op jit(solution)/shard_map/ppermute | solution.py:479
  158.0 6.3 %collective-permute-done.2.came_2 = bf16[128,1024]{1,0:T(8,128)(2,1)} collective-permute-done((bf16[128,1024]{1,0:T(8,128)(2,1)}, bf16[128,1024]{1,0:T(8,128)(2,1)}, u32[]{:S(2)}, u32[]{:S(2)}) %collective-permute-start.2) | collective-permute-done | bytes 262176 | tf_op jit(solution)/shard_map/ppermute | solution.py:479
  165.2 2.1 payload.1
  167.3 10.0 %all-to-all-start.4 = ((bf16[16,64,128]{2,1,0:T(8,128)(2,1)}), bf16[16,64,128]{2,1,0:T(8,128)(2,1)S(1)}, u32[]{:S(2)}, u32[]{:S(2)}) async-start(bf16[16,64,128]{2,1,0:T(8,128)(2,1)} %payload.1), calls=%async_computation.4 | async-start | bytes 524288 | tf_op jit(solution)/shard_map/all_to_all | solution.py:41
  178.6 19.5 %all-to-all-done.4.merged = bf16[16,64,128]{2,1,0:T(8,128)(2,1)S(1)} async-done(((bf16[16,64,128]{2,1,0:T(8,128)(2,1)}), bf16[16,64,128]{2,1,0:T(8,128)(2,1)S(1)}, u32[]{:S(2)}, u32[]{:S(2)}) %all-to-all-start.4) | async-done | bytes 262176 | tf_op jit(solution)/shard_map/all_to_all | solution.py:41
  199.4 7.5 %all-to-all-start.5 = ((bf16[32,80,128]{2,1,0:T(8,128)(2,1)}), bf16[32,80,128]{2,1,0:T(8,128)(2,1)S(1)}, u32[]{:S(2)}, u32[]{:S(2)}) async-start(bf16[32,80,128]{2,1,0:T(8,128)(2,1)} %place.1), calls=%async_computation.5 | async-start | bytes 1310720 | tf_op jit(solution)/shard_map/all_to_all | solution.py:41
  207.8 2.0 collective-permute-start.4
  209.8 2.9 %collective-permute-done.4 = f32[48,128]{1,0:T(8,128)S(1)} collective-permute-done((f32[48,128]{1,0:T(8,128)S(1)}, f32[48,128]{1,0:T(8,128)S(1)}, u32[]{:S(2)}, u32[]{:S(2)}) %collective-permute-start.4) | collective-permute-done | bytes 24608 | tf_op jit(solution)/shard_map/ppermute | solution.py:496
  214.0 6.0 %all-to-all-done.5.owned = bf16[32,80,128]{2,1,0:T(8,128)(2,1)S(1)} async-done(((bf16[32,80,128]{2,1,0:T(8,128)(2,1)}), bf16[32,80,128]{2,1,0:T(8,128)(2,1)S(1)}, u32[]{:S(2)}, u32[]{:S(2)}) %all-to-all-start.5) | async-done | bytes 655392 | tf_op jit(solution)/shard_map/all_to_all | solution.py:41
  (87 shorter events, 18.2 us)
Async XLA Ops:
  7.2 12.6 %copy-start = (s32[8192]{0:T(1024)S(1)}, s32[8192]{0:T(1024)}, u32[]{:S(2)}) copy-start(s32[8192]{0:T(1024)} %param.11) | copy-start | bytes 98308
  7.2 12.3 %copy-start.7 = (s32[1,2,64]{2,1,0:T(2,128)S(1)}, s32[1,2,64]{2,1,0:T(2,128)}, u32[]{:S(2)}) copy-start(s32[1,2,64]{2,1,0:T(2,128)} %param.10) | copy-start | bytes 1540
  7.2 13.9 %copy-start.8 = (s32[1,2,3]{2,1,0:T(2,128)S(1)}, s32[1,2,3]{2,1,0:T(2,128)}, u32[]{:S(2)}) copy-start(s32[1,2,3]{2,1,0:T(2,128)} %param.9) | copy-start | bytes 76
  7.2 14.1 %copy-start.6 = (bf16[64,32]{0,1:T(8,128)(2,1)S(1)}, bf16[64,32]{0,1:T(8,128)(2,1)}, u32[]{:S(2)}) copy-start(bf16[64,32]{0,1:T(8,128)(2,1)} %param.13) | copy-start | bytes 12292
  7.2 14.3 %copy-start.5 = (bf16[32,256]{1,0:T(8,128)(2,1)S(1)}, bf16[32,256]{1,0:T(8,128)(2,1)}, u32[]{:S(2)}) copy-start(bf16[32,256]{1,0:T(8,128)(2,1)} %param.12) | copy-start | bytes 49156
  9.2 19.8 %all-to-all-start = ((bf16[8,2,2,64,128]{4,3,2,1,0:T(8,128)(2,1)}), bf16[8,2,2,64,128]{4,3,2,1,0:T(8,128)(2,1)S(1)}, u32[]{:S(2)}, u32[]{:S(2)}) async-start(bf16[8,2,2,64,128]{4,3,2,1,0:T(8,128)(2,1)} %split_columns.1), calls=%async_computation | async-start | bytes 1048576 | tf_op jit(solution)/shard_map/all_to_all | solution.py:41
  19.5 93.2 %all-gather.2.cloned.1.call-start = ((), (), s32[]{:S(2)}) async-start(), calls=%async_computation.8 | async-start | bytes 4718592 | tf_op jit(solution)/shard_map/all_gather | solution.py:446
  90.0 22.7 %all-to-all-start.3 = ((bf16[8,8,16,640]{3,2,1,0:T(8,128)(2,1)}), bf16[8,8,16,640]{3,2,1,0:T(8,128)(2,1)S(1)}, u32[]{:S(2)}, u32[]{:S(2)}) async-start(bf16[8,8,16,640]{3,2,1,0:T(8,128)(2,1)} %broadcast_in_dim.66), calls=%async_computation.3 | async-start | bytes 2621440 | tf_op jit(solution)/shard_map/all_to_all | solution.py:41
  112.7 1.1 copy-start.4
  126.8 11.7 %copy-start.1 = (bf16[4,128,1024]{2,1,0:T(8,128)(2,1)S(1)}, bf16[4,128,1024]{2,1,0:T(8,128)(2,1)}, u32[]{:S(2)}) copy-start(bf16[4,128,1024]{2,1,0:T(8,128)(2,1)} %get-tuple-element.16.kept) | copy-start | bytes 3145732
  126.8 26.8 %all-to-all-start.6 = ((bf16[64,16,640]{2,1,0:T(8,128)(2,1)}), bf16[64,16,640]{2,1,0:T(8,128)(2,1)S(1)}, u32[]{:S(2)}, u32[]{:S(2)}) async-start(bf16[64,16,640]{2,1,0:T(8,128)(2,1)} %bitcast.93), calls=%async_computation.6 | async-start | bytes 2621440 | tf_op jit(solution)/shard_map/all_to_all | solution.py:41
  133.5 73.5 %reduce-scatter.2.cloned.1.call-start = ((), (), s32[]{:S(2)}) async-start(), calls=%async_computation.9 | async-start | bytes 589824 | tf_op jit(solution)/shard_map/reduce_scatter | solution.py:492
  133.5 5.0 %collective-permute-start = (bf16[4,128,1024]{2,1,0:T(8,128)(2,1)}, bf16[4,128,1024]{2,1,0:T(8,128)(2,1)S(1)}, u32[]{:S(2)}, u32[]{:S(2)}) collective-permute-start(bf16[4,128,1024]{2,1,0:T(8,128)(2,1)} %get-tuple-element.17), channel_id=1, source_target_pairs={{0,16},{16,0},{1,17},{17,1},{2,18},{18,2},{3,19},{19,3},{4,20},{20... | collective-permute-start | bytes 3145736 | tf_op jit(solution)/shard_map/ppermute | solution.py:476
  140.2 17.9 %collective-permute-start.1 = (bf16[128,1024]{1,0:T(8,128)(2,1)}, bf16[128,1024]{1,0:T(8,128)(2,1)}, u32[]{:S(2)}, u32[]{:S(2)}) collective-permute-start(bf16[128,1024]{1,0:T(8,128)(2,1)} %get-tuple-element.18), channel_id=1, source_target_pairs={{0,32},{32,64},{64,96},{96,0},{1,33},{33,65},{65,97},{97,1},{2,34}... | collective-permute-start | bytes 786440 | tf_op jit(solution)/shard_map/ppermute | solution.py:479
  143.3 21.0 %collective-permute-start.2 = (bf16[128,1024]{1,0:T(8,128)(2,1)}, bf16[128,1024]{1,0:T(8,128)(2,1)}, u32[]{:S(2)}, u32[]{:S(2)}) collective-permute-start(bf16[128,1024]{1,0:T(8,128)(2,1)} %get-tuple-element.19), channel_id=1, source_target_pairs={{0,64},{32,96},{64,0},{96,32},{1,65},{33,97},{65,1},{97,33},{2,66}... | collective-permute-start | bytes 786440 | tf_op jit(solution)/shard_map/ppermute | solution.py:479
  147.7 16.6 %collective-permute-start.3 = (bf16[128,1024]{1,0:T(8,128)(2,1)}, bf16[128,1024]{1,0:T(8,128)(2,1)}, u32[]{:S(2)}, u32[]{:S(2)}) collective-permute-start(bf16[128,1024]{1,0:T(8,128)(2,1)} %get-tuple-element.20), channel_id=1, source_target_pairs={{0,96},{32,0},{64,32},{96,64},{1,97},{33,1},{65,33},{97,65},{2,98}... | collective-permute-start | bytes 786440 | tf_op jit(solution)/shard_map/ppermute | solution.py:479
  154.2 0.8 copy-start.3
  164.3 1.0 copy-start.2
  167.3 30.8 %all-to-all-start.4 = ((bf16[16,64,128]{2,1,0:T(8,128)(2,1)}), bf16[16,64,128]{2,1,0:T(8,128)(2,1)S(1)}, u32[]{:S(2)}, u32[]{:S(2)}) async-start(bf16[16,64,128]{2,1,0:T(8,128)(2,1)} %payload.1), calls=%async_computation.4 | async-start | bytes 524288 | tf_op jit(solution)/shard_map/all_to_all | solution.py:41
  199.4 20.6 %all-to-all-start.5 = ((bf16[32,80,128]{2,1,0:T(8,128)(2,1)}), bf16[32,80,128]{2,1,0:T(8,128)(2,1)S(1)}, u32[]{:S(2)}, u32[]{:S(2)}) async-start(bf16[32,80,128]{2,1,0:T(8,128)(2,1)} %place.1), calls=%async_computation.5 | async-start | bytes 1310720 | tf_op jit(solution)/shard_map/all_to_all | solution.py:41
  207.8 4.9 %collective-permute-start.4 = (f32[48,128]{1,0:T(8,128)S(1)}, f32[48,128]{1,0:T(8,128)S(1)}, u32[]{:S(2)}, u32[]{:S(2)}) collective-permute-start(f32[48,128]{1,0:T(8,128)S(1)} %get-tuple-element.36), channel_id=1, source_target_pairs={{0,1},{1,0},{2,3},{3,2},{4,5},{5,4},{6,7},{7,6},{8,9},{9,8},{10,11... | collective-permute-start | bytes 73736 | tf_op jit(solution)/shard_map/ppermute | solution.py:496
Sparse Core Ops, SparseCore 0:
  74.6 37.4 all-gather.1
  155.2 46.7 reduce-scatter.1
